TPU v7x, 128 devices: a whole 4x4x4 slice. The times are simulated.
128 devices in a mesh: fsdp: 16 (over x, y), ctx: 4 (over z_lo, core), tp: 2 (over z_hi).
Axes of the slice: x: 4, y: 4, z: 4 (z_hi: 2, z_lo: 2; z = z_hi * 2 + z_lo), core: 2. Of those that a mesh axis runs over, the one named last changes fastest.
Arguments:
- tokens: bfloat16 [32, 512, 1536], P('fsdp', 'ctx'), may hold values from -6 to 6
- text: bfloat16 [32, 512, 1536], P('fsdp', 'ctx'), may hold values from -6 to 6
- time_embedding: float32 [32, 6, 1536], P('fsdp'), may hold values from -5 to 5
- positions: int32 [3, 32, 512], P(None, 'fsdp', 'ctx'), may hold values from 0 to 15, as said below
- cotangent: bfloat16 [32, 512, 1536], P('fsdp', 'ctx'), may hold values from -6 to 6
- attn_in: float32 [1536, 6, 1536], P(('fsdp', 'ctx'), None, 'tp'), may hold values from -0.15625 to 0.15625
- attn_out: float32 [1536, 2, 1536], P(('fsdp', 'ctx'), None, 'tp'), may hold values from -1.25 to 1.25
- mlp: float32 [1536, 2, 8960], P(('fsdp', 'ctx'), None, 'tp'), may hold values from -0.09375 to 0.09375
- head_vectors: float32 [10, 1536], P(None, 'tp'), may hold values from -1.2 to 1.2
- model_vectors: float32 [11, 1536], replicated, may hold values from -1.2 to 1.2
- up_bias: float32 [8960], P('tp'), may hold values from -0.6 to 0.6
- attn_in_moment: float32 [1536, 6, 1536], P(('fsdp', 'ctx'), None, 'tp'), may hold values from -80 to 80
- attn_out_moment: float32 [1536, 2, 1536], P(('fsdp', 'ctx'), None, 'tp'), may hold values from -80 to 80
- mlp_moment: float32 [1536, 2, 8960], P(('fsdp', 'ctx'), None, 'tp'), may hold values from -80 to 80
- head_moment: float32 [10, 1536], P(None, 'tp'), may hold values from -160 to 160
- model_moment: float32 [11, 1536], replicated, may hold values from -384 to 384
- up_moment: float32 [8960], P('tp'), may hold values from -80 to 80
Outputs:
- layer_out: bfloat16 [32, 512, 1536], P('fsdp', 'ctx')
- grad_tokens: float32 [32, 512, 1536], P('fsdp', 'ctx')
- grad_text: float32 [32, 512, 1536], P('fsdp', 'ctx')
- grad_time: float32 [32, 6, 1536], P('fsdp')
- new_attn_in: float32 [1536, 6, 1536], P(('fsdp', 'ctx'), None, 'tp')
- new_attn_out: float32 [1536, 2, 1536], P(('fsdp', 'ctx'), None, 'tp')
- new_mlp: float32 [1536, 2, 8960], P(('fsdp', 'ctx'), None, 'tp')
- new_attn_in_moment: float32 [1536, 6, 1536], P(('fsdp', 'ctx'), None, 'tp')
- new_attn_out_moment: float32 [1536, 2, 1536], P(('fsdp', 'ctx'), None, 'tp')
- new_mlp_moment: float32 [1536, 2, 8960], P(('fsdp', 'ctx'), None, 'tp')
- new_head_vectors: float32 [10, 1536], P(None, 'tp')
- new_model_vectors: float32 [11, 1536], replicated
- new_up_bias: float32 [8960], P('tp')
- new_head_moment: float32 [10, 1536], P(None, 'tp')
- new_model_moment: float32 [11, 1536], replicated
- new_up_moment: float32 [8960], P('tp')
Inputs may be any that keep to these rules, and one draw needn't show every extreme that they name: `positions`: within each clip the 512 tokens take distinct places numbered 0 to 511 in a random order; a place n has frame n // 256, row (n // 16) % 16 and column n % 16.
All inputs are finite; a program needn't handle non-finite values.
Results may differ from a plain program's by a relative error of at most 0.015.
Values may be sent and summed in bfloat16 or wider, within the bound.
A program may use at most 704 MiB of HBM per device.

v0:
```python
from functools import partial
import math

import jax
import jax.numpy as jnp
from jax import lax
from jax.sharding import PartitionSpec as P

D = 1536
HEAD = 128
MUON_ROWS = 24
NS_STEPS = 5


NORM_EPSILON = 1e-06
ORTHO_EPSILON = 1e-07
HIGHEST_PRECISION = lax.Precision.HIGHEST
NEWTON_FIRST = 3.4445
NEWTON_SECOND = -4.775
NEWTON_THIRD = 2.0315
MOMENTUM = 0.9
DECAY = 0.01
RATE_IN = 0.5
RATE_OUT = 4.0
RATE_MLP = 1.0
RATE_VECTOR = 0.005


def rope_tables(places):
    pair_index = jnp.arange(HEAD // 2, dtype=jnp.int32)
    side_pairs = HEAD // 6
    frame_pairs = (HEAD - 4 * side_pairs) // 2
    part_of = (pair_index >= frame_pairs).astype(jnp.int32) + (
        pair_index >= frame_pairs + side_pairs
    ).astype(jnp.int32)
    offset = jnp.where(
        part_of == 0, 0, jnp.where(part_of == 1, frame_pairs, frame_pairs + side_pairs)
    ).astype(jnp.int32)
    extent = jnp.where(part_of == 0, 2 * frame_pairs, 2 * side_pairs).astype(jnp.float32)
    frequency = jnp.exp(
        (pair_index - offset).astype(jnp.float32) * (-2.0 * math.log(10000.0)) / extent
    )
    chosen = (
        places[0][:, None] * (part_of == 0)
        + places[1][:, None] * (part_of == 1)
        + places[2][:, None] * (part_of == 2)
    )
    angles = chosen.astype(jnp.float32) * frequency
    return (jnp.cos(angles), jnp.sin(angles))


def rotate(values, cosine, sine):
    half_head = HEAD // 2
    front_half = values[..., :half_head]
    back_half = values[..., half_head:]
    return jnp.concatenate(
        [front_half * cosine - back_half * sine, back_half * cosine + front_half * sine], -1
    )


def rotate_back(grads, cosine, sine):
    half_head = HEAD // 2
    front_half = grads[..., :half_head]
    back_half = grads[..., half_head:]
    return jnp.concatenate(
        [front_half * cosine + back_half * sine, back_half * cosine - front_half * sine], -1
    )


def plain_norm(values):
    centred = values - jnp.mean(values, -1, keepdims=True)
    inverse = lax.rsqrt(jnp.mean(centred * centred, -1, keepdims=True) + NORM_EPSILON)
    return (centred * inverse, inverse)


def norm_back(grads, normed, inverse):
    return inverse * (
        grads
        - jnp.mean(grads, -1, keepdims=True)
        - normed * jnp.mean(grads * normed, -1, keepdims=True)
    )


def split_heads(values):
    return values.reshape(values.shape[0], -1, HEAD)


def product(left, right):
    return jnp.dot(left, right, preferred_element_type=jnp.float32)


def contract_last(left, right):
    return lax.dot_general(
        left, right, (((1,), (1,)), ((), ())), preferred_element_type=jnp.float32
    )


def contract_rows(left, right):
    return lax.dot_general(
        left, right, (((0,), (0,)), ((), ())), preferred_element_type=jnp.float32
    )


def column_sum(values):
    return jnp.sum(values, 0, dtype=jnp.float32)


def tensor_total(partial_sum):
    return lax.psum(partial_sum, "tp")


def pair_total(first, second):
    return lax.psum((first, second), "tp")


def attend(query, keys, values):
    scores = jnp.einsum("qhe,khe->hqk", query, keys, preferred_element_type=jnp.float32) * HEAD ** (
        -0.5
    )
    row_peak = jnp.max(scores, -1, keepdims=True)
    log_total = row_peak + jnp.log(jnp.sum(jnp.exp(scores - row_peak), -1, keepdims=True))
    softmax_weights = jnp.exp(scores - log_total).astype(jnp.bfloat16)
    mixed = jnp.einsum("hqk,khe->qhe", softmax_weights, values, preferred_element_type=jnp.float32)
    return (mixed.reshape(mixed.shape[0], -1), log_total)


def attend_back(query, keys, values, log_total, grad_mixed):
    scores = jnp.einsum("qhe,khe->hqk", query, keys, preferred_element_type=jnp.float32) * HEAD ** (
        -0.5
    )
    softmax_weights = jnp.exp(scores - log_total)
    grad_weights = jnp.einsum(
        "qhe,khe->hqk", grad_mixed, values, preferred_element_type=jnp.float32
    )
    row_delta = jnp.sum(softmax_weights * grad_weights, -1, keepdims=True)
    grad_scores = (softmax_weights * (grad_weights - row_delta)).astype(jnp.bfloat16)
    grad_query = jnp.einsum(
        "hqk,khe->qhe", grad_scores, keys, preferred_element_type=jnp.float32
    ) * HEAD ** (-0.5)
    grad_keys = jnp.einsum(
        "hqk,qhe->khe", grad_scores, query, preferred_element_type=jnp.float32
    ) * HEAD ** (-0.5)
    grad_values = jnp.einsum(
        "hqk,qhe->khe",
        softmax_weights.astype(jnp.bfloat16),
        grad_mixed,
        preferred_element_type=jnp.float32,
    )
    return (
        grad_query,
        grad_keys.reshape(grad_keys.shape[0], -1),
        grad_values.reshape(grad_values.shape[0], -1),
    )


def root_back(linear, gain, grads):
    scaled = grads * (1.0 + gain)
    return (scaled, jnp.sum(linear * scaled, -1))


def clip_pass(
    copies,
    head_vectors,
    model_vectors,
    up_bias,
    tokens_in,
    words,
    modulation_row,
    places,
    grad_result,
):
    in_weights, out_weights, mlp_weights = copies
    row_count = tokens_in.shape[0]
    local_width = in_weights.shape[2]
    residual = tokens_in.astype(jnp.float32)
    modulation = model_vectors[5:] + modulation_row
    cosine, sine = rope_tables(places)
    cosine = cosine[:, None, :]
    sine = sine[:, None, :]
    key_two_lin = product(words, in_weights[:, 4]) + head_vectors[6]
    value_two_lin = product(words, in_weights[:, 5]) + head_vectors[7]
    normed_one, inverse_one = plain_norm(residual)
    input_one = (normed_one * (1.0 + modulation[1]) + modulation[0]).astype(jnp.bfloat16)
    query_lin = product(input_one, in_weights[:, 0]) + head_vectors[0]
    key_lin = product(input_one, in_weights[:, 1]) + head_vectors[1]
    value_lin = product(input_one, in_weights[:, 2]) + head_vectors[2]
    square_query, square_key = pair_total(
        jnp.sum(query_lin * query_lin, -1), jnp.sum(key_lin * key_lin, -1)
    )
    inverse_query = lax.rsqrt(square_query[:, None] / D + NORM_EPSILON)
    inverse_key = lax.rsqrt(square_key[:, None] / D + NORM_EPSILON)
    query_rot = rotate(
        split_heads(query_lin * inverse_query * (1.0 + head_vectors[3])), cosine, sine
    ).astype(jnp.bfloat16)
    key_rot = rotate(
        split_heads(key_lin * inverse_key * (1.0 + head_vectors[4])), cosine, sine
    ).astype(jnp.bfloat16)
    value_low = value_lin.astype(jnp.bfloat16)
    all_keys, all_values = (
        lax.all_gather(key_rot.reshape(row_count, local_width), "ctx", axis=0, tiled=True),
        lax.all_gather(value_low, "ctx", axis=0, tiled=True),
    )
    mixed, log_one = attend(query_rot, split_heads(all_keys), split_heads(all_values))
    mixed_low = mixed.astype(jnp.bfloat16)
    branch_one = tensor_total(contract_last(mixed_low, out_weights[:, 0])) + model_vectors[0]
    after_one = residual + modulation[2] * branch_one
    normed_three, inverse_three = plain_norm(after_one)
    input_three = (normed_three * (1.0 + model_vectors[3]) + model_vectors[4]).astype(jnp.bfloat16)
    query_two_lin = product(input_three, in_weights[:, 3]) + head_vectors[5]
    square_query_two, square_key_two = pair_total(
        jnp.sum(query_two_lin * query_two_lin, -1), jnp.sum(key_two_lin * key_two_lin, -1)
    )
    inverse_query_two = lax.rsqrt(square_query_two[:, None] / D + NORM_EPSILON)
    inverse_key_two = lax.rsqrt(square_key_two[:, None] / D + NORM_EPSILON)
    query_two = (query_two_lin * inverse_query_two * (1.0 + head_vectors[8])).astype(jnp.bfloat16)
    key_two = (key_two_lin * inverse_key_two * (1.0 + head_vectors[9])).astype(jnp.bfloat16)
    value_two = value_two_lin.astype(jnp.bfloat16)
    text_keys, text_values = (
        lax.all_gather(key_two, "ctx", axis=0, tiled=True),
        lax.all_gather(value_two, "ctx", axis=0, tiled=True),
    )
    mixed_two, log_two = attend(
        split_heads(query_two), split_heads(text_keys), split_heads(text_values)
    )
    mixed_two_low = mixed_two.astype(jnp.bfloat16)
    branch_two = tensor_total(contract_last(mixed_two_low, out_weights[:, 1])) + model_vectors[1]
    after_two = after_one + branch_two
    normed_two, inverse_two = plain_norm(after_two)
    input_mlp = (normed_two * (1.0 + modulation[4]) + modulation[3]).astype(jnp.bfloat16)
    hidden_lin = product(input_mlp, mlp_weights[:, 0]) + up_bias
    hidden_act, gelu_pullback = jax.vjp(partial(jax.nn.gelu, approximate=True), hidden_lin)
    hidden_low = hidden_act.astype(jnp.bfloat16)
    branch_mlp = tensor_total(contract_last(hidden_low, mlp_weights[:, 1])) + model_vectors[2]
    result = (after_two + modulation[5] * branch_mlp).astype(jnp.bfloat16)
    grads = grad_result.astype(jnp.float32)
    grad_gate_two = jnp.sum(grads * branch_mlp, 0)
    grad_branch_mlp = (grads * modulation[5]).astype(jnp.bfloat16)
    grad_hidden_low = product(grad_branch_mlp, mlp_weights[:, 1])
    grad_hidden = gelu_pullback(grad_hidden_low)[0].astype(jnp.bfloat16)
    grad_input_mlp = tensor_total(contract_last(grad_hidden, mlp_weights[:, 0]))
    grad_shift_two = jnp.sum(grad_input_mlp, 0)
    grad_scale_two = jnp.sum(grad_input_mlp * normed_two, 0)
    grad_after_two = grads + norm_back(
        grad_input_mlp * (1.0 + modulation[4]), normed_two, inverse_two
    )
    grad_branch_two = grad_after_two.astype(jnp.bfloat16)
    grad_mixed_two = product(grad_branch_two, out_weights[:, 1]).astype(jnp.bfloat16)
    grad_query_two, grad_text_keys, grad_text_values = attend_back(
        split_heads(query_two),
        split_heads(text_keys),
        split_heads(text_values),
        log_two,
        split_heads(grad_mixed_two),
    )
    grad_key_two, grad_value_two = (
        lax.psum_scatter(grad_text_keys, "ctx", scatter_dimension=0, tiled=True),
        lax.psum_scatter(grad_text_values, "ctx", scatter_dimension=0, tiled=True),
    )
    grad_query_two = grad_query_two.reshape(row_count, local_width)
    scaled_query_two, local_query_two = root_back(query_two_lin, head_vectors[8], grad_query_two)
    scaled_key_two, local_key_two = root_back(key_two_lin, head_vectors[9], grad_key_two)
    dot_query_two, dot_key_two = pair_total(local_query_two, local_key_two)
    grad_query_two_lin = (
        inverse_query_two * scaled_query_two
        - query_two_lin * inverse_query_two**3 * dot_query_two[:, None] / D
    ).astype(jnp.bfloat16)
    grad_key_two_lin = (
        inverse_key_two * scaled_key_two
        - key_two_lin * inverse_key_two**3 * dot_key_two[:, None] / D
    ).astype(jnp.bfloat16)
    grad_value_two_lin = grad_value_two.astype(jnp.bfloat16)
    grad_input_three, grad_words = pair_total(
        contract_last(grad_query_two_lin, in_weights[:, 3]),
        contract_last(grad_key_two_lin, in_weights[:, 4])
        + contract_last(grad_value_two_lin, in_weights[:, 5]),
    )
    grad_norm_bias = jnp.sum(grad_input_three, 0)
    grad_norm_gain = jnp.sum(grad_input_three * normed_three, 0)
    grad_after_one = grad_after_two + norm_back(
        grad_input_three * (1.0 + model_vectors[3]), normed_three, inverse_three
    )
    grad_gate_one = jnp.sum(grad_after_one * branch_one, 0)
    grad_branch_one = (grad_after_one * modulation[2]).astype(jnp.bfloat16)
    grad_mixed = product(grad_branch_one, out_weights[:, 0]).astype(jnp.bfloat16)
    grad_query_rot, grad_all_keys, grad_all_values = attend_back(
        query_rot, split_heads(all_keys), split_heads(all_values), log_one, split_heads(grad_mixed)
    )
    grad_key_rot, grad_value = (
        lax.psum_scatter(grad_all_keys, "ctx", scatter_dimension=0, tiled=True),
        lax.psum_scatter(grad_all_values, "ctx", scatter_dimension=0, tiled=True),
    )
    grad_query_norm = rotate_back(grad_query_rot, cosine, sine).reshape(row_count, local_width)
    grad_key_norm = rotate_back(split_heads(grad_key_rot), cosine, sine).reshape(
        row_count, local_width
    )
    scaled_query, local_query = root_back(query_lin, head_vectors[3], grad_query_norm)
    scaled_key, local_key = root_back(key_lin, head_vectors[4], grad_key_norm)
    dot_query, dot_key = pair_total(local_query, local_key)
    grad_query_lin = (
        inverse_query * scaled_query - query_lin * inverse_query**3 * dot_query[:, None] / D
    ).astype(jnp.bfloat16)
    grad_key_lin = (
        inverse_key * scaled_key - key_lin * inverse_key**3 * dot_key[:, None] / D
    ).astype(jnp.bfloat16)
    grad_value_lin = grad_value.astype(jnp.bfloat16)
    grad_input_one = tensor_total(
        contract_last(grad_query_lin, in_weights[:, 0])
        + contract_last(grad_key_lin, in_weights[:, 1])
        + contract_last(grad_value_lin, in_weights[:, 2])
    )
    grad_shift_one = jnp.sum(grad_input_one, 0)
    grad_scale_one = jnp.sum(grad_input_one * normed_one, 0)
    grad_tokens = grad_after_one + norm_back(
        grad_input_one * (1.0 + modulation[1]), normed_one, inverse_one
    )
    head_part = jnp.stack(
        [
            column_sum(grad_query_lin),
            column_sum(grad_key_lin),
            column_sum(grad_value_lin),
            jnp.sum(grad_query_norm * query_lin * inverse_query, 0),
            jnp.sum(grad_key_norm * key_lin * inverse_key, 0),
            column_sum(grad_query_two_lin),
            column_sum(grad_key_two_lin),
            column_sum(grad_value_two_lin),
            jnp.sum(grad_query_two * query_two_lin * inverse_query_two, 0),
            jnp.sum(grad_key_two * key_two_lin * inverse_key_two, 0),
        ]
    )
    modulation_grad = jnp.stack(
        [
            grad_shift_one,
            grad_scale_one,
            grad_gate_one,
            grad_shift_two,
            grad_scale_two,
            grad_gate_two,
        ]
    )
    model_part = jnp.concatenate(
        [
            jnp.stack(
                [
                    column_sum(grad_branch_one),
                    column_sum(grad_branch_two),
                    column_sum(grad_branch_mlp),
                    grad_norm_gain,
                    grad_norm_bias,
                ]
            ),
            modulation_grad,
        ],
        0,
    )
    up_part = column_sum(grad_hidden)

    def term(start, count):
        in_part = jnp.stack(
            [
                contract_rows(input_one, grad_query_lin),
                contract_rows(input_one, grad_key_lin),
                contract_rows(input_one, grad_value_lin),
                contract_rows(input_three, grad_query_two_lin),
                contract_rows(words, grad_key_two_lin),
                contract_rows(words, grad_value_two_lin),
            ],
            1,
        )
        out_part = jnp.stack(
            [
                contract_rows(grad_branch_one, mixed_low),
                contract_rows(grad_branch_two, mixed_two_low),
            ],
            1,
        )
        mlp_part = jnp.stack(
            [contract_rows(input_mlp, grad_hidden), contract_rows(grad_branch_mlp, hidden_low)], 1
        )
        return jnp.concatenate(
            [in_part.reshape(count, -1), out_part.reshape(count, -1), mlp_part.reshape(count, -1)],
            1,
        )

    return (result, grad_tokens, grad_words, modulation_grad, head_part, model_part, up_part, term)


def block_view(values):
    return values.reshape(values.shape[0] // MUON_ROWS, MUON_ROWS, values.shape[1], values.shape[2])


def gram_of(blocks):
    return jnp.einsum("bikc,bjkc->bkij", blocks, blocks, precision=HIGHEST_PRECISION)


def gram_total(first, second, third):
    return lax.psum((first, second, third), "tp")


def newton_step(current, gram_matrix):
    square = jnp.einsum("bkij,bkjl->bkil", gram_matrix, gram_matrix, precision=HIGHEST_PRECISION)
    polynomial = NEWTON_SECOND * gram_matrix + NEWTON_THIRD * square
    return NEWTON_FIRST * current + jnp.einsum(
        "bkij,bjkc->bikc", polynomial, current, precision=HIGHEST_PRECISION
    )


def orthogonalize_shards(first_moment, second_moment, third_moment):
    blocks = [block_view(first_moment), block_view(second_moment), block_view(third_moment)]
    squares = lax.psum(
        (
            jnp.sum(blocks[0] * blocks[0], axis=(1, 3)),
            jnp.sum(blocks[1] * blocks[1], axis=(1, 3)),
            jnp.sum(blocks[2] * blocks[2], axis=(1, 3)),
        ),
        "tp",
    )
    current = [
        block / (jnp.sqrt(total)[:, None, :, None] + ORTHO_EPSILON)
        for block, total in zip(blocks, squares)
    ]
    grams = gram_total(gram_of(current[0]), gram_of(current[1]), gram_of(current[2]))
    for newton_turn in range(NS_STEPS):
        if newton_turn > 0:
            grams = gram_total(gram_of(current[0]), gram_of(current[1]), gram_of(current[2]))
        current = [newton_step(block, matrix) for block, matrix in zip(current, grams)]
    return (
        current[0].reshape(first_moment.shape),
        current[1].reshape(second_moment.shape),
        current[2].reshape(third_moment.shape),
    )


def body(
    tokens,
    text,
    time_embedding,
    positions,
    cotangent,
    attn_in,
    attn_out,
    mlp,
    head_vectors,
    model_vectors,
    up_bias,
    attn_in_moment,
    attn_out_moment,
    mlp_moment,
    head_moment,
    model_moment,
    up_moment,
):
    micro_count = tokens.shape[0]
    local_rows = attn_in.shape[0]
    local_width = attn_in.shape[2]
    local_hidden = mlp.shape[2]
    grad_rows = jnp.zeros((local_rows, 8 * local_width + 2 * local_hidden), jnp.float32)
    head_sums = jnp.zeros(head_vectors.shape, jnp.float32)
    model_sums = jnp.zeros(model_vectors.shape, jnp.float32)
    up_sums = jnp.zeros(up_bias.shape, jnp.float32)
    results, token_grads, word_grads, time_parts = ([], [], [], [])
    for batch_index in range(micro_count):
        copies = (
            lax.all_gather(attn_in.astype(jnp.bfloat16), ("fsdp", "ctx"), axis=0, tiled=True),
            lax.all_gather(attn_out.astype(jnp.bfloat16), ("fsdp", "ctx"), axis=0, tiled=True),
            lax.all_gather(mlp.astype(jnp.bfloat16), ("fsdp", "ctx"), axis=0, tiled=True),
        )
        outcome = clip_pass(
            copies,
            head_vectors,
            model_vectors,
            up_bias,
            tokens[batch_index],
            text[batch_index],
            time_embedding[batch_index],
            positions[:, batch_index],
            cotangent[batch_index],
        )
        result, grad_tokens, grad_words, modulation_grad, head_part, model_part, up_part, term = (
            outcome
        )
        grad_rows = grad_rows + lax.psum_scatter(
            term(jnp.int32(0), lax.axis_size(("fsdp", "ctx")) * local_rows),
            ("fsdp", "ctx"),
            scatter_dimension=0,
            tiled=True,
        )
        head_sums = head_sums + head_part
        model_sums = model_sums + model_part
        up_sums = up_sums + up_part
        results.append(result)
        token_grads.append(grad_tokens)
        word_grads.append(grad_words)
        time_parts.append(modulation_grad)
    head_total, model_total, up_total = lax.psum((head_sums, model_sums, up_sums), ("fsdp", "ctx"))
    time_total = lax.psum(jnp.stack(time_parts), "ctx")
    grad_in = grad_rows[:, : 6 * local_width].reshape(local_rows, 6, local_width)
    grad_out = grad_rows[:, 6 * local_width : 8 * local_width].reshape(local_rows, 2, local_width)
    grad_mlp = grad_rows[:, 8 * local_width :].reshape(local_rows, 2, local_hidden)
    new_in_moment = MOMENTUM * attn_in_moment + grad_in
    new_out_moment = MOMENTUM * attn_out_moment + grad_out
    new_mlp_moment = MOMENTUM * mlp_moment + grad_mlp
    in_direction, out_direction, mlp_direction = orthogonalize_shards(
        new_in_moment, new_out_moment, new_mlp_moment
    )
    new_attn_in = attn_in * (1.0 - RATE_IN * DECAY) - RATE_IN * in_direction
    new_attn_out = attn_out * (1.0 - RATE_OUT * DECAY) - RATE_OUT * out_direction
    new_mlp = mlp * (1.0 - RATE_MLP * DECAY) - RATE_MLP * mlp_direction
    new_head_moment = MOMENTUM * head_moment + head_total
    new_model_moment = MOMENTUM * model_moment + model_total
    new_up_moment = MOMENTUM * up_moment + up_total
    new_head = head_vectors - RATE_VECTOR * new_head_moment
    new_model = model_vectors - RATE_VECTOR * new_model_moment
    new_up = up_bias - RATE_VECTOR * new_up_moment
    return (
        jnp.stack(results),
        jnp.stack(token_grads),
        jnp.stack(word_grads),
        time_total,
        new_attn_in,
        new_attn_out,
        new_mlp,
        new_in_moment,
        new_out_moment,
        new_mlp_moment,
        new_head,
        new_model,
        new_up,
        new_head_moment,
        new_model_moment,
        new_up_moment,
    )


def solution(mesh):
    in_specs = (
        P("fsdp", "ctx", None),
        P("fsdp", "ctx", None),
        P("fsdp", None, None),
        P(None, "fsdp", "ctx"),
        P("fsdp", "ctx", None),
        P(("fsdp", "ctx"), None, "tp"),
        P(("fsdp", "ctx"), None, "tp"),
        P(("fsdp", "ctx"), None, "tp"),
        P(None, "tp"),
        P(),
        P("tp"),
        P(("fsdp", "ctx"), None, "tp"),
        P(("fsdp", "ctx"), None, "tp"),
        P(("fsdp", "ctx"), None, "tp"),
        P(None, "tp"),
        P(),
        P("tp"),
    )
    out_specs = (
        P("fsdp", "ctx", None),
        P("fsdp", "ctx", None),
        P("fsdp", "ctx", None),
        P("fsdp", None, None),
        P(("fsdp", "ctx"), None, "tp"),
        P(("fsdp", "ctx"), None, "tp"),
        P(("fsdp", "ctx"), None, "tp"),
        P(("fsdp", "ctx"), None, "tp"),
        P(("fsdp", "ctx"), None, "tp"),
        P(("fsdp", "ctx"), None, "tp"),
        P(None, "tp"),
        P(),
        P("tp"),
        P(None, "tp"),
        P(),
        P("tp"),
    )
    return jax.shard_map(body, mesh=mesh, in_specs=in_specs, out_specs=out_specs, check_vma=False)
```

profile of v0, /device:TPU:1, one launch (start us, length us, event | category | flops | bytes accessed | tf_op | source)
XLA Modules:
  0.0 2906.9 jit_solution(5013345736567264497)
XLA Ops:
  23.3 110.5 %all-gather.4.cloned.1.call-done = bf16[1536,6,768]{2,0,1:T(8,128)(2,1)} async-done(((bf16[24,6,768]{2,0,1:T(8,128)(2,1)}), bf16[1536,6,768]{2,0,1:T(8,128)(2,1)}) %all-gather.4.cloned.1.call-update) | async-done | bytes 14155792 | tf_op jit(solution)/shard_map/all_gather | solution.py:463
  199.0 11.1 all_gather.38
  225.6 16.8 all-gather.6.cloned.1.call-done
  264.0 14.3 all_gather.45
  284.4 27.9 all-reduce.36.cloned.1.call-done
  363.3 58.4 %all-reduce.34.cloned.1.call-done = (f32[128,1536]{1,0:T(8,128)}, f32[128,1536]{1,0:T(8,128)}) async-done(((f32[128,1536]{1,0:T(8,128)}, f32[128,1536]{1,0:T(8,128)}), (f32[128,1536]{1,0:T(8,128)}, f32[128,1536]{1,0:T(8,128)})) %all-reduce.34.cloned.1.call-update) | async-done | bytes 1572880 | tf_op jit(solution)/shard_map/psum | solution.py:109
  424.4 155.0 %all-gather.8.cloned.1.call-done = bf16[1536,2,4480]{2,0,1:T(8,128)(2,1)} async-done(((bf16[24,2,4480]{2,0,1:T(8,128)(2,1)}), bf16[1536,2,4480]{2,0,1:T(8,128)(2,1)}) %all-gather.8.cloned.1.call-update) | async-done | bytes 27525136 | tf_op jit(solution)/shard_map/all_gather | solution.py:465
  630.4 60.1 %all-reduce.32.cloned.1.call-done = (f32[128,1536]{1,0:T(8,128)}, f32[128,1536]{1,0:T(8,128)}) async-done(((f32[128,1536]{1,0:T(8,128)}, f32[128,1536]{1,0:T(8,128)}), (f32[128,1536]{1,0:T(8,128)}, f32[128,1536]{1,0:T(8,128)})) %all-reduce.32.cloned.1.call-update) | async-done | bytes 1572880 | tf_op jit(solution)/shard_map/psum | solution.py:109
  748.1 48.4 %all-reduce.30.cloned.1.call-done = (f32[128,1536]{1,0:T(8,128)}, f32[128,1536]{1,0:T(8,128)}) async-done(((f32[128,1536]{1,0:T(8,128)}, f32[128,1536]{1,0:T(8,128)}), (f32[128,1536]{1,0:T(8,128)}, f32[128,1536]{1,0:T(8,128)})) %all-reduce.30.cloned.1.call-update) | async-done | bytes 1572880 | tf_op jit(solution)/shard_map/psum | solution.py:113
  826.9 12.9 convolution_bitcast_fusion.3
  839.8 11.3 convolution_bitcast_fusion.1
  851.1 11.4 convolution_bitcast_fusion
  862.6 11.2 convolution_bitcast_fusion.2
  875.5 36.8 %pad_maximum_fusion = f32[1536,2,4480]{2,0,1:T(8,128)} fusion(f32[1536,1,4480]{2,0,1:T(8,128)} %convolution_bitcast_fusion.2, f32[1536,1,4480]{2,0,1:T(8,128)} %convolution_bitcast_fusion.3), kind=kLoop, calls=%fused_computation.1 | loop fusion | flops 13762560 | bytes 110100480 | tf_op jit(solution)/shard_map/stack | solution.py:376
  914.2 38.0 %pad_maximum_fusion.1 = f32[1536,2,4480]{2,0,1:T(8,128)} fusion(f32[1536,1,4480]{2,0,1:T(8,128)} %convolution_bitcast_fusion, f32[1536,1,4480]{2,0,1:T(8,128)} %convolution_bitcast_fusion.1), kind=kLoop, calls=%fused_computation.2 | loop fusion | flops 13762560 | bytes 110100480 | tf_op jit(solution)/shard_map/stack | solution.py:376
  952.2 54.6 %copy.350 = f32[1536,2,4480]{0,2,1:T(8,128)} copy(f32[1536,2,4480]{2,0,1:T(8,128)} %pad_maximum_fusion) | data formatting | bytes 110100480 | tf_op jit(solution)/shard_map/stack | solution.py:376
  1006.8 54.6 %copy.351 = f32[1536,2,4480]{0,2,1:T(8,128)} copy(f32[1536,2,4480]{2,0,1:T(8,128)} %pad_maximum_fusion.1) | data formatting | bytes 110100480 | tf_op jit(solution)/shard_map/stack | solution.py:376
  1210.4 82.4 %all-reduce.28.cloned.1.call-done = (f32[128,1536]{1,0:T(8,128)}, f32[128,1536]{1,0:T(8,128)}, f32[128,1536]{1,0:T(8,128)}, f32[128,1536]{1,0:T(8,128)}, f32[1,1...) async-done(((f32[128,1536]{1,0:T(8,128)}, f32[128,1536]{1,0:T(8,128)}, f32[128,1536]{1,0:T(8,128)}, f32[128,1536]{1,0:T(8,128)}, f32[1,128,1536]{2,1,0:T(8,128)}, ...) | async-done | bytes 4718608 | tf_op jit(solution)/shard_map/psum | solution.py:109
  1301.7 95.3 %maximum_add_fusion = f32[1536,15104]{0,1:T(8,128)} fusion(f32[1536,8960]{0,1:T(8,128)} %bitcast.925, f32[1536,1536]{0,1:T(8,128)} %bitcast.927, f32[1536,4608]{0,1:T(8,128)} %bitcast.100, f32[1536,8960]{0,1:T(8,128)} %bitcast.926, f32[1536,1536]{0,1:T(8,128)} %bitcast.928, f32[1536,4608]{0,1:T(8,128)} %bitcast.117), kind=kLoop, calls=%fused_computation | loop fusion | flops 115998720 | bytes 278396928 | tf_op jit(solution)/shard_map/add | solution.py:481
  1397.0 90.7 %copy.399 = f32[1536,15104]{1,0:T(8,128)} copy(f32[1536,15104]{0,1:T(8,128)} %maximum_add_fusion) | data formatting | bytes 185597952
  1499.8 273.5 %all-reduce = (f32[10,768]{1,0:T(8,128)S(1)}, f32[4480]{0:T(1024)S(1)}) all-reduce(f32[10,768]{1,0:T(8,128)S(1)} %add.1004, f32[4480]{0:T(1024)} %add.1008), channel_id=1, replica_groups=mesh['fsdp'=16,'ctx'=4,'tp'=2] {'fsdp','ctx'}, use_global_device_ids=true, to_apply=%region_146.147 | all-reduce | flops 12160 | bytes 97280 | tf_op jit(solution)/shard_map/psum | solution.py:494
  1782.4 30.3 %all-reduce.24.cloned.1.call-done = f32[2,6,1536]{2,1,0:T(8,128)} async-done(((f32[2,6,1536]{2,1,0:T(8,128)}), f32[2,6,1536]{2,1,0:T(8,128)}) %all-reduce.24.cloned.1.call-update) | async-done | bytes 73744 | tf_op jit(solution)/shard_map/psum | solution.py:495
  1814.3 992.8 %reduce-scatter.28.cloned.1.call-done = f32[24,15104]{1,0:T(8,128)} async-done(((f32[1536,15104]{1,0:T(8,128)}), f32[24,15104]{1,0:T(8,128)}) %reduce-scatter.28.cloned.1.call-update) | async-done | bytes 1450000
  2827.5 10.8 all-reduce.5
  (954 shorter events, 579.7 us)
Async XLA Ops:
  7.2 126.6 %all-gather.4.cloned.1.call-start = ((), (), s32[]{:S(2)}) async-start(), calls=%async_computation.9 | async-start | bytes 14376960 | tf_op jit(solution)/shard_map/all_gather | solution.py:463
  9.0 233.4 %all-gather.6.cloned.1.call-start = ((), (), s32[]{:S(2)}) async-start(), calls=%async_computation.10 | async-start | bytes 4792320 | tf_op jit(solution)/shard_map/all_gather | solution.py:464
  10.7 301.6 %all-reduce.36.cloned.1.call-start = ((), (), s32[]{:S(2)}) async-start(), calls=%async_computation.27 | async-start | bytes 3145728 | tf_op jit(solution)/shard_map/psum | solution.py:109
  249.4 172.3 %all-reduce.34.cloned.1.call-start = ((), (), s32[]{:S(2)}) async-start(), calls=%async_computation.26 | async-start | bytes 3145728 | tf_op jit(solution)/shard_map/psum | solution.py:109
  362.2 217.2 %all-gather.8.cloned.1.call-start = ((), (), s32[]{:S(2)}) async-start(), calls=%async_computation.11 | async-start | bytes 27955200 | tf_op jit(solution)/shard_map/all_gather | solution.py:465
  363.1 327.5 %all-reduce.32.cloned.1.call-start = ((), (), s32[]{:S(2)}) async-start(), calls=%async_computation.25 | async-start | bytes 3145728 | tf_op jit(solution)/shard_map/psum | solution.py:109
  423.8 403.0 %copy-start.10 = (f32[128,1536]{1,0:T(8,128)}, f32[128,1536]{1,0:T(8,128)S(1)}, u32[]{:S(2)}) copy-start(f32[128,1536]{1,0:T(8,128)S(1)} %get-tuple-element.249) | copy-start | bytes 2359300
  423.9 415.9 %copy-start.12 = (f32[128,1536]{1,0:T(8,128)}, f32[128,1536]{1,0:T(8,128)S(1)}, u32[]{:S(2)}) copy-start(f32[128,1536]{1,0:T(8,128)S(1)} %get-tuple-element.309) | copy-start | bytes 2359300
  630.2 166.3 %all-reduce.30.cloned.1.call-start = ((), (), s32[]{:S(2)}) async-start(), calls=%async_computation.24 | async-start | bytes 3145728 | tf_op jit(solution)/shard_map/psum | solution.py:113
  736.1 368.5 %reduce-scatter.24.cloned.1.call-start = ((), (), s32[]{:S(2)}) async-start(), calls=%async_computation.18 | async-start | bytes 1966080 | tf_op jit(solution)/shard_map/reduce_scatter | solution.py:256
  741.9 362.7 %reduce-scatter.20.cloned.1.call-start = ((), (), s32[]{:S(2)}) async-start(), calls=%async_computation.16 | async-start | bytes 1966080 | tf_op jit(solution)/shard_map/reduce_scatter | solution.py:256
  748.1 358.6 %reduce-scatter.16.cloned.1.call-start = ((), (), s32[]{:S(2)}) async-start(), calls=%async_computation.14 | async-start | bytes 1966080 | tf_op jit(solution)/shard_map/reduce_scatter | solution.py:289
  813.8 296.6 %reduce-scatter.12.cloned.1.call-start = ((), (), s32[]{:S(2)}) async-start(), calls=%async_computation.12 | async-start | bytes 1966080 | tf_op jit(solution)/shard_map/reduce_scatter | solution.py:289
  823.7 312.5 %reduce-scatter.22.cloned.1.call-start = ((), (), s32[]{:S(2)}) async-start(), calls=%async_computation.17 | async-start | bytes 1966080 | tf_op jit(solution)/shard_map/reduce_scatter | solution.py:257
  826.8 326.0 %reduce-scatter.14.cloned.1.call-start = ((), (), s32[]{:S(2)}) async-start(), calls=%async_computation.13 | async-start | bytes 1966080 | tf_op jit(solution)/shard_map/reduce_scatter | solution.py:290
  875.5 280.9 %reduce-scatter.18.cloned.1.call-start = ((), (), s32[]{:S(2)}) async-start(), calls=%async_computation.15 | async-start | bytes 1966080 | tf_op jit(solution)/shard_map/reduce_scatter | solution.py:290
  914.0 246.0 %reduce-scatter.26.cloned.1.call-start = ((), (), s32[]{:S(2)}) async-start(), calls=%async_computation.19 | async-start | bytes 1966080 | tf_op jit(solution)/shard_map/reduce_scatter | solution.py:257
  1090.5 202.4 %all-reduce.28.cloned.1.call-start = ((), (), s32[]{:S(2)}) async-start(), calls=%async_computation.23 | async-start | bytes 9437184 | tf_op jit(solution)/shard_map/psum | solution.py:109
  1163.7 617.1 %all-reduce.26.cloned.1.call-start = ((), (), s32[]{:S(2)}) async-start(), calls=%async_computation.21 | async-start | bytes 196608 | tf_op jit(solution)/shard_map/psum | solution.py:494
  1300.9 511.8 %all-reduce.24.cloned.1.call-start = ((), (), s32[]{:S(2)}) async-start(), calls=%async_computation.20 | async-start | bytes 196608 | tf_op jit(solution)/shard_map/psum | solution.py:495
  1301.6 1505.5 %reduce-scatter.28.cloned.1.call-start = ((), (), s32[]{:S(2)}) async-start(), calls=%async_computation.22 | async-start | bytes 94248960
  1487.8 290.4 %copy-start.75 = (f32[1,128,1536]{2,1,0:T(8,128)S(1)}, f32[1,128,1536]{2,1,0:T(8,128)}, u32[]{:S(2)}) copy-start(f32[1,128,1536]{2,1,0:T(8,128)} %get-tuple-element.272) | copy-start | bytes 2359300
  1487.9 290.4 %copy-start.76 = (f32[1,128,1536]{2,1,0:T(8,128)S(1)}, f32[1,128,1536]{2,1,0:T(8,128)}, u32[]{:S(2)}) copy-start(f32[1,128,1536]{2,1,0:T(8,128)} %get-tuple-element.273) | copy-start | bytes 2359300
  1779.5 1029.0 %copy-start.161 = (f32[24,2,768]{2,1,0:T(2,128)S(1)}, f32[24,2,768]{2,1,0:T(2,128)}, u32[]{:S(2)}) copy-start(f32[24,2,768]{2,1,0:T(2,128)} %param.29) | copy-start | bytes 442372
  (261 other events, 5259.9 us)
Sparse Core Ops, SparseCore 0:
  10.3 123.4 all-gather.3
  136.0 106.3 all-gather.5
  249.5 62.6 all-reduce.35
  362.3 59.3 all-reduce.33
  423.8 155.5 all-gather.7
  630.3 60.2 all-reduce.31
  736.3 60.1 all-reduce.29
  798.9 23.4 reduce-scatter.23
  824.8 24.9 reduce-scatter.19
  852.1 24.9 reduce-scatter.15
  879.5 24.9 reduce-scatter.11
  906.7 24.9 reduce-scatter.21
  934.7 24.9 reduce-scatter.13
  962.5 24.9 reduce-scatter.17
  1090.6 23.0 reduce-scatter.25
  1163.7 129.0 all-reduce.27
  1301.0 473.5 all-reduce.25
  1777.5 35.1 all-reduce.23
  1815.2 991.8 reduce-scatter.27
where the time goes:
time: 2930 us; the launch traced here: 2910 us
  waiting for transfers between devices  1580 us (54%)
  blocking collectives  434 us (15%)
  matrix products  303 us (10%)
  local copies, waits for them, and re-layouts  299 us (10%)
  other arithmetic  267 us (9%)
    unnamed x20, waiting for transfers between devices  993 us
    psum x1, blocking collectives, body(): lax.psum((head_sums, model_sums, up_sums), ('fsdp', 'ctx'))  274 us
    psum x4, waiting for transfers between devices, tensor_total(): return lax.psum(partial_sum, 'tp')  229 us
    all_gather x1, waiting for transfers between devices, body(): lax.all_gather(mlp.astype(jnp.bfloat16), ('fsdp', 'ctx'), axis=0, tiled=T...  155 us
    unnamed x551, local copies, waits for them, and re-layouts  124 us
    all_gather x1, waiting for transfers between devices, body(): lax.all_gather(attn_in.astype(jnp.bfloat16), ('fsdp', 'ctx'), axis=0, til...  110 us
    another operation x2, local copies, waits for them, and re-layouts, term(): jnp.stack([contract_rows(input_mlp, grad_hidden), contract_rows(grad_bran...  109 us
    add x1, other arithmetic, body(): grad_rows + lax.psum_scatter(term(jnp.int32(0), lax.axis_size(('fsdp', 'c...  95.3 us
  transfers between devices with their start and end apart: 19, of which 10 were waited for; matrix products, arithmetic and copies ran while one was open for 24% of the time, Pallas kernels for 0%

commit v1 on v0

v1 whole, which is shorter than its diff:
```python
from functools import partial
import math

import jax
import jax.numpy as jnp
from jax import lax
from jax.experimental import pallas as pl
from jax.experimental.pallas import tpu as pltpu
from jax.sharding import PartitionSpec as P

D = 1536
HEAD = 128
ROWS = 24
HEADS = 3
NORM_EPSILON = 1e-06
ORTHO_EPSILON = 1e-07
NEWTON_FIRST = 3.4445
NEWTON_SECOND = -4.775
NEWTON_THIRD = 2.0315
NS_STEPS = 5
MOMENTUM = 0.9
DECAY = 0.01
RATE_IN = 0.5
RATE_OUT = 4.0
RATE_MLP = 1.0
RATE_VECTOR = 0.005
HIGHEST = lax.Precision.HIGHEST

MESH = pl.DeviceIdType.MESH
BF = jnp.bfloat16
F32 = jnp.float32

SIDE = 4
TOK = 128
SEQ = SIDE * TOK
HW = HEADS * HEAD
FF_REAL = 2240
FF = 2304
C_IN, C_OUT, C_UP, C_DOWN = 0, 6 * HW, 8 * HW, 8 * HW + FF
COLS = 8 * HW + 2 * FF
HALF = COLS // 2
QUARTER = HALF // 2
PAIR = 2 * ROWS
VMEM_LIMIT = 60 * 1024 * 1024


def here():
    f = lax.axis_index("fsdp")
    c = lax.axis_index("ctx")
    t = lax.axis_index("tp")
    x, y = lax.div(f, SIDE), lax.rem(f, SIDE)
    zl, core = lax.div(c, 2), lax.rem(c, 2)
    return x, y, 2 * t + zl, core


def chip(x, y, z, core):
    x, y, z = lax.rem(x + SIDE, SIDE), lax.rem(y + SIDE, SIDE), lax.rem(z + SIDE, SIDE)
    return {"fsdp": x * SIDE + y, "ctx": lax.rem(z, 2) * 2 + core, "tp": lax.div(z, 2)}


def block_of(z):
    z = lax.rem(z + SIDE, SIDE)
    return 2 * lax.rem(z, 2) + lax.div(z, 2)


def greet(devices):
    barrier = pltpu.get_barrier_semaphore()
    for device in devices:
        pl.semaphore_signal(barrier, inc=1, device_id=device, device_id_type=MESH)
    pl.semaphore_wait(barrier, len(devices))


def column(x, y, z, core):
    return [chip(x, y, z + k, core) for k in (1, 2, 3)] + [
        chip(x, y, z + k, 1 - core) for k in range(4)
    ]


def remote(src, dst, send, recv, device):
    return pltpu.make_async_remote_copy(
        src_ref=src, dst_ref=dst, send_sem=send, recv_sem=recv, device_id=device, device_id_type=MESH
    )


def params(cid):
    return pltpu.CompilerParams(
        collective_id=cid, has_side_effects=True, vmem_limit_bytes=VMEM_LIMIT
    )


VM = pl.BlockSpec(memory_space=pltpu.VMEM)
HB = pl.BlockSpec(memory_space=pltpu.HBM)


def gather_kernel(
    wsend, tok, txt, cot, pos, wg, tok_all, txt_all, cot_all, pos_all,
    wrecv, own, wx_s, wx_r, ac_s, ac_r, loc, xs, xr, ks, kr,
):
    x, y, z, core = here()
    zl = lax.rem(z, 2)
    mine = x * SIDE + y
    greet(
        [chip(x + 1, y, z, core), chip(x - 1, y, z, core), chip(x, y + 1, z, core), chip(x, y - 1, z, core)]
        + column(x, y, z, core)
    )
    other = z + 1 - 2 * zl
    away = remote(
        wsend.at[1 - zl], wrecv.at[core], wx_s.at[0], wx_r.at[core], chip(x, y, other, zl)
    )
    away.start()
    near = remote(wsend.at[zl], wrecv.at[core], wx_s.at[1], wx_r.at[core], chip(x, y, z, zl))
    self_copy = pltpu.make_async_copy(wsend.at[zl], wrecv.at[core], loc.at[0])

    @pl.when(core == zl)
    def _():
        self_copy.start()

    @pl.when(core != zl)
    def _():
        near.start()

    block = 2 * zl + core
    acts, locals_ = [], []
    for i, (src, dst) in enumerate(
        ((tok, tok_all), (txt, txt_all), (cot, cot_all), (pos, pos_all))
    ):
        put = dst.at[block]
        acts.append(
            remote(src.at[1 - core], put, ac_s.at[i, 0], ac_r.at[i, 0], chip(x, y, z, 1 - core))
        )
        acts.append(
            remote(src.at[0], put, ac_s.at[i, 1], ac_r.at[i, 1 + core], chip(x, y, z + 1, 0))
        )
        acts.append(
            remote(src.at[1], put, ac_s.at[i, 2], ac_r.at[i, 1 + core], chip(x, y, z - 1, 1))
        )
        locals_.append(pltpu.make_async_copy(src.at[core], put, loc.at[1 + i]))
    for copy in acts + locals_:
        copy.start()

    def got(slot):
        remote(wsend.at[0], wrecv.at[slot], wx_s.at[0], wx_r.at[slot], chip(x, y, z, core)).wait_recv()

    @pl.when(core == zl)
    def _():
        self_copy.wait()
        got(1 - core)

    @pl.when(core != zl)
    def _():
        near.wait_send()
        got(0)
        got(1)

    first = wrecv[0].astype(F32)
    second = wrecv[1].astype(F32)
    own[0] = jnp.concatenate([first[:ROWS], second[:ROWS]], 0).astype(BF)
    own[1] = jnp.concatenate([first[ROWS:], second[ROWS:]], 0).astype(BF)

    flat = lambda a, b: lax.rem(a + SIDE, SIDE) * SIDE + lax.rem(b + SIDE, SIDE)

    def place(part, index, half=None):
        start, size = part * HALF, HALF
        if half is not None:
            start, size = start + half * QUARTER, QUARTER
        return wg.at[index, core, :, pl.ds(start, size)]

    sends, recvs, sibs = [], [], []

    def push(part, slot, src, index, device, half=None):
        copy = remote(src, place(part, index, half), xs.at[part, slot], xr.at[part, slot], device)
        copy.start()
        sends.append(copy)
        return copy

    def to_sibling(part, slot, src, index):
        copy = remote(
            src, place(part, index), ks.at[part, slot], kr.at[part, slot], chip(x, y, z, 1 - core)
        )
        copy.start()
        sibs.append(copy)

    steps = (
        (chip(x + 1, y, z, core), chip(x - 1, y, z, core)),
        (chip(x, y + 1, z, core), chip(x, y - 1, z, core)),
    )

    def index_of(part, first_off, second_off):
        if part == 0:
            return flat(x + first_off, y + second_off)
        return flat(x + second_off, y + first_off)

    one, two = {}, {}
    for part in (0, 1):
        a_next, a_prev = steps[part]
        one[part, "next"] = push(part, 0, own.at[part], mine, a_next)
        one[part, "prev"] = push(part, 1, own.at[part], mine, a_prev)
    for part in (0, 1):
        b_next, b_prev = steps[1 - part]
        two[part, 0, "next"] = push(part, 4, own.at[part], mine, b_next)
        two[part, 0, "prev"] = push(part, 5, own.at[part], mine, b_prev)
        to_sibling(part, 0, own.at[part], mine)
        local = pltpu.make_async_copy(own.at[part], place(part, mine), loc.at[5 + part])
        local.start()
        locals_.append(local)

    def second_start(part, k, offset):
        b_next, b_prev = steps[1 - part]
        index = index_of(part, offset, 0)
        src = place(part, index)
        two[part, k, "next"] = push(part, 4 + 4 * k, src, index, b_next)
        two[part, k, "prev"] = push(part, 5 + 4 * k, src, index, b_prev)
        to_sibling(part, 4 * k, src, index)

    offsets = (0, -1, 1, 2)
    for part in (0, 1):
        a_next, a_prev = steps[part]
        one[part, "next"].wait_recv()
        index = index_of(part, -1, 0)
        one[part, "far0"] = push(part, 2, place(part, index, 0), index, a_next, 0)
        second_start(part, 1, -1)
        one[part, "prev"].wait_recv()
        index = index_of(part, 1, 0)
        one[part, "far1"] = push(part, 3, place(part, index, 1), index, a_prev, 1)
        second_start(part, 2, 1)

    def second_forward(part, k):
        b_next, b_prev = steps[1 - part]
        two[part, k, "next"].wait_recv()
        index = index_of(part, offsets[k], -1)
        two[part, k, "far0"] = push(part, 6 + 4 * k, place(part, index, 0), index, b_next, 0)
        to_sibling(part, 4 * k + 1, place(part, index), index)
        two[part, k, "prev"].wait_recv()
        index = index_of(part, offsets[k], 1)
        two[part, k, "far1"] = push(part, 7 + 4 * k, place(part, index, 1), index, b_prev, 1)
        to_sibling(part, 4 * k + 2, place(part, index), index)

    def second_finish(part, k):
        two[part, k, "far0"].wait_recv()
        two[part, k, "far1"].wait_recv()
        index = index_of(part, offsets[k], 2)
        to_sibling(part, 4 * k + 3, place(part, index), index)

    for part in (0, 1):
        second_forward(part, 0)
    for part in (0, 1):
        one[part, "far0"].wait_recv()
        one[part, "far1"].wait_recv()
        second_start(part, 3, 2)
    for k in (1, 2, 3):
        for part in (0, 1):
            second_forward(part, k)
        for part in (0, 1):
            second_finish(part, k - 1)
    for part in (0, 1):
        second_finish(part, 3)

    away.wait_send()
    for copy in locals_:
        copy.wait()
    for copy in acts:
        copy.wait_send()
    for i in range(4):
        for slot in range(3):
            acts[3 * i].wait_recv() if slot == 0 else remote(
                (tok, txt, cot, pos)[i].at[0], (tok_all, txt_all, cot_all, pos_all)[i].at[0],
                ac_s.at[i, 0], ac_r.at[i, slot], chip(x, y, z, core),
            ).wait_recv()
    for copy in sends:
        copy.wait_send()
    for copy in sibs:
        copy.wait_send()
        copy.wait_recv()


def gather_all(wsend, tok, txt, cot, pos):
    acts = jax.ShapeDtypeStruct((SIDE, TOK, D), BF)
    dma = pltpu.SemaphoreType.DMA
    return pl.pallas_call(
        gather_kernel,
        out_shape=[
            jax.ShapeDtypeStruct((SIDE * SIDE, 2, PAIR, COLS), BF),
            acts,
            acts,
            acts,
            jax.ShapeDtypeStruct((SIDE, 8, TOK), F32),
        ],
        in_specs=[VM, HB, HB, HB, VM],
        out_specs=[HB, HB, HB, HB, VM],
        scratch_shapes=[
            pltpu.VMEM((2, PAIR, HALF), BF),
            pltpu.VMEM((2, PAIR, HALF), BF),
            dma((2,)), dma((2,)), dma((4, 3)), dma((4, 3)), dma((7,)),
            dma((2, 20)), dma((2, 20)), dma((2, 16)), dma((2, 16)),
        ],
        compiler_params=params(0),
        name="gather_weights",
    )(wsend, tok, txt, cot, pos)


def z_peers(x, y, z, core):
    return [chip(x, y, z + k, core) for k in (1, 2, 3)]


def total_kernel(part, out, got, send, recv):
    x, y, z, core = here()
    greet(z_peers(x, y, z, core))
    copies = []
    for k in (1, 2, 3):
        copies.append(
            remote(part, got.at[k - 1], send.at[k - 1], recv.at[k - 1], chip(x, y, z + k, core))
        )
        copies[-1].start()
    for copy in copies:
        copy.wait()
    out[...] = part[...] + got[0] + got[1] + got[2]


def z_total(values, cid):
    dma = pltpu.SemaphoreType.DMA
    return pl.pallas_call(
        total_kernel,
        out_shape=jax.ShapeDtypeStruct(values.shape, F32),
        in_specs=[VM],
        out_specs=VM,
        scratch_shapes=[pltpu.VMEM((3,) + values.shape, F32), dma((3,)), dma((3,))],
        compiler_params=params(cid),
        name=f"z_total_{cid}",
    )(values)


def scatter_start(parts, got, send, recv):
    x, y, z, core = here()
    copies = []
    for i, part in enumerate(parts):
        for k in (2, 1, 3):
            rows = pl.ds(pl.multiple_of(block_of(z + k) * TOK, TOK), TOK)
            copy = remote(
                part.at[rows], got.at[i, k - 1], send.at[i, k - 1], recv.at[i, k - 1],
                chip(x, y, z + k, core),
            )
            copy.start()
            copies.append(copy)
    return copies


def own_sum(part, got, i, z):
    rows = pl.ds(pl.multiple_of(block_of(z) * TOK, TOK), TOK)
    total = part[rows].astype(F32)
    for k in range(3):
        total = total + got[i, k].astype(F32)
    return total


def step_kernel(compute, extra_count, out_count, *refs):
    part = refs[0]
    extras = refs[1 : 1 + extra_count]
    gathered = refs[1 + extra_count]
    outs = refs[2 + extra_count : 2 + extra_count + out_count]
    got, send, recv, gsend, grecv = refs[2 + extra_count + out_count :]
    x, y, z, core = here()
    greet(z_peers(x, y, z, core))
    copies = scatter_start([part], got, send, recv)
    for copy in copies:
        copy.wait_recv()
    total = own_sum(part, got, 0, z)
    result = compute(total, extras, outs)
    rows = pl.ds(pl.multiple_of(block_of(z) * TOK, TOK), TOK)
    gathered[rows] = result
    gathers = []
    for k in (2, 1, 3):
        copy = remote(
            gathered.at[rows], gathered.at[rows], gsend.at[k - 1], grecv.at[k - 1],
            chip(x, y, z + k, core),
        )
        copy.start()
        gathers.append(copy)
    for copy in gathers:
        copy.wait()
    for copy in copies:
        copy.wait_send()


def z_step(part, extras, compute, out_shapes, cid):
    dma = pltpu.SemaphoreType.DMA
    return pl.pallas_call(
        partial(step_kernel, compute, len(extras), len(out_shapes)),
        out_shape=[jax.ShapeDtypeStruct((SEQ, D), BF)] + out_shapes,
        in_specs=[VM] * (1 + len(extras)),
        out_specs=[VM] * (1 + len(out_shapes)),
        scratch_shapes=[pltpu.VMEM((1, 3, TOK, D), BF), dma((1, 3)), dma((1, 3)), dma((3,)), dma((3,))],
        compiler_params=params(cid),
        name=f"z_step_{cid}",
    )(part, *extras)


def scatter_kernel(count, *refs):
    parts, outs = refs[:count], refs[count : 2 * count]
    got, send, recv = refs[2 * count :]
    x, y, z, core = here()
    greet(z_peers(x, y, z, core))
    copies = scatter_start(parts, got, send, recv)
    for i in range(count):
        for copy in copies[3 * i : 3 * i + 3]:
            copy.wait()
        outs[i][...] = own_sum(parts[i], got, i, z)


def z_scatter(parts, cid):
    count = len(parts)
    dma = pltpu.SemaphoreType.DMA
    return pl.pallas_call(
        partial(scatter_kernel, count),
        out_shape=[jax.ShapeDtypeStruct((TOK, D), F32)] * count,
        in_specs=[VM] * count,
        out_specs=[VM] * count,
        scratch_shapes=[pltpu.VMEM((count, 3, TOK, D), BF), dma((count, 3)), dma((count, 3))],
        compiler_params=params(cid),
        name=f"z_scatter_{cid}",
    )(*parts)


def deliver_kernel(count, *refs):
    srcs, dsts = refs[:count], refs[count : 2 * count]
    send, recv, loc = refs[2 * count :]
    x, y, z, core = here()
    zh = lax.div(z, 2)
    greet(column(x, y, z, core))
    far = [
        remote(s, d.at[core], send.at[i, 0], recv.at[i, core], chip(x, y, z + 2, zh))
        for i, (s, d) in enumerate(zip(srcs, dsts))
    ]
    near = [
        remote(s, d.at[core], send.at[i, 1], recv.at[i, core], chip(x, y, z, zh))
        for i, (s, d) in enumerate(zip(srcs, dsts))
    ]
    self_copies = [
        pltpu.make_async_copy(s, d.at[core], loc.at[i]) for i, (s, d) in enumerate(zip(srcs, dsts))
    ]
    for copy in far:
        copy.start()

    def got(i, slot):
        remote(
            srcs[i], dsts[i].at[slot], send.at[i, 0], recv.at[i, slot], chip(x, y, z, core)
        ).wait_recv()

    @pl.when(core == zh)
    def _():
        for copy in self_copies:
            copy.start()
        for i in range(count):
            self_copies[i].wait()
            got(i, 1 - core)

    @pl.when(core != zh)
    def _():
        for copy in near:
            copy.start()
        for i in range(count):
            near[i].wait_send()
            got(i, 0)
            got(i, 1)

    for copy in far:
        copy.wait_send()


def deliver(arrays, cid):
    count = len(arrays)
    dma = pltpu.SemaphoreType.DMA
    return pl.pallas_call(
        partial(deliver_kernel, count),
        out_shape=[jax.ShapeDtypeStruct((2,) + a.shape, a.dtype) for a in arrays],
        in_specs=[VM] * count,
        out_specs=[VM] * count,
        scratch_shapes=[dma((count, 2)), dma((count, 2)), dma((count,))],
        compiler_params=params(cid),
        name=f"deliver_{cid}",
    )(*arrays)


def vector_kernel(model, heads, time_out, model_out, head_out, col, hsib, mx, hx, sends, recvs):
    x, y, z, core = here()
    zl = lax.rem(z, 2)
    rows = [chip(x + k, y, z, core) for k in (1, 2, 3)]
    lines = [chip(x, y + k, z, core) for k in (1, 2, 3)]
    greet(column(x, y, z, core) + rows + lines)
    copies = []
    for k in (1, 2, 3):
        copies.append(
            remote(model, col.at[0, k - 1], sends.at[0, k], recvs.at[0, k], chip(x, y, z + k, core))
        )
    for k in range(4):
        copies.append(
            remote(model, col.at[1, k], sends.at[1, k], recvs.at[1, k], chip(x, y, z + k, 1 - core))
        )
    copies.append(remote(heads, hsib, sends.at[0, 0], recvs.at[0, 0], chip(x, y, z, 1 - core)))
    for copy in copies:
        copy.start()
    for copy in copies:
        copy.wait()
    same = model[...] + col[0, 0] + col[0, 1] + col[0, 2]
    sib = col[1, 0] + col[1, 1] + col[1, 2] + col[1, 3]
    time_out[core] = same
    time_out[1 - core] = sib
    mx[0] = same + sib
    hx[0] = heads[...] + hsib[...]
    for stage, peers in enumerate((rows, lines)):
        copies = []
        for k in (1, 2, 3):
            at = 1 + 3 * stage + k - 1
            copies.append(
                remote(mx.at[4 * stage], mx.at[4 * stage + k], sends.at[2 + 2 * stage, k],
                       recvs.at[2 + 2 * stage, k], peers[k - 1])
            )
            copies.append(
                remote(hx.at[4 * stage], hx.at[4 * stage + k], sends.at[3 + 2 * stage, k],
                       recvs.at[3 + 2 * stage, k], peers[k - 1])
            )
        for copy in copies:
            copy.start()
        for copy in copies:
            copy.wait()
        base = 4 * stage
        mx[base + 4] = mx[base] + mx[base + 1] + mx[base + 2] + mx[base + 3]
        hx[base + 4] = hx[base] + hx[base + 1] + hx[base + 2] + hx[base + 3]
    model_out[...] = mx[8]
    head_out[zl] = hx[8]
    last = remote(
        hx.at[8], head_out.at[zl], sends.at[6, 0], recvs.at[6, 0], chip(x, y, z + 1 - 2 * zl, core)
    )
    last.start()
    last.wait()


def vector_sums(model, heads, cid):
    dma = pltpu.SemaphoreType.DMA
    return pl.pallas_call(
        vector_kernel,
        out_shape=[
            jax.ShapeDtypeStruct((2, 16, D), F32),
            jax.ShapeDtypeStruct((16, D), F32),
            jax.ShapeDtypeStruct((2, 16, HW), F32),
        ],
        in_specs=[VM, VM],
        out_specs=[VM, VM, VM],
        scratch_shapes=[
            pltpu.VMEM((2, 4, 16, D), F32),
            pltpu.VMEM((16, HW), F32),
            pltpu.VMEM((9, 16, D), F32),
            pltpu.VMEM((9, 16, HW), F32),
            dma((7, 4)),
            dma((7, 4)),
        ],
        compiler_params=params(cid),
        name="vector_sums",
    )(model, heads)


GRAD_WIDTHS = (3 * HW, HW, 2 * HW, HW, HW, FF, FF)


def grad_kernel(*refs):
    grads = refs[: len(GRAD_WIDTHS)]
    out, own, sib, r1, r2, tosend, ls, ss, sr, s1, q1, s2, q2, s3, q3, l3 = refs[len(GRAD_WIDTHS) :]
    x, y, z, core = here()
    zl = lax.rem(z, 2)
    rows = [chip(x + k, y, z, core) for k in (1, 2, 3)]
    lines = [chip(x, y + k, z, core) for k in (1, 2, 3)]
    greet(column(x, y, z, core) + rows + lines)
    start, pairs = 0, []
    for i, width in enumerate(GRAD_WIDTHS):
        cols = pl.ds(start, width)
        mine = pltpu.make_async_copy(grads[i].at[:, :, core], own.at[:, :, :, cols], ls.at[i])
        theirs = remote(
            grads[i].at[:, :, 1 - core], sib.at[:, :, :, cols], ss.at[i], sr.at[i], chip(x, y, z, 1 - core)
        )
        mine.start()
        theirs.start()
        pairs.append((mine, theirs))
        start += width
    for mine, theirs in pairs:
        mine.wait()
        theirs.wait()

    def add_pair(k, carry):
        a, b = lax.div(k, SIDE), lax.rem(k, SIDE)
        own[a, b] = (own[a, b].astype(F32) + sib[a, b].astype(F32)).astype(BF)
        return carry

    lax.fori_loop(0, SIDE * SIDE, add_pair, 0)
    wrap = lambda v: lax.rem(v, SIDE)
    first, second = pl.ds(0, HALF), pl.ds(HALF, HALF)
    one = []
    for k in (2, 1, 3):
        one.append(
            remote(own.at[:, wrap(y + k), :, first], r1.at[0, k - 1], s1.at[0, k - 1], q1.at[0, k - 1], lines[k - 1])
        )
        one.append(
            remote(own.at[wrap(x + k), :, :, second], r1.at[1, k - 1], s1.at[1, k - 1], q1.at[1, k - 1], rows[k - 1])
        )
    for copy in one:
        copy.start()
    for copy in one:
        copy.wait()

    def add_line(k, carry):
        total = own[k, y, :, :HALF].astype(F32)
        for i in range(3):
            total = total + r1[0, i, k].astype(F32)
        own[k, y, :, :HALF] = total.astype(BF)
        total = own[x, k, :, HALF:].astype(F32)
        for i in range(3):
            total = total + r1[1, i, k].astype(F32)
        own[x, k, :, HALF:] = total.astype(BF)
        return carry

    lax.fori_loop(0, SIDE, add_line, 0)
    two = []
    for k in (2, 1, 3):
        two.append(
            remote(own.at[wrap(x + k), y, :, first], r2.at[0, k - 1], s2.at[0, k - 1], q2.at[0, k - 1], rows[k - 1])
        )
        two.append(
            remote(own.at[x, wrap(y + k), :, second], r2.at[1, k - 1], s2.at[1, k - 1], q2.at[1, k - 1], lines[k - 1])
        )
    for copy in two:
        copy.start()
    for copy in two:
        copy.wait()
    final = []
    for part in (0, 1):
        total = own[x, y, :, pl.ds(part * HALF, HALF)].astype(F32)
        for i in range(3):
            total = total + r2[part, i].astype(F32)
        final.append(total)
    for target in (0, 1):
        rows_of = slice(target * ROWS, target * ROWS + ROWS)
        tosend[target] = jnp.concatenate([final[0][rows_of], final[1][rows_of]], 0).astype(BF)
    other = z + 1 - 2 * zl
    far = [
        remote(tosend.at[t], out.at[zl], s3.at[t], q3.at[zl], chip(x, y, other, t)) for t in (0, 1)
    ]
    self_copy = pltpu.make_async_copy(tosend.at[core], out.at[zl], l3.at[0])
    near = remote(tosend.at[1 - core], out.at[zl], s3.at[0], q3.at[zl], chip(x, y, z, 1 - core))

    def got(slot):
        remote(tosend.at[0], out.at[slot], s3.at[0], q3.at[slot], chip(x, y, z, core)).wait_recv()

    @pl.when(core == zl)
    def _():
        self_copy.start()
        near.start()
        self_copy.wait()
        near.wait_send()
        got(1 - zl)

    @pl.when(core != zl)
    def _():
        for copy in far:
            copy.start()
        for copy in far:
            copy.wait_send()
        got(zl)
        got(1 - zl)


def grad_sums(grads, cid):
    dma = pltpu.SemaphoreType.DMA
    count = len(GRAD_WIDTHS)
    return pl.pallas_call(
        grad_kernel,
        out_shape=jax.ShapeDtypeStruct((2, PAIR, HALF), BF),
        in_specs=[HB] * count,
        out_specs=VM,
        scratch_shapes=[
            pltpu.VMEM((SIDE, SIDE, PAIR, COLS), BF),
            pltpu.VMEM((SIDE, SIDE, PAIR, COLS), BF),
            pltpu.VMEM((2, 3, SIDE, PAIR, HALF), BF),
            pltpu.VMEM((2, 3, PAIR, HALF), BF),
            pltpu.VMEM((2, PAIR, HALF), BF),
            dma((count,)), dma((count,)), dma((count,)),
            dma((2, 3)), dma((2, 3)), dma((2, 3)), dma((2, 3)),
            dma((2,)), dma((2,)), dma((1,)),
        ],
        compiler_params=params(cid),
        name="grad_sums",
    )(*grads)


def newton_kernel(narrow, wide, narrow_out, wide_out, mine, theirs, send, recv):
    x, y, z, core = here()
    partner = chip(x, y, z + 2, core)
    greet([partner])
    n, w = narrow.shape[0], wide.shape[0]
    size = n + w
    contract = (((1,), (1,)), ((), ()))
    mine[...] = jnp.zeros_like(mine)
    mine[:n, :n] = lax.dot_general(
        narrow[...], narrow[...], contract, precision=HIGHEST, preferred_element_type=F32
    )
    mine[n:, n:] = lax.dot_general(
        wide[...], wide[...], contract, precision=HIGHEST, preferred_element_type=F32
    )
    copy = remote(mine, theirs, send.at[0], recv.at[0], partner)
    copy.start()
    copy.wait()
    block_row = lax.div(lax.broadcasted_iota(jnp.int32, (size, size), 0), ROWS)
    block_col = lax.div(lax.broadcasted_iota(jnp.int32, (size, size), 1), ROWS)
    same = block_row == block_col
    eye = lax.broadcasted_iota(jnp.int32, (size, size), 0) == lax.broadcasted_iota(
        jnp.int32, (size, size), 1
    )
    gram = jnp.where(same, mine[...] + theirs[...], 0.0)
    diagonal = jnp.where(eye, gram, 0.0)
    by_row = jnp.sum(diagonal, 1, keepdims=True)
    by_col = jnp.sum(diagonal, 0, keepdims=True)
    total_row = jnp.sum(jnp.where(same, by_col, 0.0), 1, keepdims=True)
    total_col = jnp.sum(jnp.where(same, by_row, 0.0), 0, keepdims=True)
    scale_row = 1.0 / (jnp.sqrt(total_row) + ORTHO_EPSILON)
    scale_col = 1.0 / (jnp.sqrt(total_col) + ORTHO_EPSILON)
    current = gram * scale_row * scale_col

    def times(a, b):
        return jnp.dot(a, b, precision=HIGHEST, preferred_element_type=F32)

    whole = None
    for turn in range(NS_STEPS):
        square = times(current, current)
        step = NEWTON_SECOND * current + NEWTON_THIRD * square + jnp.where(eye, NEWTON_FIRST, 0.0)
        whole = step if whole is None else times(step, whole)
        if turn + 1 < NS_STEPS:
            current = times(times(step, current), step)
    whole = whole * scale_col
    narrow_out[...] = times(whole[:n, :n], narrow[...])
    wide_out[...] = times(whole[n:, n:], wide[...])


def newton(narrow, wide, cid):
    size = narrow.shape[0] + wide.shape[0]
    dma = pltpu.SemaphoreType.DMA
    return pl.pallas_call(
        newton_kernel,
        out_shape=[
            jax.ShapeDtypeStruct(narrow.shape, F32),
            jax.ShapeDtypeStruct(wide.shape, F32),
        ],
        in_specs=[VM, VM],
        out_specs=[VM, VM],
        scratch_shapes=[
            pltpu.VMEM((size, size), F32),
            pltpu.VMEM((size, size), F32),
            dma((1,)),
            dma((1,)),
        ],
        compiler_params=params(cid),
        name="newton",
    )(narrow, wide)


def rope_tables(places):
    pair_index = jnp.arange(HEAD // 2, dtype=jnp.int32)
    side_pairs = HEAD // 6
    frame_pairs = (HEAD - 4 * side_pairs) // 2
    part_of = (pair_index >= frame_pairs).astype(jnp.int32) + (
        pair_index >= frame_pairs + side_pairs
    ).astype(jnp.int32)
    offset = jnp.where(
        part_of == 0, 0, jnp.where(part_of == 1, frame_pairs, frame_pairs + side_pairs)
    ).astype(jnp.int32)
    extent = jnp.where(part_of == 0, 2 * frame_pairs, 2 * side_pairs).astype(jnp.float32)
    frequency = jnp.exp(
        (pair_index - offset).astype(jnp.float32) * (-2.0 * math.log(10000.0)) / extent
    )
    chosen = (
        places[0][:, None] * (part_of == 0)
        + places[1][:, None] * (part_of == 1)
        + places[2][:, None] * (part_of == 2)
    )
    angles = chosen.astype(jnp.float32) * frequency
    return (jnp.cos(angles), jnp.sin(angles))


def rotate(values, cosine, sine):
    half_head = HEAD // 2
    front_half = values[..., :half_head]
    back_half = values[..., half_head:]
    return jnp.concatenate(
        [front_half * cosine - back_half * sine, back_half * cosine + front_half * sine], -1
    )


def plain_norm(values):
    centred = values - jnp.mean(values, -1, keepdims=True)
    inverse = lax.rsqrt(jnp.mean(centred * centred, -1, keepdims=True) + NORM_EPSILON)
    return (centred * inverse, inverse)


def norm_back(grads, normed, inverse):
    return inverse * (
        grads
        - jnp.mean(grads, -1, keepdims=True)
        - normed * jnp.mean(grads * normed, -1, keepdims=True)
    )


def split_heads(values):
    return values.reshape(values.shape[0], -1, HEAD)


def merge_heads(values):
    return values.reshape(values.shape[0], -1)


def product(left, right):
    return jnp.dot(left, right, preferred_element_type=F32)


def contract_last(left, right):
    return lax.dot_general(left, right, (((1,), (1,)), ((), ())), preferred_element_type=F32)


def contract_rows(left, right):
    return lax.dot_general(left, right, (((0,), (0,)), ((), ())), preferred_element_type=F32)


def attend(query, keys, values):
    scores = jnp.einsum("qhe,khe->hqk", query, keys, preferred_element_type=F32) * HEAD ** (-0.5)
    row_peak = jnp.max(scores, -1, keepdims=True)
    log_total = row_peak + jnp.log(jnp.sum(jnp.exp(scores - row_peak), -1, keepdims=True))
    weights = jnp.exp(scores - log_total).astype(BF)
    mixed = jnp.einsum("hqk,khe->qhe", weights, values, preferred_element_type=F32)
    return (merge_heads(mixed), log_total)


def attend_back(query, keys, values, log_total, grad_mixed):
    scores = jnp.einsum("qhe,khe->hqk", query, keys, preferred_element_type=F32) * HEAD ** (-0.5)
    weights = jnp.exp(scores - log_total)
    grad_weights = jnp.einsum("qhe,khe->hqk", grad_mixed, values, preferred_element_type=F32)
    row_delta = jnp.sum(weights * grad_weights, -1, keepdims=True)
    grad_scores = (weights * (grad_weights - row_delta)).astype(BF)
    grad_query = jnp.einsum("hqk,khe->qhe", grad_scores, keys, preferred_element_type=F32) * HEAD ** (
        -0.5
    )
    grad_keys = jnp.einsum("hqk,qhe->khe", grad_scores, query, preferred_element_type=F32) * HEAD ** (
        -0.5
    )
    grad_values = jnp.einsum(
        "hqk,qhe->khe", weights.astype(BF), grad_mixed, preferred_element_type=F32
    )
    return grad_query, grad_keys, merge_heads(grad_values)


def block_struct():
    return jax.ShapeDtypeStruct((TOK, D), F32)


def after_self(total, extras, outs):
    residual, rows = extras
    branch = total + rows[0:1]
    after = residual[...].astype(F32) + rows[1:2] * branch
    normed, _ = plain_norm(after)
    outs[0][...] = branch
    outs[1][...] = after
    return (normed * (1.0 + rows[2:3]) + rows[3:4]).astype(BF)


def after_cross(total, extras, outs):
    residual, rows = extras
    after = residual[...] + total + rows[0:1]
    normed, _ = plain_norm(after)
    outs[0][...] = after
    return (normed * (1.0 + rows[1:2]) + rows[2:3]).astype(BF)


def back_mlp(total, extras, outs):
    after, grads, rows = extras
    normed, inverse = plain_norm(after[...])
    outs[1][0:1] = jnp.sum(total, 0, keepdims=True)
    outs[1][1:2] = jnp.sum(total * normed, 0, keepdims=True)
    result = grads[...].astype(F32) + norm_back(total * (1.0 + rows[0:1]), normed, inverse)
    outs[0][...] = result
    low = result.astype(BF)
    outs[1][2:3] = jnp.sum(low.astype(F32), 0, keepdims=True)
    return low


def back_cross(total, extras, outs):
    after, grads, branch, rows = extras
    normed, inverse = plain_norm(after[...])
    outs[1][0:1] = jnp.sum(total, 0, keepdims=True)
    outs[1][1:2] = jnp.sum(total * normed, 0, keepdims=True)
    result = grads[...] + norm_back(total * (1.0 + rows[0:1]), normed, inverse)
    outs[0][...] = result
    outs[1][2:3] = jnp.sum(result * branch[...], 0, keepdims=True)
    low = (result * rows[1:2]).astype(BF)
    outs[1][3:4] = jnp.sum(low.astype(F32), 0, keepdims=True)
    return low


def stack_rows(rows, count=8):
    out = jnp.stack(rows)
    return jnp.pad(out, ((0, count - len(rows)), (0, 0)))


def body(
    tokens, text, time_embedding, positions, cotangent, attn_in, attn_out, mlp, head_vectors,
    model_vectors, up_bias, attn_in_moment, attn_out_moment, mlp_moment, head_moment, model_moment,
    up_moment,
):
    x, y, z, core = here()
    zl = lax.rem(z, 2)
    block = block_of(z)

    low_in = attn_in.astype(BF).reshape(ROWS, 6, 2, HW).transpose(2, 0, 1, 3).reshape(2, ROWS, -1)
    low_out = attn_out.astype(BF).reshape(ROWS, 2, 2, HW).transpose(2, 0, 1, 3).reshape(2, ROWS, -1)
    low_mlp = jnp.pad(
        mlp.astype(BF).reshape(ROWS, 2, 2, FF_REAL).transpose(2, 0, 1, 3),
        ((0, 0), (0, 0), (0, 0), (0, FF - FF_REAL)),
    ).reshape(2, ROWS, -1)
    packed = jnp.concatenate([low_in, low_out, low_mlp], -1)
    packed = packed.reshape(2, ROWS, 2, HALF).transpose(0, 2, 1, 3).reshape(2, PAIR, HALF)
    places = jnp.pad(positions.transpose(1, 0, 2), ((0, 0), (0, 5), (0, 0))).astype(F32)
    gathered, tok_all, txt_all, cot_all, pos_all = gather_all(packed, tokens, text, cotangent, places)
    weights = gathered.reshape(D, COLS)

    def matrix(start, width):
        return lax.slice(weights, (0, start), (D, start + width))

    w_qkv = matrix(C_IN, 3 * HW)
    w_query = matrix(C_IN + 3 * HW, HW)
    w_text = matrix(C_IN + 4 * HW, 2 * HW)
    w_self = matrix(C_OUT, HW)
    w_cross = matrix(C_OUT + HW, HW)
    w_up = matrix(C_UP, FF)
    w_down = matrix(C_DOWN, FF)

    heads = lax.dynamic_slice(head_vectors, (0, zl * HW), (10, HW))
    bias_up = jnp.pad(lax.dynamic_slice(up_bias, (zl * FF_REAL,), (FF_REAL,)), (0, FF - FF_REAL))
    modulation = model_vectors[5:] + lax.dynamic_index_in_dim(time_embedding, core, 0, False)
    shift_one, scale_one, gate_one, shift_two, scale_two, gate_two = [modulation[i] for i in range(6)]
    cosine, sine = rope_tables(pos_all[:, :3].transpose(1, 0, 2).reshape(3, SEQ))
    cosine, sine = cosine[:, None, :], sine[:, None, :]

    def block_rows(values):
        return lax.dynamic_slice(values, (block * TOK, 0), (TOK, values.shape[1]))

    tok_all = tok_all.reshape(SEQ, D)
    words = txt_all.reshape(SEQ, D)
    cot_all = cot_all.reshape(SEQ, D)
    tok_own = block_rows(tok_all)
    cot_own = block_rows(cot_all)

    normed_one, _ = plain_norm(tok_all.astype(F32))
    input_one = (normed_one * (1.0 + scale_one) + shift_one).astype(BF)
    qkv = product(input_one, w_qkv) + heads[0:3].reshape(-1)
    query_lin, key_lin, value_lin = qkv[:, :HW], qkv[:, HW : 2 * HW], qkv[:, 2 * HW :]
    kv_two = product(words, w_text) + heads[6:8].reshape(-1)
    key_two_lin, value_two_lin = kv_two[:, :HW], kv_two[:, HW:]
    squares = z_total(
        stack_rows([jnp.sum(v * v, -1) for v in (query_lin, key_lin, key_two_lin)]), 1
    )
    inverses = lax.rsqrt(squares / D + NORM_EPSILON)
    inverse_query, inverse_key, inverse_key_two = [inverses[i][:, None] for i in range(3)]
    query_rot = rotate(
        split_heads(query_lin * inverse_query * (1.0 + heads[3])), cosine, sine
    ).astype(BF)
    key_rot = rotate(split_heads(key_lin * inverse_key * (1.0 + heads[4])), cosine, sine).astype(BF)
    value_low = split_heads(value_lin.astype(BF))
    mixed, log_one = attend(query_rot, key_rot, value_low)
    mixed_low = mixed.astype(BF)
    part = contract_last(mixed_low, w_self).astype(BF)
    input_three, branch_one, after_one = z_step(
        part,
        [tok_own, stack_rows([model_vectors[0], gate_one, model_vectors[3], model_vectors[4]])],
        after_self,
        [block_struct(), block_struct()],
        2,
    )
    query_two_lin = product(input_three, w_query) + heads[5]
    squares_two = z_total(stack_rows([jnp.sum(query_two_lin * query_two_lin, -1)]), 3)
    inverse_query_two = lax.rsqrt(squares_two[0] / D + NORM_EPSILON)[:, None]
    query_two = split_heads((query_two_lin * inverse_query_two * (1.0 + heads[8])).astype(BF))
    key_two = split_heads((key_two_lin * inverse_key_two * (1.0 + heads[9])).astype(BF))
    value_two = split_heads(value_two_lin.astype(BF))
    mixed_two, log_two = attend(query_two, key_two, value_two)
    mixed_two_low = mixed_two.astype(BF)
    part = contract_last(mixed_two_low, w_cross).astype(BF)
    input_mlp, after_two = z_step(
        part,
        [after_one, stack_rows([model_vectors[1], scale_two, shift_two])],
        after_cross,
        [block_struct()],
        4,
    )
    hidden_lin = product(input_mlp, w_up) + bias_up
    hidden_act, gelu_pullback = jax.vjp(partial(jax.nn.gelu, approximate=True), hidden_lin)
    hidden_low = hidden_act.astype(BF)
    part_mlp = contract_last(hidden_low, w_down).astype(BF)
    grad_branch_mlp = (cot_all.astype(F32) * gate_two).astype(BF)
    grad_hidden = gelu_pullback(product(grad_branch_mlp, w_down))[0].astype(BF)
    part = contract_last(grad_hidden, w_up).astype(BF)
    grad_branch_two, grad_after_two, sums_mlp = z_step(
        part,
        [after_two, cot_own, stack_rows([scale_two])],
        back_mlp,
        [block_struct(), jax.ShapeDtypeStruct((8, D), F32)],
        5,
    )
    grad_mixed_two = product(grad_branch_two, w_cross).astype(BF)
    grad_query_two, grad_key_two, grad_value_two = attend_back(
        query_two, key_two, value_two, log_two, split_heads(grad_mixed_two)
    )
    grad_query_two, grad_key_two = merge_heads(grad_query_two), merge_heads(grad_key_two)
    scaled_query_two = grad_query_two * (1.0 + heads[8])
    scaled_key_two = grad_key_two * (1.0 + heads[9])
    dots = z_total(
        stack_rows(
            [jnp.sum(query_two_lin * scaled_query_two, -1), jnp.sum(key_two_lin * scaled_key_two, -1)]
        ),
        6,
    )

    def root_back(linear, inverse, scaled, dot):
        return (inverse * scaled - linear * (inverse**3 * dot[:, None] / D)).astype(BF)

    grad_query_two_lin = root_back(query_two_lin, inverse_query_two, scaled_query_two, dots[0])
    grad_key_two_lin = root_back(key_two_lin, inverse_key_two, scaled_key_two, dots[1])
    grad_kv_two_lin = jnp.concatenate([grad_key_two_lin, grad_value_two.astype(BF)], 1)
    part = contract_last(grad_query_two_lin, w_query).astype(BF)
    part_words = contract_last(grad_kv_two_lin, w_text).astype(BF)
    grad_branch_one, grad_after_one, sums_cross = z_step(
        part,
        [after_one, grad_after_two, branch_one, stack_rows([model_vectors[3], gate_one])],
        back_cross,
        [block_struct(), jax.ShapeDtypeStruct((8, D), F32)],
        7,
    )
    grad_mixed = product(grad_branch_one, w_self).astype(BF)
    grad_query_rot, grad_key_rot, grad_value = attend_back(
        query_rot, key_rot, value_low, log_one, split_heads(grad_mixed)
    )
    grad_query_norm = merge_heads(rotate(grad_query_rot, cosine, -sine))
    grad_key_norm = merge_heads(rotate(grad_key_rot, cosine, -sine))
    scaled_query = grad_query_norm * (1.0 + heads[3])
    scaled_key = grad_key_norm * (1.0 + heads[4])
    dots_one = z_total(
        stack_rows([jnp.sum(query_lin * scaled_query, -1), jnp.sum(key_lin * scaled_key, -1)]), 8
    )
    grad_query_lin = root_back(query_lin, inverse_query, scaled_query, dots_one[0])
    grad_key_lin = root_back(key_lin, inverse_key, scaled_key, dots_one[1])
    grad_qkv = jnp.concatenate([grad_query_lin, grad_key_lin, grad_value.astype(BF)], 1)
    part_tokens = contract_last(grad_qkv, w_qkv).astype(BF)

    def rows_of(left, right):
        out = contract_rows(left, right).astype(BF)
        return out.reshape(SIDE, SIDE, 2, PAIR, out.shape[1])

    matrix_grads = [
        rows_of(input_one, grad_qkv),
        rows_of(input_three, grad_query_two_lin),
        rows_of(words, grad_kv_two_lin),
        rows_of(grad_branch_one, mixed_low),
        rows_of(grad_branch_two, mixed_two_low),
        rows_of(input_mlp, grad_hidden),
        rows_of(grad_branch_mlp, hidden_low),
    ]

    sum_mlp, sum_tokens, sum_words = z_scatter([part_mlp, part_tokens, part_words], 9)
    branch_mlp = sum_mlp + model_vectors[2]
    cot_f32 = cot_own.astype(F32)
    result = (after_two + gate_two * branch_mlp).astype(BF)
    normed_own, inverse_own = plain_norm(tok_own.astype(F32))
    grad_tokens = grad_after_one + norm_back(sum_tokens * (1.0 + scale_one), normed_own, inverse_own)
    column_sum = lambda v: jnp.sum(v.astype(F32), 0)
    model_part = stack_rows(
        [
            sums_cross[3],
            sums_mlp[2],
            column_sum(block_rows(grad_branch_mlp)),
            sums_cross[1],
            sums_cross[0],
            column_sum(sum_tokens),
            column_sum(sum_tokens * normed_own),
            sums_cross[2],
            sums_mlp[0],
            sums_mlp[1],
            column_sum(cot_f32 * branch_mlp),
        ],
        16,
    )
    grad_qkv_sum = column_sum(grad_qkv).reshape(3, HW)
    grad_kv_sum = column_sum(grad_kv_two_lin).reshape(2, HW)
    head_part = jnp.concatenate(
        [
            grad_qkv_sum,
            jnp.stack(
                [
                    column_sum(grad_query_norm * query_lin * inverse_query),
                    column_sum(grad_key_norm * key_lin * inverse_key),
                    column_sum(grad_query_two_lin),
                ]
            ),
            grad_kv_sum,
            jnp.stack(
                [
                    column_sum(grad_query_two * query_two_lin * inverse_query_two),
                    column_sum(grad_key_two * key_two_lin * inverse_key_two),
                ]
            ),
            column_sum(grad_hidden).reshape(6, HW),
        ],
        0,
    )
    out_result, out_tokens, out_words = deliver(
        [result, grad_tokens.astype(BF), sum_words.astype(BF)], 10
    )
    time_sums, model_sums, head_sums = vector_sums(model_part, head_part, 11)
    grad_time = time_sums[:, 5:11]
    model_total = model_sums[:11]
    head_total = head_sums[:, :10].transpose(1, 0, 2).reshape(10, 2 * HW)
    up_total = head_sums[:, 10:].reshape(2, FF)[:, :FF_REAL].reshape(-1)

    sums = grad_sums(matrix_grads, 12)
    sums = sums.reshape(2, 2, ROWS, HALF).transpose(0, 2, 1, 3).reshape(2, ROWS, COLS).astype(F32)
    def unpack(start, count, width, real):
        part = sums[:, :, start : start + count * width].reshape(2, ROWS, count, width)[..., :real]
        return part.transpose(2, 1, 0, 3).reshape(count, ROWS, 2 * real)

    swap = lambda v: v.transpose(1, 0, 2)
    new_in_moment = MOMENTUM * swap(attn_in_moment) + unpack(C_IN, 6, HW, HW)
    new_out_moment = MOMENTUM * swap(attn_out_moment) + unpack(C_OUT, 2, HW, HW)
    new_mlp_moment = MOMENTUM * swap(mlp_moment) + unpack(C_UP, 2, FF, FF_REAL)
    narrow = jnp.concatenate([new_in_moment, new_out_moment], 0).reshape(8 * ROWS, 2 * HW)
    wide = new_mlp_moment.reshape(2 * ROWS, 2 * FF_REAL)
    narrow_dir, wide_dir = newton(narrow, wide, 13)
    narrow_dir = narrow_dir.reshape(8, ROWS, 2 * HW)
    wide_dir = wide_dir.reshape(2, ROWS, 2 * FF_REAL)
    new_attn_in = attn_in * (1.0 - RATE_IN * DECAY) - RATE_IN * swap(narrow_dir[:6])
    new_attn_out = attn_out * (1.0 - RATE_OUT * DECAY) - RATE_OUT * swap(narrow_dir[6:])
    new_mlp = mlp * (1.0 - RATE_MLP * DECAY) - RATE_MLP * swap(wide_dir)
    new_head_moment = MOMENTUM * head_moment + head_total
    new_model_moment = MOMENTUM * model_moment + model_total
    new_up_moment = MOMENTUM * up_moment + up_total
    return (
        out_result,
        out_tokens.astype(F32),
        out_words.astype(F32),
        grad_time,
        new_attn_in,
        new_attn_out,
        new_mlp,
        swap(new_in_moment),
        swap(new_out_moment),
        swap(new_mlp_moment),
        head_vectors - RATE_VECTOR * new_head_moment,
        model_vectors - RATE_VECTOR * new_model_moment,
        up_bias - RATE_VECTOR * new_up_moment,
        new_head_moment,
        new_model_moment,
        new_up_moment,
    )


def solution(mesh):
    clip = P("fsdp", "ctx", None)
    whole = P("fsdp", None, None)
    matrix = P(("fsdp", "ctx"), None, "tp")
    in_specs = (
        clip, clip, whole, P(None, "fsdp", "ctx"), clip, matrix, matrix, matrix, P(None, "tp"), P(),
        P("tp"), matrix, matrix, matrix, P(None, "tp"), P(), P("tp"),
    )
    out_specs = (
        clip, clip, clip, whole, matrix, matrix, matrix, matrix, matrix, matrix, P(None, "tp"), P(),
        P("tp"), P(None, "tp"), P(), P("tp"),
    )
    return jax.shard_map(body, mesh=mesh, in_specs=in_specs, out_specs=out_specs, check_vma=False)
```

time: 2930 us -> 787 us (0.27)
  waiting for transfers between devices: 1580 us -> 0 us
  Pallas kernels: 0 us -> 539 us
  blocking collectives: 434 us -> 0 us
  local copies, waits for them, and re-layouts: 299 us -> 54.7 us
  other arithmetic: 267 us -> 64.5 us
  matrix products: 303 us -> 115 us
    unnamed x20 -> x0, waiting for transfers between devices: 993 us -> none
    pallas_call x0 -> x14, Pallas kernels: none -> 539 us  [the longest x4 171 us: z_step(): pl.pallas_call(partial(step_kernel, compute, len(extras), len(out_shapes)...]
    psum x11 -> x0, blocking collectives: 352 us -> none  [the longest x1 274 us: body(): lax.psum((head_sums, model_sums, up_sums), ('fsdp', 'ctx'))]
    psum x7 -> x0, waiting for transfers between devices: 308 us -> none  [the longest x4 229 us: tensor_total(): return lax.psum(partial_sum, 'tp')]
    all_gather x3 -> x0, waiting for transfers between devices: 282 us -> none  [the longest x1 155 us: body(): lax.all_gather(mlp.astype(jnp.bfloat16), ('fsdp', 'ctx'), axis=0, tiled=T...]
    another operation x48 -> x10, local copies, waits for them, and re-layouts: 126 us -> 0.15 us  [the longest x5 0.14 us: stack_rows(): out = jnp.stack(rows)]
    unnamed x551 -> x175, local copies, waits for them, and re-layouts: 124 us -> 12.8 us
    add x11 -> x5, other arithmetic: 102 us -> 4.19 us  [the longest x1 2.27 us: body(): new_mlp_moment = MOMENTUM * swap(mlp_moment) + unpack(C_UP, 2, FF, FF_REAL)]
  transfers between devices with their start and end apart: 19 -> 0, of which waited for: 10 -> 0; matrix products, arithmetic and copies ran while one was open for 24% -> 0% of each run, Pallas kernels for 0% -> 0%
where the time goes in v1:
time: 787 us; the launch traced here: 776 us
  Pallas kernels  539 us (68%)
  matrix products  115 us (15%)
  other arithmetic  64.5 us (8%)
  local copies, waits for them, and re-layouts  54.7 us (7%)
    pallas_call x4, Pallas kernels, z_step(): pl.pallas_call(partial(step_kernel, compute, len(extras), len(out_shapes)...  171 us
    pallas_call x1, Pallas kernels, grad_sums(): pl.pallas_call(grad_kernel, out_shape=jax.ShapeDtypeStruct((2, PAIR, HALF...  124 us
    pallas_call x1, Pallas kernels, gather_all(): pl.pallas_call(gather_kernel, out_shape=[jax.ShapeDtypeStruct((SIDE * SID...  77.9 us
    pallas_call x1, Pallas kernels, z_scatter(): pl.pallas_call(partial(scatter_kernel, count), out_shape=[jax.ShapeDtypeS...  58.7 us
    dot_general x7, matrix products, contract_last(): lax.dot_general(left, right, (((1,), (1,)), ((), ())), preferred_element_...  39.3 us
    dot_general x7, matrix products, product(): return jnp.dot(left, right, preferred_element_type=F32)  33.5 us
    pallas_call x1, Pallas kernels, deliver(): pl.pallas_call(partial(deliver_kernel, count), out_shape=[jax.ShapeDtypeS...  32.5 us
    pallas_call x1, Pallas kernels, vector_sums(): pl.pallas_call(vector_kernel, out_shape=[jax.ShapeDtypeStruct((2, 16, D),...  30.9 us

profile of v1, /device:TPU:1, one launch (start us, length us, event | category | flops | bytes accessed | tf_op | source)
XLA Modules:
  0.0 776.0 jit_solution(8036655785797270420)
XLA Ops:
  6.1 77.9 %gather_weights.1 = (bf16[16,2,48,7680]{3,2,1,0:T(8,128)(2,1)}, bf16[4,128,1536]{2,1,0:T(8,128)(2,1)}, bf16[4,128,1536]{2,1,0:T(8,128)(2,1)}, bf16[4,128,1536]{2,1,0:T(8,128)(2,1)}, f32[4,8,128]{2,1,0:T(8,128)}) custom-call(bf16[2,48,3840]{2,1,0:T(8,128)(2,1)} %bitcast.203, bf16[2,128,1536]{2,1,0:T(8,128)(2,1)} %tok.1, bf16[2,128,1536]{2,1,0:T(8,128)(2,1)} %txt.1, ...), custom_call_target="tpu_custom_call" | custom-call | tf_op jit(solution)/shard_map/gather_weights/pallas_call | solution.py:279
  95.2 4.7 convolution_add_fusion
  103.2 6.9 z_total_1.1
  130.9 42.2 %z_step_2.1 = (bf16[512,1536]{1,0:T(8,128)(2,1)}, f32[128,1536]{1,0:T(8,128)}, f32[128,1536]{1,0:T(8,128)}) custom-call(bf16[512,1536]{1,0:T(8,128)(2,1)} %convolution_convert_fusion.7.refs_0_, bf16[128,1536]{1,0:T(8,128)(2,1)} %get-tuple-element.151.refs_1_, f32[8,1536]{1,0:T(8,128)} %get-tuple-element.202.refs_2_), custom_call_target="tpu_custom_call" | custom-call | tf_op jit(solution)/shard_map/z_step_2/pallas_call | solution.py:386
  177.2 6.0 z_total_3.1
  198.2 42.7 %z_step_4.1 = (bf16[512,1536]{1,0:T(8,128)(2,1)}, f32[128,1536]{1,0:T(8,128)}) custom-call(bf16[512,1536]{1,0:T(8,128)(2,1)} %convolution_convert_fusion.6.refs_0_, f32[128,1536]{1,0:T(8,128)} %get-tuple-element.48.refs_1_, f32[8,1536]{1,0:T(8,128)} %get-tuple-element.204.refs_2_), custom_call_target="tpu_custom_call" | custom-call | tf_op jit(solution)/shard_map/z_step_4/pallas_call | solution.py:386
  241.0 7.1 fusion.8
  248.2 10.0 %fusion.31.refs_0_ = bf16[512,1536]{1,0:T(8,128)(2,1)} fusion(bf16[1536,7680]{1,0:T(8,128)(2,1)} %bitcast.273, f32[512,2304]{1,0:T(8,128)S(1)} %fusion.8), kind=kOutput, calls=%fused_computation.44 | convolution fusion | flops 3635281920 | bytes 13369344 | tf_op jit(solution)/shard_map/dot_general | solution.py:821
  258.6 9.3 %convert_reduce_fusion = (f32[2304]{0:T(1024)S(1)}, bf16[512,2304]{1,0:T(8,128)(2,1)S(1)}) fusion(f32[512,2304]{1,0:T(8,128)S(1)} %fusion.8, bf16[512,1536]{1,0:T(8,128)(2,1)S(1)} %multiply_convert_fusion.3, bf16[1536,7680]{1,0:T(8,128)(2,1)} %bitcast.274), kind=kOutput, calls=%fused_computation.21 | convolution fusion | flops 3649828608 | bytes 15737856 | tf_op jit(solution)/shard_map/dot_general | solution.py:817
  268.0 9.0 %fusion.28.refs_0_ = bf16[512,1536]{1,0:T(8,128)(2,1)} fusion(bf16[512,2304]{1,0:T(8,128)(2,1)S(1)} %get-tuple-element.218, bf16[1536,7680]{1,0:T(8,128)(2,1)} %bitcast.275), kind=kOutput, calls=%fused_computation.43 | convolution fusion | flops 3624665088 | bytes 11010048 | tf_op jit(solution)/shard_map/dot_general | solution.py:821
  277.7 42.8 %z_step_5.1 = (bf16[512,1536]{1,0:T(8,128)(2,1)}, f32[128,1536]{1,0:T(8,128)}, f32[8,1536]{1,0:T(8,128)}) custom-call(bf16[512,1536]{1,0:T(8,128)(2,1)} %fusion.28.refs_0_, f32[128,1536]{1,0:T(8,128)} %get-tuple-element.49.refs_1_, bf16[128,1536]{1,0:T(8,128)(2,1)} %constant_dynamic-slice_fusion.1.refs_2_, f32[8,1536]{1,0:T(8,128)} %get-tuple-element.203.refs_3_), custom_call_target="tpu_custom_call" | custom-call | tf_op jit(solution)/shard_map/z_step_5/pallas_call | solution.py:386
  341.5 6.2 z_total_6.1
  354.4 43.8 %z_step_7.1 = (bf16[512,1536]{1,0:T(8,128)(2,1)}, f32[128,1536]{1,0:T(8,128)}, f32[8,1536]{1,0:T(8,128)}) custom-call(bf16[512,1536]{1,0:T(8,128)(2,1)} %convolution_convert_fusion.5.refs_0_, f32[128,1536]{1,0:T(8,128)} %get-tuple-element.48.refs_1_, f32[128,1536]{1,0:T(8,128)} %get-tuple-element.53.refs_2_, f32[128,1536]{1,0:T(8,128)} %get-tuple-element.54.refs_3_, ...), custom_call_target="tpu_custom_call" | custom-call | tf_op jit(solution)/shard_map/z_step_7/pallas_call | solution.py:386
  424.0 5.8 z_total_8.1
  432.5 5.7 fusion.25.refs_1_
  439.9 4.3 convolution_convert_fusion.4.refs_2_
  444.2 58.7 %z_scatter_9.1 = (f32[128,1536]{1,0:T(8,128)}, f32[128,1536]{1,0:T(8,128)}, f32[128,1536]{1,0:T(8,128)}) custom-call(bf16[512,1536]{1,0:T(8,128)(2,1)} %fusion.31.refs_0_, bf16[512,1536]{1,0:T(8,128)(2,1)} %fusion.25.refs_1_, bf16[512,1536]{1,0:T(8,128)(2,1)} %convolution_convert_fusion.4.refs_2_), custom_call_target="tpu_custom_call" | custom-call | tf_op jit(solution)/shard_map/z_scatter_9/pallas_call | solution.py:412
  507.9 32.5 %deliver_10.1 = (bf16[2,128,1536]{2,1,0:T(8,128)(2,1)}, bf16[2,128,1536]{2,1,0:T(8,128)(2,1)}, bf16[2,128,1536]{2,1,0:T(8,128)(2,1)}) custom-call(bf16[128,1536]{1,0:T(8,128)(2,1)} %get-tuple-element.165.refs_0_, bf16[128,1536]{1,0:T(8,128)(2,1)} %fusion.61.refs_1_, bf16[128,1536]{1,0:T(8,128)(2,1)} %convert_element_type.354.refs_2_), custom_call_target="tpu_custom_call" | custom-call | tf_op jit(solution)/shard_map/deliver_10/pallas_call | solution.py:472
  552.0 30.9 %vector_sums.1 = (f32[2,16,1536]{2,1,0:T(8,128)}, f32[16,1536]{1,0:T(8,128)}, f32[2,16,384]{2,1,0:T(8,128)}) custom-call(f32[16,1536]{1,0:T(8,128)} %pad.58.model, f32[16,384]{1,0:T(8,128)} %concatenate.36.heads), custom_call_target="tpu_custom_call" | custom-call | tf_op jit(solution)/shard_map/vector_sums/pallas_call | solution.py:539
  584.6 5.3 convolution_convert_fusion.2
  599.2 5.9 convolution_convert_fusion.1
  605.1 6.6 convolution_convert_fusion
  611.7 124.2 %grad_sums.1 = bf16[2,48,3840]{2,1,0:T(8,128)(2,1)} custom-call(bf16[4,4,2,48,1152]{4,3,2,1,0:T(8,128)(2,1)} %bitcast.193, bf16[4,4,2,48,384]{4,3,2,1,0:T(8,128)(2,1)} %bitcast.220, bf16[4,4,2,48,768]{4,3,2,1,0:T(8,128)(2,1)} %bitcast.208, bf16[4,4,2,48,384]{4,3,2,1,0:T(8,128)(2,1)} %bitcast.221, bf16[4,4,2,48,384]{4,3,2,1,0:T(8,128)(2,1)} %bitcast.222, ...), custom_call_target="tpu_custom_call" | custom-call | tf_op jit(solution)/shard_map/grad_sums/pallas_call | solution.py:672
  746.4 18.7 %newton.1 = (f32[192,768]{1,0:T(8,128)}, f32[48,4480]{1,0:T(8,128)}) custom-call(f32[192,768]{1,0:T(8,128)} %bitcast.206, f32[48,4480]{1,0:T(8,128)} %bitcast.182), custom_call_target="tpu_custom_call" | custom-call | tf_op jit(solution)/shard_map/newton/pallas_call | solution.py:743
  (358 shorter events, 166.5 us)
Async XLA Ops:
  0.6 91.0 %copy-start = (f32[2,6,1536]{2,0,1:T(2,128)S(1)}, f32[2,6,1536]{2,0,1:T(2,128)}, u32[]{:S(2)}) copy-start(f32[2,6,1536]{2,0,1:T(2,128)} %param.19) | copy-start | bytes 221188
  84.9 6.8 copy-start.59
  84.9 6.9 copy-start.7
  99.8 12.0 %copy-start.5 = (f32[512,1152]{1,0:T(8,128)}, f32[512,1152]{1,0:T(8,128)S(1)}, u32[]{:S(2)}) copy-start(f32[512,1152]{1,0:T(8,128)S(1)} %convolution_add_fusion) | copy-start | bytes 7077892
  193.4 47.5 %copy-start.65 = (f32[4480]{0:T(1024)S(1)}, f32[4480]{0:T(1024)}, u32[]{:S(2)}) copy-start(f32[4480]{0:T(1024)} %param.27) | copy-start | bytes 53764
  248.2 10.4 %copy-start.76 = (f32[512,2304]{1,0:T(8,128)}, f32[512,2304]{1,0:T(8,128)S(1)}, u32[]{:S(2)}) copy-start(f32[512,2304]{1,0:T(8,128)S(1)} %fusion.8) | copy-start | bytes 14155780
  248.2 10.0 %copy-start.21 = (bf16[4,128,1536]{2,1,0:T(8,128)(2,1)S(1)}, bf16[4,128,1536]{2,1,0:T(8,128)(2,1)}, u32[]{:S(2)}) copy-start(bf16[4,128,1536]{2,1,0:T(8,128)(2,1)} %get-tuple-element.51) | copy-start | bytes 4718596
  258.6 9.4 %copy-start.29 = (bf16[512,1536]{1,0:T(8,128)(2,1)}, bf16[512,1536]{1,0:T(8,128)(2,1)S(1)}, u32[]{:S(2)}) copy-start(bf16[512,1536]{1,0:T(8,128)(2,1)S(1)} %multiply_convert_fusion.3) | copy-start | bytes 4718596
  267.9 9.0 %copy-start.77 = (bf16[512,2304]{1,0:T(8,128)(2,1)}, bf16[512,2304]{1,0:T(8,128)(2,1)S(1)}, u32[]{:S(2)}) copy-start(bf16[512,2304]{1,0:T(8,128)(2,1)S(1)} %get-tuple-element.218) | copy-start | bytes 7077892
  277.7 45.5 %copy-start.23 = (bf16[512,384]{0,1:T(8,128)(2,1)S(1)}, bf16[512,384]{0,1:T(8,128)(2,1)}, u32[]{:S(2)}) copy-start(bf16[512,384]{0,1:T(8,128)(2,1)} %copy.130) | copy-start | bytes 1179652
  413.1 7.3 copy-start.6
  413.1 7.3 copy-start.12
  423.4 9.1 %copy-start.39 = (bf16[512,384]{1,0:T(8,128)(2,1)S(1)}, bf16[512,384]{1,0:T(8,128)(2,1)}, u32[]{:S(2)}) copy-start(bf16[512,384]{1,0:T(8,128)(2,1)} %copy.166) | copy-start | bytes 1179652
  444.2 58.7 %copy-start.28 = (f32[128,1536]{1,0:T(8,128)S(1)}, f32[128,1536]{1,0:T(8,128)}, u32[]{:S(2)}) copy-start(f32[128,1536]{1,0:T(8,128)} %get-tuple-element.49.refs_1_) | copy-start | bytes 2359300
  444.2 61.1 %copy-start.9 = (bf16[128,1536]{1,0:T(8,128)(2,1)S(1)}, bf16[128,1536]{1,0:T(8,128)(2,1)}, u32[]{:S(2)}) copy-start(bf16[128,1536]{1,0:T(8,128)(2,1)} %get-tuple-element.151.refs_1_) | copy-start | bytes 1179652
  507.9 37.5 %copy-start.68 = (f32[8,1536]{1,0:T(8,128)S(1)}, f32[8,1536]{1,0:T(8,128)}, u32[]{:S(2)}) copy-start(f32[8,1536]{1,0:T(8,128)} %get-tuple-element.63) | copy-start | bytes 147460
  507.9 38.4 %copy-start.30 = (bf16[512,1536]{1,0:T(8,128)(2,1)S(1)}, bf16[512,1536]{1,0:T(8,128)(2,1)}, u32[]{:S(2)}) copy-start(bf16[512,1536]{1,0:T(8,128)(2,1)} %copy-done.29) | copy-start | bytes 4718596
  542.9 41.7 %copy-start.34 = (bf16[512,1536]{1,0:T(8,128)(2,1)S(1)}, bf16[512,1536]{1,0:T(8,128)(2,1)}, u32[]{:S(2)}) copy-start(bf16[512,1536]{1,0:T(8,128)(2,1)} %add_convert_fusion) | copy-start | bytes 4718596
  597.1 8.0 %slice-start = ((s8[4718592]{0:T(1024)(128)(4,1)}), s8[4194304]{0:T(1024)(128)(4,1)S(1)}, s32[]{:S(2)}) async-start(s8[4718592]{0:T(1024)(128)(4,1)} %bitcast.283), calls=%async_computation | async-start | bytes 8388608
  743.4 22.9 %copy-start.32 = (f32[24,6,768]{2,0,1:T(8,128)S(1)}, f32[24,6,768]{2,0,1:T(8,128)}, u32[]{:S(2)}) copy-start(f32[24,6,768]{2,0,1:T(8,128)} %param.22) | copy-start | bytes 1327108
  744.1 24.0 %copy-start.51 = (f32[24,2,768]{2,1,0:T(2,128)S(1)}, f32[24,2,768]{2,1,0:T(2,128)}, u32[]{:S(2)}) copy-start(f32[24,2,768]{2,1,0:T(2,128)} %param.23) | copy-start | bytes 442372
  744.1 24.8 %copy-start.26 = (f32[24,2,4480]{2,1,0:T(2,128)S(1)}, f32[24,2,4480]{2,1,0:T(2,128)}, u32[]{:S(2)}) copy-start(f32[24,2,4480]{2,1,0:T(2,128)} %param.24) | copy-start | bytes 2580484
  768.1 6.7 copy-start.47
  768.9 6.8 copy-start.1
  (57 other events, 171.4 us)

commit v2 on v1

--- a/solution.py
+++ b/solution.py
@@ -92,80 +92,23 @@
 HB = pl.BlockSpec(memory_space=pltpu.HBM)
 
 
-def gather_kernel(
-    wsend, tok, txt, cot, pos, wg, tok_all, txt_all, cot_all, pos_all,
-    wrecv, own, wx_s, wx_r, ac_s, ac_r, loc, xs, xr, ks, kr,
-):
+def flat(a, b):
+    return lax.rem(a + SIDE, SIDE) * SIDE + lax.rem(b + SIDE, SIDE)
+
+
+def steps_of(x, y, z, core):
+    return (
+        (chip(x + 1, y, z, core), chip(x - 1, y, z, core)),
+        (chip(x, y + 1, z, core), chip(x, y - 1, z, core)),
+    )
+
+
+def gather_xy(own, place, xs, xr, ks, kr):
     x, y, z, core = here()
-    zl = lax.rem(z, 2)
     mine = x * SIDE + y
-    greet(
-        [chip(x + 1, y, z, core), chip(x - 1, y, z, core), chip(x, y + 1, z, core), chip(x, y - 1, z, core)]
-        + column(x, y, z, core)
-    )
-    other = z + 1 - 2 * zl
-    away = remote(
-        wsend.at[1 - zl], wrecv.at[core], wx_s.at[0], wx_r.at[core], chip(x, y, other, zl)
-    )
-    away.start()
-    near = remote(wsend.at[zl], wrecv.at[core], wx_s.at[1], wx_r.at[core], chip(x, y, z, zl))
-    self_copy = pltpu.make_async_copy(wsend.at[zl], wrecv.at[core], loc.at[0])
-
-    @pl.when(core == zl)
-    def _():
-        self_copy.start()
-
-    @pl.when(core != zl)
-    def _():
-        near.start()
-
-    block = 2 * zl + core
-    acts, locals_ = [], []
-    for i, (src, dst) in enumerate(
-        ((tok, tok_all), (txt, txt_all), (cot, cot_all), (pos, pos_all))
-    ):
-        put = dst.at[block]
-        acts.append(
-            remote(src.at[1 - core], put, ac_s.at[i, 0], ac_r.at[i, 0], chip(x, y, z, 1 - core))
-        )
-        acts.append(
-            remote(src.at[0], put, ac_s.at[i, 1], ac_r.at[i, 1 + core], chip(x, y, z + 1, 0))
-        )
-        acts.append(
-            remote(src.at[1], put, ac_s.at[i, 2], ac_r.at[i, 1 + core], chip(x, y, z - 1, 1))
-        )
-        locals_.append(pltpu.make_async_copy(src.at[core], put, loc.at[1 + i]))
-    for copy in acts + locals_:
-        copy.start()
-
-    def got(slot):
-        remote(wsend.at[0], wrecv.at[slot], wx_s.at[0], wx_r.at[slot], chip(x, y, z, core)).wait_recv()
-
-    @pl.when(core == zl)
-    def _():
-        self_copy.wait()
-        got(1 - core)
-
-    @pl.when(core != zl)
-    def _():
-        near.wait_send()
-        got(0)
-        got(1)
-
-    first = wrecv[0].astype(F32)
-    second = wrecv[1].astype(F32)
-    own[0] = jnp.concatenate([first[:ROWS], second[:ROWS]], 0).astype(BF)
-    own[1] = jnp.concatenate([first[ROWS:], second[ROWS:]], 0).astype(BF)
-
-    flat = lambda a, b: lax.rem(a + SIDE, SIDE) * SIDE + lax.rem(b + SIDE, SIDE)
-
-    def place(part, index, half=None):
-        start, size = part * HALF, HALF
-        if half is not None:
-            start, size = start + half * QUARTER, QUARTER
-        return wg.at[index, core, :, pl.ds(start, size)]
-
-    sends, recvs, sibs = [], [], []
+    steps = steps_of(x, y, z, core)
+    sibling = chip(x, y, z, 1 - core)
+    sends, sibs = [], []
 
     def push(part, slot, src, index, device, half=None):
         copy = remote(src, place(part, index, half), xs.at[part, slot], xr.at[part, slot], device)
@@ -174,16 +117,9 @@
         return copy
 
     def to_sibling(part, slot, src, index):
-        copy = remote(
-            src, place(part, index), ks.at[part, slot], kr.at[part, slot], chip(x, y, z, 1 - core)
-        )
+        copy = remote(src, place(part, index), ks.at[part, slot], kr.at[part, slot], sibling)
         copy.start()
         sibs.append(copy)
-
-    steps = (
-        (chip(x + 1, y, z, core), chip(x - 1, y, z, core)),
-        (chip(x, y + 1, z, core), chip(x, y - 1, z, core)),
-    )
 
     def index_of(part, first_off, second_off):
         if part == 0:
@@ -200,9 +136,6 @@
         two[part, 0, "next"] = push(part, 4, own.at[part], mine, b_next)
         two[part, 0, "prev"] = push(part, 5, own.at[part], mine, b_prev)
         to_sibling(part, 0, own.at[part], mine)
-        local = pltpu.make_async_copy(own.at[part], place(part, mine), loc.at[5 + part])
-        local.start()
-        locals_.append(local)
 
     def second_start(part, k, offset):
         b_next, b_prev = steps[1 - part]
@@ -215,6 +148,7 @@
     offsets = (0, -1, 1, 2)
     for part in (0, 1):
         a_next, a_prev = steps[part]
+        yield
         one[part, "next"].wait_recv()
         index = index_of(part, -1, 0)
         one[part, "far0"] = push(part, 2, place(part, index, 0), index, a_next, 0)
@@ -242,30 +176,23 @@
         to_sibling(part, 4 * k + 3, place(part, index), index)
 
     for part in (0, 1):
+        yield
         second_forward(part, 0)
     for part in (0, 1):
+        yield
         one[part, "far0"].wait_recv()
         one[part, "far1"].wait_recv()
         second_start(part, 3, 2)
     for k in (1, 2, 3):
         for part in (0, 1):
+            yield
             second_forward(part, k)
         for part in (0, 1):
             second_finish(part, k - 1)
     for part in (0, 1):
+        yield
         second_finish(part, 3)
-
-    away.wait_send()
-    for copy in locals_:
-        copy.wait()
-    for copy in acts:
-        copy.wait_send()
-    for i in range(4):
-        for slot in range(3):
-            acts[3 * i].wait_recv() if slot == 0 else remote(
-                (tok, txt, cot, pos)[i].at[0], (tok_all, txt_all, cot_all, pos_all)[i].at[0],
-                ac_s.at[i, 0], ac_r.at[i, slot], chip(x, y, z, core),
-            ).wait_recv()
+    yield
     for copy in sends:
         copy.wait_send()
     for copy in sibs:
@@ -273,29 +200,398 @@
         copy.wait_recv()
 
 
-def gather_all(wsend, tok, txt, cot, pos):
-    acts = jax.ShapeDtypeStruct((SIDE, TOK, D), BF)
+GATHER_SEMS = ((2, 20), (2, 20), (2, 16), (2, 16))
+
+
+def advance(job, count=1):
+    for _ in range(count):
+        next(job, None)
+
+
+def finish(job):
+    for _ in job:
+        pass
+
+
+def share_rows(send, recv, s, r, l):
+    x, y, z, core = here()
+    zl = lax.rem(z, 2)
+    away = remote(send.at[1 - zl], recv.at[core], s.at[0], r.at[core], chip(x, y, z + 1 - 2 * zl, zl))
+    near = remote(send.at[zl], recv.at[core], s.at[1], r.at[core], chip(x, y, z, zl))
+    self_copy = pltpu.make_async_copy(send.at[zl], recv.at[core], l.at[0])
+
+    def got(slot):
+        remote(send.at[0], recv.at[slot], s.at[0], r.at[slot], chip(x, y, z, core)).wait_recv()
+
+    def start():
+        away.start()
+
+        @pl.when(core == zl)
+        def _():
+            self_copy.start()
+
+        @pl.when(core != zl)
+        def _():
+            near.start()
+
+    def wait(own):
+        @pl.when(core == zl)
+        def _():
+            self_copy.wait()
+            got(1 - core)
+
+        @pl.when(core != zl)
+        def _():
+            near.wait_send()
+            got(0)
+            got(1)
+
+        first = recv[0].astype(F32)
+        second = recv[1].astype(F32)
+        own[0] = jnp.concatenate([first[:ROWS], second[:ROWS]], 0).astype(BF)
+        own[1] = jnp.concatenate([first[ROWS:], second[ROWS:]], 0).astype(BF)
+
+    return start, wait, away.wait_send
+
+
+def share_clip(src, dst, s, r, l):
+    x, y, z, core = here()
+    put = dst.at[2 * lax.rem(z, 2) + core]
+    copies = [
+        remote(src.at[1 - core], put, s.at[0], r.at[0], chip(x, y, z, 1 - core)),
+        remote(src.at[0], put, s.at[1], r.at[1 + core], chip(x, y, z + 1, 0)),
+        remote(src.at[1], put, s.at[2], r.at[1 + core], chip(x, y, z - 1, 1)),
+    ]
+    local = pltpu.make_async_copy(src.at[core], put, l)
+
+    def start():
+        for copy in copies:
+            copy.start()
+        local.start()
+
+    def wait():
+        local.wait()
+        for slot in range(3):
+            remote(src.at[0], dst.at[0], s.at[0], r.at[slot], chip(x, y, z, core)).wait_recv()
+
+    def drain():
+        for copy in copies:
+            copy.wait_send()
+
+    return start, wait, drain
+
+
+def split3(values):
+    return [values[:, i * HW : (i + 1) * HW] for i in range(values.shape[1] // HW)]
+
+
+def swap_halves(values):
+    return pltpu.roll(values, HEAD // 2, 1)
+
+
+def rope_pair(table):
+    lane = lax.broadcasted_iota(jnp.int32, table.shape, 1)
+    other = swap_halves(table)
+    front = lane < HEAD // 2
+    return jnp.where(front, table, other), jnp.where(front, -other, table)
+
+
+def head_slice(h):
+    return slice(h * HEAD, (h + 1) * HEAD)
+
+
+SCALE = HEAD ** (-0.5)
+
+
+def softmax_rows(query, keys):
+    scores = contract_last(query, keys) * SCALE
+    peak = jnp.max(scores, -1, keepdims=True)
+    raised = jnp.exp(scores - peak)
+    return raised * (1.0 / jnp.sum(raised, -1, keepdims=True))
+
+
+def attend_clip(query, keys, values, out):
+    for h in range(HEADS):
+        cols = head_slice(h)
+        for start in range(0, SEQ, 256):
+            rows = slice(start, start + 256)
+            weights = softmax_rows(query[rows, cols], keys[:, cols]).astype(BF)
+            out[rows, cols] = product(weights, values[:, cols]).astype(BF)
+
+
+class Stats:
+    def __init__(self, buffer, send, recv):
+        self.buffer, self.send, self.recv = buffer, send, recv
+
+    def start(self, turn, columns):
+        x, y, z, core = here()
+        lane = lax.broadcasted_iota(jnp.int32, (SEQ, 128), 1)
+        packed = jnp.zeros((SEQ, 128), F32)
+        for i, column_values in enumerate(columns):
+            packed = jnp.where(lane == i, column_values, packed)
+        self.buffer[turn, 0] = packed.T[:8]
+        copies = []
+        for k in (2, 1, 3):
+            copies.append(
+                remote(self.buffer.at[turn, 0], self.buffer.at[turn, k], self.send.at[turn, k - 1],
+                       self.recv.at[turn, k - 1], chip(x, y, z + k, core))
+            )
+            copies[-1].start()
+
+        def wait():
+            for copy in copies:
+                copy.wait()
+            total = (self.buffer[turn, 0] + self.buffer[turn, 1]) + (
+                self.buffer[turn, 2] + self.buffer[turn, 3]
+            )
+            spread = jnp.concatenate([total, jnp.zeros((120, SEQ), F32)], 0).T
+            return [spread[:, i : i + 1] for i in range(len(columns))]
+
+        return wait
+
+
+def block_slice(index):
+    return pl.ds(pl.multiple_of(index * TOK, TOK), TOK)
+
+
+def scatter_product(left, right, part, got, send, recv):
+    x, y, z, core = here()
+    copies = []
+    for k in (2, 1, 3, 0):
+        rows = block_slice(block_of(z + k))
+        part[rows] = contract_last(left[rows], right).astype(BF)
+        if k:
+            copies.append(
+                remote(part.at[rows], got.at[k - 1], send.at[k - 1], recv.at[k - 1], chip(x, y, z + k, core))
+            )
+            copies[-1].start()
+    return copies
+
+
+def collect(part, got, copies):
+    z = here()[2]
+    for copy in copies:
+        copy.wait_recv()
+    total = part[block_slice(block_of(z))].astype(F32)
+    for k in range(3):
+        total = total + got[k].astype(F32)
+    return total
+
+
+def spread_block(out, value, send, recv):
+    x, y, z, core = here()
+    rows = block_slice(block_of(z))
+    out[rows] = value
+    copies = []
+    for k in (2, 1, 3):
+        copies.append(
+            remote(out.at[rows], out.at[rows], send.at[k - 1], recv.at[k - 1], chip(x, y, z + k, core))
+        )
+        copies[-1].start()
+    return copies
+
+
+def inverse_root(total):
+    return lax.rsqrt(total * (1.0 / D) + NORM_EPSILON)
+
+
+V_SELF, V_CROSS, V_DOWN, V_GAIN, V_BIAS = 6, 7, 8, 9, 10
+W_QKV, W_QUERY, W_TEXT, W_SELF, W_CROSS = (
+    slice(0, 3 * HW), slice(3 * HW, 4 * HW), slice(4 * HW, 6 * HW), slice(6 * HW, 7 * HW), slice(7 * HW, 8 * HW),
+)
+ATTN = 8 * HW
+
+
+def forward_kernel(
+    send_attn, send_mlp, tok, txt, cot, tab, heads, vec,
+    w_attn, w_up, w_down, cot_all, tab_all, input_one, input_three, input_mlp, query_lin, key_lin,
+    query_two_lin, key_two_lin, inv, query_rot, key_rot, value_low, query_two, key_two, value_two,
+    mixed, mixed_two, branch_one, after_one, after_two, tok_all, txt_all,
+    wa, got_attn, got_mlp, own_attn, own_mlp, part_one, part_two, blocks, stat,
+    xs, xr, ks, kr, ms, mr, js, jr, rs, rr, cs, cr, loc, stat_s, stat_r, zs, zr, gs, gr,
+):
+    x, y, z, core = here()
+    mine = x * SIDE + y
+    greet(
+        [device for pair in steps_of(x, y, z, core) for device in pair] + column(x, y, z, core)
+    )
+    attn_start, attn_wait, attn_drain = share_rows(send_attn, got_attn, rs.at[0], rr.at[0], loc.at[0])
+    mlp_start, mlp_wait, mlp_drain = share_rows(send_mlp, got_mlp, rs.at[1], rr.at[1], loc.at[1])
+    acts = [
+        share_clip(src, dst, cs.at[i], cr.at[i], loc.at[2 + i, 0])
+        for i, (src, dst) in enumerate(
+            ((tok, tok_all), (tab, tab_all), (txt, txt_all), (cot, cot_all))
+        )
+    ]
+    attn_start()
+    acts[0][0]()
+    acts[1][0]()
+    attn_wait(own_attn)
+
+    def attn_place(part, index, half=None):
+        start, size = part * (ATTN // 2), ATTN // 2
+        if half is not None:
+            start, size = start + half * (ATTN // 4), ATTN // 4
+        rows = pl.ds(pl.multiple_of(index * (2 * PAIR) + core * PAIR, PAIR), PAIR)
+        return wa.at[rows, pl.ds(start, size)]
+
+    def mlp_place(part, index, half=None):
+        start, size = (0, FF) if half is None else (half * (FF // 2), FF // 2)
+        rows = pl.ds(pl.multiple_of(index * (2 * PAIR) + core * PAIR, PAIR), PAIR)
+        return (w_up, w_down)[part].at[rows, pl.ds(start, size)]
+
+    gather_attn = gather_xy(own_attn, attn_place, xs, xr, ks, kr)
+    advance(gather_attn)
+    for part in (0, 1):
+        attn_place(part, mine)[...] = own_attn[part]
+    acts[2][0]()
+    mlp_start()
+    acts[3][0]()
+    acts[0][1]()
+
+    def norm_block(i, carry):
+        normed, _ = plain_norm(tok_all[i].astype(F32))
+        input_one[block_slice(i)] = (normed * (1.0 + vec[1:2]) + vec[0:1]).astype(BF)
+        return carry
+
+    advance(gather_attn, 2)
+    lax.fori_loop(0, 2, norm_block, 0)
+    advance(gather_attn, 2)
+    lax.fori_loop(2, 4, norm_block, 0)
+    advance(gather_attn, 2)
+    mlp_wait(own_mlp)
+    locals_ = []
+    for part in (0, 1):
+        locals_.append(pltpu.make_async_copy(own_mlp.at[part], mlp_place(part, mine), loc.at[6, part]))
+        locals_[-1].start()
+    finish(gather_attn)
+    gather_mlp = gather_xy(own_mlp, mlp_place, ms, mr, js, jr)
+    advance(gather_mlp)
+    locals_.append(pltpu.make_async_copy(wa, w_attn, loc.at[7, 0]))
+    locals_[-1].start()
+    acts[1][1]()
+    acts[2][1]()
+
+    stats = Stats(stat, stat_s, stat_r)
+    query_lin[...] = product(input_one[...], wa[:, 0:HW]) + heads[0:1]
+    key_lin[...] = product(input_one[...], wa[:, HW : 2 * HW]) + heads[1:2]
+    words = txt_all[...].reshape(SEQ, D)
+    key_two_lin[...] = product(words, wa[:, 4 * HW : 5 * HW]) + heads[6:7]
+    advance(gather_mlp)
+    norm_wait = stats.start(
+        0,
+        [
+            jnp.sum(ref[...] * ref[...], -1, keepdims=True)
+            for ref in (query_lin, key_lin, key_two_lin)
+        ],
+    )
+    value_low[...] = (product(input_one[...], wa[:, 2 * HW : 3 * HW]) + heads[2:3]).astype(BF)
+    advance(gather_mlp)
+    value_two[...] = (product(words, wa[:, 5 * HW : 6 * HW]) + heads[7:8]).astype(BF)
+    advance(gather_mlp)
+    lane = lax.broadcasted_iota(jnp.int32, (SEQ, 128), 1)
+    inverse_query, inverse_key, inverse_key_two = [inverse_root(v) for v in norm_wait()]
+    inv[...] = jnp.where(
+        lane == 0, inverse_query, jnp.where(lane == 1, inverse_key, jnp.where(lane == 2, inverse_key_two, 0.0))
+    )
+    cosine, sine = rope_pair(tab_all[...].reshape(SEQ, HEAD))
+    for h in range(HEADS):
+        cols = head_slice(h)
+        for lin, inverse, gain, out in (
+            (query_lin, inverse_query, 3, query_rot),
+            (key_lin, inverse_key, 4, key_rot),
+        ):
+            value = lin[:, cols] * inverse * (1.0 + heads[gain : gain + 1, cols])
+            out[:, cols] = (value * cosine + swap_halves(value) * sine).astype(BF)
+    key_two[...] = (key_two_lin[...] * inverse_key_two * (1.0 + heads[9:10])).astype(BF)
+    attend_clip(query_rot, key_rot, value_low, mixed)
+    advance(gather_mlp)
+    copies = scatter_product(mixed, wa[:, W_SELF], part_one, blocks.at[0], zs.at[0], zr.at[0])
+    drains = list(copies)
+    advance(gather_mlp, 3)
+    branch = collect(part_one, blocks.at[0], copies) + vec[V_SELF : V_SELF + 1]
+    branch_one[...] = branch
+    after = tok_all[block_of(z)].astype(F32) + vec[2:3] * branch
+    after_one[...] = after
+    normed, _ = plain_norm(after)
+    copies = spread_block(
+        input_three,
+        (normed * (1.0 + vec[V_GAIN : V_GAIN + 1]) + vec[V_BIAS : V_BIAS + 1]).astype(BF),
+        gs.at[0],
+        gr.at[0],
+    )
+    drains += copies
+    advance(gather_mlp, 3)
+    for copy in copies:
+        copy.wait_recv()
+    query_two_lin[...] = product(input_three[...], wa[:, W_QUERY]) + heads[5:6]
+    norm_wait = stats.start(1, [jnp.sum(query_two_lin[...] * query_two_lin[...], -1, keepdims=True)])
+    advance(gather_mlp, 1)
+    inverse_query_two = inverse_root(norm_wait()[0])
+    inv[...] = jnp.where(lane == 3, inverse_query_two, inv[...])
+    query_two[...] = (query_two_lin[...] * inverse_query_two * (1.0 + heads[8:9])).astype(BF)
+    attend_clip(query_two, key_two, value_two, mixed_two)
+    copies = scatter_product(mixed_two, wa[:, W_CROSS], part_two, blocks.at[1], zs.at[1], zr.at[1])
+    drains += copies
+    advance(gather_mlp, 2)
+    after = after_one[...] + collect(part_two, blocks.at[1], copies) + vec[V_CROSS : V_CROSS + 1]
+    after_two[...] = after
+    normed, _ = plain_norm(after)
+    copies = spread_block(
+        input_mlp, (normed * (1.0 + vec[4:5]) + vec[3:4]).astype(BF), gs.at[1], gr.at[1]
+    )
+    drains += copies
+    finish(gather_mlp)
+    for copy in copies:
+        copy.wait_recv()
+    for copy in drains:
+        copy.wait_send()
+    for copy in locals_:
+        copy.wait()
+    acts[3][1]()
+    for act in acts:
+        act[2]()
+    attn_drain()
+    mlp_drain()
+
+
+def forward(send_attn, send_mlp, tok, txt, cot, tab, heads, vec):
     dma = pltpu.SemaphoreType.DMA
+    sds = jax.ShapeDtypeStruct
+    wide, lin, low = sds((SEQ, D), BF), sds((SEQ, HW), F32), sds((SEQ, HW), BF)
+    block = sds((TOK, D), F32)
+    outs = [
+        (sds((D, ATTN), BF), HB), (sds((D, FF), BF), HB), (sds((D, FF), BF), HB),
+        (sds((SIDE, TOK, D), BF), HB), (sds((SIDE, TOK, HEAD), F32), VM),
+        (wide, VM), (wide, VM), (wide, VM),
+        (lin, VM), (lin, VM), (lin, VM), (lin, VM), (sds((SEQ, 128), F32), VM),
+        (low, VM), (low, VM), (low, VM), (low, VM), (low, VM), (low, VM), (low, VM), (low, VM),
+        (block, VM), (block, VM), (block, VM),
+        (sds((SIDE, TOK, D), BF), VM), (sds((SIDE, TOK, D), BF), VM),
+    ]
     return pl.pallas_call(
-        gather_kernel,
-        out_shape=[
-            jax.ShapeDtypeStruct((SIDE * SIDE, 2, PAIR, COLS), BF),
-            acts,
-            acts,
-            acts,
-            jax.ShapeDtypeStruct((SIDE, 8, TOK), F32),
-        ],
-        in_specs=[VM, HB, HB, HB, VM],
-        out_specs=[HB, HB, HB, HB, VM],
+        forward_kernel,
+        out_shape=[shape for shape, _ in outs],
+        in_specs=[VM, VM, HB, HB, HB, VM, VM, VM],
+        out_specs=[spec for _, spec in outs],
         scratch_shapes=[
-            pltpu.VMEM((2, PAIR, HALF), BF),
-            pltpu.VMEM((2, PAIR, HALF), BF),
-            dma((2,)), dma((2,)), dma((4, 3)), dma((4, 3)), dma((7,)),
-            dma((2, 20)), dma((2, 20)), dma((2, 16)), dma((2, 16)),
+            pltpu.VMEM((D, ATTN), BF),
+            pltpu.VMEM((2, PAIR, ATTN // 2), BF),
+            pltpu.VMEM((2, PAIR, FF), BF),
+            pltpu.VMEM((2, PAIR, ATTN // 2), BF),
+            pltpu.VMEM((2, PAIR, FF), BF),
+            pltpu.VMEM((SEQ, D), BF),
+            pltpu.VMEM((SEQ, D), BF),
+            pltpu.VMEM((2, 3, TOK, D), BF),
+            pltpu.VMEM((2, 4, 8, SEQ), F32),
+            *[dma(s) for s in GATHER_SEMS],
+            *[dma(s) for s in GATHER_SEMS],
+            dma((2, 2)), dma((2, 2)), dma((4, 3)), dma((4, 3)), dma((8, 2)),
+            dma((2, 3)), dma((2, 3)), dma((2, 3)), dma((2, 3)), dma((2, 3)), dma((2, 3)),
         ],
         compiler_params=params(0),
-        name="gather_weights",
-    )(wsend, tok, txt, cot, pos)
+        name="forward",
+    )(send_attn, send_mlp, tok, txt, cot, tab, heads, vec)
 
 
 def z_peers(x, y, z, core):
@@ -825,18 +1121,9 @@
     return lax.dot_general(left, right, (((0,), (0,)), ((), ())), preferred_element_type=F32)
 
 
-def attend(query, keys, values):
+def attend_back(query, keys, values, grad_mixed):
     scores = jnp.einsum("qhe,khe->hqk", query, keys, preferred_element_type=F32) * HEAD ** (-0.5)
-    row_peak = jnp.max(scores, -1, keepdims=True)
-    log_total = row_peak + jnp.log(jnp.sum(jnp.exp(scores - row_peak), -1, keepdims=True))
-    weights = jnp.exp(scores - log_total).astype(BF)
-    mixed = jnp.einsum("hqk,khe->qhe", weights, values, preferred_element_type=F32)
-    return (merge_heads(mixed), log_total)
-
-
-def attend_back(query, keys, values, log_total, grad_mixed):
-    scores = jnp.einsum("qhe,khe->hqk", query, keys, preferred_element_type=F32) * HEAD ** (-0.5)
-    weights = jnp.exp(scores - log_total)
+    weights = jax.nn.softmax(scores, -1)
     grad_weights = jnp.einsum("qhe,khe->hqk", grad_mixed, values, preferred_element_type=F32)
     row_delta = jnp.sum(weights * grad_weights, -1, keepdims=True)
     grad_scores = (weights * (grad_weights - row_delta)).astype(BF)
@@ -854,24 +1141,6 @@
 
 def block_struct():
     return jax.ShapeDtypeStruct((TOK, D), F32)
-
-
-def after_self(total, extras, outs):
-    residual, rows = extras
-    branch = total + rows[0:1]
-    after = residual[...].astype(F32) + rows[1:2] * branch
-    normed, _ = plain_norm(after)
-    outs[0][...] = branch
-    outs[1][...] = after
-    return (normed * (1.0 + rows[2:3]) + rows[3:4]).astype(BF)
-
-
-def after_cross(total, extras, outs):
-    residual, rows = extras
-    after = residual[...] + total + rows[0:1]
-    normed, _ = plain_norm(after)
-    outs[0][...] = after
-    return (normed * (1.0 + rows[1:2]) + rows[2:3]).astype(BF)
 
 
 def back_mlp(total, extras, outs):
@@ -915,85 +1184,49 @@
 
     low_in = attn_in.astype(BF).reshape(ROWS, 6, 2, HW).transpose(2, 0, 1, 3).reshape(2, ROWS, -1)
     low_out = attn_out.astype(BF).reshape(ROWS, 2, 2, HW).transpose(2, 0, 1, 3).reshape(2, ROWS, -1)
-    low_mlp = jnp.pad(
-        mlp.astype(BF).reshape(ROWS, 2, 2, FF_REAL).transpose(2, 0, 1, 3),
+    send_attn = jnp.concatenate([low_in, low_out], -1).reshape(2, ROWS, 2, ATTN // 2)
+    send_attn = send_attn.transpose(0, 2, 1, 3).reshape(2, PAIR, ATTN // 2)
+    send_mlp = jnp.pad(
+        mlp.astype(BF).reshape(ROWS, 2, 2, FF_REAL).transpose(2, 1, 0, 3),
         ((0, 0), (0, 0), (0, 0), (0, FF - FF_REAL)),
-    ).reshape(2, ROWS, -1)
-    packed = jnp.concatenate([low_in, low_out, low_mlp], -1)
-    packed = packed.reshape(2, ROWS, 2, HALF).transpose(0, 2, 1, 3).reshape(2, PAIR, HALF)
-    places = jnp.pad(positions.transpose(1, 0, 2), ((0, 0), (0, 5), (0, 0))).astype(F32)
-    gathered, tok_all, txt_all, cot_all, pos_all = gather_all(packed, tokens, text, cotangent, places)
-    weights = gathered.reshape(D, COLS)
-
-    def matrix(start, width):
-        return lax.slice(weights, (0, start), (D, start + width))
-
-    w_qkv = matrix(C_IN, 3 * HW)
-    w_query = matrix(C_IN + 3 * HW, HW)
-    w_text = matrix(C_IN + 4 * HW, 2 * HW)
-    w_self = matrix(C_OUT, HW)
-    w_cross = matrix(C_OUT + HW, HW)
-    w_up = matrix(C_UP, FF)
-    w_down = matrix(C_DOWN, FF)
+    ).reshape(2, PAIR, FF)
+    cosine, sine = rope_tables(positions.reshape(3, 2 * TOK))
+    table = jnp.concatenate([cosine, sine], -1).reshape(2, TOK, HEAD)
 
     heads = lax.dynamic_slice(head_vectors, (0, zl * HW), (10, HW))
     bias_up = jnp.pad(lax.dynamic_slice(up_bias, (zl * FF_REAL,), (FF_REAL,)), (0, FF - FF_REAL))
     modulation = model_vectors[5:] + lax.dynamic_index_in_dim(time_embedding, core, 0, False)
     shift_one, scale_one, gate_one, shift_two, scale_two, gate_two = [modulation[i] for i in range(6)]
-    cosine, sine = rope_tables(pos_all[:, :3].transpose(1, 0, 2).reshape(3, SEQ))
-    cosine, sine = cosine[:, None, :], sine[:, None, :]
+    vectors = jnp.pad(jnp.concatenate([modulation, model_vectors[:5]], 0), ((0, 5), (0, 0)))
+
+    (
+        w_attn, w_up, w_down, cot_all, tab_all, input_one, input_three, input_mlp, query_lin, key_lin,
+        query_two_lin, key_two_lin, inv, query_rot, key_rot, value_low, query_two, key_two, value_two,
+        mixed_low, mixed_two_low, branch_one, after_one, after_two, tok_all, txt_all,
+    ) = forward(
+        send_attn, send_mlp, tokens, text, cotangent, table,
+        jnp.pad(heads, ((0, 6), (0, 0))), vectors,
+    )
+    w_qkv, w_query, w_text, w_self, w_cross = [
+        w_attn[:, s] for s in (W_QKV, W_QUERY, W_TEXT, W_SELF, W_CROSS)
+    ]
+    inverse_query, inverse_key, inverse_key_two, inverse_query_two = [
+        inv[:, i : i + 1] for i in range(4)
+    ]
+    query_rot, key_rot, value_low, query_two, key_two, value_two = [
+        split_heads(v) for v in (query_rot, key_rot, value_low, query_two, key_two, value_two)
+    ]
+    tab_all = tab_all.reshape(SEQ, 1, HEAD)
+    cosine, sine = tab_all[..., : HEAD // 2], tab_all[..., HEAD // 2 :]
 
     def block_rows(values):
         return lax.dynamic_slice(values, (block * TOK, 0), (TOK, values.shape[1]))
 
-    tok_all = tok_all.reshape(SEQ, D)
+    cot_all = cot_all.reshape(SEQ, D)
     words = txt_all.reshape(SEQ, D)
-    cot_all = cot_all.reshape(SEQ, D)
-    tok_own = block_rows(tok_all)
+    tok_own = lax.dynamic_index_in_dim(tok_all, block, 0, False)
     cot_own = block_rows(cot_all)
 
-    normed_one, _ = plain_norm(tok_all.astype(F32))
-    input_one = (normed_one * (1.0 + scale_one) + shift_one).astype(BF)
-    qkv = product(input_one, w_qkv) + heads[0:3].reshape(-1)
-    query_lin, key_lin, value_lin = qkv[:, :HW], qkv[:, HW : 2 * HW], qkv[:, 2 * HW :]
-    kv_two = product(words, w_text) + heads[6:8].reshape(-1)
-    key_two_lin, value_two_lin = kv_two[:, :HW], kv_two[:, HW:]
-    squares = z_total(
-        stack_rows([jnp.sum(v * v, -1) for v in (query_lin, key_lin, key_two_lin)]), 1
-    )
-    inverses = lax.rsqrt(squares / D + NORM_EPSILON)
-    inverse_query, inverse_key, inverse_key_two = [inverses[i][:, None] for i in range(3)]
-    query_rot = rotate(
-        split_heads(query_lin * inverse_query * (1.0 + heads[3])), cosine, sine
-    ).astype(BF)
-    key_rot = rotate(split_heads(key_lin * inverse_key * (1.0 + heads[4])), cosine, sine).astype(BF)
-    value_low = split_heads(value_lin.astype(BF))
-    mixed, log_one = attend(query_rot, key_rot, value_low)
-    mixed_low = mixed.astype(BF)
-    part = contract_last(mixed_low, w_self).astype(BF)
-    input_three, branch_one, after_one = z_step(
-        part,
-        [tok_own, stack_rows([model_vectors[0], gate_one, model_vectors[3], model_vectors[4]])],
-        after_self,
-        [block_struct(), block_struct()],
-        2,
-    )
-    query_two_lin = product(input_three, w_query) + heads[5]
-    squares_two = z_total(stack_rows([jnp.sum(query_two_lin * query_two_lin, -1)]), 3)
-    inverse_query_two = lax.rsqrt(squares_two[0] / D + NORM_EPSILON)[:, None]
-    query_two = split_heads((query_two_lin * inverse_query_two * (1.0 + heads[8])).astype(BF))
-    key_two = split_heads((key_two_lin * inverse_key_two * (1.0 + heads[9])).astype(BF))
-    value_two = split_heads(value_two_lin.astype(BF))
-    mixed_two, log_two = attend(query_two, key_two, value_two)
-    mixed_two_low = mixed_two.astype(BF)
-    part = contract_last(mixed_two_low, w_cross).astype(BF)
-    input_mlp, after_two = z_step(
-        part,
-        [after_one, stack_rows([model_vectors[1], scale_two, shift_two])],
-        after_cross,
-        [block_struct()],
-        4,
-    )
     hidden_lin = product(input_mlp, w_up) + bias_up
     hidden_act, gelu_pullback = jax.vjp(partial(jax.nn.gelu, approximate=True), hidden_lin)
     hidden_low = hidden_act.astype(BF)
@@ -1010,7 +1243,7 @@
     )
     grad_mixed_two = product(grad_branch_two, w_cross).astype(BF)
     grad_query_two, grad_key_two, grad_value_two = attend_back(
-        query_two, key_two, value_two, log_two, split_heads(grad_mixed_two)
+        query_two, key_two, value_two, split_heads(grad_mixed_two)
     )
     grad_query_two, grad_key_two = merge_heads(grad_query_two), merge_heads(grad_key_two)
     scaled_query_two = grad_query_two * (1.0 + heads[8])
@@ -1039,7 +1272,7 @@
     )
     grad_mixed = product(grad_branch_one, w_self).astype(BF)
     grad_query_rot, grad_key_rot, grad_value = attend_back(
-        query_rot, key_rot, value_low, log_one, split_heads(grad_mixed)
+        query_rot, key_rot, value_low, split_heads(grad_mixed)
     )
     grad_query_norm = merge_heads(rotate(grad_query_rot, cosine, -sine))
     grad_key_norm = merge_heads(rotate(grad_key_rot, cosine, -sine))

time: 787 us -> 736 us (0.935)
  Pallas kernels: 539 us -> 519 us
  local copies, waits for them, and re-layouts: 54.7 us -> 43.7 us
    pallas_call x4 -> x2, Pallas kernels: 171 us -> 86.6 us  [z_step(): pl.pallas_call(partial(step_kernel, compute, len(extras), len(out_shapes)...]
    pallas_call x1, Pallas kernels: 77.9 us -> 156 us  [forward(): pl.pallas_call(forward_kernel, out_shape=[shape for shape, _ in outs], in...]
    pallas_call x4 -> x2, Pallas kernels: 24.8 us -> 11.3 us  [z_total(): pl.pallas_call(total_kernel, out_shape=jax.ShapeDtypeStruct(values.shape,...]
    dot_general x7 -> x5, matrix products: 39.3 us -> 33.5 us  [contract_last(): lax.dot_general(left, right, (((1,), (1,)), ((), ())), preferred_element_...]
    dot_general x7 -> x4, matrix products: 33.5 us -> 27.8 us  [product(): return jnp.dot(left, right, preferred_element_type=F32)]
where the time goes in v2:
time: 736 us; the launch traced here: 730 us
  Pallas kernels  519 us (71%)
  matrix products  108 us (15%)
  other arithmetic  57.4 us (8%)
  local copies, waits for them, and re-layouts  43.7 us (6%)
    pallas_call x1, Pallas kernels, forward(): pl.pallas_call(forward_kernel, out_shape=[shape for shape, _ in outs], in...  156 us
    pallas_call x1, Pallas kernels, grad_sums(): pl.pallas_call(grad_kernel, out_shape=jax.ShapeDtypeStruct((2, PAIR, HALF...  125 us
    pallas_call x2, Pallas kernels, z_step(): pl.pallas_call(partial(step_kernel, compute, len(extras), len(out_shapes)...  86.6 us
    pallas_call x1, Pallas kernels, z_scatter(): pl.pallas_call(partial(scatter_kernel, count), out_shape=[jax.ShapeDtypeS...  58 us
    dot_general x5, matrix products, contract_last(): lax.dot_general(left, right, (((1,), (1,)), ((), ())), preferred_element_...  33.5 us
    pallas_call x1, Pallas kernels, deliver(): pl.pallas_call(partial(deliver_kernel, count), out_shape=[jax.ShapeDtypeS...  33 us
    pallas_call x1, Pallas kernels, vector_sums(): pl.pallas_call(vector_kernel, out_shape=[jax.ShapeDtypeStruct((2, 16, D),...  30.8 us
    dot_general x4, matrix products, product(): return jnp.dot(left, right, preferred_element_type=F32)  27.8 us

profile of v2, /device:TPU:1, one launch (start us, length us, event | category | flops | bytes accessed | tf_op | source)
XLA Modules:
  0.0 730.5 jit_solution(8921390758093416689)
XLA Ops:
  8.7 155.7 %forward.1 = (bf16[1536,3072]{1,0:T(8,128)(2,1)}, bf16[1536,2304]{1,0:T(8,128)(2,1)}, bf16[1536,2304]{1,0:T(8,128)(2,1)}, bf16[4,128,1536]{2,1,0:T(8,128)(2,1)},...) custom-call(bf16[2,48,1536]{2,1,0:T(8,128)(2,1)} %bitcast.219, ...), custom_call_target="tpu_custom_call" | custom-call | tf_op jit(solution)/shard_map/forward/pallas_call | solution.py:572
  167.9 8.6 %fusion.89 = f32[512,2304]{1,0:T(8,128)} fusion(bf16[512,1536]{1,0:T(8,128)(2,1)S(1)} %multiply_convert_fusion.3, bf16[1536,2304]{1,0:T(8,128)(2,1)} %get-tuple-element.62), kind=kOutput, calls=%fused_computation.211 | convolution fusion | flops 3623878656 | bytes 13369344 | tf_op jit(solution)/shard_map/dot_general | solution.py:1113
  176.6 12.1 %convert_reduce_fusion = (f32[2304]{0:T(1024)}, bf16[512,2304]{1,0:T(8,128)(2,1)}, f32[512,2304]{1,0:T(8,128)S(1)}) fusion(f32[512,2304]{1,0:T(8,128)} %fusion.89, f32[2304]{0:T(1024)S(1)} %pad.37, bf16[512,1536]{1,0:T(8,128)(2,1)S(1)} %copy-done.62, bf16[1536,2304]{1,0:T(8,128)(2,1)} %get-tuple-element.61), kind=kOutput, calls=%fused_computation.15 | convolution fusion | flops 3651008256 | bytes 20465664 | tf_op jit(solution)/shard_map/dot_general | solution.py:1113
  188.7 10.2 %convolution_convert_fusion.7.refs_0_ = bf16[512,1536]{1,0:T(8,128)(2,1)} fusion(bf16[1536,2304]{1,0:T(8,128)(2,1)} %get-tuple-element.62, f32[512,2304]{1,0:T(8,128)S(1)} %get-tuple-element.230), kind=kOutput, calls=%fused_computation.31 | convolution fusion | flops 3635281920 | bytes 13369344 | tf_op jit(solution)/shard_map/dot_general | solution.py:1117
  203.1 9.8 %convolution_convert_fusion.6.refs_0_ = bf16[512,1536]{1,0:T(8,128)(2,1)} fusion(bf16[512,2304]{1,0:T(8,128)(2,1)} %get-tuple-element.198, bf16[1536,2304]{1,0:T(8,128)(2,1)} %get-tuple-element.61), kind=kOutput, calls=%fused_computation.30 | convolution fusion | flops 3624665088 | bytes 11010048 | tf_op jit(solution)/shard_map/dot_general | solution.py:1117
  215.4 43.2 %z_step_5.1 = (bf16[512,1536]{1,0:T(8,128)(2,1)}, f32[128,1536]{1,0:T(8,128)}, f32[8,1536]{1,0:T(8,128)}) custom-call(bf16[512,1536]{1,0:T(8,128)(2,1)} %convolution_convert_fusion.6.refs_0_, f32[128,1536]{1,0:T(8,128)} %get-tuple-element.59.refs_1_, bf16[128,1536]{1,0:T(8,128)(2,1)} %constant_dynamic-slice_fusion.refs_2_, f32[8,1536]{1,0:T(8,128)} %pad.38.refs_3_), custom_call_target="tpu_custom_call" | custom-call | tf_op jit(solution)/shard_map/z_step_5/pallas_call | solution.py:682
  258.6 3.3 convolution_convert_fusion.12
  279.3 5.6 z_total_6.1
  289.9 3.6 convolution_convert_fusion.5.refs_0_
  294.1 43.4 %z_step_7.1 = (bf16[512,1536]{1,0:T(8,128)(2,1)}, f32[128,1536]{1,0:T(8,128)}, f32[8,1536]{1,0:T(8,128)}) custom-call(bf16[512,1536]{1,0:T(8,128)(2,1)} %convolution_convert_fusion.5.refs_0_, f32[128,1536]{1,0:T(8,128)} %get-tuple-element.74.refs_1_, f32[128,1536]{1,0:T(8,128)} %get-tuple-element.75.refs_2_, f32[128,1536]{1,0:T(8,128)} %get-tuple-element.76.refs_3_, ...), custom_call_target="tpu_custom_call" | custom-call | tf_op jit(solution)/shard_map/z_step_7/pallas_call | solution.py:682
  337.5 3.9 convolution_convert_fusion.11
  341.8 2.9 fusion.88
  371.6 5.6 z_total_8.1
  383.0 5.6 fusion.11.refs_1_
  389.7 4.3 convolution_convert_fusion.4.refs_2_
  394.0 58.0 %z_scatter_9.1 = (f32[128,1536]{1,0:T(8,128)}, f32[128,1536]{1,0:T(8,128)}, f32[128,1536]{1,0:T(8,128)}) custom-call(bf16[512,1536]{1,0:T(8,128)(2,1)} %convolution_convert_fusion.7.refs_0_, bf16[512,1536]{1,0:T(8,128)(2,1)} %fusion.11.refs_1_, bf16[512,1536]{1,0:T(8,128)(2,1)} %convolution_convert_fusion.4.refs_2_), custom_call_target="tpu_custom_call" | custom-call | tf_op jit(solution)/shard_map/z_scatter_9/pallas_call | solution.py:708
  462.6 33.0 %deliver_10.1 = (bf16[2,128,1536]{2,1,0:T(8,128)(2,1)}, bf16[2,128,1536]{2,1,0:T(8,128)(2,1)}, bf16[2,128,1536]{2,1,0:T(8,128)(2,1)}) custom-call(bf16[128,1536]{1,0:T(8,128)(2,1)} %get-tuple-element.206.refs_0_, bf16[128,1536]{1,0:T(8,128)(2,1)} %fusion.48.refs_1_, bf16[128,1536]{1,0:T(8,128)(2,1)} %convert_element_type.296.refs_2_), custom_call_target="tpu_custom_call" | custom-call | tf_op jit(solution)/shard_map/deliver_10/pallas_call | solution.py:768
  505.9 30.8 %vector_sums.1 = (f32[2,16,1536]{2,1,0:T(8,128)}, f32[16,1536]{1,0:T(8,128)}, f32[2,16,384]{2,1,0:T(8,128)}) custom-call(f32[16,1536]{1,0:T(8,128)} %pad.42.model, f32[16,384]{1,0:T(8,128)} %concatenate.35.heads), custom_call_target="tpu_custom_call" | custom-call | tf_op jit(solution)/shard_map/vector_sums/pallas_call | solution.py:835
  538.3 5.6 convolution_convert_fusion.2
  546.0 2.8 convolution_convert_fusion.3
  553.0 5.9 convolution_convert_fusion.1
  558.9 6.6 convolution_convert_fusion
  565.6 124.8 %grad_sums.1 = bf16[2,48,3840]{2,1,0:T(8,128)(2,1)} custom-call(bf16[4,4,2,48,1152]{4,3,2,1,0:T(8,128)(2,1)} %bitcast.197, bf16[4,4,2,48,384]{4,3,2,1,0:T(8,128)(2,1)} %bitcast.222, bf16[4,4,2,48,768]{4,3,2,1,0:T(8,128)(2,1)} %bitcast.205, bf16[4,4,2,48,384]{4,3,2,1,0:T(8,128)(2,1)} %bitcast.223, bf16[4,4,2,48,384]{4,3,2,1,0:T(8,128)(2,1)} %bitcast.224, ...), custom_call_target="tpu_custom_call" | custom-call | tf_op jit(solution)/shard_map/grad_sums/pallas_call | solution.py:968
  700.8 18.7 %newton.1 = (f32[192,768]{1,0:T(8,128)}, f32[48,4480]{1,0:T(8,128)}) custom-call(f32[192,768]{1,0:T(8,128)} %bitcast.203, f32[48,4480]{1,0:T(8,128)} %bitcast.190), custom_call_target="tpu_custom_call" | custom-call | tf_op jit(solution)/shard_map/newton/pallas_call | solution.py:1039
  (309 shorter events, 124.2 us)
Async XLA Ops:
  0.6 7.3 %copy-start = (f32[2,6,1536]{2,0,1:T(2,128)S(1)}, f32[2,6,1536]{2,0,1:T(2,128)}, u32[]{:S(2)}) copy-start(f32[2,6,1536]{2,0,1:T(2,128)} %param.19) | copy-start | bytes 221188
  167.9 8.6 %copy-start.48 = (f32[4480]{0:T(1024)S(1)}, f32[4480]{0:T(1024)}, u32[]{:S(2)}) copy-start(f32[4480]{0:T(1024)} %param.27) | copy-start | bytes 53764
  167.9 8.6 %copy-start.62 = (bf16[512,1536]{1,0:T(8,128)(2,1)S(1)}, bf16[512,1536]{1,0:T(8,128)(2,1)}, u32[]{:S(2)}) copy-start(bf16[512,1536]{1,0:T(8,128)(2,1)} %get-tuple-element.60) | copy-start | bytes 4718596
  188.7 10.2 %copy-start.71 = (f32[512,2304]{1,0:T(8,128)}, f32[512,2304]{1,0:T(8,128)S(1)}, u32[]{:S(2)}) copy-start(f32[512,2304]{1,0:T(8,128)S(1)} %get-tuple-element.230) | copy-start | bytes 14155780
  188.7 10.2 %copy-start.40 = (bf16[512,384]{1,0:T(8,128)(2,1)S(1)}, bf16[512,384]{1,0:T(8,128)(2,1)}, u32[]{:S(2)}) copy-start(bf16[512,384]{1,0:T(8,128)(2,1)} %get-tuple-element.67) | copy-start | bytes 1179652
  188.7 11.2 %copy-start.39 = (bf16[512,384]{1,0:T(8,128)(2,1)S(1)}, bf16[512,384]{1,0:T(8,128)(2,1)}, u32[]{:S(2)}) copy-start(bf16[512,384]{1,0:T(8,128)(2,1)} %get-tuple-element.66) | copy-start | bytes 1179652
  203.1 60.7 %copy-start.10 = (f32[3,512,512]{1,2,0:T(8,128)}, f32[3,512,512]{1,2,0:T(8,128)S(1)}, u32[]{:S(2)}) copy-start(f32[3,512,512]{1,2,0:T(8,128)S(1)} %get-tuple-element.232) | copy-start | bytes 9437188
  203.1 62.5 %copy-start.59 = (f32[3,512]{1,0:T(4,128)}, f32[3,512]{1,0:T(4,128)S(1)}, u32[]{:S(2)}) copy-start(f32[3,512]{1,0:T(4,128)S(1)} %get-tuple-element.231) | copy-start | bytes 18436
  275.2 13.9 %copy-start.9 = (f32[512,384]{1,0:T(8,128)S(1)}, f32[512,384]{1,0:T(8,128)}, u32[]{:S(2)}) copy-start(f32[512,384]{1,0:T(8,128)} %get-tuple-element.72) | copy-start | bytes 2359300
  278.7 14.8 %copy-start.50 = (f32[1,1536]{1,0:T(1,128)S(1)}, f32[1,1536]{1,0:T(1,128)}, u32[]{:S(2)}) copy-start(f32[1,1536]{1,0:T(1,128)} %get-tuple-element.212) | copy-start | bytes 18436
  278.7 14.8 %copy-start.51 = (f32[1,1536]{1,0:T(1,128)S(1)}, f32[1,1536]{1,0:T(1,128)}, u32[]{:S(2)}) copy-start(f32[1,1536]{1,0:T(1,128)} %get-tuple-element.244) | copy-start | bytes 18436
  294.1 47.3 %copy-start.38 = (bf16[512,384]{1,0:T(8,128)(2,1)S(1)}, bf16[512,384]{1,0:T(8,128)(2,1)}, u32[]{:S(2)}) copy-start(bf16[512,384]{1,0:T(8,128)(2,1)} %get-tuple-element.65) | copy-start | bytes 1179652
  394.0 58.0 %copy-start.13 = (f32[128,1536]{1,0:T(8,128)S(1)}, f32[128,1536]{1,0:T(8,128)}, u32[]{:S(2)}) copy-start(f32[128,1536]{1,0:T(8,128)} %get-tuple-element.59.refs_1_) | copy-start | bytes 2359300
  462.6 38.0 %copy-start.53 = (f32[8,1536]{1,0:T(8,128)S(1)}, f32[8,1536]{1,0:T(8,128)}, u32[]{:S(2)}) copy-start(f32[8,1536]{1,0:T(8,128)} %get-tuple-element.90) | copy-start | bytes 147460
  462.6 38.8 %copy-start.17 = (bf16[512,1536]{1,0:T(8,128)(2,1)S(1)}, bf16[512,1536]{1,0:T(8,128)(2,1)}, u32[]{:S(2)}) copy-start(bf16[512,1536]{1,0:T(8,128)(2,1)} %copy-done.16) | copy-start | bytes 4718596
  462.6 40.6 %copy-start.21 = (bf16[512,384]{1,0:T(8,128)(2,1)S(1)}, bf16[512,384]{1,0:T(8,128)(2,1)}, u32[]{:S(2)}) copy-start(bf16[512,384]{1,0:T(8,128)(2,1)} %copy.199) | copy-start | bytes 1179652
  462.6 40.6 %copy-start.23 = (bf16[512,384]{1,0:T(8,128)(2,1)S(1)}, bf16[512,384]{1,0:T(8,128)(2,1)}, u32[]{:S(2)}) copy-start(bf16[512,384]{1,0:T(8,128)(2,1)} %copy-done.22) | copy-start | bytes 1179652
  495.6 8.7 %copy-start.57 = (f32[384]{0:T(512)S(1)}, f32[384]{0:T(512)}, u32[]{:S(2)}) copy-start(f32[384]{0:T(512)} %get-tuple-element.174) | copy-start | bytes 4612
  495.7 8.8 %copy-start.58 = (f32[384]{0:T(512)S(1)}, f32[384]{0:T(512)}, u32[]{:S(2)}) copy-start(f32[384]{0:T(512)} %get-tuple-element.199) | copy-start | bytes 4612
  550.9 8.0 %slice-start.1 = ((s8[4718592]{0:T(1024)(128)(4,1)}), s8[4194304]{0:T(1024)(128)(4,1)S(1)}, s32[]{:S(2)}) async-start(s8[4718592]{0:T(1024)(128)(4,1)} %bitcast.247), calls=%async_computation.1 | async-start | bytes 8388608
  697.8 23.0 %copy-start.18 = (f32[24,6,768]{2,0,1:T(8,128)S(1)}, f32[24,6,768]{2,0,1:T(8,128)}, u32[]{:S(2)}) copy-start(f32[24,6,768]{2,0,1:T(8,128)} %param.22) | copy-start | bytes 1327108
  698.5 24.1 %copy-start.32 = (f32[24,2,768]{2,1,0:T(2,128)S(1)}, f32[24,2,768]{2,1,0:T(2,128)}, u32[]{:S(2)}) copy-start(f32[24,2,768]{2,1,0:T(2,128)} %param.23) | copy-start | bytes 442372
  698.5 24.9 %copy-start.5 = (f32[24,2,4480]{2,1,0:T(2,128)S(1)}, f32[24,2,4480]{2,1,0:T(2,128)}, u32[]{:S(2)}) copy-start(f32[24,2,4480]{2,1,0:T(2,128)} %param.24) | copy-start | bytes 2580484
  723.4 6.8 copy-start.1
  (52 other events, 221.8 us)

commit v3 on v2

--- a/solution.py
+++ b/solution.py
@@ -36,10 +36,6 @@
 HW = HEADS * HEAD
 FF_REAL = 2240
 FF = 2304
-C_IN, C_OUT, C_UP, C_DOWN = 0, 6 * HW, 8 * HW, 8 * HW + FF
-COLS = 8 * HW + 2 * FF
-HALF = COLS // 2
-QUARTER = HALF // 2
 PAIR = 2 * ROWS
 VMEM_LIMIT = 60 * 1024 * 1024
 
@@ -594,194 +590,463 @@
     )(send_attn, send_mlp, tok, txt, cot, tab, heads, vec)
 
 
-def z_peers(x, y, z, core):
-    return [chip(x, y, z + k, core) for k in (1, 2, 3)]
-
-
-def total_kernel(part, out, got, send, recv):
+TILE = 256
+CUBE = 0.044715
+ROOT = math.sqrt(2.0 / math.pi)
+
+
+def gelu_pair(u):
+    square = u * u
+    t = jnp.tanh(ROOT * u * (1.0 + CUBE * square))
+    half = 0.5 * (1.0 + t)
+    return u * half, half + 0.5 * u * (1.0 - t * t) * (ROOT * (1.0 + 3.0 * CUBE * square))
+
+
+def mlp_kernel(
+    a_ref, cot_ref, gate, bias, up, down, part_out, part_back, grad_up, grad_down, bias_sum,
+    acc_out, acc_back, low, a_turned, low_turned,
+):
+    step = pl.program_id(0)
+
+    @pl.when(step == 0)
+    def _():
+        acc_out[...] = jnp.zeros_like(acc_out)
+        acc_back[...] = jnp.zeros_like(acc_back)
+        for start in range(0, SEQ, TOK):
+            rows = slice(start, start + TOK)
+            value = (cot_ref[rows].astype(F32) * gate[0:1]).astype(BF)
+            low[rows] = value
+            low_turned[:, rows] = value.T
+            a_turned[:, rows] = a_ref[rows].T
+
+    u = product(a_ref[...], up[...]) + bias[0:1]
+    act, slope = gelu_pair(u)
+    act = act.astype(BF)
+    acc_out[...] += contract_last(act, down[...])
+    grad_down[...] = product(low_turned[...], act).astype(BF)
+    back = (product(low[...], down[...]) * slope).astype(BF)
+    acc_back[...] += contract_last(back, up[...])
+    grad_up[...] = product(a_turned[...], back).astype(BF)
+    bias_sum[...] = jnp.broadcast_to(jnp.sum(back.astype(F32), 0, keepdims=True), bias_sum.shape)
+
+    @pl.when(step == FF // TILE - 1)
+    def _():
+        part_out[...] = acc_out[...].astype(BF)
+        part_back[...] = acc_back[...].astype(BF)
+
+
+def mlp_pass(a, cot, gate, bias, up, down):
+    sds = jax.ShapeDtypeStruct
+    fixed = pl.BlockSpec((SEQ, D), lambda i: (0, 0))
+    tile = pl.BlockSpec((D, TILE), lambda i: (0, i))
+    line = pl.BlockSpec((8, TILE), lambda i: (0, i))
+    return pl.pallas_call(
+        mlp_kernel,
+        grid=(FF // TILE,),
+        in_specs=[fixed, fixed, pl.BlockSpec((8, D), lambda i: (0, 0)), line, tile, tile],
+        out_specs=[fixed, fixed, tile, tile, line],
+        out_shape=[sds((SEQ, D), BF), sds((SEQ, D), BF), sds((D, FF), BF), sds((D, FF), BF), sds((8, FF), F32)],
+        scratch_shapes=[
+            pltpu.VMEM((SEQ, D), F32), pltpu.VMEM((SEQ, D), F32), pltpu.VMEM((SEQ, D), BF),
+            pltpu.VMEM((D, SEQ), BF), pltpu.VMEM((D, SEQ), BF),
+        ],
+        compiler_params=pltpu.CompilerParams(vmem_limit_bytes=VMEM_LIMIT, dimension_semantics=("arbitrary",)),
+        name="mlp",
+    )(a, cot, gate, bias, up, down)
+
+
+def peers_xy(x, y, z, core):
+    rows = [chip(x + k, y, z, core) for k in (1, 2, 3)]
+    lines = [chip(x, y + k, z, core) for k in (1, 2, 3)]
+    return rows, lines
+
+
+def reduce_xy(sources, out, own, sib, r1, r2, tosend, ls, ss, sr, s1, q1, s2, q2, s3, q3, l3, credit):
     x, y, z, core = here()
-    greet(z_peers(x, y, z, core))
+    zl = lax.rem(z, 2)
+    rows, lines = peers_xy(x, y, z, core)
+    sibling = chip(x, y, z, 1 - core)
+    pairs = {0: [], 1: []}
+    for i, (ref, part, start) in enumerate(sources):
+        cols = pl.ds(start, ref.shape[-1])
+        mine = pltpu.make_async_copy(ref.at[:, :, core], own.at[part, :, :, :, cols], ls.at[i])
+        theirs = remote(
+            ref.at[:, :, 1 - core], sib.at[:, :, :, cols], ss.at[i], sr.at[i], sibling
+        )
+        mine.start()
+        if part == 0:
+            theirs.start()
+        pairs[part].append((mine, theirs))
+    wrap = lambda v: lax.rem(v, SIDE)
+    one = {0: [], 1: []}
+    for part in (0, 1):
+        yield
+        for mine, theirs in pairs[part]:
+            mine.wait()
+            theirs.wait_recv()
+
+        def add_pair(k, carry):
+            a, b = lax.div(k, SIDE), lax.rem(k, SIDE)
+            own[part, a, b] = own[part, a, b] + sib[a, b]
+            return carry
+
+        lax.fori_loop(0, SIDE * SIDE, add_pair, 0)
+        if part == 0:
+            pl.semaphore_signal(credit, inc=1, device_id=sibling, device_id_type=MESH)
+            pl.semaphore_wait(credit, 1)
+            for _, theirs in pairs[1]:
+                theirs.start()
+        for k in (2, 1, 3):
+            src = own.at[0, :, wrap(y + k)] if part == 0 else own.at[1, wrap(x + k)]
+            device = (lines, rows)[part][k - 1]
+            copy = remote(src, r1.at[part, k - 1], s1.at[part, k - 1], q1.at[part, k - 1], device)
+            copy.start()
+            one[part].append(copy)
+    two = {0: [], 1: []}
+    for part in (0, 1):
+        yield
+        for copy in one[part]:
+            copy.wait_recv()
+
+        def add_line(k, carry):
+            a, b = (k, y) if part == 0 else (x, k)
+            total = own[part, a, b].astype(F32)
+            for i in range(3):
+                total = total + r1[part, i, k].astype(F32)
+            own[part, a, b] = total.astype(BF)
+            return carry
+
+        lax.fori_loop(0, SIDE, add_line, 0)
+        for k in (2, 1, 3):
+            src = own.at[0, wrap(x + k), y] if part == 0 else own.at[1, x, wrap(y + k)]
+            device = (rows, lines)[part][k - 1]
+            copy = remote(src, r2.at[part, k - 1], s2.at[part, k - 1], q2.at[part, k - 1], device)
+            copy.start()
+            two[part].append(copy)
+    final = []
+    for part in (0, 1):
+        yield
+        for copy in two[part]:
+            copy.wait_recv()
+        total = own[part, x, y].astype(F32)
+        for i in range(3):
+            total = total + r2[part, i].astype(F32)
+        for target in (0, 1):
+            tosend[target, part * ROWS : part * ROWS + ROWS] = total[target * ROWS : target * ROWS + ROWS]
+    other = z + 1 - 2 * zl
+    far = [
+        remote(tosend.at[t], out.at[zl], s3.at[t], q3.at[zl], chip(x, y, other, t)) for t in (0, 1)
+    ]
+    self_copy = pltpu.make_async_copy(tosend.at[core], out.at[zl], l3.at[0])
+    near = remote(tosend.at[1 - core], out.at[zl], s3.at[0], q3.at[zl], sibling)
+
+    def got(slot):
+        remote(tosend.at[0], out.at[slot], s3.at[0], q3.at[slot], chip(x, y, z, core)).wait_recv()
+
+    @pl.when(core == zl)
+    def _():
+        self_copy.start()
+        near.start()
+
+    @pl.when(core != zl)
+    def _():
+        for copy in far:
+            copy.start()
+
+    yield
+
+    @pl.when(core == zl)
+    def _():
+        self_copy.wait()
+        near.wait_send()
+        got(1 - zl)
+
+    @pl.when(core != zl)
+    def _():
+        for copy in far:
+            copy.wait_send()
+        got(zl)
+        got(1 - zl)
+
+    for part in (0, 1):
+        for mine, theirs in pairs[part]:
+            theirs.wait_send()
+        for copy in one[part] + two[part]:
+            copy.wait_send()
+
+
+def reduce_scratch(width, count):
+    dma = pltpu.SemaphoreType.DMA
+    return [
+        pltpu.VMEM((2, SIDE, SIDE, PAIR, width), BF),
+        pltpu.VMEM((SIDE, SIDE, PAIR, width), BF),
+        pltpu.VMEM((2, 3, SIDE, PAIR, width), BF),
+        pltpu.VMEM((2, 3, PAIR, width), BF),
+        pltpu.VMEM((2, PAIR, width), F32),
+        dma((count,)), dma((count,)), dma((count,)),
+        dma((2, 3)), dma((2, 3)), dma((2, 3)), dma((2, 3)),
+        dma((2,)), dma((2,)), dma((1,)), pltpu.SemaphoreType.REGULAR,
+    ]
+
+
+def attend_clip_back(query, keys, values, grad, grad_query, grad_keys, grad_values):
+    for h in range(HEADS):
+        cols = head_slice(h)
+        k, v = keys[:, cols], values[:, cols]
+        for start in range(0, SEQ, 256):
+            rows = slice(start, start + 256)
+            q, do = query[rows, cols], grad[rows, cols]
+            weights = softmax_rows(q, k)
+            grad_weights = contract_last(do, v)
+            delta = jnp.sum(weights * grad_weights, -1, keepdims=True)
+            grad_scores = (weights * (grad_weights - delta)).astype(BF)
+            grad_query[rows, cols] = product(grad_scores, k) * SCALE
+            to_keys = contract_rows(grad_scores, q) * SCALE
+            to_values = contract_rows(weights.astype(BF), do)
+            if start:
+                grad_keys[:, cols] += to_keys
+                grad_values[:, cols] += to_values
+            else:
+                grad_keys[:, cols] = to_keys
+                grad_values[:, cols] = to_values
+
+
+def column_sum(values):
+    return jnp.sum(values.astype(F32), 0, keepdims=True)
+
+
+def scatter_held(part, got, send, recv):
+    x, y, z, core = here()
     copies = []
-    for k in (1, 2, 3):
+    for k in (2, 1, 3):
+        rows = block_slice(block_of(z + k))
         copies.append(
-            remote(part, got.at[k - 1], send.at[k - 1], recv.at[k - 1], chip(x, y, z + k, core))
+            remote(part.at[rows], got.at[k - 1], send.at[k - 1], recv.at[k - 1], chip(x, y, z + k, core))
         )
         copies[-1].start()
-    for copy in copies:
-        copy.wait()
-    out[...] = part[...] + got[0] + got[1] + got[2]
-
-
-def z_total(values, cid):
-    dma = pltpu.SemaphoreType.DMA
-    return pl.pallas_call(
-        total_kernel,
-        out_shape=jax.ShapeDtypeStruct(values.shape, F32),
-        in_specs=[VM],
-        out_specs=VM,
-        scratch_shapes=[pltpu.VMEM((3,) + values.shape, F32), dma((3,)), dma((3,))],
-        compiler_params=params(cid),
-        name=f"z_total_{cid}",
-    )(values)
-
-
-def scatter_start(parts, got, send, recv):
+    return copies
+
+
+def root_back(linear, inverse, scaled, dot):
+    return (inverse * scaled - linear * (inverse * inverse * inverse * dot * (1.0 / D))).astype(BF)
+
+
+def backward_kernel(
+    part_back, part_down, grad_up, grad_down, wa, after_two, cot_own, vec, heads, query_lin, key_lin,
+    query_two_lin, key_two_lin, inv, query_rot, key_rot, value_low, query_two, key_two, value_two,
+    tab, branch_one, after_one,
+    low_two, low_one, grad_query_two, grad_kv_two, grad_qkv, part_tokens, grad_after_one, sums,
+    head_sums, result, grad_words, mlp_sums,
+    mine_back, mine_down, part_cross, part_words, blocks, held, gq, gk, gv, stat,
+    stat_s, stat_r, zs, zr, gs, gr, loc, *reduce_refs,
+):
     x, y, z, core = here()
-    copies = []
-    for i, part in enumerate(parts):
-        for k in (2, 1, 3):
-            rows = pl.ds(pl.multiple_of(block_of(z + k) * TOK, TOK), TOK)
-            copy = remote(
-                part.at[rows], got.at[i, k - 1], send.at[i, k - 1], recv.at[i, k - 1],
-                chip(x, y, z + k, core),
-            )
-            copy.start()
-            copies.append(copy)
-    return copies
-
-
-def own_sum(part, got, i, z):
-    rows = pl.ds(pl.multiple_of(block_of(z) * TOK, TOK), TOK)
-    total = part[rows].astype(F32)
-    for k in range(3):
-        total = total + got[i, k].astype(F32)
-    return total
-
-
-def step_kernel(compute, extra_count, out_count, *refs):
-    part = refs[0]
-    extras = refs[1 : 1 + extra_count]
-    gathered = refs[1 + extra_count]
-    outs = refs[2 + extra_count : 2 + extra_count + out_count]
-    got, send, recv, gsend, grecv = refs[2 + extra_count + out_count :]
-    x, y, z, core = here()
-    greet(z_peers(x, y, z, core))
-    copies = scatter_start([part], got, send, recv)
+    rows, lines = peers_xy(x, y, z, core)
+    greet(column(x, y, z, core) + rows + lines)
+    own_rows = block_slice(block_of(z))
+    copies = scatter_held(part_back, blocks.at[0], zs.at[0], zr.at[0])
+    drains = list(copies)
+    fetch_back = pltpu.make_async_copy(part_back.at[own_rows], mine_back, loc.at[0])
+    fetch_down = pltpu.make_async_copy(part_down.at[own_rows], mine_down, loc.at[1])
+    fetch_back.start()
+    fetch_down.start()
+    job = reduce_xy([(grad_up, 0, 0), (grad_down, 1, 0)], mlp_sums, *reduce_refs)
+    advance(job)
+    sums[...] = jnp.zeros_like(sums)
+    head_sums[...] = jnp.zeros_like(head_sums)
+    dy = cot_own[...].astype(F32)
+    sums[2:3] = column_sum((dy * vec[5:6]).astype(BF))
+    advance(job)
+
+    def total_of(mine, i):
+        total = mine[...].astype(F32)
+        for k in range(3):
+            total = total + blocks[i, k].astype(F32)
+        return total
+
+    fetch_back.wait()
     for copy in copies:
         copy.wait_recv()
-    total = own_sum(part, got, 0, z)
-    result = compute(total, extras, outs)
-    rows = pl.ds(pl.multiple_of(block_of(z) * TOK, TOK), TOK)
-    gathered[rows] = result
-    gathers = []
-    for k in (2, 1, 3):
-        copy = remote(
-            gathered.at[rows], gathered.at[rows], gsend.at[k - 1], grecv.at[k - 1],
-            chip(x, y, z + k, core),
-        )
-        copy.start()
-        gathers.append(copy)
-    for copy in gathers:
-        copy.wait()
+    total = total_of(mine_back, 0)
+    normed, inverse = plain_norm(after_two[...])
+    sums[8:9] = column_sum(total)
+    sums[9:10] = column_sum(total * normed)
+    value = dy + norm_back(total * (1.0 + vec[4:5]), normed, inverse)
+    grad_after_one[...] = value
+    low = value.astype(BF)
+    sums[1:2] = column_sum(low)
+    copies = spread_block(low_two, low, gs.at[0], gr.at[0])
+    drains += copies
+    down_copies = scatter_held(part_down, blocks.at[1], zs.at[1], zr.at[1])
+    drains += down_copies
+    advance(job)
     for copy in copies:
+        copy.wait_recv()
+
+    stats = Stats(stat, stat_s, stat_r)
+    inverse_query, inverse_key, inverse_key_two, inverse_query_two = [inv[:, i : i + 1] for i in range(4)]
+    held[...] = product(low_two[...], wa[:, W_CROSS]).astype(BF)
+    attend_clip_back(query_two, key_two, value_two, held, gq, gk, gv)
+    scaled_query = gq[...] * (1.0 + heads[8:9])
+    scaled_key = gk[...] * (1.0 + heads[9:10])
+    dots = stats.start(
+        0,
+        [
+            jnp.sum(query_two_lin[...] * scaled_query, -1, keepdims=True),
+            jnp.sum(key_two_lin[...] * scaled_key, -1, keepdims=True),
+        ],
+    )
+    head_sums[8:9] = column_sum(gq[...] * query_two_lin[...] * inverse_query_two)
+    head_sums[9:10] = column_sum(gk[...] * key_two_lin[...] * inverse_key_two)
+    low = gv[...].astype(BF)
+    grad_kv_two[:, HW:] = low
+    head_sums[7:8] = column_sum(low)
+    advance(job)
+    dot_query, dot_key = dots()
+    low = root_back(query_two_lin[...], inverse_query_two, gq[...] * (1.0 + heads[8:9]), dot_query)
+    grad_query_two[...] = low
+    head_sums[5:6] = column_sum(low)
+    cross_copies = scatter_product(
+        grad_query_two, wa[:, W_QUERY], part_cross, blocks.at[2], zs.at[2], zr.at[2]
+    )
+    low = root_back(key_two_lin[...], inverse_key_two, gk[...] * (1.0 + heads[9:10]), dot_key)
+    grad_kv_two[:, :HW] = low
+    head_sums[6:7] = column_sum(low)
+    word_copies = scatter_product(grad_kv_two, wa[:, W_TEXT], part_words, blocks.at[3], zs.at[3], zr.at[3])
+    drains += word_copies
+    for copy in down_copies:
+        copy.wait_recv()
+    fetch_down.wait()
+    branch = total_of(mine_down, 1) + vec[V_DOWN : V_DOWN + 1]
+    result[...] = (after_two[...] + vec[5:6] * branch).astype(BF)
+    sums[10:11] = column_sum(cot_own[...].astype(F32) * branch)
+    advance(job)
+
+    total = collect(part_cross, blocks.at[2], cross_copies)
+    normed, inverse = plain_norm(after_one[...])
+    sums[4:5] = column_sum(total)
+    sums[3:4] = column_sum(total * normed)
+    value = grad_after_one[...] + norm_back(total * (1.0 + vec[V_GAIN : V_GAIN + 1]), normed, inverse)
+    grad_after_one[...] = value
+    sums[7:8] = column_sum(value * branch_one[...])
+    low = (value * vec[2:3]).astype(BF)
+    sums[0:1] = column_sum(low)
+    copies = spread_block(low_one, low, gs.at[1], gr.at[1])
+    drains += copies
+    advance(job)
+    for copy in copies:
+        copy.wait_recv()
+
+    held[...] = product(low_one[...], wa[:, W_SELF]).astype(BF)
+    attend_clip_back(query_rot, key_rot, value_low, held, gq, gk, gv)
+    cosine, sine = rope_pair(tab[...].reshape(SEQ, HEAD))
+    for ref in (gq, gk):
+        for h in range(HEADS):
+            cols = head_slice(h)
+            value = ref[:, cols]
+            ref[:, cols] = value * cosine - swap_halves(value) * sine
+    dots = stats.start(
+        1,
+        [
+            jnp.sum(query_lin[...] * (gq[...] * (1.0 + heads[3:4])), -1, keepdims=True),
+            jnp.sum(key_lin[...] * (gk[...] * (1.0 + heads[4:5])), -1, keepdims=True),
+        ],
+    )
+    head_sums[3:4] = column_sum(gq[...] * query_lin[...] * inverse_query)
+    head_sums[4:5] = column_sum(gk[...] * key_lin[...] * inverse_key)
+    low = gv[...].astype(BF)
+    grad_qkv[:, 2 * HW :] = low
+    head_sums[2:3] = column_sum(low)
+    advance(job)
+    dot_query, dot_key = dots()
+    for i, (lin, inverse, ref, dot) in enumerate(
+        ((query_lin, inverse_query, gq, dot_query), (key_lin, inverse_key, gk, dot_key))
+    ):
+        low = root_back(lin[...], inverse, ref[...] * (1.0 + heads[3 + i : 4 + i]), dot)
+        grad_qkv[:, i * HW : (i + 1) * HW] = low
+        head_sums[i : i + 1] = column_sum(low)
+    for copy in cross_copies:
         copy.wait_send()
-
-
-def z_step(part, extras, compute, out_shapes, cid):
+    part_cross[...] = contract_last(grad_qkv[...], wa[:, W_QKV]).astype(BF)
+    store = pltpu.make_async_copy(part_cross, part_tokens, loc.at[2])
+    store.start()
+    grad_words[...] = collect(part_words, blocks.at[3], word_copies).astype(BF)
+    finish(job)
+    store.wait()
+    for copy in drains:
+        copy.wait_send()
+
+
+def backward(hbm, vmem):
     dma = pltpu.SemaphoreType.DMA
+    sds = jax.ShapeDtypeStruct
+    wide, low = sds((SEQ, D), BF), sds((SEQ, HW), BF)
+    block, low_block = sds((TOK, D), F32), sds((TOK, D), BF)
+    lin = pltpu.VMEM((SEQ, HW), F32)
+    outs = [
+        wide, wide, low, sds((SEQ, 2 * HW), BF), sds((SEQ, 3 * HW), BF), wide, block,
+        sds((16, D), F32), sds((16, HW), F32), low_block, low_block, sds((2, PAIR, FF), F32),
+    ]
     return pl.pallas_call(
-        partial(step_kernel, compute, len(extras), len(out_shapes)),
-        out_shape=[jax.ShapeDtypeStruct((SEQ, D), BF)] + out_shapes,
-        in_specs=[VM] * (1 + len(extras)),
-        out_specs=[VM] * (1 + len(out_shapes)),
-        scratch_shapes=[pltpu.VMEM((1, 3, TOK, D), BF), dma((1, 3)), dma((1, 3)), dma((3,)), dma((3,))],
-        compiler_params=params(cid),
-        name=f"z_step_{cid}",
-    )(part, *extras)
-
-
-def scatter_kernel(count, *refs):
-    parts, outs = refs[:count], refs[count : 2 * count]
-    got, send, recv = refs[2 * count :]
-    x, y, z, core = here()
-    greet(z_peers(x, y, z, core))
-    copies = scatter_start(parts, got, send, recv)
-    for i in range(count):
-        for copy in copies[3 * i : 3 * i + 3]:
-            copy.wait()
-        outs[i][...] = own_sum(parts[i], got, i, z)
-
-
-def z_scatter(parts, cid):
-    count = len(parts)
-    dma = pltpu.SemaphoreType.DMA
-    return pl.pallas_call(
-        partial(scatter_kernel, count),
-        out_shape=[jax.ShapeDtypeStruct((TOK, D), F32)] * count,
-        in_specs=[VM] * count,
-        out_specs=[VM] * count,
-        scratch_shapes=[pltpu.VMEM((count, 3, TOK, D), BF), dma((count, 3)), dma((count, 3))],
-        compiler_params=params(cid),
-        name=f"z_scatter_{cid}",
-    )(*parts)
-
-
-def deliver_kernel(count, *refs):
-    srcs, dsts = refs[:count], refs[count : 2 * count]
-    send, recv, loc = refs[2 * count :]
+        backward_kernel,
+        out_shape=outs,
+        in_specs=[HB] * len(hbm) + [VM] * len(vmem),
+        out_specs=[HB if i == 5 else VM for i in range(len(outs))],
+        scratch_shapes=[
+            pltpu.VMEM((TOK, D), BF), pltpu.VMEM((TOK, D), BF),
+            pltpu.VMEM((SEQ, D), BF), pltpu.VMEM((SEQ, D), BF),
+            pltpu.VMEM((4, 3, TOK, D), BF), pltpu.VMEM((SEQ, HW), BF),
+            lin, lin, lin, pltpu.VMEM((2, 4, 8, SEQ), F32),
+            dma((2, 3)), dma((2, 3)), dma((4, 3)), dma((4, 3)), dma((2, 3)), dma((2, 3)), dma((3,)),
+            *reduce_scratch(FF, 2),
+        ],
+        compiler_params=params(1),
+        name="backward",
+    )(*hbm, *vmem)
+
+
+def deliver(src, dst, s, r, l):
     x, y, z, core = here()
     zh = lax.div(z, 2)
-    greet(column(x, y, z, core))
-    far = [
-        remote(s, d.at[core], send.at[i, 0], recv.at[i, core], chip(x, y, z + 2, zh))
-        for i, (s, d) in enumerate(zip(srcs, dsts))
-    ]
-    near = [
-        remote(s, d.at[core], send.at[i, 1], recv.at[i, core], chip(x, y, z, zh))
-        for i, (s, d) in enumerate(zip(srcs, dsts))
-    ]
-    self_copies = [
-        pltpu.make_async_copy(s, d.at[core], loc.at[i]) for i, (s, d) in enumerate(zip(srcs, dsts))
-    ]
-    for copy in far:
-        copy.start()
-
-    def got(i, slot):
-        remote(
-            srcs[i], dsts[i].at[slot], send.at[i, 0], recv.at[i, slot], chip(x, y, z, core)
-        ).wait_recv()
-
-    @pl.when(core == zh)
-    def _():
-        for copy in self_copies:
-            copy.start()
-        for i in range(count):
-            self_copies[i].wait()
-            got(i, 1 - core)
-
-    @pl.when(core != zh)
-    def _():
-        for copy in near:
-            copy.start()
-        for i in range(count):
-            near[i].wait_send()
-            got(i, 0)
-            got(i, 1)
-
-    for copy in far:
-        copy.wait_send()
-
-
-def deliver(arrays, cid):
-    count = len(arrays)
-    dma = pltpu.SemaphoreType.DMA
-    return pl.pallas_call(
-        partial(deliver_kernel, count),
-        out_shape=[jax.ShapeDtypeStruct((2,) + a.shape, a.dtype) for a in arrays],
-        in_specs=[VM] * count,
-        out_specs=[VM] * count,
-        scratch_shapes=[dma((count, 2)), dma((count, 2)), dma((count,))],
-        compiler_params=params(cid),
-        name=f"deliver_{cid}",
-    )(*arrays)
-
-
-def vector_kernel(model, heads, time_out, model_out, head_out, col, hsib, mx, hx, sends, recvs):
+    far = remote(src, dst.at[core], s.at[0], r.at[core], chip(x, y, z + 2, zh))
+    near = remote(src, dst.at[core], s.at[1], r.at[core], chip(x, y, z, zh))
+    self_copy = pltpu.make_async_copy(src, dst.at[core], l)
+
+    def got(slot):
+        remote(src, dst.at[slot], s.at[0], r.at[slot], chip(x, y, z, core)).wait_recv()
+
+    def start():
+        far.start()
+
+        @pl.when(core == zh)
+        def _():
+            self_copy.start()
+
+        @pl.when(core != zh)
+        def _():
+            near.start()
+
+    def wait():
+        @pl.when(core == zh)
+        def _():
+            self_copy.wait()
+            got(1 - core)
+
+        @pl.when(core != zh)
+        def _():
+            near.wait_send()
+            got(0)
+            got(1)
+
+        far.wait_send()
+
+    return start, wait
+
+
+def vector_job(model, heads, time_out, model_out, head_out, col, hsib, mx, hx, sends, recvs):
     x, y, z, core = here()
     zl = lax.rem(z, 2)
-    rows = [chip(x + k, y, z, core) for k in (1, 2, 3)]
-    lines = [chip(x, y + k, z, core) for k in (1, 2, 3)]
-    greet(column(x, y, z, core) + rows + lines)
+    rows, lines = peers_xy(x, y, z, core)
     copies = []
     for k in (1, 2, 3):
         copies.append(
@@ -794,6 +1059,7 @@
     copies.append(remote(heads, hsib, sends.at[0, 0], recvs.at[0, 0], chip(x, y, z, 1 - core)))
     for copy in copies:
         copy.start()
+    yield
     for copy in copies:
         copy.wait()
     same = model[...] + col[0, 0] + col[0, 1] + col[0, 2]
@@ -805,7 +1071,6 @@
     for stage, peers in enumerate((rows, lines)):
         copies = []
         for k in (1, 2, 3):
-            at = 1 + 3 * stage + k - 1
             copies.append(
                 remote(mx.at[4 * stage], mx.at[4 * stage + k], sends.at[2 + 2 * stage, k],
                        recvs.at[2 + 2 * stage, k], peers[k - 1])
@@ -816,6 +1081,7 @@
             )
         for copy in copies:
             copy.start()
+        yield
         for copy in copies:
             copy.wait()
         base = 4 * stage
@@ -827,162 +1093,107 @@
         hx.at[8], head_out.at[zl], sends.at[6, 0], recvs.at[6, 0], chip(x, y, z + 1 - 2 * zl, core)
     )
     last.start()
+    yield
     last.wait()
 
 
-def vector_sums(model, heads, cid):
+def vector_scratch():
     dma = pltpu.SemaphoreType.DMA
+    return [
+        pltpu.VMEM((2, 4, 16, D), F32),
+        pltpu.VMEM((16, HW), F32),
+        pltpu.VMEM((9, 16, D), F32),
+        pltpu.VMEM((9, 16, HW), F32),
+        dma((7, 4)),
+        dma((7, 4)),
+    ]
+
+
+GRAD_PLACES = ((0, 0, 3 * HW), (0, 3 * HW, HW), (1, 0, 2 * HW), (1, 2 * HW, HW), (1, 3 * HW, HW))
+
+
+def tail_kernel(*refs):
+    count = len(GRAD_PLACES)
+    grads, refs = refs[:count], refs[count:]
+    (
+        part_tokens, tok_own, grad_after_one, vec, sums, head_sums, result, words,
+        out_result, out_tokens, out_words, time_out, model_out, head_out, attn_sums,
+        mine, blocks, model, low_tokens, got_tokens, got_words, zs, zr, ds, dr, loc,
+    ), refs = refs[:26], refs[26:]
+    vector_refs, reduce_refs = refs[:6], refs[6:]
+    x, y, z, core = here()
+    rows, lines = peers_xy(x, y, z, core)
+    greet(column(x, y, z, core) + rows + lines)
+    copies = scatter_held(part_tokens, blocks, zs, zr)
+    fetch = pltpu.make_async_copy(part_tokens.at[block_slice(block_of(z))], mine, loc.at[0])
+    fetch.start()
+    job = reduce_xy(
+        [(ref, part, start) for ref, (part, start, _) in zip(grads, GRAD_PLACES)], attn_sums, *reduce_refs
+    )
+    advance(job)
+    sends = [
+        deliver(src, dst, ds.at[i], dr.at[i], loc.at[1 + i])
+        for i, (src, dst) in enumerate(
+            ((result, out_result), (words, got_words), (low_tokens, got_tokens))
+        )
+    ]
+    sends[0][0]()
+    sends[1][0]()
+    advance(job, 2)
+    fetch.wait()
+    for copy in copies:
+        copy.wait_recv()
+    total = mine[...].astype(F32)
+    for k in range(3):
+        total = total + blocks[k].astype(F32)
+    normed, inverse = plain_norm(tok_own[...].astype(F32))
+    model[...] = sums[...]
+    model[5:6] = column_sum(total)
+    model[6:7] = column_sum(total * normed)
+    vectors = vector_job(model, head_sums, time_out, model_out, head_out, *vector_refs)
+    advance(vectors)
+    value = grad_after_one[...] + norm_back(total * (1.0 + vec[1:2]), normed, inverse)
+    low_tokens[...] = value.astype(BF)
+    sends[2][0]()
+    advance(job)
+    advance(vectors)
+    advance(job)
+    advance(vectors)
+    advance(job)
+    advance(vectors)
+    advance(job)
+    finish(vectors)
+    for send in sends:
+        send[1]()
+    out_tokens[...] = got_tokens[...].astype(F32)
+    out_words[...] = got_words[...].astype(F32)
+    finish(job)
+    for copy in copies:
+        copy.wait_send()
+
+
+def tail(grads, part_tokens, vmem):
+    dma = pltpu.SemaphoreType.DMA
+    sds = jax.ShapeDtypeStruct
+    outs = [
+        sds((2, TOK, D), BF), sds((2, TOK, D), F32), sds((2, TOK, D), F32), sds((2, 16, D), F32),
+        sds((16, D), F32), sds((2, 16, HW), F32), sds((2, PAIR, ATTN // 2), F32),
+    ]
     return pl.pallas_call(
-        vector_kernel,
-        out_shape=[
-            jax.ShapeDtypeStruct((2, 16, D), F32),
-            jax.ShapeDtypeStruct((16, D), F32),
-            jax.ShapeDtypeStruct((2, 16, HW), F32),
+        tail_kernel,
+        out_shape=outs,
+        in_specs=[HB] * (len(grads) + 1) + [VM] * len(vmem),
+        out_specs=[VM] * len(outs),
+        scratch_shapes=[
+            pltpu.VMEM((TOK, D), BF), pltpu.VMEM((3, TOK, D), BF), pltpu.VMEM((16, D), F32),
+            pltpu.VMEM((TOK, D), BF), pltpu.VMEM((2, TOK, D), BF), pltpu.VMEM((2, TOK, D), BF),
+            dma((3,)), dma((3,)), dma((3, 2)), dma((3, 2)), dma((4,)),
+            *vector_scratch(),
+            *reduce_scratch(ATTN // 2, len(grads)),
         ],
-        in_specs=[VM, VM],
-        out_specs=[VM, VM, VM],
-        scratch_shapes=[
-            pltpu.VMEM((2, 4, 16, D), F32),
-            pltpu.VMEM((16, HW), F32),
-            pltpu.VMEM((9, 16, D), F32),
-            pltpu.VMEM((9, 16, HW), F32),
-            dma((7, 4)),
-            dma((7, 4)),
-        ],
-        compiler_params=params(cid),
-        name="vector_sums",
-    )(model, heads)
-
-
-GRAD_WIDTHS = (3 * HW, HW, 2 * HW, HW, HW, FF, FF)
-
-
-def grad_kernel(*refs):
-    grads = refs[: len(GRAD_WIDTHS)]
-    out, own, sib, r1, r2, tosend, ls, ss, sr, s1, q1, s2, q2, s3, q3, l3 = refs[len(GRAD_WIDTHS) :]
-    x, y, z, core = here()
-    zl = lax.rem(z, 2)
-    rows = [chip(x + k, y, z, core) for k in (1, 2, 3)]
-    lines = [chip(x, y + k, z, core) for k in (1, 2, 3)]
-    greet(column(x, y, z, core) + rows + lines)
-    start, pairs = 0, []
-    for i, width in enumerate(GRAD_WIDTHS):
-        cols = pl.ds(start, width)
-        mine = pltpu.make_async_copy(grads[i].at[:, :, core], own.at[:, :, :, cols], ls.at[i])
-        theirs = remote(
-            grads[i].at[:, :, 1 - core], sib.at[:, :, :, cols], ss.at[i], sr.at[i], chip(x, y, z, 1 - core)
-        )
-        mine.start()
-        theirs.start()
-        pairs.append((mine, theirs))
-        start += width
-    for mine, theirs in pairs:
-        mine.wait()
-        theirs.wait()
-
-    def add_pair(k, carry):
-        a, b = lax.div(k, SIDE), lax.rem(k, SIDE)
-        own[a, b] = (own[a, b].astype(F32) + sib[a, b].astype(F32)).astype(BF)
-        return carry
-
-    lax.fori_loop(0, SIDE * SIDE, add_pair, 0)
-    wrap = lambda v: lax.rem(v, SIDE)
-    first, second = pl.ds(0, HALF), pl.ds(HALF, HALF)
-    one = []
-    for k in (2, 1, 3):
-        one.append(
-            remote(own.at[:, wrap(y + k), :, first], r1.at[0, k - 1], s1.at[0, k - 1], q1.at[0, k - 1], lines[k - 1])
-        )
-        one.append(
-            remote(own.at[wrap(x + k), :, :, second], r1.at[1, k - 1], s1.at[1, k - 1], q1.at[1, k - 1], rows[k - 1])
-        )
-    for copy in one:
-        copy.start()
-    for copy in one:
-        copy.wait()
-
-    def add_line(k, carry):
-        total = own[k, y, :, :HALF].astype(F32)
-        for i in range(3):
-            total = total + r1[0, i, k].astype(F32)
-        own[k, y, :, :HALF] = total.astype(BF)
-        total = own[x, k, :, HALF:].astype(F32)
-        for i in range(3):
-            total = total + r1[1, i, k].astype(F32)
-        own[x, k, :, HALF:] = total.astype(BF)
-        return carry
-
-    lax.fori_loop(0, SIDE, add_line, 0)
-    two = []
-    for k in (2, 1, 3):
-        two.append(
-            remote(own.at[wrap(x + k), y, :, first], r2.at[0, k - 1], s2.at[0, k - 1], q2.at[0, k - 1], rows[k - 1])
-        )
-        two.append(
-            remote(own.at[x, wrap(y + k), :, second], r2.at[1, k - 1], s2.at[1, k - 1], q2.at[1, k - 1], lines[k - 1])
-        )
-    for copy in two:
-        copy.start()
-    for copy in two:
-        copy.wait()
-    final = []
-    for part in (0, 1):
-        total = own[x, y, :, pl.ds(part * HALF, HALF)].astype(F32)
-        for i in range(3):
-            total = total + r2[part, i].astype(F32)
-        final.append(total)
-    for target in (0, 1):
-        rows_of = slice(target * ROWS, target * ROWS + ROWS)
-        tosend[target] = jnp.concatenate([final[0][rows_of], final[1][rows_of]], 0).astype(BF)
-    other = z + 1 - 2 * zl
-    far = [
-        remote(tosend.at[t], out.at[zl], s3.at[t], q3.at[zl], chip(x, y, other, t)) for t in (0, 1)
-    ]
-    self_copy = pltpu.make_async_copy(tosend.at[core], out.at[zl], l3.at[0])
-    near = remote(tosend.at[1 - core], out.at[zl], s3.at[0], q3.at[zl], chip(x, y, z, 1 - core))
-
-    def got(slot):
-        remote(tosend.at[0], out.at[slot], s3.at[0], q3.at[slot], chip(x, y, z, core)).wait_recv()
-
-    @pl.when(core == zl)
-    def _():
-        self_copy.start()
-        near.start()
-        self_copy.wait()
-        near.wait_send()
-        got(1 - zl)
-
-    @pl.when(core != zl)
-    def _():
-        for copy in far:
-            copy.start()
-        for copy in far:
-            copy.wait_send()
-        got(zl)
-        got(1 - zl)
-
-
-def grad_sums(grads, cid):
-    dma = pltpu.SemaphoreType.DMA
-    count = len(GRAD_WIDTHS)
-    return pl.pallas_call(
-        grad_kernel,
-        out_shape=jax.ShapeDtypeStruct((2, PAIR, HALF), BF),
-        in_specs=[HB] * count,
-        out_specs=VM,
-        scratch_shapes=[
-            pltpu.VMEM((SIDE, SIDE, PAIR, COLS), BF),
-            pltpu.VMEM((SIDE, SIDE, PAIR, COLS), BF),
-            pltpu.VMEM((2, 3, SIDE, PAIR, HALF), BF),
-            pltpu.VMEM((2, 3, PAIR, HALF), BF),
-            pltpu.VMEM((2, PAIR, HALF), BF),
-            dma((count,)), dma((count,)), dma((count,)),
-            dma((2, 3)), dma((2, 3)), dma((2, 3)), dma((2, 3)),
-            dma((2,)), dma((2,)), dma((1,)),
-        ],
-        compiler_params=params(cid),
-        name="grad_sums",
-    )(*grads)
+        compiler_params=params(2),
+        name="tail",
+    )(*grads, part_tokens, *vmem)
 
 
 def newton_kernel(narrow, wide, narrow_out, wide_out, mine, theirs, send, recv):
@@ -1078,15 +1289,6 @@
     return (jnp.cos(angles), jnp.sin(angles))
 
 
-def rotate(values, cosine, sine):
-    half_head = HEAD // 2
-    front_half = values[..., :half_head]
-    back_half = values[..., half_head:]
-    return jnp.concatenate(
-        [front_half * cosine - back_half * sine, back_half * cosine + front_half * sine], -1
-    )
-
-
 def plain_norm(values):
     centred = values - jnp.mean(values, -1, keepdims=True)
     inverse = lax.rsqrt(jnp.mean(centred * centred, -1, keepdims=True) + NORM_EPSILON)
@@ -1101,14 +1303,6 @@
     )
 
 
-def split_heads(values):
-    return values.reshape(values.shape[0], -1, HEAD)
-
-
-def merge_heads(values):
-    return values.reshape(values.shape[0], -1)
-
-
 def product(left, right):
     return jnp.dot(left, right, preferred_element_type=F32)
 
@@ -1119,58 +1313,6 @@
 
 def contract_rows(left, right):
     return lax.dot_general(left, right, (((0,), (0,)), ((), ())), preferred_element_type=F32)
-
-
-def attend_back(query, keys, values, grad_mixed):
-    scores = jnp.einsum("qhe,khe->hqk", query, keys, preferred_element_type=F32) * HEAD ** (-0.5)
-    weights = jax.nn.softmax(scores, -1)
-    grad_weights = jnp.einsum("qhe,khe->hqk", grad_mixed, values, preferred_element_type=F32)
-    row_delta = jnp.sum(weights * grad_weights, -1, keepdims=True)
-    grad_scores = (weights * (grad_weights - row_delta)).astype(BF)
-    grad_query = jnp.einsum("hqk,khe->qhe", grad_scores, keys, preferred_element_type=F32) * HEAD ** (
-        -0.5
-    )
-    grad_keys = jnp.einsum("hqk,qhe->khe", grad_scores, query, preferred_element_type=F32) * HEAD ** (
-        -0.5
-    )
-    grad_values = jnp.einsum(
-        "hqk,qhe->khe", weights.astype(BF), grad_mixed, preferred_element_type=F32
-    )
-    return grad_query, grad_keys, merge_heads(grad_values)
-
-
-def block_struct():
-    return jax.ShapeDtypeStruct((TOK, D), F32)
-
-
-def back_mlp(total, extras, outs):
-    after, grads, rows = extras
-    normed, inverse = plain_norm(after[...])
-    outs[1][0:1] = jnp.sum(total, 0, keepdims=True)
-    outs[1][1:2] = jnp.sum(total * normed, 0, keepdims=True)
-    result = grads[...].astype(F32) + norm_back(total * (1.0 + rows[0:1]), normed, inverse)
-    outs[0][...] = result
-    low = result.astype(BF)
-    outs[1][2:3] = jnp.sum(low.astype(F32), 0, keepdims=True)
-    return low
-
-
-def back_cross(total, extras, outs):
-    after, grads, branch, rows = extras
-    normed, inverse = plain_norm(after[...])
-    outs[1][0:1] = jnp.sum(total, 0, keepdims=True)
-    outs[1][1:2] = jnp.sum(total * normed, 0, keepdims=True)
-    result = grads[...] + norm_back(total * (1.0 + rows[0:1]), normed, inverse)
-    outs[0][...] = result
-    outs[1][2:3] = jnp.sum(result * branch[...], 0, keepdims=True)
-    low = (result * rows[1:2]).astype(BF)
-    outs[1][3:4] = jnp.sum(low.astype(F32), 0, keepdims=True)
-    return low
-
-
-def stack_rows(rows, count=8):
-    out = jnp.stack(rows)
-    return jnp.pad(out, ((0, count - len(rows)), (0, 0)))
 
 
 def body(
@@ -1193,7 +1335,7 @@
     cosine, sine = rope_tables(positions.reshape(3, 2 * TOK))
     table = jnp.concatenate([cosine, sine], -1).reshape(2, TOK, HEAD)
 
-    heads = lax.dynamic_slice(head_vectors, (0, zl * HW), (10, HW))
+    heads = jnp.pad(lax.dynamic_slice(head_vectors, (0, zl * HW), (10, HW)), ((0, 6), (0, 0)))
     bias_up = jnp.pad(lax.dynamic_slice(up_bias, (zl * FF_REAL,), (FF_REAL,)), (0, FF - FF_REAL))
     modulation = model_vectors[5:] + lax.dynamic_index_in_dim(time_embedding, core, 0, False)
     shift_one, scale_one, gate_one, shift_two, scale_two, gate_two = [modulation[i] for i in range(6)]
@@ -1204,170 +1346,65 @@
         query_two_lin, key_two_lin, inv, query_rot, key_rot, value_low, query_two, key_two, value_two,
         mixed_low, mixed_two_low, branch_one, after_one, after_two, tok_all, txt_all,
     ) = forward(
-        send_attn, send_mlp, tokens, text, cotangent, table,
-        jnp.pad(heads, ((0, 6), (0, 0))), vectors,
-    )
-    w_qkv, w_query, w_text, w_self, w_cross = [
-        w_attn[:, s] for s in (W_QKV, W_QUERY, W_TEXT, W_SELF, W_CROSS)
-    ]
-    inverse_query, inverse_key, inverse_key_two, inverse_query_two = [
-        inv[:, i : i + 1] for i in range(4)
-    ]
-    query_rot, key_rot, value_low, query_two, key_two, value_two = [
-        split_heads(v) for v in (query_rot, key_rot, value_low, query_two, key_two, value_two)
-    ]
-    tab_all = tab_all.reshape(SEQ, 1, HEAD)
-    cosine, sine = tab_all[..., : HEAD // 2], tab_all[..., HEAD // 2 :]
-
-    def block_rows(values):
-        return lax.dynamic_slice(values, (block * TOK, 0), (TOK, values.shape[1]))
-
-    cot_all = cot_all.reshape(SEQ, D)
+        send_attn, send_mlp, tokens, text, cotangent, table, heads, vectors,
+    )
+    tok_own = lax.dynamic_index_in_dim(tok_all, block, 0, False)
+    cot_own = lax.dynamic_index_in_dim(cot_all, block, 0, False)
     words = txt_all.reshape(SEQ, D)
-    tok_own = lax.dynamic_index_in_dim(tok_all, block, 0, False)
-    cot_own = block_rows(cot_all)
-
-    hidden_lin = product(input_mlp, w_up) + bias_up
-    hidden_act, gelu_pullback = jax.vjp(partial(jax.nn.gelu, approximate=True), hidden_lin)
-    hidden_low = hidden_act.astype(BF)
-    part_mlp = contract_last(hidden_low, w_down).astype(BF)
-    grad_branch_mlp = (cot_all.astype(F32) * gate_two).astype(BF)
-    grad_hidden = gelu_pullback(product(grad_branch_mlp, w_down))[0].astype(BF)
-    part = contract_last(grad_hidden, w_up).astype(BF)
-    grad_branch_two, grad_after_two, sums_mlp = z_step(
-        part,
-        [after_two, cot_own, stack_rows([scale_two])],
-        back_mlp,
-        [block_struct(), jax.ShapeDtypeStruct((8, D), F32)],
-        5,
-    )
-    grad_mixed_two = product(grad_branch_two, w_cross).astype(BF)
-    grad_query_two, grad_key_two, grad_value_two = attend_back(
-        query_two, key_two, value_two, split_heads(grad_mixed_two)
-    )
-    grad_query_two, grad_key_two = merge_heads(grad_query_two), merge_heads(grad_key_two)
-    scaled_query_two = grad_query_two * (1.0 + heads[8])
-    scaled_key_two = grad_key_two * (1.0 + heads[9])
-    dots = z_total(
-        stack_rows(
-            [jnp.sum(query_two_lin * scaled_query_two, -1), jnp.sum(key_two_lin * scaled_key_two, -1)]
-        ),
-        6,
-    )
-
-    def root_back(linear, inverse, scaled, dot):
-        return (inverse * scaled - linear * (inverse**3 * dot[:, None] / D)).astype(BF)
-
-    grad_query_two_lin = root_back(query_two_lin, inverse_query_two, scaled_query_two, dots[0])
-    grad_key_two_lin = root_back(key_two_lin, inverse_key_two, scaled_key_two, dots[1])
-    grad_kv_two_lin = jnp.concatenate([grad_key_two_lin, grad_value_two.astype(BF)], 1)
-    part = contract_last(grad_query_two_lin, w_query).astype(BF)
-    part_words = contract_last(grad_kv_two_lin, w_text).astype(BF)
-    grad_branch_one, grad_after_one, sums_cross = z_step(
-        part,
-        [after_one, grad_after_two, branch_one, stack_rows([model_vectors[3], gate_one])],
-        back_cross,
-        [block_struct(), jax.ShapeDtypeStruct((8, D), F32)],
-        7,
-    )
-    grad_mixed = product(grad_branch_one, w_self).astype(BF)
-    grad_query_rot, grad_key_rot, grad_value = attend_back(
-        query_rot, key_rot, value_low, split_heads(grad_mixed)
-    )
-    grad_query_norm = merge_heads(rotate(grad_query_rot, cosine, -sine))
-    grad_key_norm = merge_heads(rotate(grad_key_rot, cosine, -sine))
-    scaled_query = grad_query_norm * (1.0 + heads[3])
-    scaled_key = grad_key_norm * (1.0 + heads[4])
-    dots_one = z_total(
-        stack_rows([jnp.sum(query_lin * scaled_query, -1), jnp.sum(key_lin * scaled_key, -1)]), 8
-    )
-    grad_query_lin = root_back(query_lin, inverse_query, scaled_query, dots_one[0])
-    grad_key_lin = root_back(key_lin, inverse_key, scaled_key, dots_one[1])
-    grad_qkv = jnp.concatenate([grad_query_lin, grad_key_lin, grad_value.astype(BF)], 1)
-    part_tokens = contract_last(grad_qkv, w_qkv).astype(BF)
+    part_down, part_back, grad_up, grad_down, up_sum = mlp_pass(
+        input_mlp, cot_all.reshape(SEQ, D), jnp.broadcast_to(gate_two[None], (8, D)),
+        jnp.broadcast_to(bias_up[None], (8, FF)), w_up, w_down,
+    )
+
+    def by_chip(grads):
+        return grads.reshape(SIDE, SIDE, 2, PAIR, grads.shape[1])
+
+    (
+        low_two, low_one, grad_query_two, grad_kv_two, grad_qkv, part_tokens, grad_after_one, sums,
+        head_sums, result, grad_words, mlp_sums,
+    ) = backward(
+        [part_back, part_down, by_chip(grad_up), by_chip(grad_down)],
+        [
+            w_attn, after_two, cot_own, vectors, heads, query_lin, key_lin, query_two_lin, key_two_lin,
+            inv, query_rot, key_rot, value_low, query_two, key_two, value_two, tab_all, branch_one, after_one,
+        ],
+    )
 
     def rows_of(left, right):
-        out = contract_rows(left, right).astype(BF)
-        return out.reshape(SIDE, SIDE, 2, PAIR, out.shape[1])
+        return by_chip(contract_rows(left, right).astype(BF))
 
     matrix_grads = [
         rows_of(input_one, grad_qkv),
-        rows_of(input_three, grad_query_two_lin),
-        rows_of(words, grad_kv_two_lin),
-        rows_of(grad_branch_one, mixed_low),
-        rows_of(grad_branch_two, mixed_two_low),
-        rows_of(input_mlp, grad_hidden),
-        rows_of(grad_branch_mlp, hidden_low),
+        rows_of(input_three, grad_query_two),
+        rows_of(words, grad_kv_two),
+        rows_of(low_one, mixed_low),
+        rows_of(low_two, mixed_two_low),
     ]
-
-    sum_mlp, sum_tokens, sum_words = z_scatter([part_mlp, part_tokens, part_words], 9)
-    branch_mlp = sum_mlp + model_vectors[2]
-    cot_f32 = cot_own.astype(F32)
-    result = (after_two + gate_two * branch_mlp).astype(BF)
-    normed_own, inverse_own = plain_norm(tok_own.astype(F32))
-    grad_tokens = grad_after_one + norm_back(sum_tokens * (1.0 + scale_one), normed_own, inverse_own)
-    column_sum = lambda v: jnp.sum(v.astype(F32), 0)
-    model_part = stack_rows(
-        [
-            sums_cross[3],
-            sums_mlp[2],
-            column_sum(block_rows(grad_branch_mlp)),
-            sums_cross[1],
-            sums_cross[0],
-            column_sum(sum_tokens),
-            column_sum(sum_tokens * normed_own),
-            sums_cross[2],
-            sums_mlp[0],
-            sums_mlp[1],
-            column_sum(cot_f32 * branch_mlp),
-        ],
-        16,
-    )
-    grad_qkv_sum = column_sum(grad_qkv).reshape(3, HW)
-    grad_kv_sum = column_sum(grad_kv_two_lin).reshape(2, HW)
-    head_part = jnp.concatenate(
-        [
-            grad_qkv_sum,
-            jnp.stack(
-                [
-                    column_sum(grad_query_norm * query_lin * inverse_query),
-                    column_sum(grad_key_norm * key_lin * inverse_key),
-                    column_sum(grad_query_two_lin),
-                ]
-            ),
-            grad_kv_sum,
-            jnp.stack(
-                [
-                    column_sum(grad_query_two * query_two_lin * inverse_query_two),
-                    column_sum(grad_key_two * key_two_lin * inverse_key_two),
-                ]
-            ),
-            column_sum(grad_hidden).reshape(6, HW),
-        ],
-        0,
-    )
-    out_result, out_tokens, out_words = deliver(
-        [result, grad_tokens.astype(BF), sum_words.astype(BF)], 10
-    )
-    time_sums, model_sums, head_sums = vector_sums(model_part, head_part, 11)
+    head_part = jnp.concatenate([head_sums[:10], up_sum[0].reshape(6, HW)], 0)
+    out_result, out_tokens, out_words, time_sums, model_sums, head_totals, attn_sums = tail(
+        matrix_grads, part_tokens,
+        [tok_own, grad_after_one, vectors, sums, head_part, result, grad_words],
+    )
     grad_time = time_sums[:, 5:11]
     model_total = model_sums[:11]
-    head_total = head_sums[:, :10].transpose(1, 0, 2).reshape(10, 2 * HW)
-    up_total = head_sums[:, 10:].reshape(2, FF)[:, :FF_REAL].reshape(-1)
-
-    sums = grad_sums(matrix_grads, 12)
-    sums = sums.reshape(2, 2, ROWS, HALF).transpose(0, 2, 1, 3).reshape(2, ROWS, COLS).astype(F32)
-    def unpack(start, count, width, real):
-        part = sums[:, :, start : start + count * width].reshape(2, ROWS, count, width)[..., :real]
-        return part.transpose(2, 1, 0, 3).reshape(count, ROWS, 2 * real)
-
+    head_total = head_totals[:, :10].transpose(1, 0, 2).reshape(10, 2 * HW)
+    up_total = head_totals[:, 10:].reshape(2, FF)[:, :FF_REAL].reshape(-1)
+
+    attn_sums = attn_sums.reshape(2, 2, ROWS, ATTN // 2).transpose(0, 2, 1, 3).reshape(2, ROWS, ATTN)
+    mlp_sums = mlp_sums.reshape(2, 2, ROWS, FF)[..., :FF_REAL]
+
+    def unpack(first, count):
+        part = attn_sums[:, :, first * HW : (first + count) * HW].reshape(2, ROWS, count, HW)
+        return part.transpose(2, 1, 0, 3).reshape(count, ROWS, 2 * HW)
+
+    mlp_grad = mlp_sums.transpose(1, 2, 0, 3).reshape(2, ROWS, 2 * FF_REAL)
     swap = lambda v: v.transpose(1, 0, 2)
-    new_in_moment = MOMENTUM * swap(attn_in_moment) + unpack(C_IN, 6, HW, HW)
-    new_out_moment = MOMENTUM * swap(attn_out_moment) + unpack(C_OUT, 2, HW, HW)
-    new_mlp_moment = MOMENTUM * swap(mlp_moment) + unpack(C_UP, 2, FF, FF_REAL)
+    new_in_moment = MOMENTUM * swap(attn_in_moment) + unpack(0, 6)
+    new_out_moment = MOMENTUM * swap(attn_out_moment) + unpack(6, 2)
+    new_mlp_moment = MOMENTUM * swap(mlp_moment) + mlp_grad
     narrow = jnp.concatenate([new_in_moment, new_out_moment], 0).reshape(8 * ROWS, 2 * HW)
     wide = new_mlp_moment.reshape(2 * ROWS, 2 * FF_REAL)
-    narrow_dir, wide_dir = newton(narrow, wide, 13)
+    narrow_dir, wide_dir = newton(narrow, wide, 3)
     narrow_dir = narrow_dir.reshape(8, ROWS, 2 * HW)
     wide_dir = wide_dir.reshape(2, ROWS, 2 * FF_REAL)
     new_attn_in = attn_in * (1.0 - RATE_IN * DECAY) - RATE_IN * swap(narrow_dir[:6])
@@ -1378,8 +1415,8 @@
     new_up_moment = MOMENTUM * up_moment + up_total
     return (
         out_result,
-        out_tokens.astype(F32),
-        out_words.astype(F32),
+        out_tokens,
+        out_words,
         grad_time,
         new_attn_in,
         new_attn_out,

time: 736 us -> 493 us (0.67)
  matrix products: 108 us -> 15.9 us
  Pallas kernels: 519 us -> 431 us
  other arithmetic: 57.4 us -> 13.9 us
  local copies, waits for them, and re-layouts: 43.7 us -> 25.5 us
    pallas_call x8 -> x3, Pallas kernels: 344 us -> 256 us  [the longest x1 142 us: backward(): pl.pallas_call(backward_kernel, out_shape=outs, in_specs=[HB] * len(hbm)...]
    dot_general x17 -> x0, matrix products: 76 us -> none  [the longest x5 33.5 us: contract_last(): lax.dot_general(left, right, (((1,), (1,)), ((), ())), preferred_element_...]
    convert_element_type x10 -> x0, other arithmetic: 16.3 us -> none  [the longest x2 3.64 us: attend_back(): grad_scores = (weights * (grad_weights - row_delta)).astype(BF)]
    reduce_sum x12 -> x0, other arithmetic: 13.7 us -> none  [the longest x10 11.3 us: body(): column_sum = lambda v: jnp.sum(v.astype(F32), 0)]
    dot_general x7 -> x5, matrix products: 27.2 us -> 15.9 us  [contract_rows(): lax.dot_general(left, right, (((0,), (0,)), ((), ())), preferred_element_...]
where the time goes in v3:
time: 493 us; the launch traced here: 488 us
  Pallas kernels  431 us (87%)
  local copies, waits for them, and re-layouts  25.5 us (5%)
  matrix products  15.9 us (3%)
  other arithmetic  13.9 us (3%)
    pallas_call x1, Pallas kernels, forward(): pl.pallas_call(forward_kernel, out_shape=[shape for shape, _ in outs], in...  156 us
    pallas_call x1, Pallas kernels, backward(): pl.pallas_call(backward_kernel, out_shape=outs, in_specs=[HB] * len(hbm)...  142 us
    pallas_call x1, Pallas kernels, tail(): pl.pallas_call(tail_kernel, out_shape=outs, in_specs=[HB] * (len(grads) +...  76 us
    pallas_call x1, Pallas kernels, mlp_pass(): pl.pallas_call(mlp_kernel, grid=(FF // TILE,), in_specs=[fixed, fixed, pl...  38.1 us
    pallas_call x1, Pallas kernels, newton(): pl.pallas_call(newton_kernel, out_shape=[jax.ShapeDtypeStruct(narrow.shap...  19.3 us
    dot_general x5, matrix products, contract_rows(): lax.dot_general(left, right, (((0,), (0,)), ((), ())), preferred_element_...  15.9 us

profile of v3, /device:TPU:1, one launch (start us, length us, event | category | flops | bytes accessed | tf_op | source)
XLA Modules:
  0.0 488.3 jit_solution(4978440540609921098)
XLA Ops:
  3.7 0.9 fusion.2
  7.4 1.0 convert_element_type.117
  12.9 155.7 %forward.1 = (bf16[1536,3072]{1,0:T(8,128)(2,1)}, bf16[1536,2304]{1,0:T(8,128)(2,1)}, bf16[1536,2304]{1,0:T(8,128)(2,1)}, bf16[4,128,1536]{2,1,0:T(8,128)(2,1)},...) custom-call(bf16[2,48,1536]{2,1,0:T(8,128)(2,1)} %bitcast.107, ...), custom_call_target="tpu_custom_call" | custom-call | tf_op jit(solution)/shard_map/forward/pallas_call | solution.py:568
  168.6 1.8 dynamic-slice_bitcast_fusion.refs_6_
  170.4 1.8 dynamic-slice_bitcast_fusion.1.cot_own
  172.2 38.1 %mlp.1 = (bf16[512,1536]{1,0:T(8,128)(2,1)}, bf16[512,1536]{1,0:T(8,128)(2,1)}, bf16[1536,2304]{1,0:T(8,128)(2,1)}, bf16[1536,2304]{1,0:T(8,128)(2,1)}, f32[8,2304]{1,0:T(8,128)}) custom-call(bf16[512,1536]{1,0:T(8,128)(2,1)} %get-tuple-element.69.a_ref, bf16[512,1536]{1,0:T(8,128)(2,1)} %bitcast.97, f32[8,1536]{1,0:T(8,128)} %broadcast_in_dim.32.gate, ...), custom_call_target="tpu_custom_call" | custom-call | tf_op jit(solution)/shard_map/mlp/pallas_call | solution.py:643
  210.2 142.2 %backward.1 = (bf16[512,1536]{1,0:T(8,128)(2,1)}, bf16[512,1536]{1,0:T(8,128)(2,1)}, bf16[512,384]{1,0:T(8,128)(2,1)}, bf16[512,768]{1,0:T(8,128)(2,1)}, bf16[51...) custom-call(bf16[512,1536]{1,0:T(8,128)(2,1)} %get-tuple-element.73., ...), custom_call_target="tpu_custom_call" | custom-call | tf_op jit(solution)/shard_map/backward/pallas_call | solution.py:990
  352.5 3.6 convolution_convert_fusion.4
  356.1 0.9 slice_reduce_fusion
  357.7 5.4 %convolution_convert_fusion = bf16[1536,1152]{1,0:T(8,128)(2,1)} fusion(bf16[512,1536]{1,0:T(8,128)(2,1)S(1)} %copy-done.25, bf16[512,1152]{1,0:T(8,128)(2,1)} %get-tuple-element.93), kind=kOutput, calls=%fused_computation | convolution fusion | flops 1813708800 | bytes 6291456 | tf_op jit(solution)/shard_map/dot_general | solution.py:1315
  363.1 2.8 convolution_convert_fusion.1
  365.9 2.0 convolution_convert_fusion.3
  368.0 2.1 convolution_convert_fusion.2
  370.1 76.0 %tail.1 = (bf16[2,128,1536]{2,1,0:T(8,128)(2,1)}, f32[2,128,1536]{2,1,0:T(8,128)}, f32[2,128,1536]{2,1,0:T(8,128)}, f32[2,16,1536]{2,1,0:T(8,128)}, f32[16,1536]...) custom-call(bf16[4,4,2,48,1152]{4,3,2,1,0:T(8,128)(2,1)} %bitcast.94, ...), custom_call_target="tpu_custom_call" | custom-call | tf_op jit(solution)/shard_map/tail/pallas_call | solution.py:1182
  449.1 0.9 slice.67
  450.8 1.6 multiply_subtract_fusion.1
  455.4 1.0 pad_maximum_fusion
  457.1 1.1 reshape.273
  458.8 1.0 copy.63
  459.9 19.3 %newton.1 = (f32[192,768]{1,0:T(8,128)}, f32[48,4480]{1,0:T(8,128)}) custom-call(f32[192,768]{1,0:T(8,128)} %bitcast.98, f32[48,4480]{1,0:T(8,128)} %bitcast.96), custom_call_target="tpu_custom_call" | custom-call | tf_op jit(solution)/shard_map/newton/pallas_call | solution.py:1250
  479.2 2.9 bitcast_subtract_fusion
  483.8 0.9 copy.92
  484.7 1.1 copy.93
  486.7 1.1 copy.94
  (123 shorter events, 21.4 us)
Async XLA Ops:
  0.6 3.0 copy-start
  0.7 7.8 %copy-start.4 = (f32[24,6,768]{2,0,1:T(8,128)S(1)}, f32[24,6,768]{2,0,1:T(8,128)}, u32[]{:S(2)}) copy-start(f32[24,6,768]{2,0,1:T(8,128)} %param.22) | copy-start | bytes 1327108
  8.6 2.6 copy-start.2
  352.5 4.6 copy-start.22
  352.5 5.2 %copy-start.25 = (bf16[512,1536]{1,0:T(8,128)(2,1)S(1)}, bf16[512,1536]{1,0:T(8,128)(2,1)}, u32[]{:S(2)}) copy-start(bf16[512,1536]{1,0:T(8,128)(2,1)} %get-tuple-element.68) | copy-start | bytes 4718596
  357.7 5.4 %copy-start.24 = (bf16[4,128,1536]{2,1,0:T(8,128)(2,1)S(1)}, bf16[4,128,1536]{2,1,0:T(8,128)(2,1)}, u32[]{:S(2)}) copy-start(bf16[4,128,1536]{2,1,0:T(8,128)(2,1)} %get-tuple-element.96) | copy-start | bytes 4718596
  357.7 5.4 %copy-start.28 = (bf16[512,768]{1,0:T(8,128)(2,1)S(1)}, bf16[512,768]{1,0:T(8,128)(2,1)}, u32[]{:S(2)}) copy-start(bf16[512,768]{1,0:T(8,128)(2,1)} %get-tuple-element.97) | copy-start | bytes 2359300
  363.1 2.8 copy-start.27
  363.1 2.8 copy-start.30
  365.9 2.0 copy-start.26
  365.9 2.0 copy-start.29
  370.0 77.8 %copy-start.20 = (f32[4480]{0:T(1024)S(1)}, f32[4480]{0:T(1024)}, u32[]{:S(2)}) copy-start(f32[4480]{0:T(1024)} %param.27) | copy-start | bytes 53764
  370.0 77.8 %copy-start.23 = (f32[4480]{0:T(1024)S(1)}, f32[4480]{0:T(1024)}, u32[]{:S(2)}) copy-start(f32[4480]{0:T(1024)} %param.33) | copy-start | bytes 53764
  370.0 78.4 %copy-start.18 = (f32[10,768]{1,0:T(8,128)S(1)}, f32[10,768]{1,0:T(8,128)}, u32[]{:S(2)}) copy-start(f32[10,768]{1,0:T(8,128)} %param.25) | copy-start | bytes 92164
  370.0 78.4 %copy-start.21 = (f32[10,768]{1,0:T(8,128)S(1)}, f32[10,768]{1,0:T(8,128)}, u32[]{:S(2)}) copy-start(f32[10,768]{1,0:T(8,128)} %param.31) | copy-start | bytes 92164
  370.0 80.7 %copy-start.16 = (f32[11,1536]{1,0:T(8,128)S(1)}, f32[11,1536]{1,0:T(8,128)}, u32[]{:S(2)}) copy-start(f32[11,1536]{1,0:T(8,128)} %param.26) | copy-start | bytes 202756
  370.0 80.7 %copy-start.19 = (f32[11,1536]{1,0:T(8,128)S(1)}, f32[11,1536]{1,0:T(8,128)}, u32[]{:S(2)}) copy-start(f32[11,1536]{1,0:T(8,128)} %param.32) | copy-start | bytes 202756
  446.1 6.3 %copy-start.14 = (f32[2,48,1536]{2,1,0:T(8,128)S(1)}, f32[2,48,1536]{2,1,0:T(8,128)}, u32[]{:S(2)}) copy-start(f32[2,48,1536]{2,1,0:T(8,128)} %get-tuple-element.114) | copy-start | bytes 1769476
  458.8 20.4 %copy-start.3 = (f32[2,24,4480]{2,0,1:T(2,128)}, f32[2,24,4480]{2,0,1:T(2,128)S(1)}, u32[]{:S(2)}) copy-start(f32[2,24,4480]{2,0,1:T(2,128)S(1)} %bitcast_add_fusion) | copy-start | bytes 2580484
  479.2 2.9 copy-start.13
  479.2 3.0 copy-start.5
  482.2 2.5 copy-start.8
  484.7 2.0 copy-start.7
  484.7 3.1 copy-start.1
  (7 other events, 9.3 us)

commit v4 on v3

v4 whole, which is shorter than its diff:
```python
from functools import partial
import math

import jax
import jax.numpy as jnp
from jax import lax
from jax.experimental import pallas as pl
from jax.experimental.pallas import tpu as pltpu
from jax.sharding import PartitionSpec as P

D = 1536
HEAD = 128
ROWS = 24
HEADS = 3
NORM_EPSILON = 1e-06
ORTHO_EPSILON = 1e-07
NEWTON_FIRST = 3.4445
NEWTON_SECOND = -4.775
NEWTON_THIRD = 2.0315
NS_STEPS = 5
MOMENTUM = 0.9
DECAY = 0.01
RATE_IN = 0.5
RATE_OUT = 4.0
RATE_MLP = 1.0
RATE_VECTOR = 0.005
HIGHEST = lax.Precision.HIGHEST

MESH = pl.DeviceIdType.MESH
BF = jnp.bfloat16
F32 = jnp.float32

SIDE = 4
TOK = 128
SEQ = SIDE * TOK
HW = HEADS * HEAD
FF_REAL = 2240
FF = 2304
PAIR = 2 * ROWS
VMEM_LIMIT = 57 * 1024 * 1024


def here():
    f = lax.axis_index("fsdp")
    c = lax.axis_index("ctx")
    t = lax.axis_index("tp")
    x, y = lax.div(f, SIDE), lax.rem(f, SIDE)
    zl, core = lax.div(c, 2), lax.rem(c, 2)
    return x, y, 2 * t + zl, core


def chip(x, y, z, core):
    x, y, z = lax.rem(x + SIDE, SIDE), lax.rem(y + SIDE, SIDE), lax.rem(z + SIDE, SIDE)
    return {"fsdp": x * SIDE + y, "ctx": lax.rem(z, 2) * 2 + core, "tp": lax.div(z, 2)}


def block_of(z):
    z = lax.rem(z + SIDE, SIDE)
    return 2 * lax.rem(z, 2) + lax.div(z, 2)


def greet(devices):
    barrier = pltpu.get_barrier_semaphore()
    for device in devices:
        pl.semaphore_signal(barrier, inc=1, device_id=device, device_id_type=MESH)
    pl.semaphore_wait(barrier, len(devices))


def column(x, y, z, core):
    return [chip(x, y, z + k, core) for k in (1, 2, 3)] + [
        chip(x, y, z + k, 1 - core) for k in range(4)
    ]


def remote(src, dst, send, recv, device):
    return pltpu.make_async_remote_copy(
        src_ref=src, dst_ref=dst, send_sem=send, recv_sem=recv, device_id=device, device_id_type=MESH
    )


def params(cid):
    return pltpu.CompilerParams(
        collective_id=cid, has_side_effects=True, vmem_limit_bytes=VMEM_LIMIT
    )


VM = pl.BlockSpec(memory_space=pltpu.VMEM)
HB = pl.BlockSpec(memory_space=pltpu.HBM)


def flat(a, b):
    return lax.rem(a + SIDE, SIDE) * SIDE + lax.rem(b + SIDE, SIDE)


def steps_of(x, y, z, core):
    return (
        (chip(x + 1, y, z, core), chip(x - 1, y, z, core)),
        (chip(x, y + 1, z, core), chip(x, y - 1, z, core)),
    )


def gather_xy(own, place, xs, xr, ks, kr):
    x, y, z, core = here()
    mine = x * SIDE + y
    steps = steps_of(x, y, z, core)
    sibling = chip(x, y, z, 1 - core)
    sends, sibs = [], []

    def push(part, slot, src, index, device, half=None):
        copy = remote(src, place(part, index, half), xs.at[part, slot], xr.at[part, slot], device)
        copy.start()
        sends.append(copy)
        return copy

    def to_sibling(part, slot, src, index):
        copy = remote(src, place(part, index), ks.at[part, slot], kr.at[part, slot], sibling)
        copy.start()
        sibs.append(copy)

    def index_of(part, first_off, second_off):
        if part == 0:
            return flat(x + first_off, y + second_off)
        return flat(x + second_off, y + first_off)

    one, two = {}, {}
    for part in (0, 1):
        a_next, a_prev = steps[part]
        one[part, "next"] = push(part, 0, own.at[part], mine, a_next)
        one[part, "prev"] = push(part, 1, own.at[part], mine, a_prev)
    for part in (0, 1):
        b_next, b_prev = steps[1 - part]
        two[part, 0, "next"] = push(part, 4, own.at[part], mine, b_next)
        two[part, 0, "prev"] = push(part, 5, own.at[part], mine, b_prev)
        to_sibling(part, 0, own.at[part], mine)

    def second_start(part, k, offset):
        b_next, b_prev = steps[1 - part]
        index = index_of(part, offset, 0)
        src = place(part, index)
        two[part, k, "next"] = push(part, 4 + 4 * k, src, index, b_next)
        two[part, k, "prev"] = push(part, 5 + 4 * k, src, index, b_prev)
        to_sibling(part, 4 * k, src, index)

    offsets = (0, -1, 1, 2)
    for part in (0, 1):
        a_next, a_prev = steps[part]
        yield
        one[part, "next"].wait_recv()
        index = index_of(part, -1, 0)
        one[part, "far0"] = push(part, 2, place(part, index, 0), index, a_next, 0)
        second_start(part, 1, -1)
        one[part, "prev"].wait_recv()
        index = index_of(part, 1, 0)
        one[part, "far1"] = push(part, 3, place(part, index, 1), index, a_prev, 1)
        second_start(part, 2, 1)

    def second_forward(part, k):
        b_next, b_prev = steps[1 - part]
        two[part, k, "next"].wait_recv()
        index = index_of(part, offsets[k], -1)
        two[part, k, "far0"] = push(part, 6 + 4 * k, place(part, index, 0), index, b_next, 0)
        to_sibling(part, 4 * k + 1, place(part, index), index)
        two[part, k, "prev"].wait_recv()
        index = index_of(part, offsets[k], 1)
        two[part, k, "far1"] = push(part, 7 + 4 * k, place(part, index, 1), index, b_prev, 1)
        to_sibling(part, 4 * k + 2, place(part, index), index)

    def second_finish(part, k):
        two[part, k, "far0"].wait_recv()
        two[part, k, "far1"].wait_recv()
        index = index_of(part, offsets[k], 2)
        to_sibling(part, 4 * k + 3, place(part, index), index)

    for part in (0, 1):
        yield
        second_forward(part, 0)
    for part in (0, 1):
        yield
        one[part, "far0"].wait_recv()
        one[part, "far1"].wait_recv()
        second_start(part, 3, 2)
    for k in (1, 2, 3):
        for part in (0, 1):
            yield
            second_forward(part, k)
        for part in (0, 1):
            second_finish(part, k - 1)
    for part in (0, 1):
        yield
        second_finish(part, 3)
    yield
    for copy in sends:
        copy.wait_send()
    for copy in sibs:
        copy.wait_send()
        copy.wait_recv()


GATHER_SEMS = ((2, 20), (2, 20), (2, 16), (2, 16))


def advance(job, count=1):
    for _ in range(count):
        next(job, None)


def finish(job):
    for _ in job:
        pass


def share_rows(send, recv, s, r, l):
    x, y, z, core = here()
    zl = lax.rem(z, 2)
    away = remote(send.at[1 - zl], recv.at[core], s.at[0], r.at[core], chip(x, y, z + 1 - 2 * zl, zl))
    near = remote(send.at[zl], recv.at[core], s.at[1], r.at[core], chip(x, y, z, zl))
    self_copy = pltpu.make_async_copy(send.at[zl], recv.at[core], l.at[0])

    def got(slot):
        remote(send.at[0], recv.at[slot], s.at[0], r.at[slot], chip(x, y, z, core)).wait_recv()

    def start():
        away.start()

        @pl.when(core == zl)
        def _():
            self_copy.start()

        @pl.when(core != zl)
        def _():
            near.start()

    def wait(own):
        @pl.when(core == zl)
        def _():
            self_copy.wait()
            got(1 - core)

        @pl.when(core != zl)
        def _():
            near.wait_send()
            got(0)
            got(1)

        first = recv[0].astype(F32)
        second = recv[1].astype(F32)
        own[0] = jnp.concatenate([first[:ROWS], second[:ROWS]], 0).astype(BF)
        own[1] = jnp.concatenate([first[ROWS:], second[ROWS:]], 0).astype(BF)

    return start, wait, away.wait_send


def share_clip(src, dst, s, r, l):
    x, y, z, core = here()
    put = dst.at[2 * lax.rem(z, 2) + core]
    copies = [
        remote(src.at[1 - core], put, s.at[0], r.at[0], chip(x, y, z, 1 - core)),
        remote(src.at[0], put, s.at[1], r.at[1 + core], chip(x, y, z + 1, 0)),
        remote(src.at[1], put, s.at[2], r.at[1 + core], chip(x, y, z - 1, 1)),
    ]
    local = pltpu.make_async_copy(src.at[core], put, l)

    def start():
        for copy in copies:
            copy.start()
        local.start()

    def wait():
        local.wait()
        for slot in range(3):
            remote(src.at[0], dst.at[0], s.at[0], r.at[slot], chip(x, y, z, core)).wait_recv()

    def drain():
        for copy in copies:
            copy.wait_send()

    return start, wait, drain


def split3(values):
    return [values[:, i * HW : (i + 1) * HW] for i in range(values.shape[1] // HW)]


def swap_halves(values):
    return pltpu.roll(values, HEAD // 2, 1)


def rope_pair(table):
    lane = lax.broadcasted_iota(jnp.int32, table.shape, 1)
    other = swap_halves(table)
    front = lane < HEAD // 2
    return jnp.where(front, table, other), jnp.where(front, -other, table)


def head_slice(h):
    return slice(h * HEAD, (h + 1) * HEAD)


SCALE = HEAD ** (-0.5)


def softmax_rows(query, keys):
    scores = contract_last(query, keys) * SCALE
    peak = jnp.max(scores, -1, keepdims=True)
    raised = jnp.exp(scores - peak)
    return raised * (1.0 / jnp.sum(raised, -1, keepdims=True))


def attend_clip(query, keys, values, out):
    for h in range(HEADS):
        cols = head_slice(h)
        for start in range(0, SEQ, 256):
            rows = slice(start, start + 256)
            weights = softmax_rows(query[rows, cols], keys[:, cols]).astype(BF)
            out[rows, cols] = product(weights, values[:, cols]).astype(BF)


class Stats:
    def __init__(self, buffer, send, recv):
        self.buffer, self.send, self.recv = buffer, send, recv

    def start(self, turn, columns):
        x, y, z, core = here()
        lane = lax.broadcasted_iota(jnp.int32, (SEQ, 128), 1)
        packed = jnp.zeros((SEQ, 128), F32)
        for i, column_values in enumerate(columns):
            packed = jnp.where(lane == i, column_values, packed)
        self.buffer[turn, 0] = packed.T[:8]
        copies = []
        for k in (2, 1, 3):
            copies.append(
                remote(self.buffer.at[turn, 0], self.buffer.at[turn, k], self.send.at[turn, k - 1],
                       self.recv.at[turn, k - 1], chip(x, y, z + k, core))
            )
            copies[-1].start()

        def wait():
            for copy in copies:
                copy.wait()
            total = (self.buffer[turn, 0] + self.buffer[turn, 1]) + (
                self.buffer[turn, 2] + self.buffer[turn, 3]
            )
            spread = jnp.concatenate([total, jnp.zeros((120, SEQ), F32)], 0).T
            return [spread[:, i : i + 1] for i in range(len(columns))]

        return wait


def block_slice(index):
    return pl.ds(pl.multiple_of(index * TOK, TOK), TOK)


def scatter_product(left, right, part, got, send, recv):
    x, y, z, core = here()
    copies = []
    for k in (2, 1, 3, 0):
        rows = block_slice(block_of(z + k))
        part[rows] = contract_last(left[rows], right).astype(BF)
        if k:
            copies.append(
                remote(part.at[rows], got.at[k - 1], send.at[k - 1], recv.at[k - 1], chip(x, y, z + k, core))
            )
            copies[-1].start()
    return copies


def collect(part, got, copies):
    z = here()[2]
    for copy in copies:
        copy.wait_recv()
    total = part[block_slice(block_of(z))].astype(F32)
    for k in range(3):
        total = total + got[k].astype(F32)
    return total


def spread_block(out, value, send, recv):
    x, y, z, core = here()
    rows = block_slice(block_of(z))
    out[rows] = value
    copies = []
    for k in (2, 1, 3):
        copies.append(
            remote(out.at[rows], out.at[rows], send.at[k - 1], recv.at[k - 1], chip(x, y, z + k, core))
        )
        copies[-1].start()
    return copies


def inverse_root(total):
    return lax.rsqrt(total * (1.0 / D) + NORM_EPSILON)


V_SELF, V_CROSS, V_DOWN, V_GAIN, V_BIAS = 6, 7, 8, 9, 10
W_QKV, W_QUERY, W_TEXT, W_SELF, W_CROSS = (
    slice(0, 3 * HW), slice(3 * HW, 4 * HW), slice(4 * HW, 6 * HW), slice(6 * HW, 7 * HW), slice(7 * HW, 8 * HW),
)
ATTN = 8 * HW


SAVED = 22


def forward_kernel(
    send_attn, send_mlp, tok, txt, cot, tab, heads, vec,
    w_attn, w_up, w_down, cot_all, *rest,
):
    saved, held, rest = rest[:SAVED], rest[SAVED : 2 * SAVED], rest[2 * SAVED :]
    (
        tab_all, input_one, input_three, input_mlp, query_lin, key_lin, query_two_lin, key_two_lin, inv,
        query_rot, key_rot, value_low, query_two, key_two, value_two, mixed, mixed_two, branch_one,
        after_one, after_two, tok_all, txt_all,
    ) = held
    (
        wa, got_attn, got_mlp, own_attn, own_mlp, part_one, part_two, blocks, stat,
        xs, xr, ks, kr, ms, mr, js, jr, rs, rr, cs, cr, loc, stat_s, stat_r, zs, zr, gs, gr, keep,
    ) = rest
    x, y, z, core = here()
    mine = x * SIDE + y
    stores = []

    def save(*refs):
        for ref in refs:
            i = [ref is other for other in held].index(True)
            stores.append(pltpu.make_async_copy(ref, saved[i], keep.at[i]))
            stores[-1].start()

    greet(
        [device for pair in steps_of(x, y, z, core) for device in pair] + column(x, y, z, core)
    )
    attn_start, attn_wait, attn_drain = share_rows(send_attn, got_attn, rs.at[0], rr.at[0], loc.at[0])
    mlp_start, mlp_wait, mlp_drain = share_rows(send_mlp, got_mlp, rs.at[1], rr.at[1], loc.at[1])
    acts = [
        share_clip(src, dst, cs.at[i], cr.at[i], loc.at[2 + i, 0])
        for i, (src, dst) in enumerate(
            ((tok, tok_all), (tab, tab_all), (txt, txt_all), (cot, cot_all))
        )
    ]
    attn_start()
    acts[0][0]()
    acts[1][0]()
    attn_wait(own_attn)

    def attn_place(part, index, half=None):
        start, size = part * (ATTN // 2), ATTN // 2
        if half is not None:
            start, size = start + half * (ATTN // 4), ATTN // 4
        rows = pl.ds(pl.multiple_of(index * (2 * PAIR) + core * PAIR, PAIR), PAIR)
        return wa.at[rows, pl.ds(start, size)]

    def mlp_place(part, index, half=None):
        start, size = (0, FF) if half is None else (half * (FF // 2), FF // 2)
        rows = pl.ds(pl.multiple_of(index * (2 * PAIR) + core * PAIR, PAIR), PAIR)
        return (w_up, w_down)[part].at[rows, pl.ds(start, size)]

    gather_attn = gather_xy(own_attn, attn_place, xs, xr, ks, kr)
    advance(gather_attn)
    for part in (0, 1):
        attn_place(part, mine)[...] = own_attn[part]
    acts[2][0]()
    mlp_start()

    def norm_block(i, carry):
        normed, _ = plain_norm(tok_all[i].astype(F32))
        input_one[block_slice(i)] = (normed * (1.0 + vec[1:2]) + vec[0:1]).astype(BF)
        return carry

    advance(gather_attn, 4)
    acts[3][0]()
    advance(gather_attn, 2)
    acts[0][1]()
    lax.fori_loop(0, 2, norm_block, 0)
    advance(gather_attn, 2)
    lax.fori_loop(2, 4, norm_block, 0)
    save(input_one, tok_all)
    advance(gather_attn, 2)
    mlp_wait(own_mlp)
    locals_ = []
    for part in (0, 1):
        locals_.append(pltpu.make_async_copy(own_mlp.at[part], mlp_place(part, mine), loc.at[6, part]))
        locals_[-1].start()
    advance(gather_attn, 2)
    gather_mlp = gather_xy(own_mlp, mlp_place, ms, mr, js, jr)
    advance(gather_mlp)
    finish(gather_attn)
    locals_.append(pltpu.make_async_copy(wa, w_attn, loc.at[7, 0]))
    locals_[-1].start()
    acts[1][1]()
    acts[2][1]()
    save(tab_all, txt_all)

    stats = Stats(stat, stat_s, stat_r)
    query_lin[...] = product(input_one[...], wa[:, 0:HW]) + heads[0:1]
    key_lin[...] = product(input_one[...], wa[:, HW : 2 * HW]) + heads[1:2]
    words = txt_all[...].reshape(SEQ, D)
    key_two_lin[...] = product(words, wa[:, 4 * HW : 5 * HW]) + heads[6:7]
    norm_wait = stats.start(
        0,
        [
            jnp.sum(ref[...] * ref[...], -1, keepdims=True)
            for ref in (query_lin, key_lin, key_two_lin)
        ],
    )
    value_low[...] = (product(input_one[...], wa[:, 2 * HW : 3 * HW]) + heads[2:3]).astype(BF)
    value_two[...] = (product(words, wa[:, 5 * HW : 6 * HW]) + heads[7:8]).astype(BF)
    save(query_lin, key_lin, key_two_lin, value_low, value_two)
    lane = lax.broadcasted_iota(jnp.int32, (SEQ, 128), 1)
    inverse_query, inverse_key, inverse_key_two = [inverse_root(v) for v in norm_wait()]
    inv[...] = jnp.where(
        lane == 0, inverse_query, jnp.where(lane == 1, inverse_key, jnp.where(lane == 2, inverse_key_two, 0.0))
    )
    cosine, sine = rope_pair(tab_all[...].reshape(SEQ, HEAD))
    for h in range(HEADS):
        cols = head_slice(h)
        for lin, inverse, gain, out in (
            (query_lin, inverse_query, 3, query_rot),
            (key_lin, inverse_key, 4, key_rot),
        ):
            value = lin[:, cols] * inverse * (1.0 + heads[gain : gain + 1, cols])
            out[:, cols] = (value * cosine + swap_halves(value) * sine).astype(BF)
    advance(gather_mlp, 2)
    attend_clip(query_rot, key_rot, value_low, mixed)
    copies = scatter_product(mixed, wa[:, W_SELF], part_one, blocks.at[0], zs.at[0], zr.at[0])
    drains = list(copies)
    key_two[...] = (key_two_lin[...] * inverse_key_two * (1.0 + heads[9:10])).astype(BF)
    save(query_rot, key_rot, key_two, mixed)
    advance(gather_mlp, 8)
    branch = collect(part_one, blocks.at[0], copies) + vec[V_SELF : V_SELF + 1]
    branch_one[...] = branch
    after = tok_all[block_of(z)].astype(F32) + vec[2:3] * branch
    after_one[...] = after
    normed, _ = plain_norm(after)
    copies = spread_block(
        input_three,
        (normed * (1.0 + vec[V_GAIN : V_GAIN + 1]) + vec[V_BIAS : V_BIAS + 1]).astype(BF),
        gs.at[0],
        gr.at[0],
    )
    drains += copies
    save(branch_one, after_one)
    finish(gather_mlp)
    for copy in copies:
        copy.wait_recv()
    query_two_lin[...] = product(input_three[...], wa[:, W_QUERY]) + heads[5:6]
    norm_wait = stats.start(1, [jnp.sum(query_two_lin[...] * query_two_lin[...], -1, keepdims=True)])
    save(input_three, query_two_lin)
    inverse_query_two = inverse_root(norm_wait()[0])
    inv[...] = jnp.where(lane == 3, inverse_query_two, inv[...])
    query_two[...] = (query_two_lin[...] * inverse_query_two * (1.0 + heads[8:9])).astype(BF)
    attend_clip(query_two, key_two, value_two, mixed_two)
    copies = scatter_product(mixed_two, wa[:, W_CROSS], part_two, blocks.at[1], zs.at[1], zr.at[1])
    drains += copies
    save(inv, query_two, mixed_two)
    after = after_one[...] + collect(part_two, blocks.at[1], copies) + vec[V_CROSS : V_CROSS + 1]
    after_two[...] = after
    normed, _ = plain_norm(after)
    copies = spread_block(
        input_mlp, (normed * (1.0 + vec[4:5]) + vec[3:4]).astype(BF), gs.at[1], gr.at[1]
    )
    drains += copies
    save(after_two)
    for copy in locals_:
        copy.wait()
    acts[3][1]()
    for act in acts:
        act[2]()
    attn_drain()
    mlp_drain()
    for copy in copies:
        copy.wait_recv()
    save(input_mlp)
    for copy in drains:
        copy.wait_send()
    for copy in stores:
        copy.wait()


def forward(send_attn, send_mlp, tok, txt, cot, tab, heads, vec):
    dma = pltpu.SemaphoreType.DMA
    sds = jax.ShapeDtypeStruct
    wide, lin, low = sds((SEQ, D), BF), sds((SEQ, HW), F32), sds((SEQ, HW), BF)
    block = sds((TOK, D), F32)
    outs = [
        sds((SIDE, TOK, HEAD), F32), wide, wide, wide, lin, lin, lin, lin, sds((SEQ, 128), F32),
        low, low, low, low, low, low, low, low, block, block, block,
        sds((SIDE, TOK, D), BF), sds((SIDE, TOK, D), BF),
    ]
    weights = [sds((D, ATTN), BF), sds((D, FF), BF), sds((D, FF), BF), sds((SIDE, TOK, D), BF)]
    return pl.pallas_call(
        forward_kernel,
        out_shape=weights + outs,
        in_specs=[VM, VM, HB, HB, HB, VM, VM, VM],
        out_specs=[HB] * (len(weights) + len(outs)),
        scratch_shapes=[
            *[pltpu.VMEM(shape.shape, shape.dtype) for shape in outs],
            pltpu.VMEM((D, ATTN), BF),
            pltpu.VMEM((2, PAIR, ATTN // 2), BF),
            pltpu.VMEM((2, PAIR, FF), BF),
            pltpu.VMEM((2, PAIR, ATTN // 2), BF),
            pltpu.VMEM((2, PAIR, FF), BF),
            pltpu.VMEM((SEQ, D), BF),
            pltpu.VMEM((SEQ, D), BF),
            pltpu.VMEM((2, 3, TOK, D), BF),
            pltpu.VMEM((2, 4, 8, SEQ), F32),
            *[dma(s) for s in GATHER_SEMS],
            *[dma(s) for s in GATHER_SEMS],
            dma((2, 2)), dma((2, 2)), dma((4, 3)), dma((4, 3)), dma((8, 2)),
            dma((2, 3)), dma((2, 3)), dma((2, 3)), dma((2, 3)), dma((2, 3)), dma((2, 3)),
            dma((SAVED,)),
        ],
        compiler_params=params(0),
        name="forward",
    )(send_attn, send_mlp, tok, txt, cot, tab, heads, vec)


BATCH = 768


def peers_xy(x, y, z, core):
    rows = [chip(x + k, y, z, core) for k in (1, 2, 3)]
    lines = [chip(x, y + k, z, core) for k in (1, 2, 3)]
    return rows, lines


def reduce_batch(grads, out, sib, r1, r2, tosend, ss, sr, s1, q1, s2, q2, *swap_sems, gates=None):
    x, y, z, core = here()
    zl = lax.rem(z, 2)
    rows, lines = peers_xy(x, y, z, core)
    sibling = chip(x, y, z, 1 - core)
    wrap = lambda v: lax.rem(v, SIDE)
    swaps, one, two = [], {0: [], 1: []}, {0: [], 1: []}
    free = gates if gates is not None else (None, None)
    if free[1] is not None:
        pl.semaphore_wait(free[1], 7)
    for part in (0, 1):
        swaps.append(
            remote(grads.at[part, :, :, 1 - core], sib.at[part], ss.at[part], sr.at[part], sibling)
        )
        swaps[part].start()
    yield
    for part in (0, 1):
        swaps[part].wait_recv()

        def add_pair(k, carry):
            a, b = lax.div(k, SIDE), lax.rem(k, SIDE)
            grads[part, a, b, core] = grads[part, a, b, core] + sib[part, a, b]
            return carry

        lax.fori_loop(0, SIDE * SIDE, add_pair, 0)
        for k in (2, 1, 3):
            src = grads.at[0, :, wrap(y + k), core] if part == 0 else grads.at[1, wrap(x + k), :, core]
            device = (lines, rows)[part][k - 1]
            copy = remote(src, r1.at[part, k - 1], s1.at[part, k - 1], q1.at[part, k - 1], device)
            copy.start()
            one[part].append(copy)
    yield
    for part in (0, 1):
        for copy in one[part]:
            copy.wait_recv()

        def add_line(k, carry):
            a, b = (k, y) if part == 0 else (x, k)
            total = grads[part, a, b, core].astype(F32)
            for i in range(3):
                total = total + r1[part, i, k].astype(F32)
            grads[part, a, b, core] = total.astype(BF)
            return carry

        lax.fori_loop(0, SIDE, add_line, 0)
        for k in (2, 1, 3):
            src = grads.at[0, wrap(x + k), y, core] if part == 0 else grads.at[1, x, wrap(y + k), core]
            device = (rows, lines)[part][k - 1]
            copy = remote(src, r2.at[part, k - 1], s2.at[part, k - 1], q2.at[part, k - 1], device)
            copy.start()
            two[part].append(copy)
    yield
    final = []
    for part in (0, 1):
        for copy in two[part]:
            copy.wait_recv()
        total = grads[part, x, y, core].astype(F32)
        for i in range(3):
            total = total + r2[part, i].astype(F32)
        final.append(total)
    if free[0] is not None:
        for device in [*rows, *lines, sibling]:
            pl.semaphore_signal(free[0], inc=1, device_id=device, device_id_type=MESH)
    for target in (0, 1):
        span = slice(target * ROWS, target * ROWS + ROWS)
        tosend[target] = jnp.concatenate([final[0][span], final[1][span]], 0).astype(tosend.dtype)
    if out is not None:
        exchange = swap_rows(tosend, out, *swap_sems)
        next(exchange)
        yield
        finish(exchange)
    for copy in swaps + one[0] + one[1] + two[0] + two[1]:
        copy.wait_send()


def swap_rows(owned, out, s3, q3, l3):
    x, y, z, core = here()
    zl = lax.rem(z, 2)
    other = z + 1 - 2 * zl
    far = [
        remote(owned.at[t], out.at[zl], s3.at[t], q3.at[zl], chip(x, y, other, t)) for t in (0, 1)
    ]
    self_copy = pltpu.make_async_copy(owned.at[core], out.at[zl], l3.at[0])
    near = remote(owned.at[1 - core], out.at[zl], s3.at[0], q3.at[zl], chip(x, y, z, 1 - core))

    def got(slot):
        remote(owned.at[0], out.at[slot], s3.at[0], q3.at[slot], chip(x, y, z, core)).wait_recv()

    @pl.when(core == zl)
    def _():
        self_copy.start()
        near.start()

    @pl.when(core != zl)
    def _():
        for copy in far:
            copy.start()

    yield

    @pl.when(core == zl)
    def _():
        self_copy.wait()
        near.wait_send()
        got(1 - zl)

    @pl.when(core != zl)
    def _():
        for copy in far:
            copy.wait_send()
        got(zl)
        got(1 - zl)


def reduce_buffers():
    return [
        pltpu.VMEM((2, SIDE, SIDE, PAIR, BATCH), BF),
        pltpu.VMEM((2, 3, SIDE, PAIR, BATCH), BF),
        pltpu.VMEM((2, 3, PAIR, BATCH), BF),
    ]


def reduce_sems():
    dma = pltpu.SemaphoreType.DMA
    return [dma((2,)), dma((2,)), dma((2, 3)), dma((2, 3)), dma((2, 3)), dma((2, 3))]


def swap_sems():
    dma = pltpu.SemaphoreType.DMA
    return [dma((2,)), dma((2,)), dma((1,))]


def reduce_scratch():
    return [*reduce_buffers(), pltpu.VMEM((2, PAIR, BATCH), F32), *reduce_sems(), *swap_sems()]


GRADS = (2, SIDE, SIDE, 2, PAIR, BATCH)
SLAB = D // SIDE


def weight_grad(left, right, grads, part, start):
    width = right.shape[1]

    def slab(i, carry):
        turned = left[:, pl.ds(pl.multiple_of(i * SLAB, SLAB), SLAB)].T
        value = product(turned, right).astype(BF).reshape(SIDE, 2, PAIR, width)
        grads[part, i, :, :, :, start : start + width] = value
        return carry

    lax.fori_loop(0, SIDE, slab, 0)


def column_sum(values):
    return jnp.sum(values.astype(F32), 0, keepdims=True)


def scatter_held(part, got, send, recv, first=0, count=TOK):
    x, y, z, core = here()
    copies = []
    for k in (2, 1, 3):
        rows = pl.ds(pl.multiple_of(block_of(z + k) * TOK + first, count), count)
        copies.append(
            remote(part.at[rows], got.at[k - 1, pl.ds(first, count)], send.at[k - 1], recv.at[k - 1],
                   chip(x, y, z + k, core))
        )
        copies[-1].start()
    return copies


def deliver(src, dst, s, r, l):
    x, y, z, core = here()
    zh = lax.div(z, 2)
    far = remote(src, dst.at[core], s.at[0], r.at[core], chip(x, y, z + 2, zh))
    near = remote(src, dst.at[core], s.at[1], r.at[core], chip(x, y, z, zh))
    self_copy = pltpu.make_async_copy(src, dst.at[core], l)

    def got(slot):
        remote(src, dst.at[slot], s.at[0], r.at[slot], chip(x, y, z, core)).wait_recv()

    def start():
        far.start()

        @pl.when(core == zh)
        def _():
            self_copy.start()

        @pl.when(core != zh)
        def _():
            near.start()

    def wait():
        @pl.when(core == zh)
        def _():
            self_copy.wait()
            got(1 - core)

        @pl.when(core != zh)
        def _():
            near.wait_send()
            got(0)
            got(1)

        far.wait_send()

    return start, wait


CUBE = 0.044715
ROOT = math.sqrt(2.0 / math.pi)


def gelu_pair(u):
    square = u * u
    t = jnp.tanh(ROOT * u * (1.0 + CUBE * square))
    half = 0.5 * (1.0 + t)
    return u * half, half + 0.5 * u * (1.0 - t * t) * (ROOT * (1.0 + 3.0 * CUBE * square))


def total_of(mine, blocks):
    total = mine.astype(F32)
    for k in range(3):
        total = total + blocks[k].astype(F32)
    return total


def mlp_kernel(
    a_in, cot_all, w_up, w_down, after_in, vec, bias,
    low_out, grad_after, sums, bias_sum, out_result, owned_a, owned_b, owned_c,
    a, low, ahead, behind, hidden, act, back, acc, part, after_two, low_two,
    blocks, result, zs, zr, gs, gr, ds, dr, loc, ring, gate, *rest,
):
    x, y, z, core = here()
    rows, lines = peers_xy(x, y, z, core)
    own_rows = block_slice(block_of(z))

    def load(src, dst, sem):
        copy = pltpu.make_async_copy(src, dst, sem)
        copy.start()
        return copy

    def third(n):
        return pl.ds(n % 3 * BATCH, BATCH)

    def load_ahead(n):
        return load((w_up, w_down)[n // 3].at[:, third(n)], ahead.at[n % 2], ring.at[0, n % 2])

    def load_behind(n):
        return load((w_down, w_up)[n // 3].at[:, third(n)], behind.at[n % 2], ring.at[1, n % 2])

    aheads, behinds = {0: load_ahead(0)}, {}
    fetch_a = load(a_in, a, loc.at[0])
    behinds[0] = load_behind(0)
    fetch_low = load(cot_all.reshape(SEQ, D), low, loc.at[1])
    aheads[1], behinds[1] = load_ahead(1), load_behind(1)
    fetch_after = load(after_in, after_two, loc.at[2])
    greet(column(x, y, z, core) + rows + lines)
    sums[...] = jnp.zeros_like(sums)
    fetch_a.wait()
    aheads[0].wait()
    hidden[0] = product(a[...], ahead[0])
    aheads[2] = load_ahead(2)
    fetch_low.wait()
    dy = low[own_rows].astype(F32)
    for start in range(0, SEQ, TOK):
        block = slice(start, start + TOK)
        low[block] = (low[block].astype(F32) * vec[5:6]).astype(BF)
    sums[2:3] = column_sum(low[own_rows])
    fetch_after.wait()

    grads = [rest[0], rest[1], rest[0]]
    first, second, sems = rest[2:5], rest[5:8], rest[8:]
    owned = (owned_a, owned_b, owned_c)
    jobs = [
        reduce_batch(
            grads[b], None, *(first, second, first)[b], owned[b], *sems[6 * b : 6 * b + 6],
            gates=((gate, None), None, (None, gate))[b],
        )
        for b in range(3)
    ]

    def step(n):
        if n < 5:
            aheads[n + 1].wait()
            left = a if n < 2 else low
            hidden[(n + 1) % 2] = product(left[...], ahead[(n + 1) % 2])
        cols = slice(n % 3 * BATCH, (n % 3 + 1) * BATCH)
        if n < 3:
            value, slope = gelu_pair(hidden[n % 2] + bias[0:1, cols])
            value = value.astype(BF)
            act[:, cols] = value
            back[:, cols] = slope.astype(BF)
        else:
            value = (hidden[n % 2] * back[:, cols].astype(F32)).astype(BF)
            back[:, cols] = value
            bias_sum[0:1, cols] = column_sum(value)
        behinds[n].wait()
        moved = contract_last(value, behind[n % 2])
        if n % 3 == 0:
            acc[...] = moved
        elif n % 3 == 1:
            acc[...] += moved
        else:
            part[...] = (acc[...] + moved).astype(BF)
        if n < 3:
            aheads[n + 3] = load_ahead(n + 3)
        if n < 4:
            behinds[n + 2] = load_behind(n + 2)

    def third_grads(n, b, half):
        cols = slice(n % 3 * BATCH, (n % 3 + 1) * BATCH)
        left, right = ((low, act), (a, back))[n // 3]
        weight_grad(left, right[:, cols], grads[b], half, 0)

    step(0)
    third_grads(0, 0, 0)
    step(1)
    third_grads(1, 0, 1)
    advance(jobs[0])
    step(2)
    down_copies = scatter_held(part, blocks.at[0], zs.at[0], zr.at[0])
    advance(jobs[0])
    third_grads(2, 1, 0)
    step(3)
    third_grads(3, 1, 1)
    advance(jobs[1])
    step(4)
    advance(jobs[1])
    advance(jobs[0])
    for copy in down_copies:
        copy.wait()
    branch = total_of(part[own_rows], blocks.at[0]) + vec[V_DOWN : V_DOWN + 1]
    result[...] = (after_two[...] + vec[5:6] * branch).astype(BF)
    sums[10:11] = column_sum(dy * branch)
    step(5)
    copies = scatter_held(part, blocks.at[1], zs.at[1], zr.at[1])
    drains = list(copies)
    send_result, wait_result = deliver(result, out_result, ds, dr, loc.at[3])
    finish(jobs[0])
    third_grads(4, 2, 0)
    third_grads(5, 2, 1)
    advance(jobs[2])
    advance(jobs[1])
    advance(jobs[2])
    for copy in copies:
        copy.wait_recv()
    total = total_of(part[own_rows], blocks.at[1])
    normed, inverse = plain_norm(after_two[...])
    sums[8:9] = column_sum(total)
    sums[9:10] = column_sum(total * normed)
    value = dy + norm_back(total * (1.0 + vec[4:5]), normed, inverse)
    grad_after[...] = value
    value = value.astype(BF)
    sums[1:2] = column_sum(value)
    copies = spread_block(low_two, value, gs, gr)
    drains += copies
    send_result()
    finish(jobs[1])
    advance(jobs[2])
    finish(jobs[2])
    for copy in copies:
        copy.wait_recv()
    store = pltpu.make_async_copy(low_two, low_out, loc.at[4])
    store.start()
    wait_result()
    store.wait()
    for copy in drains:
        copy.wait_send()


def mlp_pass(a, cot, up, down, after, vec, bias):
    dma = pltpu.SemaphoreType.DMA
    sds = jax.ShapeDtypeStruct
    wide = pltpu.VMEM((SEQ, D), BF)
    tiles = pltpu.VMEM((2, D, BATCH), BF)
    units = pltpu.VMEM((SEQ, FF), BF)
    owned = sds((2, PAIR, BATCH), BF)
    outs = [
        (sds((SEQ, D), BF), HB), (sds((TOK, D), F32), VM), (sds((16, D), F32), VM),
        (sds((8, FF), F32), VM), (sds((2, TOK, D), BF), HB), (owned, VM), (owned, VM), (owned, VM),
    ]
    return pl.pallas_call(
        mlp_kernel,
        out_shape=[shape for shape, _ in outs],
        in_specs=[HB] * 5 + [VM] * 2,
        out_specs=[spec for _, spec in outs],
        scratch_shapes=[
            wide, wide, tiles, tiles, pltpu.VMEM((2, SEQ, BATCH), F32), units, units,
            pltpu.VMEM((SEQ, D), F32), wide, pltpu.VMEM((TOK, D), F32), wide,
            pltpu.VMEM((2, 3, TOK, D), BF), pltpu.VMEM((TOK, D), BF), dma((2, 3)), dma((2, 3)),
            dma((3,)), dma((3,)), dma((2,)), dma((2,)), dma((5,)), dma((2, 2)),
            pltpu.SemaphoreType.REGULAR, pltpu.VMEM(GRADS, BF), pltpu.VMEM(GRADS, BF),
            *reduce_buffers(), *reduce_buffers(), *reduce_sems(), *reduce_sems(), *reduce_sems(),
        ],
        compiler_params=params(1),
        name="mlp",
    )(a, cot, up, down, after, vec, bias)


def vector_job(model, heads, time_out, model_out, head_out, *refs):
    col, mx, sends, recvs, *head_refs = refs
    x, y, z, core = here()
    zl = lax.rem(z, 2)
    rows, lines = peers_xy(x, y, z, core)
    sibling = chip(x, y, z, 1 - core)
    copies = []
    for k in (2, 1, 3):
        copies.append(remote(model, col.at[k], sends.at[0, k], recvs.at[0, k], chip(x, y, z + k, core)))
    if heads is not None:
        hsib, hx = head_refs
        copies.append(remote(heads, hsib, sends.at[0, 0], recvs.at[0, 0], sibling))
    for copy in copies:
        copy.start()
    yield
    for copy in copies:
        copy.wait()
    time_out[core] = model[...] + col[1] + col[2] + col[3]
    swap = remote(time_out.at[core], time_out.at[core], sends.at[1, 0], recvs.at[1, 0], sibling)
    swap.start()
    if heads is not None:
        hx[0] = heads[...] + hsib[...]
    yield
    swap.wait()
    mx[0] = time_out[0] + time_out[1]
    for stage, peers in enumerate((rows, lines)):
        copies = []
        for k in (1, 2, 3):
            copies.append(
                remote(mx.at[4 * stage], mx.at[4 * stage + k], sends.at[2 + 2 * stage, k],
                       recvs.at[2 + 2 * stage, k], peers[k - 1])
            )
            if heads is not None:
                copies.append(
                    remote(hx.at[4 * stage], hx.at[4 * stage + k], sends.at[3 + 2 * stage, k],
                           recvs.at[3 + 2 * stage, k], peers[k - 1])
                )
        for copy in copies:
            copy.start()
        yield
        for copy in copies:
            copy.wait()
        base = 4 * stage
        mx[base + 4] = mx[base] + mx[base + 1] + mx[base + 2] + mx[base + 3]
        if heads is not None:
            hx[base + 4] = hx[base] + hx[base + 1] + hx[base + 2] + hx[base + 3]
    model_out[...] = mx[8]
    if heads is not None:
        head_out[zl] = hx[8]
        last = remote(
            hx.at[8], head_out.at[zl], sends.at[6, 0], recvs.at[6, 0], chip(x, y, z + 1 - 2 * zl, core)
        )
        last.start()
        yield
        last.wait()


def vector_scratch(rows, heads):
    dma = pltpu.SemaphoreType.DMA
    refs = [pltpu.VMEM((4, rows, D), F32), pltpu.VMEM((9, rows, D), F32), dma((7, 4)), dma((7, 4))]
    if heads:
        refs += [pltpu.VMEM((16, HW), F32), pltpu.VMEM((9, 16, HW), F32)]
    return refs


def attend_clip_back(query, keys, values, grad, grad_query, grad_keys, grad_values):
    for h in range(HEADS):
        cols = head_slice(h)
        k, v = keys[:, cols], values[:, cols]
        for start in range(0, SEQ, 256):
            rows = slice(start, start + 256)
            q, do = query[rows, cols], grad[rows, cols]
            weights = softmax_rows(q, k)
            grad_weights = contract_last(do, v)
            delta = jnp.sum(weights * grad_weights, -1, keepdims=True)
            grad_scores = (weights * (grad_weights - delta)).astype(BF)
            grad_query[rows, cols] = product(grad_scores, k) * SCALE
            to_keys = contract_rows(grad_scores, q) * SCALE
            to_values = contract_rows(weights.astype(BF), do)
            if start:
                grad_keys[:, cols] += to_keys
                grad_values[:, cols] += to_values
            else:
                grad_keys[:, cols] = to_keys
                grad_values[:, cols] = to_values


def root_back(linear, inverse, scaled, dot):
    return (inverse * scaled - linear * (inverse * inverse * inverse * dot * (1.0 / D))).astype(BF)


def backward_kernel(
    wa_in, low_in, after_in, branch_in, query_lin_in, key_lin_in, query_two_lin_in, key_two_lin_in,
    query_rot_in, key_rot_in, value_low_in, query_two_in, key_two_in, value_two_in, mixed_in,
    mixed_two_in, words_in, three_in, one_in, tok_in, grad_in, tab_in, inv_in,
    vec, heads, sums, bias_sum, owned_a, owned_b, owned_c,
    out_tokens, out_words, time_out, model_out, head_out, sums_a, sums_b, mlp_a, mlp_b, mlp_c,
    wa, low_wide, after_one, branch_one, lin_a, lin_b, qa, ka, va, mixed, mixed_two, operand, tok_own,
    grad_after, tab, inv, grad_query, grad_kv, grad_qkv, part_cross, part_words, blocks,
    held, gq, gk, gv, model, head_sums, low_words, low_tokens,
    stat, stat_s, stat_r, zs, zr, gs, gr, ds, dr, loc, *rest,
):
    x, y, z, core = here()
    rows, lines = peers_xy(x, y, z, core)
    slots = iter(range(32))
    own_block = block_of(z)

    def fetch(src, dst):
        copy = pltpu.make_async_copy(src, dst, loc.at[next(slots)])
        copy.start()
        return copy

    out_cols, in_cols = pl.ds(6 * HW, 2 * HW), pl.ds(0, 6 * HW)
    first = [fetch(low_in, low_wide), fetch(wa_in.at[:, out_cols], wa.at[:, out_cols])]
    cross = [
        fetch(query_two_in, qa), fetch(key_two_in, ka), fetch(value_two_in, va),
        fetch(query_two_lin_in, lin_a), fetch(key_two_lin_in, lin_b), fetch(inv_in, inv),
    ]
    second = [
        fetch(mixed_two_in, mixed_two), fetch(wa_in.at[:, in_cols], wa.at[:, in_cols]),
        fetch(words_in.reshape(SEQ, D), operand),
    ]
    third = [
        fetch(after_in, after_one), fetch(branch_in, branch_one), fetch(grad_in, grad_after),
        fetch(mixed_in, mixed), fetch(tab_in, tab), fetch(tok_in.at[own_block], tok_own),
    ]
    greet(column(x, y, z, core) + rows + lines)
    model[...] = sums[...]
    head_sums[...] = jnp.zeros_like(head_sums)
    for i in range(6):
        head_sums[10 + i : 11 + i] = bias_sum[0:1, i * HW : (i + 1) * HW]
    refs_a, refs_b, early_refs, rest = rest[:14], rest[14:28], rest[28:32], rest[32:]
    vector_refs, (late, time_late, model_late), swap_refs = rest[:6], rest[6:9], rest[9:]
    hidden_rows = [
        swap_rows(src, dst, *swap_refs[3 * i : 3 * i + 3])
        for i, (src, dst) in enumerate(((owned_a, mlp_a), (owned_b, mlp_b), (owned_c, mlp_c)))
    ]
    for job in hidden_rows:
        advance(job)
    late[...] = jnp.zeros_like(late)
    grads_a, grads_b = refs_a[0], refs_b[0]
    job_a = reduce_batch(grads_a, sums_a, *refs_a[1:])
    job_b = reduce_batch(grads_b, sums_b, *refs_b[1:])
    stats = Stats(stat, stat_s, stat_r)
    drains = []

    for copy in first:
        copy.wait()
    held[...] = product(low_wide[...], wa[:, W_CROSS]).astype(BF)
    for copy in cross:
        copy.wait()
    attend_clip_back(qa, ka, va, held, gq, gk, gv)
    inverse_query, inverse_key, inverse_key_two, inverse_query_two = [inv[:, i : i + 1] for i in range(4)]
    dots = stats.start(
        0,
        [
            jnp.sum(lin_a[...] * (gq[...] * (1.0 + heads[8:9])), -1, keepdims=True),
            jnp.sum(lin_b[...] * (gk[...] * (1.0 + heads[9:10])), -1, keepdims=True),
        ],
    )
    head_sums[8:9] = column_sum(gq[...] * lin_a[...] * inverse_query_two)
    head_sums[9:10] = column_sum(gk[...] * lin_b[...] * inverse_key_two)
    low = gv[...].astype(BF)
    grad_kv[:, HW:] = low
    head_sums[7:8] = column_sum(low)
    for copy in second:
        copy.wait()
    weight_grad(low_wide, mixed_two[...], grads_a, 1, HW)
    dot_query, dot_key = dots()
    low = root_back(lin_a[...], inverse_query_two, gq[...] * (1.0 + heads[8:9]), dot_query)
    grad_query[...] = low
    head_sums[5:6] = column_sum(low)
    cross_copies = scatter_product(
        grad_query, wa[:, W_QUERY], part_cross, blocks.at[0], zs.at[0], zr.at[0]
    )
    low = root_back(lin_b[...], inverse_key_two, gk[...] * (1.0 + heads[9:10]), dot_key)
    grad_kv[:, :HW] = low
    head_sums[6:7] = column_sum(low)
    selfs = [
        fetch(query_rot_in, qa), fetch(key_rot_in, ka), fetch(value_low_in, va),
        fetch(query_lin_in, lin_a), fetch(key_lin_in, lin_b),
    ]
    weight_grad(operand, grad_kv[...], grads_a, 0, 0)
    next_operand = fetch(three_in, operand)
    next_operand.wait()
    weight_grad(operand, grad_query[...], grads_a, 1, 0)
    next_operand = fetch(one_in, operand)
    advance(job_a)
    part_words[...] = contract_last(grad_kv[...], wa[:, W_TEXT]).astype(BF)
    for copy in third:
        copy.wait()

    total = collect(part_cross, blocks.at[0], cross_copies)
    normed, inverse = plain_norm(after_one[...])
    model[4:5] = column_sum(total)
    model[3:4] = column_sum(total * normed)
    value = grad_after[...] + norm_back(total * (1.0 + vec[V_GAIN : V_GAIN + 1]), normed, inverse)
    grad_after[...] = value
    model[7:8] = column_sum(value * branch_one[...])
    low = (value * vec[2:3]).astype(BF)
    model[0:1] = column_sum(low)
    copies = spread_block(low_wide, low, gs, gr)
    drains += copies
    advance(job_a)
    for copy in copies:
        copy.wait_recv()
    early = vector_job(model, None, time_out, model_out, None, *early_refs)
    advance(early)
    word_copies = scatter_held(part_words, blocks.at[1], zs.at[1], zr.at[1], 0, TOK // 2)

    held[...] = product(low_wide[...], wa[:, W_SELF]).astype(BF)
    for copy in selfs:
        copy.wait()
    attend_clip_back(qa, ka, va, held, gq, gk, gv)
    cosine, sine = rope_pair(tab[...].reshape(SEQ, HEAD))
    for ref in (gq, gk):
        for h in range(HEADS):
            cols = head_slice(h)
            value = ref[:, cols]
            ref[:, cols] = value * cosine - swap_halves(value) * sine
    dots = stats.start(
        1,
        [
            jnp.sum(lin_a[...] * (gq[...] * (1.0 + heads[3:4])), -1, keepdims=True),
            jnp.sum(lin_b[...] * (gk[...] * (1.0 + heads[4:5])), -1, keepdims=True),
        ],
    )
    head_sums[3:4] = column_sum(gq[...] * lin_a[...] * inverse_query)
    head_sums[4:5] = column_sum(gk[...] * lin_b[...] * inverse_key)
    low = gv[...].astype(BF)
    grad_qkv[:, 2 * HW :] = low
    head_sums[2:3] = column_sum(low)
    next_operand.wait()
    weight_grad(low_wide, mixed[...], grads_b, 1, HW)
    for copy in cross_copies:
        copy.wait_send()
    advance(early, 2)
    dot_query, dot_key = dots()
    word_copies += scatter_held(part_words, blocks.at[1], zs.at[3], zr.at[3], TOK // 2, TOK // 2)
    drains += word_copies
    for i, (lin, inverse, ref, dot) in enumerate(
        ((lin_a, inverse_query, gq, dot_query), (lin_b, inverse_key, gk, dot_key))
    ):
        low = root_back(lin[...], inverse, ref[...] * (1.0 + heads[3 + i : 4 + i]), dot)
        grad_qkv[:, i * HW : (i + 1) * HW] = low
        head_sums[i : i + 1] = column_sum(low)
    copies = scatter_product(grad_qkv, wa[:, W_QKV], part_cross, blocks.at[0], zs.at[2], zr.at[2])
    drains += copies
    advance(job_a)
    weight_grad(operand, grad_qkv[:, : 2 * HW], grads_b, 0, 0)
    weight_grad(operand, grad_qkv[:, 2 * HW :], grads_b, 1, 0)
    advance(job_b)
    advance(early)
    advance(job_a)
    advance(job_b)
    finish(early)
    for job in hidden_rows:
        finish(job)
    low_words[...] = collect(part_words, blocks.at[1], word_copies).astype(BF)
    send_words, wait_words = deliver(low_words, out_words, ds.at[0], dr.at[0], loc.at[30])
    finish(job_a)

    total = collect(part_cross, blocks.at[0], copies)
    normed, inverse = plain_norm(tok_own[...].astype(F32))
    late[0:1] = column_sum(total)
    late[1:2] = column_sum(total * normed)
    vectors = vector_job(late, head_sums, time_late, model_late, head_out, *vector_refs)
    advance(vectors)
    value = grad_after[...] + norm_back(total * (1.0 + vec[1:2]), normed, inverse)
    low_tokens[...] = value.astype(BF)
    send_tokens, wait_tokens = deliver(low_tokens, out_tokens, ds.at[1], dr.at[1], loc.at[31])
    advance(vectors)
    send_tokens()
    send_words()
    advance(vectors)
    advance(job_b)
    advance(vectors)
    advance(job_b)
    advance(vectors)
    wait_tokens()
    advance(vectors)
    finish(job_b)
    finish(vectors)
    wait_words()
    time_out[0, 5:7] = time_late[0, 0:2]
    time_out[1, 5:7] = time_late[1, 0:2]
    model_out[5:7] = model_late[0:2]
    for copy in drains:
        copy.wait_send()


def backward(hbm, vmem):
    dma = pltpu.SemaphoreType.DMA
    sds = jax.ShapeDtypeStruct
    lin = pltpu.VMEM((SEQ, HW), F32)
    low = pltpu.VMEM((SEQ, HW), BF)
    wide = pltpu.VMEM((SEQ, D), BF)
    block = pltpu.VMEM((TOK, D), F32)
    low_block = pltpu.VMEM((TOK, D), BF)
    summed = sds((2, PAIR, BATCH), F32)
    outs = [
        (sds((2, TOK, D), BF), HB), (sds((2, TOK, D), BF), HB), (sds((2, 16, D), F32), VM),
        (sds((16, D), F32), VM), (sds((2, 16, HW), F32), VM), (summed, VM), (summed, VM),
        *[(sds((2, PAIR, BATCH), BF), VM)] * 3,
    ]
    batch = [pltpu.VMEM(GRADS, BF), *reduce_scratch()]
    return pl.pallas_call(
        backward_kernel,
        out_shape=[shape for shape, _ in outs],
        in_specs=[HB] * len(hbm) + [VM] * len(vmem),
        out_specs=[spec for _, spec in outs],
        scratch_shapes=[
            pltpu.VMEM((D, ATTN), BF), wide, block, block, lin, lin, low, low, low, low, low, wide,
            low_block, block, pltpu.VMEM((SIDE, TOK, HEAD), F32), pltpu.VMEM((SEQ, 128), F32),
            low, pltpu.VMEM((SEQ, 2 * HW), BF), pltpu.VMEM((SEQ, 3 * HW), BF), wide, wide,
            pltpu.VMEM((2, 3, TOK, D), BF), low, lin, lin, lin, pltpu.VMEM((16, D), F32),
            pltpu.VMEM((16, HW), F32), low_block, low_block,
            pltpu.VMEM((2, 4, 8, SEQ), F32),
            dma((2, 3)), dma((2, 3)), dma((4, 3)), dma((4, 3)), dma((3,)), dma((3,)), dma((2, 2)),
            dma((2, 2)), dma((32,)), *batch, *batch, *vector_scratch(16, False),
            *vector_scratch(8, True), pltpu.VMEM((8, D), F32), pltpu.VMEM((2, 8, D), F32), pltpu.VMEM((8, D), F32),
            *swap_sems(), *swap_sems(), *swap_sems(),
        ],
        compiler_params=params(2),
        name="backward",
    )(*hbm, *vmem)


def block_mask(size):
    row = lax.broadcasted_iota(jnp.int32, (size, size), 0)
    col = lax.broadcasted_iota(jnp.int32, (size, size), 1)
    return lax.div(row, ROWS) == lax.div(col, ROWS), row == col


def times(a, b):
    return jnp.dot(a, b, precision=HIGHEST, preferred_element_type=F32)


def gram_of(blocks):
    return lax.dot_general(
        blocks, blocks, (((1,), (1,)), ((), ())), precision=HIGHEST, preferred_element_type=F32
    )


def newton_factor(gram, size):
    same, eye = block_mask(size)
    gram = jnp.where(same, gram, 0.0)
    diagonal = jnp.where(eye, gram, 0.0)
    by_row = jnp.sum(diagonal, 1, keepdims=True)
    by_col = jnp.sum(diagonal, 0, keepdims=True)
    total_row = jnp.sum(jnp.where(same, by_col, 0.0), 1, keepdims=True)
    total_col = jnp.sum(jnp.where(same, by_row, 0.0), 0, keepdims=True)
    scale_row = 1.0 / (jnp.sqrt(total_row) + ORTHO_EPSILON)
    scale_col = 1.0 / (jnp.sqrt(total_col) + ORTHO_EPSILON)
    current = gram * scale_row * scale_col
    whole = None
    for turn in range(NS_STEPS):
        square = times(current, current)
        step = NEWTON_SECOND * current + NEWTON_THIRD * square + jnp.where(eye, NEWTON_FIRST, 0.0)
        whole = step if whole is None else times(step, whole)
        if turn + 1 < NS_STEPS:
            current = times(times(step, current), step)
    return whole * scale_col


WIDE = 2 * FF_REAL


def join_hidden(first, second):
    fill = jnp.zeros((first.shape[0], FF), F32)
    first = jnp.concatenate([first, fill], 1)
    second = pltpu.roll(jnp.concatenate([second, fill], 1), FF_REAL, 1)
    return (first + second)[:, :WIDE]


def gram_kernel(
    sum_a, sum_b, sum_c, attn_a, attn_b, in_m, out_m, mlp_m, narrow, wide, gram, mine, theirs, send, recv
):
    x, y, z, core = here()
    partner = chip(x, y, z + 2, core)
    greet([partner])

    def pair(ref, part, col):
        rows = slice(part * ROWS, (part + 1) * ROWS)
        return jnp.concatenate([ref[0, rows, col : col + HW], ref[1, rows, col : col + HW]], 1)

    n, w = 8 * ROWS, 2 * ROWS
    for j, (ref, part, col) in enumerate(
        ((attn_b, 0, 0), (attn_b, 0, HW), (attn_b, 1, 0), (attn_a, 1, 0), (attn_a, 0, 0), (attn_a, 0, HW))
    ):
        narrow[j * ROWS : (j + 1) * ROWS] = MOMENTUM * in_m[j] + pair(ref, part, col)
    for j, ref in enumerate((attn_b, attn_a)):
        narrow[(6 + j) * ROWS : (7 + j) * ROWS] = MOMENTUM * out_m[:, j, :] + pair(ref, 1, HW)
    mine[:n, :n] = gram_of(narrow[...])
    top, bottom = slice(0, ROWS), slice(ROWS, 2 * ROWS)
    for j, thirds in enumerate(
        (((sum_b, bottom), (sum_c, top), (sum_c, bottom)), ((sum_a, top), (sum_a, bottom), (sum_b, top)))
    ):
        chips = [jnp.concatenate([ref[i].astype(F32)[rows] for ref, rows in thirds], 1) for i in (0, 1)]
        wide[j * ROWS : (j + 1) * ROWS] = MOMENTUM * mlp_m[:, j, :] + join_hidden(*chips)
    mine[n:, n:] = gram_of(wide[...])
    mine[:n, n:] = jnp.zeros((n, w), F32)
    mine[n:, :n] = jnp.zeros((w, n), F32)
    copy = remote(mine, theirs, send.at[0], recv.at[0], partner)
    copy.start()
    copy.wait()
    gram[...] = mine[...] + theirs[...]


def gram_step(args, cid):
    sds = jax.ShapeDtypeStruct
    dma = pltpu.SemaphoreType.DMA
    size = 10 * ROWS
    return pl.pallas_call(
        gram_kernel,
        out_shape=[
            sds((8 * ROWS, 2 * HW), F32), sds((2 * ROWS, WIDE), F32), sds((size, size), F32),
        ],
        in_specs=[VM] * len(args),
        out_specs=[VM] * 3,
        scratch_shapes=[
            pltpu.VMEM((size, size), F32), pltpu.VMEM((size, size), F32), dma((1,)), dma((1,)),
        ],
        compiler_params=params(cid),
        name="gram",
    )(*args)


def finish_kernel(
    narrow, wide, gram, in_w, out_w, mlp_w, head_w, head_m, model_w, model_m, up_w, up_m, head_sum,
    model_sum, result, tokens, words, time_sum,
    new_in, new_out, new_mlp, new_in_m, new_out_m, new_mlp_m, new_head, new_model, new_up,
    new_head_m, new_model_m, new_up_m, out_result, out_tokens, out_words, out_time,
    block, stores,
):
    out_result[...] = result[...]
    copies = []
    for i, (src, dst) in enumerate(((tokens, out_tokens), (words, out_words))):
        for clip in (0, 1):
            block[2 * i + clip] = src[clip].astype(F32)
            copies.append(
                pltpu.make_async_copy(block.at[2 * i + clip], dst.at[clip], stores.at[2 * i + clip])
            )
            copies[-1].start()
    out_time[...] = time_sum[:, 5:11]
    value = MOMENTUM * head_m[...] + jnp.concatenate([head_sum[0, :10], head_sum[1, :10]], 1)
    new_head_m[...] = value
    new_head[...] = head_w[...] - RATE_VECTOR * value
    value = MOMENTUM * model_m[...] + model_sum[:11]
    new_model_m[...] = value
    new_model[...] = model_w[...] - RATE_VECTOR * value
    chips = [jnp.concatenate([head_sum[i, 10 + k : 11 + k] for k in range(6)], 1) for i in (0, 1)]
    value = MOMENTUM * up_m[...] + join_hidden(*chips)
    new_up_m[...] = value
    new_up[...] = up_w[...] - RATE_VECTOR * value
    n, w = narrow.shape[0], wide.shape[0]
    factor = newton_factor(gram[...], n + w)
    turned = times(factor[:n, :n], narrow[...])
    for j in range(6):
        rows = slice(j * ROWS, (j + 1) * ROWS)
        new_in_m[j] = narrow[rows]
        new_in[j] = in_w[j] * (1.0 - RATE_IN * DECAY) - RATE_IN * turned[rows]
    for j in range(2):
        rows = slice((6 + j) * ROWS, (7 + j) * ROWS)
        new_out_m[:, j, :] = narrow[rows]
        new_out[:, j, :] = out_w[:, j, :] * (1.0 - RATE_OUT * DECAY) - RATE_OUT * turned[rows]
    turned = times(factor[n:, n:], wide[...])
    for j in range(2):
        rows = slice(j * ROWS, (j + 1) * ROWS)
        new_mlp_m[:, j, :] = wide[rows]
        new_mlp[:, j, :] = mlp_w[:, j, :] * (1.0 - RATE_MLP * DECAY) - RATE_MLP * turned[rows]
    for copy in copies:
        copy.wait()


def finish_step(args):
    sds = jax.ShapeDtypeStruct
    matrices = [sds((6, ROWS, 2 * HW), F32), sds((ROWS, 2, 2 * HW), F32), sds((ROWS, 2, WIDE), F32)]
    vectors = [sds((10, 2 * HW), F32), sds((11, D), F32), sds((1, WIDE), F32)]
    blocks = [sds((2, TOK, D), BF), sds((2, TOK, D), F32), sds((2, TOK, D), F32)]
    return pl.pallas_call(
        finish_kernel,
        out_shape=matrices + matrices + vectors + vectors + blocks + [sds((2, 6, D), F32)],
        in_specs=[VM] * len(args),
        out_specs=[VM] * 13 + [HB] * 2 + [VM],
        scratch_shapes=[pltpu.VMEM((4, TOK, D), F32), pltpu.SemaphoreType.DMA((4,))],
        compiler_params=pltpu.CompilerParams(vmem_limit_bytes=VMEM_LIMIT),
        name="finish",
    )(*args)


def rope_tables(places):
    pair_index = jnp.arange(HEAD // 2, dtype=jnp.int32)
    side_pairs = HEAD // 6
    frame_pairs = (HEAD - 4 * side_pairs) // 2
    part_of = (pair_index >= frame_pairs).astype(jnp.int32) + (
        pair_index >= frame_pairs + side_pairs
    ).astype(jnp.int32)
    offset = jnp.where(
        part_of == 0, 0, jnp.where(part_of == 1, frame_pairs, frame_pairs + side_pairs)
    ).astype(jnp.int32)
    extent = jnp.where(part_of == 0, 2 * frame_pairs, 2 * side_pairs).astype(jnp.float32)
    frequency = jnp.exp(
        (pair_index - offset).astype(jnp.float32) * (-2.0 * math.log(10000.0)) / extent
    )
    chosen = (
        places[0][:, None] * (part_of == 0)
        + places[1][:, None] * (part_of == 1)
        + places[2][:, None] * (part_of == 2)
    )
    angles = chosen.astype(jnp.float32) * frequency
    return (jnp.cos(angles), jnp.sin(angles))


def plain_norm(values):
    centred = values - jnp.mean(values, -1, keepdims=True)
    inverse = lax.rsqrt(jnp.mean(centred * centred, -1, keepdims=True) + NORM_EPSILON)
    return (centred * inverse, inverse)


def norm_back(grads, normed, inverse):
    return inverse * (
        grads
        - jnp.mean(grads, -1, keepdims=True)
        - normed * jnp.mean(grads * normed, -1, keepdims=True)
    )


def product(left, right):
    return jnp.dot(left, right, preferred_element_type=F32)


def contract_last(left, right):
    return lax.dot_general(left, right, (((1,), (1,)), ((), ())), preferred_element_type=F32)


def contract_rows(left, right):
    return lax.dot_general(left, right, (((0,), (0,)), ((), ())), preferred_element_type=F32)


def body(
    tokens, text, time_embedding, positions, cotangent, attn_in, attn_out, mlp, head_vectors,
    model_vectors, up_bias, attn_in_moment, attn_out_moment, mlp_moment, head_moment, model_moment,
    up_moment,
):
    x, y, z, core = here()
    zl = lax.rem(z, 2)

    low_in = attn_in.astype(BF).reshape(ROWS, 6, 2, HW).transpose(2, 0, 1, 3).reshape(2, ROWS, -1)
    low_out = attn_out.astype(BF).reshape(ROWS, 2, 2, HW).transpose(2, 0, 1, 3).reshape(2, ROWS, -1)
    send_attn = jnp.concatenate([low_in, low_out], -1).reshape(2, ROWS, 2, ATTN // 2)
    send_attn = send_attn.transpose(0, 2, 1, 3).reshape(2, PAIR, ATTN // 2)
    send_mlp = jnp.pad(
        mlp.astype(BF).reshape(ROWS, 2, 2, FF_REAL).transpose(2, 1, 0, 3),
        ((0, 0), (0, 0), (0, 0), (0, FF - FF_REAL)),
    ).reshape(2, PAIR, FF)
    cosine, sine = rope_tables(positions.reshape(3, 2 * TOK))
    table = jnp.concatenate([cosine, sine], -1).reshape(2, TOK, HEAD)

    heads = jnp.pad(lax.dynamic_slice(head_vectors, (0, zl * HW), (10, HW)), ((0, 6), (0, 0)))
    bias_up = jnp.pad(lax.dynamic_slice(up_bias, (zl * FF_REAL,), (FF_REAL,)), (0, FF - FF_REAL))
    modulation = model_vectors[5:] + lax.dynamic_index_in_dim(time_embedding, core, 0, False)
    shift_one, scale_one, gate_one, shift_two, scale_two, gate_two = [modulation[i] for i in range(6)]
    vectors = jnp.pad(jnp.concatenate([modulation, model_vectors[:5]], 0), ((0, 5), (0, 0)))

    (
        w_attn, w_up, w_down, cot_all, tab_all, input_one, input_three, input_mlp, query_lin, key_lin,
        query_two_lin, key_two_lin, inv, query_rot, key_rot, value_low, query_two, key_two, value_two,
        mixed_low, mixed_two_low, branch_one, after_one, after_two, tok_all, txt_all,
    ) = forward(
        send_attn, send_mlp, tokens, text, cotangent, table, heads, vectors,
    )
    low_two, grad_after, sums, up_sum, out_result, *owned = mlp_pass(
        input_mlp, cot_all, w_up, w_down, after_two, vectors, bias_up[None]
    )
    out_tokens, out_words, time_sums, model_sums, head_totals, sums_a, sums_b, *mlp_sums = backward(
        [
            w_attn, low_two, after_one, branch_one, query_lin, key_lin, query_two_lin, key_two_lin,
            query_rot, key_rot, value_low, query_two, key_two, value_two, mixed_low, mixed_two_low,
            txt_all, input_three, input_one, tok_all, grad_after, tab_all, inv,
        ],
        [vectors, heads, sums, up_sum, *owned],
    )
    swap = lambda v: v.transpose(1, 0, 2)
    narrow, wide, gram = gram_step(
        [*mlp_sums, sums_a, sums_b, swap(attn_in_moment), attn_out_moment, mlp_moment], 3
    )
    (
        new_in, new_out, new_mlp, new_in_m, new_out_m, new_mlp_m, new_head, new_model, new_up,
        new_head_m, new_model_m, new_up_m, out_result, out_tokens, out_words, out_time,
    ) = finish_step(
        [
            narrow, wide, gram, swap(attn_in), attn_out, mlp, head_vectors, head_moment, model_vectors,
            model_moment, up_bias[None], up_moment[None], head_totals, model_sums, out_result,
            out_tokens, out_words, time_sums,
        ]
    )
    return (
        out_result, out_tokens, out_words, out_time, swap(new_in), new_out, new_mlp,
        swap(new_in_m), new_out_m, new_mlp_m, new_head, new_model, new_up.reshape(-1), new_head_m,
        new_model_m, new_up_m.reshape(-1),
    )


def solution(mesh):
    clip = P("fsdp", "ctx", None)
    whole = P("fsdp", None, None)
    matrix = P(("fsdp", "ctx"), None, "tp")
    in_specs = (
        clip, clip, whole, P(None, "fsdp", "ctx"), clip, matrix, matrix, matrix, P(None, "tp"), P(),
        P("tp"), matrix, matrix, matrix, P(None, "tp"), P(), P("tp"),
    )
    out_specs = (
        clip, clip, clip, whole, matrix, matrix, matrix, matrix, matrix, matrix, P(None, "tp"), P(),
        P("tp"), P(None, "tp"), P(), P("tp"),
    )
    return jax.shard_map(body, mesh=mesh, in_specs=in_specs, out_specs=out_specs, check_vma=False)
```

time: 493 us -> 417 us (0.85)
  Pallas kernels: 431 us -> 396 us
  local copies, waits for them, and re-layouts: 25.5 us -> 9.34 us
  matrix products: 15.9 us -> 0 us
  other arithmetic: 13.9 us -> 6.06 us
    pallas_call x5, Pallas kernels: 431 us -> 396 us  [the longest x1 145 us: forward(): pl.pallas_call(forward_kernel, out_shape=weights + outs, in_specs=[VM, VM...]
    dot_general x5 -> x0, matrix products: 15.9 us -> none  [contract_rows(): lax.dot_general(left, right, (((0,), (0,)), ((), ())), preferred_element_...]
    sub x6 -> x0, other arithmetic: 7.36 us -> none  [the longest x1 2.89 us: body(): new_mlp = mlp * (1.0 - RATE_MLP * DECAY) - RATE_MLP * swap(wide_dir)]
where the time goes in v4:
time: 417 us; the launch traced here: 413 us
  Pallas kernels  396 us (95%)
  local copies, waits for them, and re-layouts  9.34 us (2%)
  other arithmetic  6.06 us (1%)
    pallas_call x1, Pallas kernels, forward(): pl.pallas_call(forward_kernel, out_shape=weights + outs, in_specs=[VM, VM...  145 us
    pallas_call x1, Pallas kernels, backward(): pl.pallas_call(backward_kernel, out_shape=[shape for shape, _ in outs], i...  127 us
    pallas_call x1, Pallas kernels, mlp_pass(): pl.pallas_call(mlp_kernel, out_shape=[shape for shape, _ in outs], in_spe...  96.9 us
    pallas_call x1, Pallas kernels, finish_step(): pl.pallas_call(finish_kernel, out_shape=matrices + matrices + vectors + v...  15 us
    pallas_call x1, Pallas kernels, gram_step(): pl.pallas_call(gram_kernel, out_shape=[sds((8 * ROWS, 2 * HW), F32), sds(...  12.6 us

profile of v4, /device:TPU:1, one launch (start us, length us, event | category | flops | bytes accessed | tf_op | source)
XLA Modules:
  0.0 413.1 jit_solution(15498000911086815132)
XLA Ops:
  0.7 0.8 constant_dynamic-slice_fusion.1
  1.5 0.6 pad.17.heads
  2.1 0.9 fusion.2
  3.1 0.8 slice.22
  3.9 0.7 select_maximum_fusion.vec
  4.6 0.7 slice_bitcast_fusion.2
  5.3 0.6 fusion.1
  5.9 0.8 pad_maximum_fusion.1.tab
  6.8 0.3 reshape.178
  7.5 0.7 copy.37
  8.3 0.3 convert_element_type.103
  8.6 0.5 reshape.183
  9.1 0.8 pad.16
  9.9 144.6 %forward.1 = (bf16[1536,3072]{1,0:T(8,128)(2,1)}, bf16[1536,2304]{1,0:T(8,128)(2,1)}, bf16[1536,2304]{1,0:T(8,128)(2,1)}, bf16[4,128,1536]{2,1,0:T(8,128)(2,1)},...) custom-call(bf16[2,48,1536]{2,1,0:T(8,128)(2,1)} %bitcast.35, ...), custom_call_target="tpu_custom_call" | custom-call | tf_op jit(solution)/shard_map/forward/pallas_call | solution.py:589
  154.7 0.6 broadcast_in_dim.27.bias
  155.3 96.9 %mlp.1 = (bf16[512,1536]{1,0:T(8,128)(2,1)}, f32[128,1536]{1,0:T(8,128)}, f32[16,1536]{1,0:T(8,128)}, f32[8,2304]{1,0:T(8,128)}, bf16[2,128,1536]{2,1,0:T(8,128)...) custom-call(bf16[512,1536]{1,0:T(8,128)(2,1)} %get-tuple-element.80.a_in, ...), custom_call_target="tpu_custom_call" | custom-call | tf_op jit(solution)/shard_map/mlp/pallas_call | solution.py:1005
  252.2 127.2 %backward.1 = (bf16[2,128,1536]{2,1,0:T(8,128)(2,1)}, bf16[2,128,1536]{2,1,0:T(8,128)(2,1)}, f32[2,16,1536]{2,1,0:T(8,128)}, f32[16,1536]{1,0:T(8,128)}, f32[2,1...) custom-call(bf16[1536,3072]{1,0:T(8,128)(2,1)} %get-tuple-element.79, ...), custom_call_target="tpu_custom_call" | custom-call | tf_op jit(solution)/shard_map/backward/pallas_call | solution.py:1329
  379.5 12.6 %gram.1 = (f32[192,768]{1,0:T(8,128)}, f32[48,4480]{1,0:T(8,128)}, f32[240,240]{1,0:T(8,128)}) custom-call(bf16[2,48,768]{2,1,0:T(8,128)(2,1)} %get-tuple-element.112.sum_a, bf16[2,48,768]{2,1,0:T(8,128)(2,1)} %get-tuple-element.113.sum_b, bf16[2,48,768]{2,1,0:T(8,128)(2,1)} %get-tuple-element.114.sum_c, f32[2,48,768]{2,1,0:T(8,128)} %get-tuple-element.115.attn_a, ...), custom_call_target="tpu_custom_call" | custom-call | tf_op jit(solution)/shard_map/gram/pallas_call | solution.py:1436
  392.1 0.6 broadcast_in_dim.28.up_w
  392.7 0.6 broadcast_in_dim.29.up_m
  393.3 15.0 %finish.1 = (f32[6,24,768]{2,1,0:T(8,128)}, f32[24,2,768]{2,1,0:T(2,128)}, f32[24,2,4480]{2,1,0:T(2,128)}, f32[6,24,768]{2,1,0:T(8,128)}, f32[24,2,768]{2,1,0:T(...) custom-call(f32[192,768]{1,0:T(8,128)} %get-tuple-element.117.narrow, ...), custom_call_target="tpu_custom_call" | custom-call | tf_op jit(solution)/shard_map/finish/pallas_call | solution.py:1503
  408.4 1.6 copy.40
  410.0 1.4 reduce
  411.3 1.4 reduce.1
  (29 shorter events, 0.8 us)
Async XLA Ops:
  0.6 1.5 copy-start
  0.7 6.0 %copy-start.3 = (f32[24,6,768]{2,0,1:T(8,128)S(1)}, f32[24,6,768]{2,0,1:T(8,128)}, u32[]{:S(2)}) copy-start(f32[24,6,768]{2,0,1:T(8,128)} %param.22) | copy-start | bytes 1327108
  3.1 4.0 copy-start.4
  6.7 1.5 copy-start.2
  9.9 144.6 %copy-start.5 = (f32[4480]{0:T(1024)S(1)}, f32[4480]{0:T(1024)}, u32[]{:S(2)}) copy-start(f32[4480]{0:T(1024)} %param.27) | copy-start | bytes 53764
  379.5 13.2 %copy-start.6 = (f32[4480]{0:T(1024)S(1)}, f32[4480]{0:T(1024)}, u32[]{:S(2)}) copy-start(f32[4480]{0:T(1024)} %param.33) | copy-start | bytes 53764
  393.3 19.4 %copy-start.1 = (f32[2,6,1536]{2,0,1:T(2,128)S(1)}, f32[2,6,1536]{2,0,1:T(2,128)}, u32[]{:S(2)}) copy-start(f32[2,6,1536]{2,0,1:T(2,128)} %param.19) | copy-start | bytes 221188

commit v5 on v4

--- a/solution.py
+++ b/solution.py
@@ -350,41 +350,107 @@
     return pl.ds(pl.multiple_of(index * TOK, TOK), TOK)
 
 
-def scatter_product(left, right, part, got, send, recv):
-    x, y, z, core = here()
-    copies = []
-    for k in (2, 1, 3, 0):
-        rows = block_slice(block_of(z + k))
-        part[rows] = contract_last(left[rows], right).astype(BF)
-        if k:
-            copies.append(
-                remote(part.at[rows], got.at[k - 1], send.at[k - 1], recv.at[k - 1], chip(x, y, z + k, core))
-            )
-            copies[-1].start()
-    return copies
-
-
-def collect(part, got, copies):
-    z = here()[2]
-    for copy in copies:
-        copy.wait_recv()
-    total = part[block_slice(block_of(z))].astype(F32)
-    for k in range(3):
-        total = total + got[k].astype(F32)
-    return total
-
-
-def spread_block(out, value, send, recv):
-    x, y, z, core = here()
-    rows = block_slice(block_of(z))
-    out[rows] = value
-    copies = []
-    for k in (2, 1, 3):
-        copies.append(
-            remote(out.at[rows], out.at[rows], send.at[k - 1], recv.at[k - 1], chip(x, y, z + k, core))
-        )
-        copies[-1].start()
-    return copies
+HALF = TOK // 2
+
+
+def half_rows(block, half):
+    return pl.ds(pl.multiple_of(block * TOK + half * HALF, HALF), HALF)
+
+
+class Scatter:
+    def __init__(self, part, got, send, recv):
+        self.part, self.got, self.send, self.recv = part, got, send, recv
+        self.x, self.y, self.z, self.core = here()
+        self.copies, self.relayed = [], False
+
+    def push(self, slot, rows, dst, step):
+        device = chip(self.x, self.y, self.z + step, self.core)
+        copy = remote(self.part.at[rows], dst, self.send.at[slot], self.recv.at[slot], device)
+        copy.start()
+        self.copies.append(copy)
+
+    def stage(self, k):
+        front, rear = pl.ds(0, HALF), pl.ds(HALF, HALF)
+        block = block_of(self.z + k)
+        if k == 2:
+            self.push(0, half_rows(block, 0), self.got.at[2, front], 1)
+            self.push(1, half_rows(block, 1), self.got.at[2, rear], -1)
+        elif k == 1:
+            self.push(2, half_rows(block, 1), self.got.at[0, rear], 1)
+        elif k == 3:
+            self.push(3, half_rows(block, 0), self.got.at[1, front], -1)
+
+    def held(self):
+        for k in (2, 1, 3):
+            self.stage(k)
+        return self
+
+    def product(self, left, right):
+        for k in (2, 1, 3, 0):
+            rows = block_slice(block_of(self.z + k))
+            self.part[rows] = contract_last(left[rows], right).astype(BF)
+            self.stage(k)
+        return self
+
+    def relay(self):
+        if self.relayed:
+            return
+        self.relayed = True
+        for slot, step in ((0, 1), (1, -1)):
+            span = pl.ds(slot * HALF, HALF)
+            rows = half_rows(block_of(self.z + step), slot)
+            self.copies[slot].wait_recv()
+            total = self.part[rows].astype(F32) + self.got[2, span].astype(F32)
+            self.part[rows] = total.astype(BF)
+            self.push(4 + slot, rows, self.got.at[slot, span], step)
+
+    def total(self):
+        self.relay()
+        for copy in self.copies[2:]:
+            copy.wait_recv()
+        own = self.part[block_slice(block_of(self.z))].astype(F32)
+        return own + (self.got[0].astype(F32) + self.got[1].astype(F32))
+
+    def drain(self):
+        for copy in self.copies:
+            copy.wait_send()
+
+
+class Spread:
+    def __init__(self, out, value, send, recv):
+        self.out, self.send, self.recv = out, send, recv
+        self.x, self.y, self.z, self.core = here()
+        self.copies, self.relayed = [], False
+        block = block_of(self.z)
+        out[block_slice(block)] = value
+        self.push(0, half_rows(block, 0), 1)
+        self.push(1, half_rows(block, 1), -1)
+        self.push(2, half_rows(block, 1), 1)
+        self.push(3, half_rows(block, 0), -1)
+
+    def push(self, slot, rows, step):
+        device = chip(self.x, self.y, self.z + step, self.core)
+        rows = self.out.at[rows]
+        copy = remote(rows, rows, self.send.at[slot], self.recv.at[slot], device)
+        copy.start()
+        self.copies.append(copy)
+
+    def relay(self):
+        if self.relayed:
+            return
+        self.relayed = True
+        for slot, step in ((0, 1), (1, -1)):
+            self.copies[slot].wait_recv()
+            self.push(4 + slot, half_rows(block_of(self.z - step), slot), step)
+
+    def wait(self):
+        self.relay()
+        for copy in self.copies[2:]:
+            copy.wait_recv()
+
+    def drain(self):
+        for copy in self.copies:
+            copy.wait_send()
 
 
 def inverse_root(total):
@@ -520,27 +586,30 @@
             out[:, cols] = (value * cosine + swap_halves(value) * sine).astype(BF)
     advance(gather_mlp, 2)
     attend_clip(query_rot, key_rot, value_low, mixed)
-    copies = scatter_product(mixed, wa[:, W_SELF], part_one, blocks.at[0], zs.at[0], zr.at[0])
-    drains = list(copies)
+    scatter = Scatter(part_one, blocks.at[0], zs.at[0], zr.at[0]).product(mixed, wa[:, W_SELF])
+    drains = [scatter]
     key_two[...] = (key_two_lin[...] * inverse_key_two * (1.0 + heads[9:10])).astype(BF)
     save(query_rot, key_rot, key_two, mixed)
-    advance(gather_mlp, 8)
-    branch = collect(part_one, blocks.at[0], copies) + vec[V_SELF : V_SELF + 1]
+    advance(gather_mlp, 2)
+    scatter.relay()
+    advance(gather_mlp, 5)
+    branch = scatter.total() + vec[V_SELF : V_SELF + 1]
     branch_one[...] = branch
     after = tok_all[block_of(z)].astype(F32) + vec[2:3] * branch
     after_one[...] = after
     normed, _ = plain_norm(after)
-    copies = spread_block(
+    spread = Spread(
         input_three,
         (normed * (1.0 + vec[V_GAIN : V_GAIN + 1]) + vec[V_BIAS : V_BIAS + 1]).astype(BF),
         gs.at[0],
         gr.at[0],
     )
-    drains += copies
+    drains.append(spread)
     save(branch_one, after_one)
+    advance(gather_mlp, 2)
+    spread.relay()
     finish(gather_mlp)
-    for copy in copies:
-        copy.wait_recv()
+    spread.wait()
     query_two_lin[...] = product(input_three[...], wa[:, W_QUERY]) + heads[5:6]
     norm_wait = stats.start(1, [jnp.sum(query_two_lin[...] * query_two_lin[...], -1, keepdims=True)])
     save(input_three, query_two_lin)
@@ -548,17 +617,18 @@
     inv[...] = jnp.where(lane == 3, inverse_query_two, inv[...])
     query_two[...] = (query_two_lin[...] * inverse_query_two * (1.0 + heads[8:9])).astype(BF)
     attend_clip(query_two, key_two, value_two, mixed_two)
-    copies = scatter_product(mixed_two, wa[:, W_CROSS], part_two, blocks.at[1], zs.at[1], zr.at[1])
-    drains += copies
+    scatter = Scatter(part_two, blocks.at[1], zs.at[1], zr.at[1]).product(mixed_two, wa[:, W_CROSS])
+    drains.append(scatter)
     save(inv, query_two, mixed_two)
-    after = after_one[...] + collect(part_two, blocks.at[1], copies) + vec[V_CROSS : V_CROSS + 1]
+    after = after_one[...] + scatter.total() + vec[V_CROSS : V_CROSS + 1]
     after_two[...] = after
     normed, _ = plain_norm(after)
-    copies = spread_block(
+    spread = Spread(
         input_mlp, (normed * (1.0 + vec[4:5]) + vec[3:4]).astype(BF), gs.at[1], gr.at[1]
     )
-    drains += copies
+    drains.append(spread)
     save(after_two)
+    spread.relay()
     for copy in locals_:
         copy.wait()
     acts[3][1]()
@@ -566,11 +636,10 @@
         act[2]()
     attn_drain()
     mlp_drain()
-    for copy in copies:
-        copy.wait_recv()
+    spread.wait()
     save(input_mlp)
-    for copy in drains:
-        copy.wait_send()
+    for transfer in drains:
+        transfer.drain()
     for copy in stores:
         copy.wait()
 
@@ -605,7 +674,7 @@
             *[dma(s) for s in GATHER_SEMS],
             *[dma(s) for s in GATHER_SEMS],
             dma((2, 2)), dma((2, 2)), dma((4, 3)), dma((4, 3)), dma((8, 2)),
-            dma((2, 3)), dma((2, 3)), dma((2, 3)), dma((2, 3)), dma((2, 3)), dma((2, 3)),
+            dma((2, 3)), dma((2, 3)), dma((2, 6)), dma((2, 6)), dma((2, 6)), dma((2, 6)),
             dma((SAVED,)),
         ],
         compiler_params=params(0),
@@ -629,9 +698,14 @@
     sibling = chip(x, y, z, 1 - core)
     wrap = lambda v: lax.rem(v, SIDE)
     swaps, one, two = [], {0: [], 1: []}, {0: [], 1: []}
-    free = gates if gates is not None else (None, None)
-    if free[1] is not None:
-        pl.semaphore_wait(free[1], 7)
+    opens, waits = gates if gates is not None else (None, None)
+
+    def signal(gate, devices):
+        for device in devices:
+            pl.semaphore_signal(gate, inc=1, device_id=device, device_id_type=MESH)
+
+    if waits is not None:
+        pl.semaphore_wait(waits[0], 1)
     for part in (0, 1):
         swaps.append(
             remote(grads.at[part, :, :, 1 - core], sib.at[part], ss.at[part], sr.at[part], sibling)
@@ -647,12 +721,16 @@
             return carry
 
         lax.fori_loop(0, SIDE * SIDE, add_pair, 0)
+        if part == 0 and waits is not None:
+            pl.semaphore_wait(waits[1], 6)
         for k in (2, 1, 3):
             src = grads.at[0, :, wrap(y + k), core] if part == 0 else grads.at[1, wrap(x + k), :, core]
             device = (lines, rows)[part][k - 1]
             copy = remote(src, r1.at[part, k - 1], s1.at[part, k - 1], q1.at[part, k - 1], device)
             copy.start()
             one[part].append(copy)
+    if opens is not None:
+        signal(opens[0], [sibling])
     yield
     for part in (0, 1):
         for copy in one[part]:
@@ -682,9 +760,8 @@
         for i in range(3):
             total = total + r2[part, i].astype(F32)
         final.append(total)
-    if free[0] is not None:
-        for device in [*rows, *lines, sibling]:
-            pl.semaphore_signal(free[0], inc=1, device_id=device, device_id_type=MESH)
+    if opens is not None:
+        signal(opens[1], [*rows, *lines])
     for target in (0, 1):
         span = slice(target * ROWS, target * ROWS + ROWS)
         tosend[target] = jnp.concatenate([final[0][span], final[1][span]], 0).astype(tosend.dtype)
@@ -778,19 +855,6 @@
     return jnp.sum(values.astype(F32), 0, keepdims=True)
 
 
-def scatter_held(part, got, send, recv, first=0, count=TOK):
-    x, y, z, core = here()
-    copies = []
-    for k in (2, 1, 3):
-        rows = pl.ds(pl.multiple_of(block_of(z + k) * TOK + first, count), count)
-        copies.append(
-            remote(part.at[rows], got.at[k - 1, pl.ds(first, count)], send.at[k - 1], recv.at[k - 1],
-                   chip(x, y, z + k, core))
-        )
-        copies[-1].start()
-    return copies
-
-
 def deliver(src, dst, s, r, l):
     x, y, z, core = here()
     zh = lax.div(z, 2)
@@ -840,18 +904,11 @@
     return u * half, half + 0.5 * u * (1.0 - t * t) * (ROOT * (1.0 + 3.0 * CUBE * square))
 
 
-def total_of(mine, blocks):
-    total = mine.astype(F32)
-    for k in range(3):
-        total = total + blocks[k].astype(F32)
-    return total
-
-
 def mlp_kernel(
     a_in, cot_all, w_up, w_down, after_in, vec, bias,
     low_out, grad_after, sums, bias_sum, out_result, owned_a, owned_b, owned_c,
-    a, low, ahead, behind, hidden, act, back, acc, part, after_two, low_two,
-    blocks, result, zs, zr, gs, gr, ds, dr, loc, ring, gate, *rest,
+    a, low, ahead, behind, hidden, act, back, acc, part, after_two, low_two, result,
+    blocks, zs, zr, gs, gr, ds, dr, loc, ring, gate_core, gate_chips, *rest,
 ):
     x, y, z, core = here()
     rows, lines = peers_xy(x, y, z, core)
@@ -865,8 +922,11 @@
     def third(n):
         return pl.ds(n % 3 * BATCH, BATCH)
 
+    def weights(n):
+        return ahead.at[n % 2].reshape(D, BATCH)
+
     def load_ahead(n):
-        return load((w_up, w_down)[n // 3].at[:, third(n)], ahead.at[n % 2], ring.at[0, n % 2])
+        return load((w_up, w_down)[n // 3].at[:, third(n)], weights(n), ring.at[0, n % 2])
 
     def load_behind(n):
         return load((w_down, w_up)[n // 3].at[:, third(n)], behind.at[n % 2], ring.at[1, n % 2])
@@ -881,7 +941,7 @@
     sums[...] = jnp.zeros_like(sums)
     fetch_a.wait()
     aheads[0].wait()
-    hidden[0] = product(a[...], ahead[0])
+    hidden[0] = product(a[...], weights(0)[...])
     aheads[2] = load_ahead(2)
     fetch_low.wait()
     dy = low[own_rows].astype(F32)
@@ -891,13 +951,14 @@
     sums[2:3] = column_sum(low[own_rows])
     fetch_after.wait()
 
-    grads = [rest[0], rest[1], rest[0]]
+    grads = [rest[0], rest[1], ahead]
+    gates = (gate_core, gate_chips)
     first, second, sems = rest[2:5], rest[5:8], rest[8:]
     owned = (owned_a, owned_b, owned_c)
     jobs = [
         reduce_batch(
             grads[b], None, *(first, second, first)[b], owned[b], *sems[6 * b : 6 * b + 6],
-            gates=((gate, None), None, (None, gate))[b],
+            gates=((gates, None), None, (None, gates))[b],
         )
         for b in range(3)
     ]
@@ -906,7 +967,10 @@
         if n < 5:
             aheads[n + 1].wait()
             left = a if n < 2 else low
-            hidden[(n + 1) % 2] = product(left[...], ahead[(n + 1) % 2])
+            behinds[n].wait()
+            hidden[(n + 1) % 2] = product(left[...], weights(n + 1)[...])
+        else:
+            behinds[n].wait()
         cols = slice(n % 3 * BATCH, (n % 3 + 1) * BATCH)
         if n < 3:
             value, slope = gelu_pair(hidden[n % 2] + bias[0:1, cols])
@@ -917,7 +981,6 @@
             value = (hidden[n % 2] * back[:, cols].astype(F32)).astype(BF)
             back[:, cols] = value
             bias_sum[0:1, cols] = column_sum(value)
-        behinds[n].wait()
         moved = contract_last(value, behind[n % 2])
         if n % 3 == 0:
             acc[...] = moved
@@ -941,33 +1004,31 @@
     third_grads(1, 0, 1)
     advance(jobs[0])
     step(2)
-    down_copies = scatter_held(part, blocks.at[0], zs.at[0], zr.at[0])
+    down_sum = Scatter(part, blocks.at[0], zs.at[0], zr.at[0]).held()
     advance(jobs[0])
     third_grads(2, 1, 0)
     step(3)
+    down_sum.relay()
     third_grads(3, 1, 1)
     advance(jobs[1])
     step(4)
     advance(jobs[1])
     advance(jobs[0])
-    for copy in down_copies:
-        copy.wait()
-    branch = total_of(part[own_rows], blocks.at[0]) + vec[V_DOWN : V_DOWN + 1]
+    branch = down_sum.total() + vec[V_DOWN : V_DOWN + 1]
+    down_sum.drain()
     result[...] = (after_two[...] + vec[5:6] * branch).astype(BF)
     sums[10:11] = column_sum(dy * branch)
+    send_result, wait_result = deliver(result, out_result, ds, dr, loc.at[4])
     step(5)
-    copies = scatter_held(part, blocks.at[1], zs.at[1], zr.at[1])
-    drains = list(copies)
-    send_result, wait_result = deliver(result, out_result, ds, dr, loc.at[3])
-    finish(jobs[0])
+    back_sum = Scatter(part, blocks.at[1], zs.at[1], zr.at[1]).held()
     third_grads(4, 2, 0)
     third_grads(5, 2, 1)
+    back_sum.relay()
     advance(jobs[2])
+    finish(jobs[0])
     advance(jobs[1])
     advance(jobs[2])
-    for copy in copies:
-        copy.wait_recv()
-    total = total_of(part[own_rows], blocks.at[1])
+    total = back_sum.total()
     normed, inverse = plain_norm(after_two[...])
     sums[8:9] = column_sum(total)
     sums[9:10] = column_sum(total * normed)
@@ -975,20 +1036,19 @@
     grad_after[...] = value
     value = value.astype(BF)
     sums[1:2] = column_sum(value)
-    copies = spread_block(low_two, value, gs, gr)
-    drains += copies
+    spread = Spread(low_two, value, gs, gr)
+    finish(jobs[1])
+    spread.relay()
     send_result()
-    finish(jobs[1])
     advance(jobs[2])
+    spread.wait()
+    store = pltpu.make_async_copy(low_two, low_out, loc.at[3])
+    store.start()
     finish(jobs[2])
-    for copy in copies:
-        copy.wait_recv()
-    store = pltpu.make_async_copy(low_two, low_out, loc.at[4])
-    store.start()
+    store.wait()
     wait_result()
-    store.wait()
-    for copy in drains:
-        copy.wait_send()
+    back_sum.drain()
+    spread.drain()
 
 
 def mlp_pass(a, cot, up, down, after, vec, bias):
@@ -1008,11 +1068,11 @@
         in_specs=[HB] * 5 + [VM] * 2,
         out_specs=[spec for _, spec in outs],
         scratch_shapes=[
-            wide, wide, tiles, tiles, pltpu.VMEM((2, SEQ, BATCH), F32), units, units,
-            pltpu.VMEM((SEQ, D), F32), wide, pltpu.VMEM((TOK, D), F32), wide,
-            pltpu.VMEM((2, 3, TOK, D), BF), pltpu.VMEM((TOK, D), BF), dma((2, 3)), dma((2, 3)),
-            dma((3,)), dma((3,)), dma((2,)), dma((2,)), dma((5,)), dma((2, 2)),
-            pltpu.SemaphoreType.REGULAR, pltpu.VMEM(GRADS, BF), pltpu.VMEM(GRADS, BF),
+            wide, wide, pltpu.VMEM(GRADS, BF), tiles, pltpu.VMEM((2, SEQ, BATCH), F32), units, units,
+            pltpu.VMEM((SEQ, D), F32), wide, pltpu.VMEM((TOK, D), F32), wide, pltpu.VMEM((TOK, D), BF),
+            pltpu.VMEM((2, 3, TOK, D), BF), dma((2, 6)), dma((2, 6)), dma((6,)), dma((6,)), dma((2,)),
+            dma((2,)), dma((5,)), dma((2, 2)), pltpu.SemaphoreType.REGULAR, pltpu.SemaphoreType.REGULAR,
+            pltpu.VMEM(GRADS, BF), pltpu.VMEM(GRADS, BF),
             *reduce_buffers(), *reduce_buffers(), *reduce_sems(), *reduce_sems(), *reduce_sems(),
         ],
         compiler_params=params(1),
@@ -1020,69 +1080,69 @@
     )(a, cot, up, down, after, vec, bias)
 
 
-def vector_job(model, heads, time_out, model_out, head_out, *refs):
-    col, mx, sends, recvs, *head_refs = refs
+def sum_over_xy(held, sends, recvs):
     x, y, z, core = here()
-    zl = lax.rem(z, 2)
-    rows, lines = peers_xy(x, y, z, core)
-    sibling = chip(x, y, z, 1 - core)
-    copies = []
-    for k in (2, 1, 3):
-        copies.append(remote(model, col.at[k], sends.at[0, k], recvs.at[0, k], chip(x, y, z + k, core)))
-    if heads is not None:
-        hsib, hx = head_refs
-        copies.append(remote(heads, hsib, sends.at[0, 0], recvs.at[0, 0], sibling))
+    for stage, peers in enumerate(peers_xy(x, y, z, core)):
+        base = 4 * stage
+        copies = [
+            remote(held.at[base], held.at[base + k], sends.at[stage, k], recvs.at[stage, k], peers[k - 1])
+            for k in (2, 1, 3)
+        ]
+        for copy in copies:
+            copy.start()
+        yield
+        for copy in copies:
+            copy.wait()
+        held[base + 4] = (held[base] + held[base + 1]) + (held[base + 2] + held[base + 3])
+
+
+def model_job(model, time_out, col, held, sends, recvs):
+    x, y, z, core = here()
+    copies = [
+        remote(model, col.at[k], sends.at[2, k], recvs.at[2, k], chip(x, y, z + k, core)) for k in (2, 1, 3)
+    ]
     for copy in copies:
         copy.start()
     yield
     for copy in copies:
         copy.wait()
-    time_out[core] = model[...] + col[1] + col[2] + col[3]
-    swap = remote(time_out.at[core], time_out.at[core], sends.at[1, 0], recvs.at[1, 0], sibling)
+    time_out[core] = (model[...] + col[1]) + (col[2] + col[3])
+    swap = remote(
+        time_out.at[core], time_out.at[core], sends.at[2, 0], recvs.at[2, 0], chip(x, y, z, 1 - core)
+    )
     swap.start()
-    if heads is not None:
-        hx[0] = heads[...] + hsib[...]
     yield
     swap.wait()
-    mx[0] = time_out[0] + time_out[1]
-    for stage, peers in enumerate((rows, lines)):
-        copies = []
-        for k in (1, 2, 3):
-            copies.append(
-                remote(mx.at[4 * stage], mx.at[4 * stage + k], sends.at[2 + 2 * stage, k],
-                       recvs.at[2 + 2 * stage, k], peers[k - 1])
-            )
-            if heads is not None:
-                copies.append(
-                    remote(hx.at[4 * stage], hx.at[4 * stage + k], sends.at[3 + 2 * stage, k],
-                           recvs.at[3 + 2 * stage, k], peers[k - 1])
-                )
-        for copy in copies:
-            copy.start()
-        yield
-        for copy in copies:
-            copy.wait()
-        base = 4 * stage
-        mx[base + 4] = mx[base] + mx[base + 1] + mx[base + 2] + mx[base + 3]
-        if heads is not None:
-            hx[base + 4] = hx[base] + hx[base + 1] + hx[base + 2] + hx[base + 3]
-    model_out[...] = mx[8]
-    if heads is not None:
-        head_out[zl] = hx[8]
-        last = remote(
-            hx.at[8], head_out.at[zl], sends.at[6, 0], recvs.at[6, 0], chip(x, y, z + 1 - 2 * zl, core)
-        )
-        last.start()
-        yield
-        last.wait()
-
-
-def vector_scratch(rows, heads):
+    held[0] = time_out[0] + time_out[1]
+    yield from sum_over_xy(held, sends, recvs)
+
+
+def head_job(heads, head_out, other, held, sends, recvs):
+    x, y, z, core = here()
+    zl = lax.rem(z, 2)
+    swap = remote(heads, other, sends.at[2, 0], recvs.at[2, 0], chip(x, y, z, 1 - core))
+    swap.start()
+    yield
+    swap.wait()
+    held[0] = heads[...] + other[...]
+    yield from sum_over_xy(held, sends, recvs)
+    head_out[zl] = held[8]
+    last = remote(
+        held.at[8], head_out.at[zl], sends.at[2, 1], recvs.at[2, 1], chip(x, y, z + 1 - 2 * zl, core)
+    )
+    last.start()
+    yield
+    last.wait()
+
+
+def model_scratch(rows, width):
     dma = pltpu.SemaphoreType.DMA
-    refs = [pltpu.VMEM((4, rows, D), F32), pltpu.VMEM((9, rows, D), F32), dma((7, 4)), dma((7, 4))]
-    if heads:
-        refs += [pltpu.VMEM((16, HW), F32), pltpu.VMEM((9, 16, HW), F32)]
-    return refs
+    return [pltpu.VMEM((4, rows, width), F32), pltpu.VMEM((9, rows, width), F32), dma((3, 4)), dma((3, 4))]
+
+
+def head_scratch():
+    dma = pltpu.SemaphoreType.DMA
+    return [pltpu.VMEM((16, HW), F32), pltpu.VMEM((9, 16, HW), F32), dma((3, 4)), dma((3, 4))]
 
 
 def attend_clip_back(query, keys, values, grad, grad_query, grad_keys, grad_values):
@@ -1116,10 +1176,10 @@
     query_rot_in, key_rot_in, value_low_in, query_two_in, key_two_in, value_two_in, mixed_in,
     mixed_two_in, words_in, three_in, one_in, tok_in, grad_in, tab_in, inv_in,
     vec, heads, sums, bias_sum, owned_a, owned_b, owned_c,
-    out_tokens, out_words, time_out, model_out, head_out, sums_a, sums_b, mlp_a, mlp_b, mlp_c,
+    out_tokens, low_words, time_out, model_out, head_out, sums_a, sums_b, mlp_a, mlp_b, mlp_c,
     wa, low_wide, after_one, branch_one, lin_a, lin_b, qa, ka, va, mixed, mixed_two, operand, tok_own,
     grad_after, tab, inv, grad_query, grad_kv, grad_qkv, part_cross, part_words, blocks,
-    held, gq, gk, gv, model, head_sums, low_words, low_tokens,
+    held, gq, gk, gv, model, head_sums, low_tokens,
     stat, stat_s, stat_r, zs, zr, gs, gr, ds, dr, loc, *rest,
 ):
     x, y, z, core = here()
@@ -1134,7 +1194,7 @@
 
     out_cols, in_cols = pl.ds(6 * HW, 2 * HW), pl.ds(0, 6 * HW)
     first = [fetch(low_in, low_wide), fetch(wa_in.at[:, out_cols], wa.at[:, out_cols])]
-    cross = [
+    inputs = [
         fetch(query_two_in, qa), fetch(key_two_in, ka), fetch(value_two_in, va),
         fetch(query_two_lin_in, lin_a), fetch(key_two_lin_in, lin_b), fetch(inv_in, inv),
     ]
@@ -1151,15 +1211,16 @@
     head_sums[...] = jnp.zeros_like(head_sums)
     for i in range(6):
         head_sums[10 + i : 11 + i] = bias_sum[0:1, i * HW : (i + 1) * HW]
-    refs_a, refs_b, early_refs, rest = rest[:14], rest[14:28], rest[28:32], rest[32:]
-    vector_refs, (late, time_late, model_late), swap_refs = rest[:6], rest[6:9], rest[9:]
+    refs_a, refs_b, early_refs, late_refs, head_refs, rest = (
+        rest[:14], rest[14:28], rest[28:32], rest[32:36], rest[36:40], rest[40:],
+    )
+    (late, time_late), swap_refs = rest[:2], rest[2:]
     hidden_rows = [
         swap_rows(src, dst, *swap_refs[3 * i : 3 * i + 3])
         for i, (src, dst) in enumerate(((owned_a, mlp_a), (owned_b, mlp_b), (owned_c, mlp_c)))
     ]
     for job in hidden_rows:
         advance(job)
-    late[...] = jnp.zeros_like(late)
     grads_a, grads_b = refs_a[0], refs_b[0]
     job_a = reduce_batch(grads_a, sums_a, *refs_a[1:])
     job_b = reduce_batch(grads_b, sums_b, *refs_b[1:])
@@ -1169,7 +1230,7 @@
     for copy in first:
         copy.wait()
     held[...] = product(low_wide[...], wa[:, W_CROSS]).astype(BF)
-    for copy in cross:
+    for copy in inputs:
         copy.wait()
     attend_clip_back(qa, ka, va, held, gq, gk, gv)
     inverse_query, inverse_key, inverse_key_two, inverse_query_two = [inv[:, i : i + 1] for i in range(4)]
@@ -1192,9 +1253,7 @@
     low = root_back(lin_a[...], inverse_query_two, gq[...] * (1.0 + heads[8:9]), dot_query)
     grad_query[...] = low
     head_sums[5:6] = column_sum(low)
-    cross_copies = scatter_product(
-        grad_query, wa[:, W_QUERY], part_cross, blocks.at[0], zs.at[0], zr.at[0]
-    )
+    cross = Scatter(part_cross, blocks.at[0], zs.at[0], zr.at[0]).product(grad_query, wa[:, W_QUERY])
     low = root_back(lin_b[...], inverse_key_two, gk[...] * (1.0 + heads[9:10]), dot_key)
     grad_kv[:, :HW] = low
     head_sums[6:7] = column_sum(low)
@@ -1205,6 +1264,7 @@
     weight_grad(operand, grad_kv[...], grads_a, 0, 0)
     next_operand = fetch(three_in, operand)
     next_operand.wait()
+    cross.relay()
     weight_grad(operand, grad_query[...], grads_a, 1, 0)
     next_operand = fetch(one_in, operand)
     advance(job_a)
@@ -1212,7 +1272,7 @@
     for copy in third:
         copy.wait()
 
-    total = collect(part_cross, blocks.at[0], cross_copies)
+    total = cross.total()
     normed, inverse = plain_norm(after_one[...])
     model[4:5] = column_sum(total)
     model[3:4] = column_sum(total * normed)
@@ -1221,14 +1281,15 @@
     model[7:8] = column_sum(value * branch_one[...])
     low = (value * vec[2:3]).astype(BF)
     model[0:1] = column_sum(low)
-    copies = spread_block(low_wide, low, gs, gr)
-    drains += copies
+    spread = Spread(low_wide, low, gs, gr)
+    drains.append(spread)
     advance(job_a)
-    for copy in copies:
-        copy.wait_recv()
-    early = vector_job(model, None, time_out, model_out, None, *early_refs)
+    spread.relay()
+    early = model_job(model, time_out, *early_refs)
     advance(early)
-    word_copies = scatter_held(part_words, blocks.at[1], zs.at[1], zr.at[1], 0, TOK // 2)
+    spread.wait()
+    word_sum = Scatter(part_words, blocks.at[1], zs.at[1], zr.at[1]).held()
+    drains.append(word_sum)
 
     held[...] = product(low_wide[...], wa[:, W_SELF]).astype(BF)
     for copy in selfs:
@@ -1254,61 +1315,68 @@
     head_sums[2:3] = column_sum(low)
     next_operand.wait()
     weight_grad(low_wide, mixed[...], grads_b, 1, HW)
-    for copy in cross_copies:
-        copy.wait_send()
-    advance(early, 2)
+    cross.drain()
+    advance(early)
     dot_query, dot_key = dots()
-    word_copies += scatter_held(part_words, blocks.at[1], zs.at[3], zr.at[3], TOK // 2, TOK // 2)
-    drains += word_copies
+    word_sum.relay()
     for i, (lin, inverse, ref, dot) in enumerate(
         ((lin_a, inverse_query, gq, dot_query), (lin_b, inverse_key, gk, dot_key))
     ):
         low = root_back(lin[...], inverse, ref[...] * (1.0 + heads[3 + i : 4 + i]), dot)
         grad_qkv[:, i * HW : (i + 1) * HW] = low
         head_sums[i : i + 1] = column_sum(low)
-    copies = scatter_product(grad_qkv, wa[:, W_QKV], part_cross, blocks.at[0], zs.at[2], zr.at[2])
-    drains += copies
+    token_sum = Scatter(part_cross, blocks.at[0], zs.at[2], zr.at[2]).product(grad_qkv, wa[:, W_QKV])
+    drains.append(token_sum)
+    head_total = head_job(head_sums, head_out, *head_refs)
+    advance(head_total)
     advance(job_a)
+    advance(early)
     weight_grad(operand, grad_qkv[:, : 2 * HW], grads_b, 0, 0)
     weight_grad(operand, grad_qkv[:, 2 * HW :], grads_b, 1, 0)
     advance(job_b)
+    token_sum.relay()
+    advance(head_total)
+    advance(job_a)
     advance(early)
-    advance(job_a)
     advance(job_b)
-    finish(early)
+    advance(head_total)
     for job in hidden_rows:
         finish(job)
-    low_words[...] = collect(part_words, blocks.at[1], word_copies).astype(BF)
-    send_words, wait_words = deliver(low_words, out_words, ds.at[0], dr.at[0], loc.at[30])
-    finish(job_a)
-
-    total = collect(part_cross, blocks.at[0], copies)
+
+    total = token_sum.total()
     normed, inverse = plain_norm(tok_own[...].astype(F32))
-    late[0:1] = column_sum(total)
-    late[1:2] = column_sum(total * normed)
-    vectors = vector_job(late, head_sums, time_late, model_late, head_out, *vector_refs)
-    advance(vectors)
+    for i, row in enumerate((column_sum(total), column_sum(total * normed))):
+        for k in range(SIDE):
+            late[SIDE * i + k : SIDE * i + k + 1] = row[:, k * HW : (k + 1) * HW]
+    late_total = model_job(late, time_late, *late_refs)
+    advance(late_total)
     value = grad_after[...] + norm_back(total * (1.0 + vec[1:2]), normed, inverse)
     low_tokens[...] = value.astype(BF)
     send_tokens, wait_tokens = deliver(low_tokens, out_tokens, ds.at[1], dr.at[1], loc.at[31])
-    advance(vectors)
+    advance(late_total)
     send_tokens()
-    send_words()
-    advance(vectors)
+    low_words[...] = word_sum.total().astype(BF)
+    advance(late_total)
+    finish(early)
     advance(job_b)
-    advance(vectors)
+    advance(late_total)
+    finish(job_a)
+    advance(head_total)
     advance(job_b)
-    advance(vectors)
+    finish(late_total)
+    finish(head_total)
     wait_tokens()
-    advance(vectors)
     finish(job_b)
-    finish(vectors)
-    wait_words()
-    time_out[0, 5:7] = time_late[0, 0:2]
-    time_out[1, 5:7] = time_late[1, 0:2]
-    model_out[5:7] = model_late[0:2]
-    for copy in drains:
-        copy.wait_send()
+    model_out[...] = early_refs[1][8]
+    for i in range(2):
+        for k in range(SIDE):
+            cols = slice(k * HW, (k + 1) * HW)
+            row = slice(SIDE * i + k, SIDE * i + k + 1)
+            model_out[5 + i : 6 + i, cols] = late_refs[1][8, row]
+            for clip in (0, 1):
+                time_out[clip, 5 + i : 6 + i, cols] = time_late[clip, row]
+    for transfer in drains:
+        transfer.drain()
 
 
 def backward(hbm, vmem):
@@ -1321,7 +1389,7 @@
     low_block = pltpu.VMEM((TOK, D), BF)
     summed = sds((2, PAIR, BATCH), F32)
     outs = [
-        (sds((2, TOK, D), BF), HB), (sds((2, TOK, D), BF), HB), (sds((2, 16, D), F32), VM),
+        (sds((2, TOK, D), BF), HB), (sds((TOK, D), BF), VM), (sds((2, 16, D), F32), VM),
         (sds((16, D), F32), VM), (sds((2, 16, HW), F32), VM), (summed, VM), (summed, VM),
         *[(sds((2, PAIR, BATCH), BF), VM)] * 3,
     ]
@@ -1336,11 +1404,11 @@
             low_block, block, pltpu.VMEM((SIDE, TOK, HEAD), F32), pltpu.VMEM((SEQ, 128), F32),
             low, pltpu.VMEM((SEQ, 2 * HW), BF), pltpu.VMEM((SEQ, 3 * HW), BF), wide, wide,
             pltpu.VMEM((2, 3, TOK, D), BF), low, lin, lin, lin, pltpu.VMEM((16, D), F32),
-            pltpu.VMEM((16, HW), F32), low_block, low_block,
+            pltpu.VMEM((16, HW), F32), low_block,
             pltpu.VMEM((2, 4, 8, SEQ), F32),
-            dma((2, 3)), dma((2, 3)), dma((4, 3)), dma((4, 3)), dma((3,)), dma((3,)), dma((2, 2)),
-            dma((2, 2)), dma((32,)), *batch, *batch, *vector_scratch(16, False),
-            *vector_scratch(8, True), pltpu.VMEM((8, D), F32), pltpu.VMEM((2, 8, D), F32), pltpu.VMEM((8, D), F32),
+            dma((2, 3)), dma((2, 3)), dma((3, 6)), dma((3, 6)), dma((6,)), dma((6,)), dma((3, 2)),
+            dma((3, 2)), dma((32,)), *batch, *batch, *model_scratch(16, D),
+            *model_scratch(8, HW), *head_scratch(), pltpu.VMEM((8, HW), F32), pltpu.VMEM((2, 8, HW), F32),
             *swap_sems(), *swap_sems(), *swap_sems(),
         ],
         compiler_params=params(2),
@@ -1396,11 +1464,13 @@
 
 
 def gram_kernel(
-    sum_a, sum_b, sum_c, attn_a, attn_b, in_m, out_m, mlp_m, narrow, wide, gram, mine, theirs, send, recv
+    sum_a, sum_b, sum_c, attn_a, attn_b, in_m, out_m, mlp_m, words, narrow, wide, gram, out_words,
+    mine, theirs, send, recv, ds, dr, loc,
 ):
     x, y, z, core = here()
     partner = chip(x, y, z + 2, core)
-    greet([partner])
+    greet(column(x, y, z, core))
+    send_words, wait_words = deliver(words, out_words, ds, dr, loc.at[0])
 
     def pair(ref, part, col):
         rows = slice(part * ROWS, (part + 1) * ROWS)
@@ -1425,8 +1495,10 @@
     mine[n:, :n] = jnp.zeros((w, n), F32)
     copy = remote(mine, theirs, send.at[0], recv.at[0], partner)
     copy.start()
+    send_words()
     copy.wait()
     gram[...] = mine[...] + theirs[...]
+    wait_words()
 
 
 def gram_step(args, cid):
@@ -1437,11 +1509,13 @@
         gram_kernel,
         out_shape=[
             sds((8 * ROWS, 2 * HW), F32), sds((2 * ROWS, WIDE), F32), sds((size, size), F32),
+            sds((2, TOK, D), BF),
         ],
         in_specs=[VM] * len(args),
-        out_specs=[VM] * 3,
+        out_specs=[VM] * 3 + [HB],
         scratch_shapes=[
             pltpu.VMEM((size, size), F32), pltpu.VMEM((size, size), F32), dma((1,)), dma((1,)),
+            dma((2,)), dma((2,)), dma((1,)),
         ],
         compiler_params=params(cid),
         name="gram",
@@ -1464,7 +1538,9 @@
                 pltpu.make_async_copy(block.at[2 * i + clip], dst.at[clip], stores.at[2 * i + clip])
             )
             copies[-1].start()
-    out_time[...] = time_sum[:, 5:11]
+    for i in range(6):
+        for clip in (0, 1):
+            out_time[i, clip : clip + 1] = time_sum[clip, 5 + i : 6 + i]
     value = MOMENTUM * head_m[...] + jnp.concatenate([head_sum[0, :10], head_sum[1, :10]], 1)
     new_head_m[...] = value
     new_head[...] = head_w[...] - RATE_VECTOR * value
@@ -1472,9 +1548,11 @@
     new_model_m[...] = value
     new_model[...] = model_w[...] - RATE_VECTOR * value
     chips = [jnp.concatenate([head_sum[i, 10 + k : 11 + k] for k in range(6)], 1) for i in (0, 1)]
-    value = MOMENTUM * up_m[...] + join_hidden(*chips)
-    new_up_m[...] = value
-    new_up[...] = up_w[...] - RATE_VECTOR * value
+    value = join_hidden(*chips)
+    for i in range(WIDE // 128):
+        row = slice(i, i + 1)
+        new_up_m[row] = MOMENTUM * up_m[row] + value[:, i * 128 : (i + 1) * 128]
+    new_up[...] = up_w[...] - RATE_VECTOR * new_up_m[...]
     n, w = narrow.shape[0], wide.shape[0]
     factor = newton_factor(gram[...], n + w)
     turned = times(factor[:n, :n], narrow[...])
@@ -1498,11 +1576,11 @@
 def finish_step(args):
     sds = jax.ShapeDtypeStruct
     matrices = [sds((6, ROWS, 2 * HW), F32), sds((ROWS, 2, 2 * HW), F32), sds((ROWS, 2, WIDE), F32)]
-    vectors = [sds((10, 2 * HW), F32), sds((11, D), F32), sds((1, WIDE), F32)]
+    vectors = [sds((10, 2 * HW), F32), sds((11, D), F32), sds((WIDE // 128, 128), F32)]
     blocks = [sds((2, TOK, D), BF), sds((2, TOK, D), F32), sds((2, TOK, D), F32)]
     return pl.pallas_call(
         finish_kernel,
-        out_shape=matrices + matrices + vectors + vectors + blocks + [sds((2, 6, D), F32)],
+        out_shape=matrices + matrices + vectors + vectors + blocks + [sds((6, 2, D), F32)],
         in_specs=[VM] * len(args),
         out_specs=[VM] * 13 + [HB] * 2 + [VM],
         scratch_shapes=[pltpu.VMEM((4, TOK, D), F32), pltpu.SemaphoreType.DMA((4,))],
@@ -1595,7 +1673,7 @@
     low_two, grad_after, sums, up_sum, out_result, *owned = mlp_pass(
         input_mlp, cot_all, w_up, w_down, after_two, vectors, bias_up[None]
     )
-    out_tokens, out_words, time_sums, model_sums, head_totals, sums_a, sums_b, *mlp_sums = backward(
+    out_tokens, low_words, time_sums, model_sums, head_totals, sums_a, sums_b, *mlp_sums = backward(
         [
             w_attn, low_two, after_one, branch_one, query_lin, key_lin, query_two_lin, key_two_lin,
             query_rot, key_rot, value_low, query_two, key_two, value_two, mixed_low, mixed_two_low,
@@ -1604,8 +1682,8 @@
         [vectors, heads, sums, up_sum, *owned],
     )
     swap = lambda v: v.transpose(1, 0, 2)
-    narrow, wide, gram = gram_step(
-        [*mlp_sums, sums_a, sums_b, swap(attn_in_moment), attn_out_moment, mlp_moment], 3
+    narrow, wide, gram, out_words = gram_step(
+        [*mlp_sums, sums_a, sums_b, swap(attn_in_moment), attn_out_moment, mlp_moment, low_words], 3
     )
     (
         new_in, new_out, new_mlp, new_in_m, new_out_m, new_mlp_m, new_head, new_model, new_up,
@@ -1613,12 +1691,12 @@
     ) = finish_step(
         [
             narrow, wide, gram, swap(attn_in), attn_out, mlp, head_vectors, head_moment, model_vectors,
-            model_moment, up_bias[None], up_moment[None], head_totals, model_sums, out_result,
+            model_moment, up_bias.reshape(-1, 128), up_moment.reshape(-1, 128), head_totals, model_sums, out_result,
             out_tokens, out_words, time_sums,
         ]
     )
     return (
-        out_result, out_tokens, out_words, out_time, swap(new_in), new_out, new_mlp,
+        out_result, out_tokens, out_words, swap(out_time), swap(new_in), new_out, new_mlp,
         swap(new_in_m), new_out_m, new_mlp_m, new_head, new_model, new_up.reshape(-1), new_head_m,
         new_model_m, new_up_m.reshape(-1),
     )

time: 417 us -> 364 us (0.87)
  Pallas kernels: 396 us -> 348 us
    pallas_call x1, Pallas kernels: 127 us -> 103 us  [backward(): pl.pallas_call(backward_kernel, out_shape=[shape for shape, _ in outs], i...]
    pallas_call x1, Pallas kernels: 145 us -> 123 us  [forward(): pl.pallas_call(forward_kernel, out_shape=weights + outs, in_specs=[VM, VM...]
    pallas_call x1, Pallas kernels: 96.9 us -> 83.9 us  [mlp_pass(): pl.pallas_call(mlp_kernel, out_shape=[shape for shape, _ in outs], in_spe...]
    pallas_call x1, Pallas kernels: 12.6 us -> 23.1 us  [gram_step(): pl.pallas_call(gram_kernel, out_shape=[sds((8 * ROWS, 2 * HW), F32), sds(...]
where the time goes in v5:
time: 364 us; the launch traced here: 360 us
  Pallas kernels  348 us (96%)
  local copies, waits for them, and re-layouts  7.19 us (2%)
  other arithmetic  4.22 us (1%)
    pallas_call x1, Pallas kernels, forward(): pl.pallas_call(forward_kernel, out_shape=weights + outs, in_specs=[VM, VM...  123 us
    pallas_call x1, Pallas kernels, backward(): pl.pallas_call(backward_kernel, out_shape=[shape for shape, _ in outs], i...  103 us
    pallas_call x1, Pallas kernels, mlp_pass(): pl.pallas_call(mlp_kernel, out_shape=[shape for shape, _ in outs], in_spe...  83.9 us
    pallas_call x1, Pallas kernels, gram_step(): pl.pallas_call(gram_kernel, out_shape=[sds((8 * ROWS, 2 * HW), F32), sds(...  23.1 us
    pallas_call x1, Pallas kernels, finish_step(): pl.pallas_call(finish_kernel, out_shape=matrices + matrices + vectors + v...  15.1 us

profile of v5, /device:TPU:1, one launch (start us, length us, event | category | flops | bytes accessed | tf_op | source)
XLA Modules:
  0.0 360.3 jit_solution(15311777115103768055)
XLA Ops:
  0.7 0.8 slice_bitcast_fusion.2
  1.5 0.8 dynamic_slice.12
  2.3 0.6 broadcast_in_dim.21.bias
  2.9 0.7 constant_dynamic-slice_fusion.1
  3.7 0.6 pad.17.heads
  4.3 0.9 fusion.2
  5.2 0.8 slice.22
  6.0 0.7 select_maximum_fusion.vec
  6.7 1.0 convert_element_type.102
  7.8 0.1 reshape.183
  7.9 0.1 copy.48
  8.0 0.3 reshape.184
  8.3 0.2 reshape.187
  8.5 0.7 copy.36
  9.2 0.6 fusion.1
  9.8 0.8 pad_maximum_fusion.1.tab
  10.6 0.3 convert_element_type.103
  10.9 0.5 reshape.189
  11.4 0.8 pad.16
  12.2 123.0 %forward.1 = (bf16[1536,3072]{1,0:T(8,128)(2,1)}, bf16[1536,2304]{1,0:T(8,128)(2,1)}, bf16[1536,2304]{1,0:T(8,128)(2,1)}, bf16[4,128,1536]{2,1,0:T(8,128)(2,1)},...) custom-call(bf16[2,48,1536]{2,1,0:T(8,128)(2,1)} %bitcast.40, ...), custom_call_target="tpu_custom_call" | custom-call | tf_op jit(solution)/shard_map/forward/pallas_call | solution.py:658
  135.2 83.9 %mlp.1 = (bf16[512,1536]{1,0:T(8,128)(2,1)}, f32[128,1536]{1,0:T(8,128)}, f32[16,1536]{1,0:T(8,128)}, f32[8,2304]{1,0:T(8,128)}, bf16[2,128,1536]{2,1,0:T(8,128)...) custom-call(bf16[512,1536]{1,0:T(8,128)(2,1)} %get-tuple-element.81.a_in, ...), custom_call_target="tpu_custom_call" | custom-call | tf_op jit(solution)/shard_map/mlp/pallas_call | solution.py:1065
  219.1 102.7 %backward.1 = (bf16[2,128,1536]{2,1,0:T(8,128)(2,1)}, bf16[128,1536]{1,0:T(8,128)(2,1)}, f32[2,16,1536]{2,1,0:T(8,128)}, f32[16,1536]{1,0:T(8,128)}, f32[2,16,38...) custom-call(bf16[1536,3072]{1,0:T(8,128)(2,1)} %get-tuple-element.80, ...), custom_call_target="tpu_custom_call" | custom-call | tf_op jit(solution)/shard_map/backward/pallas_call | solution.py:1397
  321.8 23.1 %gram.1 = (f32[192,768]{1,0:T(8,128)}, f32[48,4480]{1,0:T(8,128)}, f32[240,240]{1,0:T(8,128)}, bf16[2,128,1536]{2,1,0:T(8,128)(2,1)}) custom-call(bf16[2,48,768]{2,1,0:T(8,128)(2,1)} %get-tuple-element.113.sum_a, bf16[2,48,768]{2,1,0:T(8,128)(2,1)} %get-tuple-element.114.sum_b, bf16[2,48,768]{2,1,0:T(8,128)(2,1)} %get-tuple-element.115.sum_c, ...), custom_call_target="tpu_custom_call" | custom-call | tf_op jit(solution)/shard_map/gram/pallas_call | solution.py:1508
  345.0 15.1 %finish.1 = (f32[6,24,768]{2,1,0:T(8,128)}, f32[24,2,768]{2,1,0:T(2,128)}, f32[24,2,4480]{2,1,0:T(2,128)}, f32[6,24,768]{2,1,0:T(8,128)}, f32[24,2,768]{2,1,0:T(...) custom-call(f32[192,768]{1,0:T(8,128)} %get-tuple-element.119.narrow, ...), custom_call_target="tpu_custom_call" | custom-call | tf_op jit(solution)/shard_map/finish/pallas_call | solution.py:1581
  (18 shorter events, 0.3 us)
Async XLA Ops:
  0.6 3.6 %copy-start = (f32[2,6,1536]{2,0,1:T(2,128)S(1)}, f32[2,6,1536]{2,0,1:T(2,128)}, u32[]{:S(2)}) copy-start(f32[2,6,1536]{2,0,1:T(2,128)} %param.19) | copy-start | bytes 221188
  0.7 7.1 %copy-start.3 = (f32[24,6,768]{2,0,1:T(8,128)S(1)}, f32[24,6,768]{2,0,1:T(8,128)}, u32[]{:S(2)}) copy-start(f32[24,6,768]{2,0,1:T(8,128)} %param.22) | copy-start | bytes 1327108
  8.0 2.6 copy-start.2
  345.0 15.1 %copy-start.1 = (f32[2,6,1536]{2,0,1:T(2,128)S(1)}, f32[2,6,1536]{2,0,1:T(2,128)}, u32[]{:S(2)}) copy-start(f32[2,6,1536]{2,0,1:T(2,128)} %param.19) | copy-start | bytes 221188

commit v6 on v5

--- a/solution.py
+++ b/solution.py
@@ -3,6 +3,7 @@
 
 import jax
 import jax.numpy as jnp
+import numpy as np
 from jax import lax
 from jax.experimental import pallas as pl
 from jax.experimental.pallas import tpu as pltpu
@@ -36,8 +37,9 @@
 HW = HEADS * HEAD
 FF_REAL = 2240
 FF = 2304
+WIDE = 2 * FF_REAL
 PAIR = 2 * ROWS
-VMEM_LIMIT = 57 * 1024 * 1024
+VMEM_LIMIT = 60 * 1024 * 1024
 
 
 def here():
@@ -59,11 +61,15 @@
     return 2 * lax.rem(z, 2) + lax.div(z, 2)
 
 
-def greet(devices):
+def knock(devices):
     barrier = pltpu.get_barrier_semaphore()
     for device in devices:
         pl.semaphore_signal(barrier, inc=1, device_id=device, device_id_type=MESH)
-    pl.semaphore_wait(barrier, len(devices))
+    return lambda: pl.semaphore_wait(barrier, len(devices))
+
+
+def greet(devices):
+    knock(devices)()
 
 
 def column(x, y, z, core):
@@ -103,6 +109,7 @@
     x, y, z, core = here()
     mine = x * SIDE + y
     steps = steps_of(x, y, z, core)
+    far_x, far_y = chip(x + 2, y, z, core), chip(x, y + 2, z, core)
     sibling = chip(x, y, z, 1 - core)
     sends, sibs = [], []
 
@@ -127,6 +134,7 @@
         a_next, a_prev = steps[part]
         one[part, "next"] = push(part, 0, own.at[part], mine, a_next)
         one[part, "prev"] = push(part, 1, own.at[part], mine, a_prev)
+        one[part, "far"] = push(part, 2, own.at[part], mine, (far_x, far_y)[part])
     for part in (0, 1):
         b_next, b_prev = steps[1 - part]
         two[part, 0, "next"] = push(part, 4, own.at[part], mine, b_next)
@@ -143,15 +151,10 @@
 
     offsets = (0, -1, 1, 2)
     for part in (0, 1):
-        a_next, a_prev = steps[part]
         yield
         one[part, "next"].wait_recv()
-        index = index_of(part, -1, 0)
-        one[part, "far0"] = push(part, 2, place(part, index, 0), index, a_next, 0)
         second_start(part, 1, -1)
         one[part, "prev"].wait_recv()
-        index = index_of(part, 1, 0)
-        one[part, "far1"] = push(part, 3, place(part, index, 1), index, a_prev, 1)
         second_start(part, 2, 1)
 
     def second_forward(part, k):
@@ -176,8 +179,7 @@
         second_forward(part, 0)
     for part in (0, 1):
         yield
-        one[part, "far0"].wait_recv()
-        one[part, "far1"].wait_recv()
+        one[part, "far"].wait_recv()
         second_start(part, 3, 2)
     for k in (1, 2, 3):
         for part in (0, 1):
@@ -468,8 +470,8 @@
 
 
 def forward_kernel(
-    send_attn, send_mlp, tok, txt, cot, tab, heads, vec,
-    w_attn, w_up, w_down, cot_all, *rest,
+    in_w, out_w, mlp_w, tok, txt, cot, places, rates, time_in, model_in, head_in,
+    w_attn, w_up, w_down, cot_all, heads_out, vec_out, *rest,
 ):
     saved, held, rest = rest[:SAVED], rest[SAVED : 2 * SAVED], rest[2 * SAVED :]
     (
@@ -478,21 +480,36 @@
         after_one, after_two, tok_all, txt_all,
     ) = held
     (
-        wa, got_attn, got_mlp, own_attn, own_mlp, part_one, part_two, blocks, stat,
+        send_attn, send_mlp, tab, heads, vec, wa, got_attn, got_mlp, own_attn, own_mlp, part_one, part_two, blocks, stat,
         xs, xr, ks, kr, ms, mr, js, jr, rs, rr, cs, cr, loc, stat_s, stat_r, zs, zr, gs, gr, keep,
     ) = rest
     x, y, z, core = here()
     mine = x * SIDE + y
     stores = []
 
+    def keep_small(ref, out, i):
+        stores.append(pltpu.make_async_copy(ref, out, keep.at[SAVED + i]))
+        stores[-1].start()
+
     def save(*refs):
         for ref in refs:
             i = [ref is other for other in held].index(True)
             stores.append(pltpu.make_async_copy(ref, saved[i], keep.at[i]))
             stores[-1].start()
 
+    def packed(values, cores_chip):
+        return values[:, cores_chip * HW : (cores_chip + 1) * HW]
+
+    for i in (0, 1):
+        rows = [
+            jnp.concatenate([packed(in_w[j], i) for j in range(4)], 1),
+            jnp.concatenate([packed(in_w[j], i) for j in (4, 5)] + [packed(out_w[:, j, :], i) for j in (0, 1)], 1),
+        ]
+        send_attn[i] = jnp.concatenate(rows, 0).astype(BF)
     greet(
-        [device for pair in steps_of(x, y, z, core) for device in pair] + column(x, y, z, core)
+        [device for pair in steps_of(x, y, z, core) for device in pair]
+        + [chip(x + 2, y, z, core), chip(x, y + 2, z, core)]
+        + column(x, y, z, core)
     )
     attn_start, attn_wait, attn_drain = share_rows(send_attn, got_attn, rs.at[0], rr.at[0], loc.at[0])
     mlp_start, mlp_wait, mlp_drain = share_rows(send_mlp, got_mlp, rs.at[1], rr.at[1], loc.at[1])
@@ -504,7 +521,15 @@
     ]
     attn_start()
     acts[0][0]()
-    acts[1][0]()
+    zl = lax.rem(z, 2)
+    for i in range(6):
+        vec[i : i + 1] = model_in[5 + i : 6 + i] + time_in[i, pl.ds(core, 1)]
+    vec[6:11] = model_in[0:5]
+    vec[11:16] = jnp.zeros((5, D), F32)
+    heads[0:10] = head_in[:, pl.ds(pl.multiple_of(zl * HW, HW), HW)]
+    heads[10:16] = jnp.zeros((6, HW), F32)
+    keep_small(heads, heads_out, 0)
+    keep_small(vec, vec_out, 1)
     attn_wait(own_attn)
 
     def attn_place(part, index, half=None):
@@ -524,7 +549,23 @@
     for part in (0, 1):
         attn_place(part, mine)[...] = own_attn[part]
     acts[2][0]()
+    fill = jnp.zeros((ROWS, 2 * FF - WIDE), F32)
+    lane = lax.broadcasted_iota(jnp.int32, (ROWS, FF), 1)
+    sides = ([], [])
+    for j in (0, 1):
+        whole = jnp.concatenate([mlp_w[:, j, :], fill], 1)
+        sides[0].append(jnp.where(lane < FF_REAL, whole[:, :FF], 0.0))
+        sides[1].append(pltpu.roll(whole, 2 * FF - FF_REAL, 1)[:, :FF])
+    for i in (0, 1):
+        send_mlp[i] = jnp.concatenate(sides[i], 0).astype(BF)
     mlp_start()
+    lane = lax.broadcasted_iota(jnp.int32, (TOK, HEAD), 1)
+    for i in (0, 1):
+        spots = [places[c, i : i + 1, :].astype(F32) for c in range(3)]
+        spots = jnp.concatenate(spots + [jnp.zeros((TOK - 3, TOK), F32)], 0).T
+        angle = spots[:, 0:1] * rates[0:1] + spots[:, 1:2] * rates[1:2] + spots[:, 2:3] * rates[2:3]
+        tab[i] = jnp.where(lane < HEAD // 2, jnp.cos(angle), jnp.sin(angle))
+    acts[1][0]()
 
     def norm_block(i, carry):
         normed, _ = plain_norm(tok_all[i].astype(F32))
@@ -644,7 +685,7 @@
         copy.wait()
 
 
-def forward(send_attn, send_mlp, tok, txt, cot, tab, heads, vec):
+def forward(*args):
     dma = pltpu.SemaphoreType.DMA
     sds = jax.ShapeDtypeStruct
     wide, lin, low = sds((SEQ, D), BF), sds((SEQ, HW), F32), sds((SEQ, HW), BF)
@@ -654,14 +695,19 @@
         low, low, low, low, low, low, low, low, block, block, block,
         sds((SIDE, TOK, D), BF), sds((SIDE, TOK, D), BF),
     ]
-    weights = [sds((D, ATTN), BF), sds((D, FF), BF), sds((D, FF), BF), sds((SIDE, TOK, D), BF)]
+    weights = [
+        sds((D, ATTN), BF), sds((D, FF), BF), sds((D, FF), BF), sds((SIDE, TOK, D), BF),
+        sds((16, HW), F32), sds((16, D), F32),
+    ]
     return pl.pallas_call(
         forward_kernel,
         out_shape=weights + outs,
-        in_specs=[VM, VM, HB, HB, HB, VM, VM, VM],
+        in_specs=[VM, VM, VM, HB, HB, HB, VM, VM, VM, VM, VM],
         out_specs=[HB] * (len(weights) + len(outs)),
         scratch_shapes=[
             *[pltpu.VMEM(shape.shape, shape.dtype) for shape in outs],
+            pltpu.VMEM((2, PAIR, ATTN // 2), BF), pltpu.VMEM((2, PAIR, FF), BF),
+            pltpu.VMEM((2, TOK, HEAD), F32), pltpu.VMEM((16, HW), F32), pltpu.VMEM((16, D), F32),
             pltpu.VMEM((D, ATTN), BF),
             pltpu.VMEM((2, PAIR, ATTN // 2), BF),
             pltpu.VMEM((2, PAIR, FF), BF),
@@ -675,11 +721,11 @@
             *[dma(s) for s in GATHER_SEMS],
             dma((2, 2)), dma((2, 2)), dma((4, 3)), dma((4, 3)), dma((8, 2)),
             dma((2, 3)), dma((2, 3)), dma((2, 6)), dma((2, 6)), dma((2, 6)), dma((2, 6)),
-            dma((SAVED,)),
+            dma((SAVED + 2,)),
         ],
         compiler_params=params(0),
         name="forward",
-    )(send_attn, send_mlp, tok, txt, cot, tab, heads, vec)
+    )(*args)
 
 
 BATCH = 768
@@ -703,6 +749,18 @@
     def signal(gate, devices):
         for device in devices:
             pl.semaphore_signal(gate, inc=1, device_id=device, device_id_type=MESH)
+
+    def push(part, slot, target, half, place, step):
+        span = pl.ds(2 * half, 2)
+        src = (
+            grads.at[0, span, wrap(y + target), core]
+            if part == 0
+            else grads.at[1, wrap(x + target), span, core]
+        )
+        device = (lines, rows)[part][step - 1]
+        copy = remote(src, r1.at[part, place, span], s1.at[part, slot], q1.at[part, slot], device)
+        copy.start()
+        one[part].append(copy)
 
     if waits is not None:
         pl.semaphore_wait(waits[0], 1)
@@ -723,24 +781,31 @@
         lax.fori_loop(0, SIDE * SIDE, add_pair, 0)
         if part == 0 and waits is not None:
             pl.semaphore_wait(waits[1], 6)
-        for k in (2, 1, 3):
-            src = grads.at[0, :, wrap(y + k), core] if part == 0 else grads.at[1, wrap(x + k), :, core]
-            device = (lines, rows)[part][k - 1]
-            copy = remote(src, r1.at[part, k - 1], s1.at[part, k - 1], q1.at[part, k - 1], device)
-            copy.start()
-            one[part].append(copy)
+        push(part, 0, 2, 0, 2, 1)
+        push(part, 1, 2, 1, 2, 3)
+        push(part, 2, 1, 1, 0, 1)
+        push(part, 3, 3, 0, 1, 3)
     if opens is not None:
         signal(opens[0], [sibling])
     yield
     for part in (0, 1):
-        for copy in one[part]:
+        for slot, step in ((0, 1), (1, 3)):
+            one[part][slot].wait_recv()
+            for i in (2 * slot, 2 * slot + 1):
+                if part == 0:
+                    grads[0, i, wrap(y + step), core] = grads[0, i, wrap(y + step), core] + r1[0, 2, i]
+                else:
+                    grads[1, wrap(x + step), i, core] = grads[1, wrap(x + step), i, core] + r1[1, 2, i]
+            push(part, 4 + slot, step, slot, slot, step)
+    yield
+    for part in (0, 1):
+        for copy in one[part][2:]:
             copy.wait_recv()
 
         def add_line(k, carry):
             a, b = (k, y) if part == 0 else (x, k)
             total = grads[part, a, b, core].astype(F32)
-            for i in range(3):
-                total = total + r1[part, i, k].astype(F32)
+            total = total + (r1[part, 0, k].astype(F32) + r1[part, 1, k].astype(F32))
             grads[part, a, b, core] = total.astype(BF)
             return carry
 
@@ -823,7 +888,7 @@
 
 def reduce_sems():
     dma = pltpu.SemaphoreType.DMA
-    return [dma((2,)), dma((2,)), dma((2, 3)), dma((2, 3)), dma((2, 3)), dma((2, 3))]
+    return [dma((2,)), dma((2,)), dma((2, 6)), dma((2, 6)), dma((2, 3)), dma((2, 3))]
 
 
 def swap_sems():
@@ -832,7 +897,7 @@
 
 
 def reduce_scratch():
-    return [*reduce_buffers(), pltpu.VMEM((2, PAIR, BATCH), F32), *reduce_sems(), *swap_sems()]
+    return [*reduce_buffers(), pltpu.VMEM((2, PAIR, BATCH), BF), *reduce_sems(), *swap_sems()]
 
 
 GRADS = (2, SIDE, SIDE, 2, PAIR, BATCH)
@@ -905,10 +970,10 @@
 
 
 def mlp_kernel(
-    a_in, cot_all, w_up, w_down, after_in, vec, bias,
-    low_out, grad_after, sums, bias_sum, out_result, owned_a, owned_b, owned_c,
-    a, low, ahead, behind, hidden, act, back, acc, part, after_two, low_two, result,
-    blocks, zs, zr, gs, gr, ds, dr, loc, ring, gate_core, gate_chips, *rest,
+    a_in, cot_all, w_up, w_down, after_in, vec, up_bias,
+    low_out, grad_out, sums_out, bias_out, result_out, owned_a_out, owned_b_out, owned_c_out,
+    grad_after, sums, bias_sum, owned_a, owned_b, owned_c, keep, a, low, ahead, behind, hidden, act, back, acc, part, after_two, low_two, result, dy_own,
+    blocks, bias, zs, zr, gs, gr, loc, ring, gate_core, gate_chips, *rest,
 ):
     x, y, z, core = here()
     rows, lines = peers_xy(x, y, z, core)
@@ -931,25 +996,31 @@
     def load_behind(n):
         return load((w_down, w_up)[n // 3].at[:, third(n)], behind.at[n % 2], ring.at[1, n % 2])
 
+    stores = []
+
+    def save(ref, out):
+        stores.append(load(ref, out, keep.at[len(stores)]))
+
     aheads, behinds = {0: load_ahead(0)}, {}
     fetch_a = load(a_in, a, loc.at[0])
-    behinds[0] = load_behind(0)
-    fetch_low = load(cot_all.reshape(SEQ, D), low, loc.at[1])
-    aheads[1], behinds[1] = load_ahead(1), load_behind(1)
-    fetch_after = load(after_in, after_two, loc.at[2])
-    greet(column(x, y, z, core) + rows + lines)
+    arrive = knock(column(x, y, z, core) + rows + lines)
+    line = jnp.concatenate(
+        [up_bias[i : i + 1] for i in range(WIDE // 128)] + [jnp.zeros((1, 2 * FF - WIDE), F32)], 1
+    )
+    moved_line = pltpu.roll(line, 2 * FF - FF_REAL, 1)
+    lane = lax.broadcasted_iota(jnp.int32, (1, FF), 1)
+    line = jnp.where(lax.rem(z, 2) == 0, line[:, :FF], moved_line[:, :FF])
+    bias[0:1] = jnp.where(lane < FF_REAL, line, 0.0)
     sums[...] = jnp.zeros_like(sums)
     fetch_a.wait()
     aheads[0].wait()
+    aheads[1], behinds[0] = load_ahead(1), load_behind(0)
+    fetch_low = load(cot_all.reshape(SEQ, D), low, loc.at[1])
+    behinds[1] = load_behind(1)
+    fetch_after = load(after_in, after_two, loc.at[2])
     hidden[0] = product(a[...], weights(0)[...])
     aheads[2] = load_ahead(2)
-    fetch_low.wait()
-    dy = low[own_rows].astype(F32)
-    for start in range(0, SEQ, TOK):
-        block = slice(start, start + TOK)
-        low[block] = (low[block].astype(F32) * vec[5:6]).astype(BF)
-    sums[2:3] = column_sum(low[own_rows])
-    fetch_after.wait()
+    dy = dy_own
 
     grads = [rest[0], rest[1], ahead]
     gates = (gate_core, gate_chips)
@@ -999,54 +1070,71 @@
         weight_grad(left, right[:, cols], grads[b], half, 0)
 
     step(0)
+    fetch_low.wait()
+    dy_own[...] = low[own_rows].astype(F32)
+    for start in range(0, SEQ, TOK):
+        block = slice(start, start + TOK)
+        low[block] = (low[block].astype(F32) * vec[5:6]).astype(BF)
+    sums[2:3] = column_sum(low[own_rows])
+    step(1)
     third_grads(0, 0, 0)
-    step(1)
+    step(2)
+    arrive()
+    down_sum = Scatter(part, blocks.at[0], zs.at[0], zr.at[0]).held()
     third_grads(1, 0, 1)
-    advance(jobs[0])
-    step(2)
-    down_sum = Scatter(part, blocks.at[0], zs.at[0], zr.at[0]).held()
     advance(jobs[0])
     third_grads(2, 1, 0)
     step(3)
+    advance(jobs[0])
     down_sum.relay()
     third_grads(3, 1, 1)
     advance(jobs[1])
     step(4)
+    advance(jobs[0])
     advance(jobs[1])
-    advance(jobs[0])
+    fetch_after.wait()
     branch = down_sum.total() + vec[V_DOWN : V_DOWN + 1]
+    result[...] = (after_two[...] + vec[5:6] * branch).astype(BF)
+    save(result, result_out)
+    sums[10:11] = column_sum(dy[...] * branch)
     down_sum.drain()
-    result[...] = (after_two[...] + vec[5:6] * branch).astype(BF)
-    sums[10:11] = column_sum(dy * branch)
-    send_result, wait_result = deliver(result, out_result, ds, dr, loc.at[4])
     step(5)
+    save(bias_sum, bias_out)
     back_sum = Scatter(part, blocks.at[1], zs.at[1], zr.at[1]).held()
     third_grads(4, 2, 0)
+    advance(jobs[0])
     third_grads(5, 2, 1)
+    advance(jobs[2])
+    advance(jobs[1])
     back_sum.relay()
+    finish(jobs[0])
+    save(owned_a, owned_a_out)
     advance(jobs[2])
-    finish(jobs[0])
     advance(jobs[1])
-    advance(jobs[2])
     total = back_sum.total()
     normed, inverse = plain_norm(after_two[...])
     sums[8:9] = column_sum(total)
     sums[9:10] = column_sum(total * normed)
-    value = dy + norm_back(total * (1.0 + vec[4:5]), normed, inverse)
+    value = dy[...] + norm_back(total * (1.0 + vec[4:5]), normed, inverse)
     grad_after[...] = value
     value = value.astype(BF)
+    spread = Spread(low_two, value, gs, gr)
     sums[1:2] = column_sum(value)
-    spread = Spread(low_two, value, gs, gr)
+    save(grad_after, grad_out)
+    save(sums, sums_out)
+    advance(jobs[2])
     finish(jobs[1])
+    save(owned_b, owned_b_out)
     spread.relay()
-    send_result()
     advance(jobs[2])
     spread.wait()
     store = pltpu.make_async_copy(low_two, low_out, loc.at[3])
     store.start()
     finish(jobs[2])
+    save(owned_c, owned_c_out)
     store.wait()
-    wait_result()
+    for copy in stores:
+        copy.wait()
     back_sum.drain()
     spread.drain()
 
@@ -1060,18 +1148,20 @@
     owned = sds((2, PAIR, BATCH), BF)
     outs = [
         (sds((SEQ, D), BF), HB), (sds((TOK, D), F32), VM), (sds((16, D), F32), VM),
-        (sds((8, FF), F32), VM), (sds((2, TOK, D), BF), HB), (owned, VM), (owned, VM), (owned, VM),
+        (sds((8, FF), F32), VM), (sds((TOK, D), BF), HB), (owned, VM), (owned, VM), (owned, VM),
     ]
     return pl.pallas_call(
         mlp_kernel,
         out_shape=[shape for shape, _ in outs],
         in_specs=[HB] * 5 + [VM] * 2,
-        out_specs=[spec for _, spec in outs],
+        out_specs=[HB] * len(outs),
         scratch_shapes=[
+            *[pltpu.VMEM(outs[i][0].shape, outs[i][0].dtype) for i in (1, 2, 3, 5, 6, 7)], dma((7,)),
             wide, wide, pltpu.VMEM(GRADS, BF), tiles, pltpu.VMEM((2, SEQ, BATCH), F32), units, units,
             pltpu.VMEM((SEQ, D), F32), wide, pltpu.VMEM((TOK, D), F32), wide, pltpu.VMEM((TOK, D), BF),
-            pltpu.VMEM((2, 3, TOK, D), BF), dma((2, 6)), dma((2, 6)), dma((6,)), dma((6,)), dma((2,)),
-            dma((2,)), dma((5,)), dma((2, 2)), pltpu.SemaphoreType.REGULAR, pltpu.SemaphoreType.REGULAR,
+            pltpu.VMEM((TOK, D), F32),
+            pltpu.VMEM((2, 3, TOK, D), BF), pltpu.VMEM((8, FF), F32), dma((2, 6)), dma((2, 6)), dma((6,)), dma((6,)),
+            dma((5,)), dma((2, 2)), pltpu.SemaphoreType.REGULAR, pltpu.SemaphoreType.REGULAR,
             pltpu.VMEM(GRADS, BF), pltpu.VMEM(GRADS, BF),
             *reduce_buffers(), *reduce_buffers(), *reduce_sems(), *reduce_sems(), *reduce_sems(),
         ],
@@ -1171,15 +1261,20 @@
     return (inverse * scaled - linear * (inverse * inverse * inverse * dot * (1.0 / D))).astype(BF)
 
 
+EARLY, LATE = (0, 1, 3, 4, 7, 8, 9, 10), (5, 6, 2)
+
+
 def backward_kernel(
     wa_in, low_in, after_in, branch_in, query_lin_in, key_lin_in, query_two_lin_in, key_two_lin_in,
     query_rot_in, key_rot_in, value_low_in, query_two_in, key_two_in, value_two_in, mixed_in,
-    mixed_two_in, words_in, three_in, one_in, tok_in, grad_in, tab_in, inv_in,
-    vec, heads, sums, bias_sum, owned_a, owned_b, owned_c,
-    out_tokens, low_words, time_out, model_out, head_out, sums_a, sums_b, mlp_a, mlp_b, mlp_c,
-    wa, low_wide, after_one, branch_one, lin_a, lin_b, qa, ka, va, mixed, mixed_two, operand, tok_own,
+    mixed_two_in, words_in, three_in, one_in, tok_in, grad_in, tab_in, inv_in, result,
+    vec, heads, sums, bias_sum, owned_a, owned_b, owned_c, in_m, out_m, mlp_m,
+    out_result, out_tokens, out_words, time_sum_out, model_sum_out, head_sum_out, narrow_out, wide_out, gram_out,
+    time_out, model_out, head_out, narrow, wide, gram, keep,
+    wa, low_wide, after_one, branch_one, lin_a, lin_b, qa, ka, va, mixed, operand, tok_own,
     grad_after, tab, inv, grad_query, grad_kv, grad_qkv, part_cross, part_words, blocks,
-    held, gq, gk, gv, model, head_sums, low_tokens,
+    held, gq, gk, gv, model, head_sums, low_tokens, low_words, mine, theirs,
+    sums_a, sums_b, mlp_a, mlp_b, mlp_c,
     stat, stat_s, stat_r, zs, zr, gs, gr, ds, dr, loc, *rest,
 ):
     x, y, z, core = here()
@@ -1199,34 +1294,58 @@
         fetch(query_two_lin_in, lin_a), fetch(key_two_lin_in, lin_b), fetch(inv_in, inv),
     ]
     second = [
-        fetch(mixed_two_in, mixed_two), fetch(wa_in.at[:, in_cols], wa.at[:, in_cols]),
+        fetch(mixed_two_in, mixed), fetch(wa_in.at[:, in_cols], wa.at[:, in_cols]),
         fetch(words_in.reshape(SEQ, D), operand),
     ]
     third = [
         fetch(after_in, after_one), fetch(branch_in, branch_one), fetch(grad_in, grad_after),
-        fetch(mixed_in, mixed), fetch(tab_in, tab), fetch(tok_in.at[own_block], tok_own),
+        fetch(tab_in, tab), fetch(tok_in.at[own_block], tok_own),
     ]
-    greet(column(x, y, z, core) + rows + lines)
-    model[...] = sums[...]
+    arrive = knock(column(x, y, z, core) + rows + lines)
+    for row in (1, 8, 9, 10):
+        i = EARLY.index(row)
+        model[i : i + 1] = sums[row : row + 1]
     head_sums[...] = jnp.zeros_like(head_sums)
     for i in range(6):
         head_sums[10 + i : 11 + i] = bias_sum[0:1, i * HW : (i + 1) * HW]
     refs_a, refs_b, early_refs, late_refs, head_refs, rest = (
         rest[:14], rest[14:28], rest[28:32], rest[32:36], rest[36:40], rest[40:],
     )
-    (late, time_late), swap_refs = rest[:2], rest[2:]
+    (late, time_late, time_early, gram_sems), swap_refs = rest[:4], rest[4:]
+    late[...] = jnp.zeros_like(late)
+    n, w = 8 * ROWS, 2 * ROWS
+    halves = (slice(0, ROWS), slice(ROWS, 2 * ROWS))
+
+    stores = []
+
+    def save(ref, out):
+        copy = pltpu.make_async_copy(ref, out, keep.at[len(stores)])
+        copy.start()
+        stores.append(copy)
+
+    def new_narrow(j, ref, part, col):
+        rows = halves[part]
+        grad = jnp.concatenate([ref[i].astype(F32)[rows, col : col + HW] for i in (0, 1)], 1)
+        old = in_m[j] if j < 6 else out_m[:, j - 6, :]
+        narrow[j * ROWS : (j + 1) * ROWS] = MOMENTUM * old + grad
+
+    def new_wide(j, thirds):
+        chips = [jnp.concatenate([ref[i].astype(F32)[rows] for ref, rows in thirds], 1) for i in (0, 1)]
+        wide[j * ROWS : (j + 1) * ROWS] = MOMENTUM * mlp_m[:, j, :] + join_hidden(*chips)
+
     hidden_rows = [
         swap_rows(src, dst, *swap_refs[3 * i : 3 * i + 3])
         for i, (src, dst) in enumerate(((owned_a, mlp_a), (owned_b, mlp_b), (owned_c, mlp_c)))
     ]
-    for job in hidden_rows:
-        advance(job)
     grads_a, grads_b = refs_a[0], refs_b[0]
     job_a = reduce_batch(grads_a, sums_a, *refs_a[1:])
     job_b = reduce_batch(grads_b, sums_b, *refs_b[1:])
     stats = Stats(stat, stat_s, stat_r)
     drains = []
 
+    arrive()
+    send_result, wait_result = deliver(result, out_result, ds.at[2], dr.at[2], loc.at[29])
+    send_result()
     for copy in first:
         copy.wait()
     held[...] = product(low_wide[...], wa[:, W_CROSS]).astype(BF)
@@ -1241,6 +1360,8 @@
             jnp.sum(lin_b[...] * (gk[...] * (1.0 + heads[9:10])), -1, keepdims=True),
         ],
     )
+    for job in hidden_rows:
+        advance(job)
     head_sums[8:9] = column_sum(gq[...] * lin_a[...] * inverse_query_two)
     head_sums[9:10] = column_sum(gk[...] * lin_b[...] * inverse_key_two)
     low = gv[...].astype(BF)
@@ -1248,7 +1369,7 @@
     head_sums[7:8] = column_sum(low)
     for copy in second:
         copy.wait()
-    weight_grad(low_wide, mixed_two[...], grads_a, 1, HW)
+    weight_grad(low_wide, mixed[...], grads_a, 1, HW)
     dot_query, dot_key = dots()
     low = root_back(lin_a[...], inverse_query_two, gq[...] * (1.0 + heads[8:9]), dot_query)
     grad_query[...] = low
@@ -1259,7 +1380,7 @@
     head_sums[6:7] = column_sum(low)
     selfs = [
         fetch(query_rot_in, qa), fetch(key_rot_in, ka), fetch(value_low_in, va),
-        fetch(query_lin_in, lin_a), fetch(key_lin_in, lin_b),
+        fetch(query_lin_in, lin_a), fetch(key_lin_in, lin_b), fetch(mixed_in, mixed),
     ]
     weight_grad(operand, grad_kv[...], grads_a, 0, 0)
     next_operand = fetch(three_in, operand)
@@ -1274,20 +1395,21 @@
 
     total = cross.total()
     normed, inverse = plain_norm(after_one[...])
-    model[4:5] = column_sum(total)
-    model[3:4] = column_sum(total * normed)
+    model[3 : 4] = column_sum(total)
+    model[2 : 3] = column_sum(total * normed)
     value = grad_after[...] + norm_back(total * (1.0 + vec[V_GAIN : V_GAIN + 1]), normed, inverse)
     grad_after[...] = value
-    model[7:8] = column_sum(value * branch_one[...])
+    model[4 : 5] = column_sum(value * branch_one[...])
     low = (value * vec[2:3]).astype(BF)
-    model[0:1] = column_sum(low)
+    model[0 : 1] = column_sum(low)
     spread = Spread(low_wide, low, gs, gr)
     drains.append(spread)
     advance(job_a)
     spread.relay()
-    early = model_job(model, time_out, *early_refs)
+    early = model_job(model, time_early, *early_refs)
     advance(early)
     spread.wait()
+    advance(job_a)
     word_sum = Scatter(part_words, blocks.at[1], zs.at[1], zr.at[1]).held()
     drains.append(word_sum)
 
@@ -1319,6 +1441,7 @@
     advance(early)
     dot_query, dot_key = dots()
     word_sum.relay()
+    advance(job_a)
     for i, (lin, inverse, ref, dot) in enumerate(
         ((lin_a, inverse_query, gq, dot_query), (lin_b, inverse_key, gk, dot_key))
     ):
@@ -1327,54 +1450,92 @@
         head_sums[i : i + 1] = column_sum(low)
     token_sum = Scatter(part_cross, blocks.at[0], zs.at[2], zr.at[2]).product(grad_qkv, wa[:, W_QKV])
     drains.append(token_sum)
+    advance(job_a)
     head_total = head_job(head_sums, head_out, *head_refs)
     advance(head_total)
-    advance(job_a)
-    advance(early)
     weight_grad(operand, grad_qkv[:, : 2 * HW], grads_b, 0, 0)
     weight_grad(operand, grad_qkv[:, 2 * HW :], grads_b, 1, 0)
     advance(job_b)
     token_sum.relay()
-    advance(head_total)
-    advance(job_a)
-    advance(early)
-    advance(job_b)
+    low_words[...] = word_sum.total().astype(BF)
+    send_words, wait_words = deliver(low_words, out_words, ds.at[0], dr.at[0], loc.at[30])
+    send_words()
     advance(head_total)
     for job in hidden_rows:
         finish(job)
+    top, bottom = halves
+    new_wide(0, ((mlp_b, bottom), (mlp_c, top), (mlp_c, bottom)))
+    new_wide(1, ((mlp_a, top), (mlp_a, bottom), (mlp_b, top)))
+    save(wide, wide_out)
+    advance(job_b)
+    mine[:n, n:] = jnp.zeros((n, w), F32)
+    mine[n:, :n] = jnp.zeros((w, n), F32)
+    mine[n:, n:] = gram_of(wide[...])
+    advance(early)
 
     total = token_sum.total()
     normed, inverse = plain_norm(tok_own[...].astype(F32))
-    for i, row in enumerate((column_sum(total), column_sum(total * normed))):
+    for i, row in enumerate((column_sum(total), column_sum(total * normed), sums[2:3])):
         for k in range(SIDE):
             late[SIDE * i + k : SIDE * i + k + 1] = row[:, k * HW : (k + 1) * HW]
     late_total = model_job(late, time_late, *late_refs)
     advance(late_total)
+    advance(job_b)
     value = grad_after[...] + norm_back(total * (1.0 + vec[1:2]), normed, inverse)
     low_tokens[...] = value.astype(BF)
     send_tokens, wait_tokens = deliver(low_tokens, out_tokens, ds.at[1], dr.at[1], loc.at[31])
+    send_tokens()
+    advance(head_total)
     advance(late_total)
-    send_tokens()
-    low_words[...] = word_sum.total().astype(BF)
-    advance(late_total)
-    finish(early)
+    advance(early)
     advance(job_b)
     advance(late_total)
     finish(job_a)
+    for j, ref, part, col in ((3, sums_a, 1, 0), (4, sums_a, 0, 0), (5, sums_a, 0, HW), (7, sums_a, 1, HW)):
+        new_narrow(j, ref, part, col)
     advance(head_total)
     advance(job_b)
+    advance(late_total)
+    finish(early)
+    finish(job_b)
+    for j, ref, part, col in ((0, sums_b, 0, 0), (1, sums_b, 0, HW), (2, sums_b, 1, 0), (6, sums_b, 1, HW)):
+        new_narrow(j, ref, part, col)
+    save(narrow, narrow_out)
+    mine[:n, :n] = gram_of(narrow[...])
+    same, _ = block_mask(10 * ROWS)
+    blocks_only = jnp.where(same, mine[...], 0.0)
+    compact = blocks_only[:ROWS]
+    for j in range(1, 10):
+        compact = compact + blocks_only[j * ROWS : (j + 1) * ROWS]
+    theirs[0] = compact
+    swap = remote(theirs.at[0], theirs.at[1], gram_sems.at[0], gram_sems.at[1], chip(x, y, z + 2, core))
+    swap.start()
     finish(late_total)
     finish(head_total)
-    wait_tokens()
-    finish(job_b)
-    model_out[...] = early_refs[1][8]
-    for i in range(2):
+    save(head_out, head_sum_out)
+    for i, row in enumerate(EARLY):
+        model_out[row : row + 1] = early_refs[1][8, i : i + 1]
+        if row > 4:
+            for clip in (0, 1):
+                time_out[row - 5, clip : clip + 1] = time_early[clip, i : i + 1]
+    for i, row in enumerate(LATE):
         for k in range(SIDE):
             cols = slice(k * HW, (k + 1) * HW)
-            row = slice(SIDE * i + k, SIDE * i + k + 1)
-            model_out[5 + i : 6 + i, cols] = late_refs[1][8, row]
-            for clip in (0, 1):
-                time_out[clip, 5 + i : 6 + i, cols] = time_late[clip, row]
+            part = slice(SIDE * i + k, SIDE * i + k + 1)
+            model_out[row : row + 1, cols] = late_refs[1][8, part]
+            if row > 4:
+                for clip in (0, 1):
+                    time_out[row - 5, clip : clip + 1, cols] = time_late[clip, part]
+    save(time_out, time_sum_out)
+    save(model_out, model_sum_out)
+    wait_result()
+    wait_tokens()
+    wait_words()
+    swap.wait()
+    gram[...] = theirs[0] + theirs[1]
+    save(gram, gram_out)
+    for copy in stores:
+        copy.wait()
     for transfer in drains:
         transfer.drain()
 
@@ -1387,29 +1548,33 @@
     wide = pltpu.VMEM((SEQ, D), BF)
     block = pltpu.VMEM((TOK, D), F32)
     low_block = pltpu.VMEM((TOK, D), BF)
-    summed = sds((2, PAIR, BATCH), F32)
+    summed = pltpu.VMEM((2, PAIR, BATCH), BF)
+    size = 10 * ROWS
+    square = pltpu.VMEM((size, size), F32)
     outs = [
-        (sds((2, TOK, D), BF), HB), (sds((TOK, D), BF), VM), (sds((2, 16, D), F32), VM),
-        (sds((16, D), F32), VM), (sds((2, 16, HW), F32), VM), (summed, VM), (summed, VM),
-        *[(sds((2, PAIR, BATCH), BF), VM)] * 3,
+        *[(sds((2, TOK, D), BF), HB)] * 3, (sds((6, 2, D), F32), VM),
+        (sds((16, D), F32), VM), (sds((2, 16, HW), F32), VM), (sds((8 * ROWS, 2 * HW), F32), VM),
+        (sds((2 * ROWS, WIDE), F32), VM), (sds((ROWS, size), F32), VM),
     ]
     batch = [pltpu.VMEM(GRADS, BF), *reduce_scratch()]
     return pl.pallas_call(
         backward_kernel,
         out_shape=[shape for shape, _ in outs],
         in_specs=[HB] * len(hbm) + [VM] * len(vmem),
-        out_specs=[spec for _, spec in outs],
+        out_specs=[HB] * len(outs),
         scratch_shapes=[
-            pltpu.VMEM((D, ATTN), BF), wide, block, block, lin, lin, low, low, low, low, low, wide,
+            *[pltpu.VMEM(shape.shape, shape.dtype) for shape, _ in outs[3:]], dma((6,)),
+            pltpu.VMEM((D, ATTN), BF), wide, block, block, lin, lin, low, low, low, low, wide,
             low_block, block, pltpu.VMEM((SIDE, TOK, HEAD), F32), pltpu.VMEM((SEQ, 128), F32),
             low, pltpu.VMEM((SEQ, 2 * HW), BF), pltpu.VMEM((SEQ, 3 * HW), BF), wide, wide,
-            pltpu.VMEM((2, 3, TOK, D), BF), low, lin, lin, lin, pltpu.VMEM((16, D), F32),
-            pltpu.VMEM((16, HW), F32), low_block,
+            pltpu.VMEM((2, 3, TOK, D), BF), low, lin, lin, lin, pltpu.VMEM((8, D), F32),
+            pltpu.VMEM((16, HW), F32), low_block, low_block, square, pltpu.VMEM((2, ROWS, size), F32),
+            summed, summed, summed, summed, summed,
             pltpu.VMEM((2, 4, 8, SEQ), F32),
             dma((2, 3)), dma((2, 3)), dma((3, 6)), dma((3, 6)), dma((6,)), dma((6,)), dma((3, 2)),
-            dma((3, 2)), dma((32,)), *batch, *batch, *model_scratch(16, D),
-            *model_scratch(8, HW), *head_scratch(), pltpu.VMEM((8, HW), F32), pltpu.VMEM((2, 8, HW), F32),
-            *swap_sems(), *swap_sems(), *swap_sems(),
+            dma((3, 2)), dma((32,)), *batch, *batch, *model_scratch(8, D),
+            *model_scratch(16, HW), *head_scratch(), pltpu.VMEM((16, HW), F32), pltpu.VMEM((2, 16, HW), F32),
+            pltpu.VMEM((2, 8, D), F32), dma((2,)), *swap_sems(), *swap_sems(), *swap_sems(),
         ],
         compiler_params=params(2),
         name="backward",
@@ -1434,7 +1599,7 @@
 
 def newton_factor(gram, size):
     same, eye = block_mask(size)
-    gram = jnp.where(same, gram, 0.0)
+    gram = jnp.where(same, jnp.concatenate([gram] * (size // ROWS), 0), 0.0)
     diagonal = jnp.where(eye, gram, 0.0)
     by_row = jnp.sum(diagonal, 1, keepdims=True)
     by_col = jnp.sum(diagonal, 0, keepdims=True)
@@ -1453,73 +1618,11 @@
     return whole * scale_col
 
 
-WIDE = 2 * FF_REAL
-
-
 def join_hidden(first, second):
     fill = jnp.zeros((first.shape[0], FF), F32)
     first = jnp.concatenate([first, fill], 1)
     second = pltpu.roll(jnp.concatenate([second, fill], 1), FF_REAL, 1)
     return (first + second)[:, :WIDE]
-
-
-def gram_kernel(
-    sum_a, sum_b, sum_c, attn_a, attn_b, in_m, out_m, mlp_m, words, narrow, wide, gram, out_words,
-    mine, theirs, send, recv, ds, dr, loc,
-):
-    x, y, z, core = here()
-    partner = chip(x, y, z + 2, core)
-    greet(column(x, y, z, core))
-    send_words, wait_words = deliver(words, out_words, ds, dr, loc.at[0])
-
-    def pair(ref, part, col):
-        rows = slice(part * ROWS, (part + 1) * ROWS)
-        return jnp.concatenate([ref[0, rows, col : col + HW], ref[1, rows, col : col + HW]], 1)
-
-    n, w = 8 * ROWS, 2 * ROWS
-    for j, (ref, part, col) in enumerate(
-        ((attn_b, 0, 0), (attn_b, 0, HW), (attn_b, 1, 0), (attn_a, 1, 0), (attn_a, 0, 0), (attn_a, 0, HW))
-    ):
-        narrow[j * ROWS : (j + 1) * ROWS] = MOMENTUM * in_m[j] + pair(ref, part, col)
-    for j, ref in enumerate((attn_b, attn_a)):
-        narrow[(6 + j) * ROWS : (7 + j) * ROWS] = MOMENTUM * out_m[:, j, :] + pair(ref, 1, HW)
-    mine[:n, :n] = gram_of(narrow[...])
-    top, bottom = slice(0, ROWS), slice(ROWS, 2 * ROWS)
-    for j, thirds in enumerate(
-        (((sum_b, bottom), (sum_c, top), (sum_c, bottom)), ((sum_a, top), (sum_a, bottom), (sum_b, top)))
-    ):
-        chips = [jnp.concatenate([ref[i].astype(F32)[rows] for ref, rows in thirds], 1) for i in (0, 1)]
-        wide[j * ROWS : (j + 1) * ROWS] = MOMENTUM * mlp_m[:, j, :] + join_hidden(*chips)
-    mine[n:, n:] = gram_of(wide[...])
-    mine[:n, n:] = jnp.zeros((n, w), F32)
-    mine[n:, :n] = jnp.zeros((w, n), F32)
-    copy = remote(mine, theirs, send.at[0], recv.at[0], partner)
-    copy.start()
-    send_words()
-    copy.wait()
-    gram[...] = mine[...] + theirs[...]
-    wait_words()
-
-
-def gram_step(args, cid):
-    sds = jax.ShapeDtypeStruct
-    dma = pltpu.SemaphoreType.DMA
-    size = 10 * ROWS
-    return pl.pallas_call(
-        gram_kernel,
-        out_shape=[
-            sds((8 * ROWS, 2 * HW), F32), sds((2 * ROWS, WIDE), F32), sds((size, size), F32),
-            sds((2, TOK, D), BF),
-        ],
-        in_specs=[VM] * len(args),
-        out_specs=[VM] * 3 + [HB],
-        scratch_shapes=[
-            pltpu.VMEM((size, size), F32), pltpu.VMEM((size, size), F32), dma((1,)), dma((1,)),
-            dma((2,)), dma((2,)), dma((1,)),
-        ],
-        compiler_params=params(cid),
-        name="gram",
-    )(*args)
 
 
 def finish_kernel(
@@ -1538,9 +1641,7 @@
                 pltpu.make_async_copy(block.at[2 * i + clip], dst.at[clip], stores.at[2 * i + clip])
             )
             copies[-1].start()
-    for i in range(6):
-        for clip in (0, 1):
-            out_time[i, clip : clip + 1] = time_sum[clip, 5 + i : 6 + i]
+    out_time[...] = time_sum[...]
     value = MOMENTUM * head_m[...] + jnp.concatenate([head_sum[0, :10], head_sum[1, :10]], 1)
     new_head_m[...] = value
     new_head[...] = head_w[...] - RATE_VECTOR * value
@@ -1589,27 +1690,18 @@
     )(*args)
 
 
-def rope_tables(places):
-    pair_index = jnp.arange(HEAD // 2, dtype=jnp.int32)
-    side_pairs = HEAD // 6
-    frame_pairs = (HEAD - 4 * side_pairs) // 2
-    part_of = (pair_index >= frame_pairs).astype(jnp.int32) + (
-        pair_index >= frame_pairs + side_pairs
-    ).astype(jnp.int32)
-    offset = jnp.where(
-        part_of == 0, 0, jnp.where(part_of == 1, frame_pairs, frame_pairs + side_pairs)
-    ).astype(jnp.int32)
-    extent = jnp.where(part_of == 0, 2 * frame_pairs, 2 * side_pairs).astype(jnp.float32)
-    frequency = jnp.exp(
-        (pair_index - offset).astype(jnp.float32) * (-2.0 * math.log(10000.0)) / extent
-    )
-    chosen = (
-        places[0][:, None] * (part_of == 0)
-        + places[1][:, None] * (part_of == 1)
-        + places[2][:, None] * (part_of == 2)
-    )
-    angles = chosen.astype(jnp.float32) * frequency
-    return (jnp.cos(angles), jnp.sin(angles))
+def rope_rates():
+    pair = np.arange(HEAD // 2)
+    side = HEAD // 6
+    frame = (HEAD - 4 * side) // 2
+    part = (pair >= frame).astype(np.int32) + (pair >= frame + side)
+    offset = np.array([0, frame, frame + side])[part]
+    extent = np.array([2 * frame, 2 * side, 2 * side])[part]
+    rate = np.exp((pair - offset) * (-2.0 * math.log(10000.0)) / extent).astype(np.float32)
+    rates = np.zeros((8, HEAD), np.float32)
+    for component in range(3):
+        rates[component] = np.tile(np.where(part == component, rate, 0.0), 2)
+    return jnp.asarray(rates)
 
 
 def plain_norm(values):
@@ -1643,47 +1735,27 @@
     model_vectors, up_bias, attn_in_moment, attn_out_moment, mlp_moment, head_moment, model_moment,
     up_moment,
 ):
-    x, y, z, core = here()
-    zl = lax.rem(z, 2)
-
-    low_in = attn_in.astype(BF).reshape(ROWS, 6, 2, HW).transpose(2, 0, 1, 3).reshape(2, ROWS, -1)
-    low_out = attn_out.astype(BF).reshape(ROWS, 2, 2, HW).transpose(2, 0, 1, 3).reshape(2, ROWS, -1)
-    send_attn = jnp.concatenate([low_in, low_out], -1).reshape(2, ROWS, 2, ATTN // 2)
-    send_attn = send_attn.transpose(0, 2, 1, 3).reshape(2, PAIR, ATTN // 2)
-    send_mlp = jnp.pad(
-        mlp.astype(BF).reshape(ROWS, 2, 2, FF_REAL).transpose(2, 1, 0, 3),
-        ((0, 0), (0, 0), (0, 0), (0, FF - FF_REAL)),
-    ).reshape(2, PAIR, FF)
-    cosine, sine = rope_tables(positions.reshape(3, 2 * TOK))
-    table = jnp.concatenate([cosine, sine], -1).reshape(2, TOK, HEAD)
-
-    heads = jnp.pad(lax.dynamic_slice(head_vectors, (0, zl * HW), (10, HW)), ((0, 6), (0, 0)))
-    bias_up = jnp.pad(lax.dynamic_slice(up_bias, (zl * FF_REAL,), (FF_REAL,)), (0, FF - FF_REAL))
-    modulation = model_vectors[5:] + lax.dynamic_index_in_dim(time_embedding, core, 0, False)
-    shift_one, scale_one, gate_one, shift_two, scale_two, gate_two = [modulation[i] for i in range(6)]
-    vectors = jnp.pad(jnp.concatenate([modulation, model_vectors[:5]], 0), ((0, 5), (0, 0)))
-
+    swap = lambda v: v.transpose(1, 0, 2)
     (
-        w_attn, w_up, w_down, cot_all, tab_all, input_one, input_three, input_mlp, query_lin, key_lin,
+        w_attn, w_up, w_down, cot_all, heads, vectors, tab_all, input_one, input_three, input_mlp, query_lin, key_lin,
         query_two_lin, key_two_lin, inv, query_rot, key_rot, value_low, query_two, key_two, value_two,
         mixed_low, mixed_two_low, branch_one, after_one, after_two, tok_all, txt_all,
     ) = forward(
-        send_attn, send_mlp, tokens, text, cotangent, table, heads, vectors,
-    )
-    low_two, grad_after, sums, up_sum, out_result, *owned = mlp_pass(
-        input_mlp, cot_all, w_up, w_down, after_two, vectors, bias_up[None]
-    )
-    out_tokens, low_words, time_sums, model_sums, head_totals, sums_a, sums_b, *mlp_sums = backward(
+        swap(attn_in), attn_out, mlp, tokens, text, cotangent, positions, rope_rates(),
+        swap(time_embedding), model_vectors, head_vectors,
+    )
+    low_two, grad_after, sums, up_sum, result, *owned = mlp_pass(
+        input_mlp, cot_all, w_up, w_down, after_two, vectors, up_bias.reshape(-1, 128)
+    )
+    out_result, out_tokens, out_words, time_sums, model_sums, head_totals, narrow, wide, gram = backward(
         [
             w_attn, low_two, after_one, branch_one, query_lin, key_lin, query_two_lin, key_two_lin,
             query_rot, key_rot, value_low, query_two, key_two, value_two, mixed_low, mixed_two_low,
-            txt_all, input_three, input_one, tok_all, grad_after, tab_all, inv,
+            txt_all, input_three, input_one, tok_all, grad_after, tab_all, inv, result,
         ],
-        [vectors, heads, sums, up_sum, *owned],
-    )
-    swap = lambda v: v.transpose(1, 0, 2)
-    narrow, wide, gram, out_words = gram_step(
-        [*mlp_sums, sums_a, sums_b, swap(attn_in_moment), attn_out_moment, mlp_moment, low_words], 3
+        [
+            vectors, heads, sums, up_sum, *owned, swap(attn_in_moment), attn_out_moment, mlp_moment,
+        ],
     )
     (
         new_in, new_out, new_mlp, new_in_m, new_out_m, new_mlp_m, new_head, new_model, new_up,

time: 364 us -> 328 us (0.901)
  Pallas kernels: 348 us -> 325 us
  local copies, waits for them, and re-layouts: 7.19 us -> 0 us
  other arithmetic: 4.22 us -> 0 us
    pallas_call x1 -> x0, Pallas kernels: 23.1 us -> none  [gram_step(): pl.pallas_call(gram_kernel, out_shape=[sds((8 * ROWS, 2 * HW), F32), sds(...]
    pallas_call x1, Pallas kernels: 83.9 us -> 68.5 us  [mlp_pass(): pl.pallas_call(mlp_kernel, out_shape=[shape for shape, _ in outs], in_spe...]
    pallas_call x1, Pallas kernels: 103 us -> 116 us  [backward(): pl.pallas_call(backward_kernel, out_shape=[shape for shape, _ in outs], i...]
where the time goes in v6:
time: 328 us; the launch traced here: 326 us
  Pallas kernels  325 us (99%)
    pallas_call x1, Pallas kernels, forward(): pl.pallas_call(forward_kernel, out_shape=weights + outs, in_specs=[VM, VM...  125 us
    pallas_call x1, Pallas kernels, backward(): pl.pallas_call(backward_kernel, out_shape=[shape for shape, _ in outs], i...  116 us
    pallas_call x1, Pallas kernels, mlp_pass(): pl.pallas_call(mlp_kernel, out_shape=[shape for shape, _ in outs], in_spe...  68.5 us
    pallas_call x1, Pallas kernels, finish_step(): pl.pallas_call(finish_kernel, out_shape=matrices + matrices + vectors + v...  15 us

profile of v6, /device:TPU:1, one launch (start us, length us, event | category | flops | bytes accessed | tf_op | source)
XLA Modules:
  0.0 325.9 jit_solution(7782565887110064053)
XLA Ops:
  0.6 125.0 %forward.1 = (bf16[1536,3072]{1,0:T(8,128)(2,1)}, bf16[1536,2304]{1,0:T(8,128)(2,1)}, bf16[1536,2304]{1,0:T(8,128)(2,1)}, bf16[4,128,1536]{2,1,0:T(8,128)(2,1)},...) custom-call(f32[6,24,768]{2,1,0:T(8,128)} %bitcast.10, ...), custom_call_target="tpu_custom_call" | custom-call | tf_op jit(solution)/shard_map/forward/pallas_call | solution.py:702
  125.6 68.5 %mlp.1 = (bf16[512,1536]{1,0:T(8,128)(2,1)}, f32[128,1536]{1,0:T(8,128)}, f32[16,1536]{1,0:T(8,128)}, f32[8,2304]{1,0:T(8,128)}, bf16[128,1536]{1,0:T(8,128)(2,1...) custom-call(bf16[512,1536]{1,0:T(8,128)(2,1)} %get-tuple-element.78.a_in, ...), custom_call_target="tpu_custom_call" | custom-call | tf_op jit(solution)/shard_map/mlp/pallas_call | solution.py:1153
  194.1 116.2 %backward.1 = (bf16[2,128,1536]{2,1,0:T(8,128)(2,1)}, bf16[2,128,1536]{2,1,0:T(8,128)(2,1)}, bf16[2,128,1536]{2,1,0:T(8,128)(2,1)}, f32[6,2,1536]{2,1,0:T(2,128)...) custom-call(bf16[1536,3072]{1,0:T(8,128)(2,1)} %get-tuple-element.77, ...), custom_call_target="tpu_custom_call" | custom-call | tf_op jit(solution)/shard_map/backward/pallas_call | solution.py:1560
  310.4 15.0 %finish.1 = (f32[6,24,768]{2,1,0:T(8,128)}, f32[24,2,768]{2,1,0:T(2,128)}, f32[24,2,4480]{2,1,0:T(2,128)}, f32[6,24,768]{2,1,0:T(8,128)}, f32[24,2,768]{2,1,0:T(...) custom-call(f32[192,768]{1,0:T(8,128)} %get-tuple-element.113.narrow, ...), custom_call_target="tpu_custom_call" | custom-call | tf_op jit(solution)/shard_map/finish/pallas_call | solution.py:1682

commit v7 on v6

--- a/solution.py
+++ b/solution.py
@@ -131,31 +131,21 @@
 
     one, two = {}, {}
     for part in (0, 1):
+        one[part, "far"] = push(part, 2, own.at[part], mine, (far_x, far_y)[part])
+    for part in (0, 1):
         a_next, a_prev = steps[part]
         one[part, "next"] = push(part, 0, own.at[part], mine, a_next)
         one[part, "prev"] = push(part, 1, own.at[part], mine, a_prev)
-        one[part, "far"] = push(part, 2, own.at[part], mine, (far_x, far_y)[part])
     for part in (0, 1):
+        to_sibling(part, 0, own.at[part], mine)
+    offsets = (0, -1, 1, 2)
+
+    def second_start(part, k):
         b_next, b_prev = steps[1 - part]
-        two[part, 0, "next"] = push(part, 4, own.at[part], mine, b_next)
-        two[part, 0, "prev"] = push(part, 5, own.at[part], mine, b_prev)
-        to_sibling(part, 0, own.at[part], mine)
-
-    def second_start(part, k, offset):
-        b_next, b_prev = steps[1 - part]
-        index = index_of(part, offset, 0)
-        src = place(part, index)
+        index = index_of(part, offsets[k], 0)
+        src = place(part, index) if k else own.at[part]
         two[part, k, "next"] = push(part, 4 + 4 * k, src, index, b_next)
         two[part, k, "prev"] = push(part, 5 + 4 * k, src, index, b_prev)
-        to_sibling(part, 4 * k, src, index)
-
-    offsets = (0, -1, 1, 2)
-    for part in (0, 1):
-        yield
-        one[part, "next"].wait_recv()
-        second_start(part, 1, -1)
-        one[part, "prev"].wait_recv()
-        second_start(part, 2, 1)
 
     def second_forward(part, k):
         b_next, b_prev = steps[1 - part]
@@ -175,20 +165,39 @@
         to_sibling(part, 4 * k + 3, place(part, index), index)
 
     for part in (0, 1):
-        yield
+        second_start(part, 0)
+    yield
+    for part in (0, 1):
+        one[part, "next"].wait_recv()
+        one[part, "prev"].wait_recv()
+        second_start(part, 1)
+        for k in (1, 2):
+            index = index_of(part, offsets[k], 0)
+            to_sibling(part, 4 * k, place(part, index), index)
+    yield
+    for part in (0, 1):
         second_forward(part, 0)
+        second_start(part, 2)
+    yield
     for part in (0, 1):
-        yield
         one[part, "far"].wait_recv()
-        second_start(part, 3, 2)
-    for k in (1, 2, 3):
-        for part in (0, 1):
-            yield
-            second_forward(part, k)
-        for part in (0, 1):
-            second_finish(part, k - 1)
+        index = index_of(part, 2, 0)
+        to_sibling(part, 12, place(part, index), index)
+        second_forward(part, 1)
+        second_start(part, 3)
+    yield
     for part in (0, 1):
-        yield
+        second_forward(part, 2)
+        second_finish(part, 0)
+    yield
+    for part in (0, 1):
+        second_forward(part, 3)
+        second_finish(part, 1)
+    yield
+    for part in (0, 1):
+        second_finish(part, 2)
+    yield
+    for part in (0, 1):
         second_finish(part, 3)
     yield
     for copy in sends:
@@ -572,21 +581,21 @@
         input_one[block_slice(i)] = (normed * (1.0 + vec[1:2]) + vec[0:1]).astype(BF)
         return carry
 
-    advance(gather_attn, 4)
+    advance(gather_attn, 2)
     acts[3][0]()
-    advance(gather_attn, 2)
+    advance(gather_attn, 1)
     acts[0][1]()
     lax.fori_loop(0, 2, norm_block, 0)
-    advance(gather_attn, 2)
+    advance(gather_attn, 1)
     lax.fori_loop(2, 4, norm_block, 0)
     save(input_one, tok_all)
-    advance(gather_attn, 2)
+    advance(gather_attn, 1)
     mlp_wait(own_mlp)
     locals_ = []
     for part in (0, 1):
         locals_.append(pltpu.make_async_copy(own_mlp.at[part], mlp_place(part, mine), loc.at[6, part]))
         locals_[-1].start()
-    advance(gather_attn, 2)
+    advance(gather_attn, 1)
     gather_mlp = gather_xy(own_mlp, mlp_place, ms, mr, js, jr)
     advance(gather_mlp)
     finish(gather_attn)
@@ -625,15 +634,15 @@
         ):
             value = lin[:, cols] * inverse * (1.0 + heads[gain : gain + 1, cols])
             out[:, cols] = (value * cosine + swap_halves(value) * sine).astype(BF)
-    advance(gather_mlp, 2)
+    advance(gather_mlp, 1)
     attend_clip(query_rot, key_rot, value_low, mixed)
     scatter = Scatter(part_one, blocks.at[0], zs.at[0], zr.at[0]).product(mixed, wa[:, W_SELF])
     drains = [scatter]
     key_two[...] = (key_two_lin[...] * inverse_key_two * (1.0 + heads[9:10])).astype(BF)
     save(query_rot, key_rot, key_two, mixed)
+    advance(gather_mlp, 1)
+    scatter.relay()
     advance(gather_mlp, 2)
-    scatter.relay()
-    advance(gather_mlp, 5)
     branch = scatter.total() + vec[V_SELF : V_SELF + 1]
     branch_one[...] = branch
     after = tok_all[block_of(z)].astype(F32) + vec[2:3] * branch
@@ -647,7 +656,7 @@
     )
     drains.append(spread)
     save(branch_one, after_one)
-    advance(gather_mlp, 2)
+    advance(gather_mlp, 1)
     spread.relay()
     finish(gather_mlp)
     spread.wait()
@@ -972,7 +981,7 @@
 def mlp_kernel(
     a_in, cot_all, w_up, w_down, after_in, vec, up_bias,
     low_out, grad_out, sums_out, bias_out, result_out, owned_a_out, owned_b_out, owned_c_out,
-    grad_after, sums, bias_sum, owned_a, owned_b, owned_c, keep, a, low, ahead, behind, hidden, act, back, acc, part, after_two, low_two, result, dy_own,
+    grad_after, sums, bias_sum, owned_a, owned_b, owned_c, keep, a, low, ahead, behind, hidden, act, back, acc, part, part_back, after_two, low_two, result, dy_own,
     blocks, bias, zs, zr, gs, gr, loc, ring, gate_core, gate_chips, *rest,
 ):
     x, y, z, core = here()
@@ -1058,7 +1067,7 @@
         elif n % 3 == 1:
             acc[...] += moved
         else:
-            part[...] = (acc[...] + moved).astype(BF)
+            (part, part_back)[n // 3][...] = (acc[...] + moved).astype(BF)
         if n < 3:
             aheads[n + 3] = load_ahead(n + 3)
         if n < 4:
@@ -1078,37 +1087,36 @@
     sums[2:3] = column_sum(low[own_rows])
     step(1)
     third_grads(0, 0, 0)
+    third_grads(1, 0, 1)
+    arrive()
+    advance(jobs[0])
     step(2)
-    arrive()
     down_sum = Scatter(part, blocks.at[0], zs.at[0], zr.at[0]).held()
-    third_grads(1, 0, 1)
     advance(jobs[0])
     third_grads(2, 1, 0)
     step(3)
     advance(jobs[0])
-    down_sum.relay()
     third_grads(3, 1, 1)
     advance(jobs[1])
+    down_sum.relay()
     step(4)
     advance(jobs[0])
+    advance(jobs[1])
+    step(5)
+    back_sum = Scatter(part_back, blocks.at[1], zs.at[1], zr.at[1]).held()
+    save(bias_sum, bias_out)
+    third_grads(4, 2, 0)
+    third_grads(5, 2, 1)
+    advance(jobs[2])
+    finish(jobs[0])
+    save(owned_a, owned_a_out)
+    back_sum.relay()
     advance(jobs[1])
     fetch_after.wait()
     branch = down_sum.total() + vec[V_DOWN : V_DOWN + 1]
     result[...] = (after_two[...] + vec[5:6] * branch).astype(BF)
     save(result, result_out)
     sums[10:11] = column_sum(dy[...] * branch)
-    down_sum.drain()
-    step(5)
-    save(bias_sum, bias_out)
-    back_sum = Scatter(part, blocks.at[1], zs.at[1], zr.at[1]).held()
-    third_grads(4, 2, 0)
-    advance(jobs[0])
-    third_grads(5, 2, 1)
-    advance(jobs[2])
-    advance(jobs[1])
-    back_sum.relay()
-    finish(jobs[0])
-    save(owned_a, owned_a_out)
     advance(jobs[2])
     advance(jobs[1])
     total = back_sum.total()
@@ -1135,6 +1143,7 @@
     store.wait()
     for copy in stores:
         copy.wait()
+    down_sum.drain()
     back_sum.drain()
     spread.drain()
 
@@ -1158,7 +1167,7 @@
         scratch_shapes=[
             *[pltpu.VMEM(outs[i][0].shape, outs[i][0].dtype) for i in (1, 2, 3, 5, 6, 7)], dma((7,)),
             wide, wide, pltpu.VMEM(GRADS, BF), tiles, pltpu.VMEM((2, SEQ, BATCH), F32), units, units,
-            pltpu.VMEM((SEQ, D), F32), wide, pltpu.VMEM((TOK, D), F32), wide, pltpu.VMEM((TOK, D), BF),
+            pltpu.VMEM((SEQ, D), F32), wide, wide, pltpu.VMEM((TOK, D), F32), wide, pltpu.VMEM((TOK, D), BF),
             pltpu.VMEM((TOK, D), F32),
             pltpu.VMEM((2, 3, TOK, D), BF), pltpu.VMEM((8, FF), F32), dma((2, 6)), dma((2, 6)), dma((6,)), dma((6,)),
             dma((5,)), dma((2, 2)), pltpu.SemaphoreType.REGULAR, pltpu.SemaphoreType.REGULAR,
@@ -1457,9 +1466,6 @@
     weight_grad(operand, grad_qkv[:, 2 * HW :], grads_b, 1, 0)
     advance(job_b)
     token_sum.relay()
-    low_words[...] = word_sum.total().astype(BF)
-    send_words, wait_words = deliver(low_words, out_words, ds.at[0], dr.at[0], loc.at[30])
-    send_words()
     advance(head_total)
     for job in hidden_rows:
         finish(job)
@@ -1484,18 +1490,21 @@
     value = grad_after[...] + norm_back(total * (1.0 + vec[1:2]), normed, inverse)
     low_tokens[...] = value.astype(BF)
     send_tokens, wait_tokens = deliver(low_tokens, out_tokens, ds.at[1], dr.at[1], loc.at[31])
+    low_words[...] = word_sum.total().astype(BF)
+    send_words, wait_words = deliver(low_words, out_words, ds.at[0], dr.at[0], loc.at[30])
+    advance(late_total)
     send_tokens()
-    advance(head_total)
-    advance(late_total)
-    advance(early)
     advance(job_b)
     advance(late_total)
+    send_words()
     finish(job_a)
     for j, ref, part, col in ((3, sums_a, 1, 0), (4, sums_a, 0, 0), (5, sums_a, 0, HW), (7, sums_a, 1, HW)):
         new_narrow(j, ref, part, col)
     advance(head_total)
+    advance(early)
     advance(job_b)
     advance(late_total)
+    advance(head_total)
     finish(early)
     finish(job_b)
     for j, ref, part, col in ((0, sums_b, 0, 0), (1, sums_b, 0, HW), (2, sums_b, 1, 0), (6, sums_b, 1, HW)):
@@ -1626,21 +1635,29 @@
 
 
 def finish_kernel(
-    narrow, wide, gram, in_w, out_w, mlp_w, head_w, head_m, model_w, model_m, up_w, up_m, head_sum,
-    model_sum, result, tokens, words, time_sum,
-    new_in, new_out, new_mlp, new_in_m, new_out_m, new_mlp_m, new_head, new_model, new_up,
-    new_head_m, new_model_m, new_up_m, out_result, out_tokens, out_words, out_time,
-    block, stores,
+    gram, head_w, head_m, model_w, model_m, up_w, up_m, head_sum, model_sum, time_sum,
+    narrow_in, wide_in, in_w_in, out_w_in, mlp_w_in, result, tokens_in, words_in,
+    new_head, new_model, new_up, new_head_m, new_model_m, new_up_m, out_time,
+    new_in_out, new_out_out, new_mlp_out, new_in_m_out, new_out_m_out, new_mlp_m_out, out_result,
+    out_tokens, out_words,
+    narrow, wide, in_w, out_w, mlp_w, low_result, tokens, words, block, new_in, new_out, new_mlp,
+    new_out_m, new_mlp_m, loads, stores,
 ):
-    out_result[...] = result[...]
+    fetched = []
+    for i, (src, dst) in enumerate(
+        (
+            (narrow_in, narrow), (wide_in, wide), (in_w_in, in_w), (out_w_in, out_w), (mlp_w_in, mlp_w),
+            (result, low_result), (tokens_in, tokens), (words_in, words),
+        )
+    ):
+        fetched.append(pltpu.make_async_copy(src, dst, loads.at[i]))
+        fetched[-1].start()
     copies = []
-    for i, (src, dst) in enumerate(((tokens, out_tokens), (words, out_words))):
-        for clip in (0, 1):
-            block[2 * i + clip] = src[clip].astype(F32)
-            copies.append(
-                pltpu.make_async_copy(block.at[2 * i + clip], dst.at[clip], stores.at[2 * i + clip])
-            )
-            copies[-1].start()
+
+    def save(ref, out):
+        copies.append(pltpu.make_async_copy(ref, out, stores.at[len(copies)]))
+        copies[-1].start()
+
     out_time[...] = time_sum[...]
     value = MOMENTUM * head_m[...] + jnp.concatenate([head_sum[0, :10], head_sum[1, :10]], 1)
     new_head_m[...] = value
@@ -1656,38 +1673,56 @@
     new_up[...] = up_w[...] - RATE_VECTOR * new_up_m[...]
     n, w = narrow.shape[0], wide.shape[0]
     factor = newton_factor(gram[...], n + w)
+    for copy in fetched:
+        copy.wait()
+    save(low_result, out_result)
+    for i, (src, dst) in enumerate(((tokens, out_tokens), (words, out_words))):
+        for clip in (0, 1):
+            block[2 * i + clip] = src[clip].astype(F32)
+            save(block.at[2 * i + clip], dst.at[clip])
     turned = times(factor[:n, :n], narrow[...])
     for j in range(6):
         rows = slice(j * ROWS, (j + 1) * ROWS)
-        new_in_m[j] = narrow[rows]
+        save(narrow.at[rows], new_in_m_out.at[j])
         new_in[j] = in_w[j] * (1.0 - RATE_IN * DECAY) - RATE_IN * turned[rows]
+    save(new_in, new_in_out)
     for j in range(2):
         rows = slice((6 + j) * ROWS, (7 + j) * ROWS)
         new_out_m[:, j, :] = narrow[rows]
         new_out[:, j, :] = out_w[:, j, :] * (1.0 - RATE_OUT * DECAY) - RATE_OUT * turned[rows]
+    save(new_out_m, new_out_m_out)
+    save(new_out, new_out_out)
+    for j in range(2):
+        new_mlp_m[:, j, :] = wide[j * ROWS : (j + 1) * ROWS]
+    save(new_mlp_m, new_mlp_m_out)
     turned = times(factor[n:, n:], wide[...])
     for j in range(2):
         rows = slice(j * ROWS, (j + 1) * ROWS)
-        new_mlp_m[:, j, :] = wide[rows]
         new_mlp[:, j, :] = mlp_w[:, j, :] * (1.0 - RATE_MLP * DECAY) - RATE_MLP * turned[rows]
+    save(new_mlp, new_mlp_out)
     for copy in copies:
         copy.wait()
 
 
-def finish_step(args):
+def finish_step(small, large):
     sds = jax.ShapeDtypeStruct
     matrices = [sds((6, ROWS, 2 * HW), F32), sds((ROWS, 2, 2 * HW), F32), sds((ROWS, 2, WIDE), F32)]
     vectors = [sds((10, 2 * HW), F32), sds((11, D), F32), sds((WIDE // 128, 128), F32)]
     blocks = [sds((2, TOK, D), BF), sds((2, TOK, D), F32), sds((2, TOK, D), F32)]
+    held = [pltpu.VMEM(v.shape, v.dtype) for v in large]
+    news = [pltpu.VMEM(v.shape, F32) for v in matrices + matrices[1:]]
     return pl.pallas_call(
         finish_kernel,
-        out_shape=matrices + matrices + vectors + vectors + blocks + [sds((6, 2, D), F32)],
-        in_specs=[VM] * len(args),
-        out_specs=[VM] * 13 + [HB] * 2 + [VM],
-        scratch_shapes=[pltpu.VMEM((4, TOK, D), F32), pltpu.SemaphoreType.DMA((4,))],
+        out_shape=vectors + vectors + [sds((6, 2, D), F32)] + matrices + matrices + blocks,
+        in_specs=[VM] * len(small) + [HB] * len(large),
+        out_specs=[VM] * 7 + [HB] * 9,
+        scratch_shapes=[
+            *held, pltpu.VMEM((4, TOK, D), F32), *news, pltpu.SemaphoreType.DMA((8,)),
+            pltpu.SemaphoreType.DMA((16,)),
+        ],
         compiler_params=pltpu.CompilerParams(vmem_limit_bytes=VMEM_LIMIT),
         name="finish",
-    )(*args)
+    )(*small, *large)
 
 
 def rope_rates():
@@ -1758,14 +1793,14 @@
         ],
     )
     (
-        new_in, new_out, new_mlp, new_in_m, new_out_m, new_mlp_m, new_head, new_model, new_up,
-        new_head_m, new_model_m, new_up_m, out_result, out_tokens, out_words, out_time,
+        new_head, new_model, new_up, new_head_m, new_model_m, new_up_m, out_time,
+        new_in, new_out, new_mlp, new_in_m, new_out_m, new_mlp_m, out_result, out_tokens, out_words,
     ) = finish_step(
         [
-            narrow, wide, gram, swap(attn_in), attn_out, mlp, head_vectors, head_moment, model_vectors,
-            model_moment, up_bias.reshape(-1, 128), up_moment.reshape(-1, 128), head_totals, model_sums, out_result,
-            out_tokens, out_words, time_sums,
-        ]
+            gram, head_vectors, head_moment, model_vectors, model_moment, up_bias.reshape(-1, 128),
+            up_moment.reshape(-1, 128), head_totals, model_sums, time_sums,
+        ],
+        [narrow, wide, swap(attn_in), attn_out, mlp, out_result, out_tokens, out_words],
     )
     return (
         out_result, out_tokens, out_words, swap(out_time), swap(new_in), new_out, new_mlp,

time: 328 us -> 323 us (0.985)
  Pallas kernels: 325 us -> 319 us
    pallas_call x1, Pallas kernels: 116 us -> 112 us  [backward(): pl.pallas_call(backward_kernel, out_shape=[shape for shape, _ in outs], i...]
    pallas_call x1, Pallas kernels: 68.5 us -> 72.4 us  [mlp_pass(): pl.pallas_call(mlp_kernel, out_shape=[shape for shape, _ in outs], in_spe...]
    pallas_call x1, Pallas kernels: 125 us -> 122 us  [forward(): pl.pallas_call(forward_kernel, out_shape=weights + outs, in_specs=[VM, VM...]
where the time goes in v7:
time: 323 us; the launch traced here: 320 us
  Pallas kernels  319 us (99%)
    pallas_call x1, Pallas kernels, forward(): pl.pallas_call(forward_kernel, out_shape=weights + outs, in_specs=[VM, VM...  122 us
    pallas_call x1, Pallas kernels, backward(): pl.pallas_call(backward_kernel, out_shape=[shape for shape, _ in outs], i...  112 us
    pallas_call x1, Pallas kernels, mlp_pass(): pl.pallas_call(mlp_kernel, out_shape=[shape for shape, _ in outs], in_spe...  72.4 us
    pallas_call x1, Pallas kernels, finish_step(): pl.pallas_call(finish_kernel, out_shape=vectors + vectors + [sds((6, 2, D...  13.3 us

profile of v7, /device:TPU:1, one launch (start us, length us, event | category | flops | bytes accessed | tf_op | source)
XLA Modules:
  0.0 319.9 jit_solution(13897017291885651861)
XLA Ops:
  0.6 121.5 %forward.1 = (bf16[1536,3072]{1,0:T(8,128)(2,1)}, bf16[1536,2304]{1,0:T(8,128)(2,1)}, bf16[1536,2304]{1,0:T(8,128)(2,1)}, bf16[4,128,1536]{2,1,0:T(8,128)(2,1)},...) custom-call(f32[6,24,768]{2,1,0:T(8,128)} %bitcast.10, ...), custom_call_target="tpu_custom_call" | custom-call | tf_op jit(solution)/shard_map/forward/pallas_call | solution.py:711
  122.2 72.4 %mlp.1 = (bf16[512,1536]{1,0:T(8,128)(2,1)}, f32[128,1536]{1,0:T(8,128)}, f32[16,1536]{1,0:T(8,128)}, f32[8,2304]{1,0:T(8,128)}, bf16[128,1536]{1,0:T(8,128)(2,1...) custom-call(bf16[512,1536]{1,0:T(8,128)(2,1)} %get-tuple-element.78.a_in, ...), custom_call_target="tpu_custom_call" | custom-call | tf_op jit(solution)/shard_map/mlp/pallas_call | solution.py:1162
  194.6 111.8 %backward.1 = (bf16[2,128,1536]{2,1,0:T(8,128)(2,1)}, bf16[2,128,1536]{2,1,0:T(8,128)(2,1)}, bf16[2,128,1536]{2,1,0:T(8,128)(2,1)}, f32[6,2,1536]{2,1,0:T(2,128)...) custom-call(bf16[1536,3072]{1,0:T(8,128)(2,1)} %get-tuple-element.77, ...), custom_call_target="tpu_custom_call" | custom-call | tf_op jit(solution)/shard_map/backward/pallas_call | solution.py:1569
  306.4 13.3 %finish.1 = (f32[10,768]{1,0:T(8,128)}, f32[11,1536]{1,0:T(8,128)}, f32[35,128]{1,0:T(8,128)}, f32[10,768]{1,0:T(8,128)}, f32[11,1536]{1,0:T(8,128)}, /*index=5*...) custom-call(f32[24,240]{1,0:T(8,128)} %get-tuple-element.113.gram, ...), custom_call_target="tpu_custom_call" | custom-call | tf_op jit(solution)/shard_map/finish/pallas_call | solution.py:1714

commit v8 on v7

--- a/solution.py
+++ b/solution.py
@@ -396,8 +396,8 @@
             self.stage(k)
         return self
 
-    def product(self, left, right):
-        for k in (2, 1, 3, 0):
+    def product(self, left, right, blocks=(2, 1, 3, 0)):
+        for k in blocks:
             rows = block_slice(block_of(self.z + k))
             self.part[rows] = contract_last(left[rows], right).astype(BF)
             self.stage(k)
@@ -1457,7 +1457,8 @@
         low = root_back(lin[...], inverse, ref[...] * (1.0 + heads[3 + i : 4 + i]), dot)
         grad_qkv[:, i * HW : (i + 1) * HW] = low
         head_sums[i : i + 1] = column_sum(low)
-    token_sum = Scatter(part_cross, blocks.at[0], zs.at[2], zr.at[2]).product(grad_qkv, wa[:, W_QKV])
+    token_sum = Scatter(part_cross, blocks.at[0], zs.at[2], zr.at[2])
+    token_sum.product(grad_qkv, wa[:, W_QKV], (2, 1, 3))
     drains.append(token_sum)
     advance(job_a)
     head_total = head_job(head_sums, head_out, *head_refs)
@@ -1466,6 +1467,7 @@
     weight_grad(operand, grad_qkv[:, 2 * HW :], grads_b, 1, 0)
     advance(job_b)
     token_sum.relay()
+    token_sum.product(grad_qkv, wa[:, W_QKV], (0,))
     advance(head_total)
     for job in hidden_rows:
         finish(job)

time: 323 us -> 322 us (level)
  no operation moved by 1% of the time
where the time goes in v8:
time: 322 us; the launch traced here: 320 us
  Pallas kernels  319 us (99%)
    pallas_call x1, Pallas kernels, forward(): pl.pallas_call(forward_kernel, out_shape=weights + outs, in_specs=[VM, VM...  122 us
    pallas_call x1, Pallas kernels, backward(): pl.pallas_call(backward_kernel, out_shape=[shape for shape, _ in outs], i...  112 us
    pallas_call x1, Pallas kernels, mlp_pass(): pl.pallas_call(mlp_kernel, out_shape=[shape for shape, _ in outs], in_spe...  72.4 us
    pallas_call x1, Pallas kernels, finish_step(): pl.pallas_call(finish_kernel, out_shape=vectors + vectors + [sds((6, 2, D...  13.3 us

profile of v8, /device:TPU:1, one launch (start us, length us, event | category | flops | bytes accessed | tf_op | source)
XLA Modules:
  0.0 319.9 jit_solution(7937900225681161576)
XLA Ops:
  0.6 121.5 %forward.1 = (bf16[1536,3072]{1,0:T(8,128)(2,1)}, bf16[1536,2304]{1,0:T(8,128)(2,1)}, bf16[1536,2304]{1,0:T(8,128)(2,1)}, bf16[4,128,1536]{2,1,0:T(8,128)(2,1)},...) custom-call(f32[6,24,768]{2,1,0:T(8,128)} %bitcast.10, ...), custom_call_target="tpu_custom_call" | custom-call | tf_op jit(solution)/shard_map/forward/pallas_call | solution.py:711
  122.2 72.4 %mlp.1 = (bf16[512,1536]{1,0:T(8,128)(2,1)}, f32[128,1536]{1,0:T(8,128)}, f32[16,1536]{1,0:T(8,128)}, f32[8,2304]{1,0:T(8,128)}, bf16[128,1536]{1,0:T(8,128)(2,1...) custom-call(bf16[512,1536]{1,0:T(8,128)(2,1)} %get-tuple-element.78.a_in, ...), custom_call_target="tpu_custom_call" | custom-call | tf_op jit(solution)/shard_map/mlp/pallas_call | solution.py:1162
  194.6 111.8 %backward.1 = (bf16[2,128,1536]{2,1,0:T(8,128)(2,1)}, bf16[2,128,1536]{2,1,0:T(8,128)(2,1)}, bf16[2,128,1536]{2,1,0:T(8,128)(2,1)}, f32[6,2,1536]{2,1,0:T(2,128)...) custom-call(bf16[1536,3072]{1,0:T(8,128)(2,1)} %get-tuple-element.77, ...), custom_call_target="tpu_custom_call" | custom-call | tf_op jit(solution)/shard_map/backward/pallas_call | solution.py:1571
  306.4 13.3 %finish.1 = (f32[10,768]{1,0:T(8,128)}, f32[11,1536]{1,0:T(8,128)}, f32[35,128]{1,0:T(8,128)}, f32[10,768]{1,0:T(8,128)}, f32[11,1536]{1,0:T(8,128)}, /*index=5*...) custom-call(f32[24,240]{1,0:T(8,128)} %get-tuple-element.113.gram, ...), custom_call_target="tpu_custom_call" | custom-call | tf_op jit(solution)/shard_map/finish/pallas_call | solution.py:1716
